TPU v7x, 32 devices: a whole 2x2x4 slice. The times are simulated.
32 devices in a mesh: grp: 4 (over y, x), par: 8 (over z, core).
Axes of the slice: x: 2, y: 2, z: 4, core: 2. Of those that a mesh axis runs over, the one named last changes fastest.
Arguments:
- particles: float32 [16, 1048576], P('grp', 'par'), may hold values from -6 to 6
- scores: float32 [16, 1048576], P('grp', 'par'), may hold values from -6 to 6
- kernel_width: float32 [1], replicated, may hold values from 1 to 4
Outputs:
- drive: float32 [16, 1048576], P('grp', 'par')
- repel: float32 [16, 1048576], P('grp', 'par')
All inputs are finite; a program needn't handle non-finite values.
Results may differ from a plain program's by a relative error of at most 0.000092.
Values sent between devices are 32-bit elements; how exact they have to be, the bound alone decides.
No kernel may reach another device: no remote copies, remote signals or barrier semaphores. Data moves between devices by JAX's collectives and lax.ppermute only.
A program may use at most 128 MiB of HBM per device.

v0:
```python
import jax
import jax.numpy as jnp
from jax import lax
from jax.sharding import PartitionSpec as P

P_SIZE = 1048576


def cross(left, right):
    return lax.dot_general(
        left,
        right,
        (((1,), (1,)), ((), ())),
        precision=lax.Precision.HIGHEST,
        preferred_element_type=jnp.float32,
    )


def weigh(kern, block):
    return jnp.dot(kern, block, precision=lax.Precision.HIGHEST, preferred_element_type=jnp.float32)


def shards(particles, scores, kernel_width):
    scale = kernel_width[0] * P_SIZE
    groups = lax.axis_size("grp")
    count = particles.shape[0] * groups
    own_norm = jnp.sum(particles * particles, axis=1)
    every_x, every_s = (
        lax.all_gather(particles, "grp", axis=0, tiled=True),
        lax.all_gather(scores, "grp", axis=0, tiled=True),
    )
    every_norm = jnp.sum(every_x * every_x, axis=1)
    partial_dist = own_norm[:, None] + every_norm[None, :] - 2.0 * cross(particles, every_x)
    dist = lax.psum(partial_dist, "par")
    kern = jnp.exp(-dist / scale)
    drive_sum = weigh(kern, every_s)
    pull = weigh(kern, every_x)
    weight = jnp.sum(kern, axis=1)
    drive = drive_sum / count
    repel = (particles * weight[:, None] - pull) / (count * kernel_width[0])
    return (drive, repel)


def solution(mesh):
    return jax.shard_map(
        shards,
        mesh=mesh,
        in_specs=(P("grp", "par"), P("grp", "par"), P()),
        out_specs=(P("grp", "par"), P("grp", "par")),
        check_vma=False,
    )
```

profile of v0, /device:TPU:0, one launch (start us, length us, event | category | flops | bytes accessed | tf_op | source)
XLA Modules:
  0.0 218.5 jit_solution(8304241457405959107)
XLA Ops:
  7.2 0.0 all-gather.5.cloned.1.call-start
  7.2 0.0 copy-start.1
  7.2 0.7 all-gather.5.cloned.1.call-update
  7.9 0.0 all-gather.7.cloned.1.call-start
  7.9 0.7 all-gather.7.cloned.1.call-update
  9.3 0.0 copy-done.1
  9.3 1.2 multiply_reduce_fusion.1
  10.5 89.7 %all-gather.5.cloned.1.call-done = f32[4,4,131072]{2,1,0:T(4,128)} async-done(((f32[1,4,131072]{2,1,0:T(4,128)}), f32[4,4,131072]{2,1,0:T(4,128)}) %all-gather.5.cloned.1.call-update) | async-done | bytes 8388624 | tf_op jit(solution)/shard_map/all_gather | solution.py:29
  100.2 7.0 %reshape.12 = f32[16,131072]{1,0:T(8,128)} reshape(f32[4,4,131072]{2,1,0:T(4,128)} %all-gather.5.cloned.1.call-done) | data formatting | bytes 16777216
  107.2 0.0 copy-start
  107.2 6.1 %multiply_reduce_fusion = f32[16]{0:T(128)S(1)} fusion(f32[16,131072]{1,0:T(8,128)} %reshape.12), kind=kLoop, calls=%fused_computation.3 | loop fusion | flops 4194288 | bytes 8388672 | tf_op jit(solution)/shard_map/reduce_sum | solution.py:32
  113.3 1.8 copy-done
  115.1 9.7 %fusion.1 = f32[4,16]{1,0:T(4,128)S(1)} fusion(f32[4,131072]{1,0:T(4,128)S(1)} %copy-done.1, f32[16,131072]{1,0:T(8,128)S(1)} %copy-done, f32[16]{0:T(128)S(1)} %multiply_reduce_fusion, f32[4]{0:T(128)S(1)} %multiply_reduce_fusion.1), kind=kOutput, calls=%fused_computation.6 | convolution fusion | flops 100663488 | bytes 10486096 | tf_op jit(solution)/shard_map/dot_general | solution.py:10
  124.9 16.5 %psum.7 = f32[4,16]{1,0:T(4,128)S(1)} all-reduce(f32[4,16]{1,0:T(4,128)S(1)} %fusion.1), channel_id=1, replica_groups=mesh['grp'=4,'par'=8] {'par'}, use_global_device_ids=true, to_apply=%region_2.0 | all-reduce | flops 64 | bytes 512 | tf_op jit(solution)/shard_map/psum | solution.py:34
  141.4 0.1 fusion.2
  141.5 48.2 %all-gather.7.cloned.1.call-done = f32[4,4,131072]{2,1,0:T(4,128)} async-done(((f32[1,4,131072]{2,1,0:T(4,128)}), f32[4,4,131072]{2,1,0:T(4,128)}) %all-gather.7.cloned.1.call-update) | async-done | bytes 8388624 | tf_op jit(solution)/shard_map/all_gather | solution.py:30
  189.7 7.0 %reshape.14 = f32[16,131072]{1,0:T(8,128)} reshape(f32[4,4,131072]{2,1,0:T(4,128)} %all-gather.7.cloned.1.call-done) | data formatting | bytes 16777216
  196.7 7.4 %convolution_multiply_fusion = f32[4,131072]{1,0:T(4,128)} fusion(f32[16,131072]{1,0:T(8,128)} %reshape.14, f32[4,16]{1,0:T(4,128)S(1)} %psum.7, f32[]{:T(128)} %bitcast.1), kind=kOutput, calls=%fused_computation.1 | convolution fusion | flops 101187712 | bytes 10486020 | tf_op jit(solution)/shard_map/dot_general | solution.py:20
  204.1 7.6 %fusion = f32[4,131072]{1,0:T(4,128)} fusion(f32[16,131072]{1,0:T(8,128)} %reshape.12, f32[4,131072]{1,0:T(4,128)S(1)} %copy-done.1, f32[]{:T(128)} %bitcast.3, f32[4]{0:T(128)S(1)} %fusion.2, f32[4,16]{1,0:T(4,128)S(1)} %psum.7, f32[]{:T(128)} %bitcast.1), kind=kOutput, calls=%fused_computation.2 | convolution fusion | flops 102236288 | bytes 12583192 | tf_op jit(solution)/shard_map/dot_general | solution.py:20
Async XLA Ops:
  7.2 93.0 %all-gather.5.cloned.1.call-start = ((), (), s32[]{:S(2)}) async-start(), calls=%async_computation | async-start | bytes 10485760 | tf_op jit(solution)/shard_map/all_gather | solution.py:29
  7.2 2.1 copy-start.1
  7.9 181.8 %all-gather.7.cloned.1.call-start = ((), (), s32[]{:S(2)}) async-start(), calls=%async_computation.1 | async-start | bytes 10485760 | tf_op jit(solution)/shard_map/all_gather | solution.py:30
  107.2 7.9 %copy-start = (f32[16,131072]{1,0:T(8,128)S(1)}, f32[16,131072]{1,0:T(8,128)}, u32[]{:S(2)}) copy-start(f32[16,131072]{1,0:T(8,128)} %reshape.12) | copy-start | bytes 25165828
Sparse Core Ops, SparseCore 0:
  9.8 90.2 all-gather.4
  102.0 87.5 all-gather.6
where the time goes:
time: 219 us
  waiting for transfers between devices  139 us (63%)
  matrix products  24.7 us (11%)
  blocking collectives  16.5 us (8%)
  local copies, waits for them, and re-layouts  15.9 us (7%)
  between operations  14.7 us (7%)
  other arithmetic  7.37 us (3%)
    all_gather x1, waiting for transfers between devices, shards(): lax.all_gather(particles, 'grp', axis=0, tiled=True)  89.7 us
    all_gather x1, waiting for transfers between devices, shards(): lax.all_gather(scores, 'grp', axis=0, tiled=True)  48.2 us
    psum x1, blocking collectives, shards(): dist = lax.psum(partial_dist, 'par')  16.5 us
    unnamed x6, local copies, waits for them, and re-layouts  15.9 us
    dot_general x2, matrix products, weigh(): jnp.dot(kern, block, precision=lax.Precision.HIGHEST, preferred_element_t...  15 us
    dot_general x1, matrix products, cross(): lax.dot_general(left, right, (((1,), (1,)), ((), ())), precision=lax.Prec...  9.74 us
    reduce_sum x1, other arithmetic, shards(): every_norm = jnp.sum(every_x * every_x, axis=1)  6.06 us
  transfers between devices with their start and end apart: 2, of which 2 were waited for; matrix products, arithmetic and copies ran while one was open for 11% of the time, Pallas kernels for 0%

commit v1 on v0

v1 whole, which is shorter than its diff:
```python
import functools

import jax
import jax.numpy as jnp
from jax import lax
from jax.experimental import pallas as pl
from jax.experimental.pallas import tpu as pltpu
from jax.sharding import PartitionSpec as P

P_SIZE = 1048576
LANES = 128
SUB = 8
VMEM_LIMIT = 48 * 2**20

SMEM_SPEC = pl.BlockSpec(memory_space=pltpu.SMEM)
VMEM_SPEC = pl.BlockSpec(memory_space=pltpu.VMEM)


def dense(block):
    rows, columns = block.shape
    return block.reshape(rows, columns // LANES, LANES).transpose(1, 0, 2).reshape(-1, LANES)


def undense(block, rows):
    return block.reshape(-1, rows, LANES).transpose(1, 0, 2).reshape(rows, -1)


def gram_kernel(rows, groups, me_ref, *refs):
    xs, out_ref, acc_ref = refs[:groups], refs[groups], refs[groups + 1]
    me = me_ref[0]
    count = rows * groups
    step = SUB * rows
    steps = xs[0].shape[0] // step

    def load(ref, t, i):
        return ref[pl.ds(t * step + i, SUB, stride=rows), :]

    for a in range(groups):
        for b in range(a, groups):
            pairs = [(i, j) for i in range(rows) for j in range(rows) if a != b or i <= j]

            def body(t, sums):
                left = [load(xs[a], t, i) for i in range(rows)]
                right = left if a == b else [load(xs[b], t, j) for j in range(rows)]
                return tuple(s + left[i] * right[j] for s, (i, j) in zip(sums, pairs))

            zero = jnp.zeros((SUB, LANES), jnp.float32)
            sums = lax.fori_loop(0, steps, body, (zero,) * len(pairs), unroll=2)
            for s, (i, j) in zip(sums, pairs):
                row = jnp.sum(s, axis=0, keepdims=True)
                left, right = (me ^ a) * rows + i, (me ^ b) * rows + j
                acc_ref[pl.ds(left * count + right, 1), :] = row
                if a != b or i != j:
                    acc_ref[pl.ds(right * count + left, 1), :] = row
    total = lax.dot_general(
        jnp.ones((SUB, LANES), jnp.float32),
        acc_ref[...],
        (((1,), (1,)), ((), ())),
        precision=lax.Precision.HIGHEST,
        preferred_element_type=jnp.float32,
    )
    out_ref[...] = total[:1]


def gram(me, xs, rows):
    groups = len(xs)
    count = rows * groups
    return pl.pallas_call(
        functools.partial(gram_kernel, rows, groups),
        out_shape=jax.ShapeDtypeStruct((1, count * count), jnp.float32),
        in_specs=[SMEM_SPEC] + [VMEM_SPEC] * groups,
        out_specs=VMEM_SPEC,
        scratch_shapes=[pltpu.VMEM((count * count, LANES), jnp.float32)],
        compiler_params=pltpu.CompilerParams(vmem_limit_bytes=VMEM_LIMIT),
        name="gram",
    )(me, *xs)


def weights_kernel(width_ref, gram_ref, drive_ref, repel_ref):
    width = width_ref[0]
    inner = gram_ref[...]
    count = inner.shape[0]
    diagonal = lax.broadcasted_iota(jnp.int32, inner.shape, 0) == lax.broadcasted_iota(jnp.int32, inner.shape, 1)
    norms = jnp.where(diagonal, inner, 0.0)
    dist = jnp.sum(norms, axis=1, keepdims=True) + jnp.sum(norms, axis=0, keepdims=True) - 2.0 * inner
    kern = jnp.exp(-dist / (width * P_SIZE))
    others = jnp.where(diagonal, 0.0, kern)
    drive_ref[...] = kern / count
    repel_ref[...] = jnp.where(diagonal, jnp.sum(others, axis=1, keepdims=True), -others) / (count * width)


def weights(width, inner):
    shape = jax.ShapeDtypeStruct(inner.shape, jnp.float32)
    return pl.pallas_call(
        weights_kernel,
        out_shape=(shape, shape),
        in_specs=[SMEM_SPEC, VMEM_SPEC],
        out_specs=(VMEM_SPEC, VMEM_SPEC),
        name="weights",
    )(width, inner)


def mix_kernel(rows, groups, dest, me_ref, coef_ref, *refs):
    xs, out_ref, splat_ref = refs[:groups], refs[groups], refs[groups + 1]
    me = me_ref[0]
    count = rows * groups
    for i in range(rows):
        for b in range(groups):
            for j in range(rows):
                value = coef_ref[(me ^ dest) * rows + i, (me ^ b) * rows + j]
                splat_ref[i * count + b * rows + j] = jnp.full((SUB, LANES), value, jnp.float32)
    step = SUB * rows
    steps = xs[0].shape[0] // step
    wide = 2 if steps % 2 == 0 else 1

    def body(t, carry):
        base = t * step * wide
        sums = [[None] * rows for _ in range(wide)]
        for b in range(groups):
            for j in range(rows):
                x = [xs[b][pl.ds(base + u * step + j, SUB, stride=rows), :] for u in range(wide)]
                for i in range(rows):
                    c = splat_ref[i * count + b * rows + j]
                    for u in range(wide):
                        term = c * x[u]
                        sums[u][i] = term if sums[u][i] is None else sums[u][i] + term
        for u in range(wide):
            for i in range(rows):
                out_ref[pl.ds(base + u * step + i, SUB, stride=rows), :] = sums[u][i]
        return carry

    lax.fori_loop(0, steps // wide, body, 0)


def mix(me, coef, xs, rows, dest, whole=False):
    groups = len(xs)
    count = rows * groups
    part = xs[0].shape
    return pl.pallas_call(
        functools.partial(mix_kernel, rows, groups, dest),
        out_shape=jax.ShapeDtypeStruct((part[0] * groups, LANES) if whole else part, jnp.float32),
        grid_spec=pltpu.PrefetchScalarGridSpec(
            num_scalar_prefetch=1,
            grid=(1,),
            in_specs=[SMEM_SPEC] + [pl.BlockSpec(part, lambda t, me: (0, 0))] * groups,
            out_specs=pl.BlockSpec(part, lambda t, me: (me[0] if whole else 0, 0)),
            scratch_shapes=[pltpu.VMEM((rows * count, SUB, LANES), jnp.float32)],
        ),
        compiler_params=pltpu.CompilerParams(vmem_limit_bytes=VMEM_LIMIT),
        name="mix",
    )(me, coef, *xs)


def shards(particles, scores, kernel_width):
    groups = lax.axis_size("grp")
    rows = particles.shape[0]
    count = rows * groups
    me = lax.axis_index("grp")
    place = me.astype(jnp.int32).reshape(1)
    x, s = dense(particles), dense(scores)
    part = x.shape[0] // groups

    def swap(block, k):
        return lax.ppermute(block, "grp", [(i, i ^ k) for i in range(groups)])

    def cut(block, k):
        return lax.dynamic_slice_in_dim(block, (me ^ k) * part, part, axis=0)

    def spread(block):
        return [cut(block, 0)] + [swap(cut(block, k), k) for k in range(1, groups)]

    xs = spread(x)
    xs, s = lax.optimization_barrier((xs, s))
    ss = spread(s)
    inner = lax.psum(gram(place, xs, rows), ("grp", "par")).reshape(count, count)
    to_drive, to_repel = weights(kernel_width, inner)

    def collect(coef, parts):
        back = [swap(mix(place, coef, parts, rows, k), k) for k in range(1, groups)]
        out = mix(place, coef, parts, rows, 0, whole=True)
        for k, block in enumerate(back, 1):
            out = lax.dynamic_update_slice_in_dim(out, block, (me ^ k) * part, axis=0)
        return undense(out, rows)

    repel = collect(to_repel, xs)
    drive = collect(to_drive, ss)
    return (drive, repel)


def solution(mesh):
    return jax.shard_map(
        shards,
        mesh=mesh,
        in_specs=(P("grp", "par"), P("grp", "par"), P()),
        out_specs=(P("grp", "par"), P("grp", "par")),
        check_vma=False,
    )
```

time: 219 us -> 147 us (0.67)
  waiting for transfers between devices: 139 us -> 49.6 us
  blocking collectives: 16.5 us -> 52.7 us
  matrix products: 24.7 us -> 0 us
  Pallas kernels: 0 us -> 20 us
  starting transfers between devices: 0.08 us -> 16 us
  between operations: 14.7 us -> 1.48 us
  local copies, waits for them, and re-layouts: 15.9 us -> 5.96 us
  other arithmetic: 7.37 us -> 0.7 us
    all_gather x2 -> x0, waiting for transfers between devices: 138 us -> none  [the longest x1 89.7 us: shards(): lax.all_gather(particles, 'grp', axis=0, tiled=True)]
    ppermute x0 -> x12, waiting for transfers between devices: none -> 49.6 us  [swap(): return lax.ppermute(block, 'grp', [(i, i ^ k) for i in range(groups)])]
    psum x1, blocking collectives: 16.5 us -> 52.7 us  [shards(): lax.psum(gram(place, xs, rows), ('grp', 'par')).reshape(count, count)]
    dot_general x3 -> x0, matrix products: 24.7 us -> none  [the longest x2 15 us: weigh(): jnp.dot(kern, block, precision=lax.Precision.HIGHEST, preferred_element_t...]
    pallas_call x0 -> x10, Pallas kernels: none -> 20 us  [the longest x8 16.2 us: mix(): pl.pallas_call(functools.partial(mix_kernel, rows, groups, dest), out_sha...]
    ppermute x0 -> x12, starting transfers between devices: none -> 16 us  [swap(): return lax.ppermute(block, 'grp', [(i, i ^ k) for i in range(groups)])]
    unnamed x6 -> x14, local copies, waits for them, and re-layouts: 15.9 us -> 2.02 us
    reduce_sum x3 -> x0, other arithmetic: 7.37 us -> none  [the longest x1 6.06 us: shards(): every_norm = jnp.sum(every_x * every_x, axis=1)]
  transfers between devices with their start and end apart: 2 -> 12, of which waited for: 2 -> 6; matrix products, arithmetic and copies ran while one was open for 11% -> 1% of each run, Pallas kernels for 0% -> 14%
where the time goes in v1:
time: 147 us; the launch traced here: 146 us
  blocking collectives  52.7 us (36%)
  waiting for transfers between devices  49.6 us (34%)
  Pallas kernels  20 us (14%)
  starting transfers between devices  16 us (11%)
  local copies, waits for them, and re-layouts  5.96 us (4%)
  between operations  1.48 us (1%)
    psum x1, blocking collectives, shards(): lax.psum(gram(place, xs, rows), ('grp', 'par')).reshape(count, count)  52.7 us
    ppermute x12, waiting for transfers between devices, swap(): return lax.ppermute(block, 'grp', [(i, i ^ k) for i in range(groups)])  49.6 us
    pallas_call x8, Pallas kernels, mix(): pl.pallas_call(functools.partial(mix_kernel, rows, groups, dest), out_sha...  16.2 us
    ppermute x12, starting transfers between devices, swap(): return lax.ppermute(block, 'grp', [(i, i ^ k) for i in range(groups)])  16 us
    dynamic_slice x2, local copies, waits for them, and re-layouts, cut(): return lax.dynamic_slice_in_dim(block, (me ^ k) * part, part, axis=0)  3.01 us
  transfers between devices with their start and end apart: 12, of which 6 were waited for; matrix products, arithmetic and copies ran while one was open for 1% of the time, Pallas kernels for 14%

profile of v1, /device:TPU:0, one launch (start us, length us, event | category | flops | bytes accessed | tf_op | source)
XLA Modules:
  0.0 146.5 jit_solution(16999688315972321610)
XLA Ops:
  0.7 1.8 %constant_dynamic-slice_fusion.4 = (f32[1024,128]{1,0:T(8,128)S(1)}, f32[1024,128]{1,0:T(8,128)S(1)}, f32[1024,128]{1,0:T(8,128)S(1)}, f32[1024,128]{1,0:T(8,128)S(1)}) fusion(f32[4096,128]{1,0:T(8,128)} %bitcast.23, s32[]{:T(128)S(6)} %select_n.11, s32[]{:T(128)S(6)} %select_n.10, s32[]{:T(128)S(6)} %select_n.9, s32[]{:T(128)S(6)} %select_n.8), kind=kLoop, calls=%fused_computation.10 | loop fusion | bytes 4194320 | tf_op jit(solution)/shard_map/dynamic_slice | solution.py:167
  2.5 4.0 %collective-permute-start.2 = (f32[1024,128]{1,0:T(8,128)S(1)}, f32[1024,128]{1,0:T(8,128)S(1)}, u32[]{:S(2)}, u32[]{:S(2)}) collective-permute-start(f32[1024,128]{1,0:T(8,128)S(1)} %get-tuple-element.20), channel_id=1, source_target_pairs={{0,24},{8,16},{16,8},{24,0},{1,25},{9,17},{17,9},{25,1},{2,26},{10... | collective-permute-start | bytes 1572872 | tf_op jit(solution)/shard_map/ppermute | solution.py:164
  7.1 12.2 %collective-permute-done.2.refs_3_ = f32[1024,128]{1,0:T(8,128)S(1)} collective-permute-done((f32[1024,128]{1,0:T(8,128)S(1)}, f32[1024,128]{1,0:T(8,128)S(1)}, u32[]{:S(2)}, u32[]{:S(2)}) %collective-permute-start.2) | collective-permute-done | bytes 524320 | tf_op jit(solution)/shard_map/ppermute | solution.py:164
  19.2 10.4 %collective-permute-done.1.refs_2_ = f32[1024,128]{1,0:T(8,128)S(1)} collective-permute-done((f32[1024,128]{1,0:T(8,128)S(1)}, f32[1024,128]{1,0:T(8,128)S(1)}, u32[]{:S(2)}, u32[]{:S(2)}) %collective-permute-start.1) | collective-permute-done | bytes 524320 | tf_op jit(solution)/shard_map/ppermute | solution.py:164
  29.9 1.2 constant_dynamic-slice_fusion
  31.1 1.5 %collective-permute-start.5 = (f32[1024,128]{1,0:T(8,128)}, f32[1024,128]{1,0:T(8,128)S(1)}, u32[]{:S(2)}, u32[]{:S(2)}) collective-permute-start(f32[1024,128]{1,0:T(8,128)} %get-tuple-element.16), channel_id=1, source_target_pairs={{0,24},{8,16},{16,8},{24,0},{1,25},{9,17},{17,9},{25,1},{2,26},{10... | collective-permute-start | bytes 1572872 | tf_op jit(solution)/shard_map/ppermute | solution.py:164
  32.6 1.4 collective-permute-start.4
  34.0 0.5 collective-permute-start.3
  35.2 2.3 %gram.1 = f32[1,256]{1,0:T(1,128)S(1)} custom-call(s32[1]{0:T(128)} %bitcast.me_ref, f32[1024,128]{1,0:T(8,128)S(1)} %get-tuple-element.9.refs_0_, f32[1024,128]{1,0:T(8,128)S(1)} %collective-permute-done.refs_1_, f32[1024,128]{1,0:T(8,128)S(1)} %collective-permute-done.1.refs_2_, f32[1024,128]{1,0:T(8,128)S(1)} %collective-permute-done.2.refs_3_), custom_call_target="tpu_custom_call" | custom-call | tf_op jit(solution)/shard_map/gram/pallas_call | solution.py:68
  37.5 0.6 broadcast.3
  38.1 0.7 reduce.3
  38.9 52.7 %psum.7.gram_ref = f32[16,16]{1,0:T(8,128)} all-reduce(f32[16,16]{1,0:T(8,128)S(1)} %reshape.39), channel_id=1, replica_groups=mesh['grp'=4,'par'=8] {'grp','par'}, use_global_device_ids=true, to_apply=%region_0.0 | all-reduce | flops 256 | bytes 2048 | tf_op jit(solution)/shard_map/psum | solution.py:175
  91.7 1.5 weights.1
  93.1 0.7 copy-done.1
  93.8 1.5 %mix.13 = f32[1024,128]{1,0:T(8,128)S(1)} custom-call(s32[1]{0:T(128)} %bitcast.me_ref, f32[16,16]{1,0:T(8,128)S(1)} %copy-done.1, f32[1024,128]{1,0:T(8,128)S(1)} %get-tuple-element.9.refs_0_, f32[1024,128]{1,0:T(8,128)S(1)} %collective-permute-done.refs_1_, f32[1024,128]{1,0:T(8,128)S(1)} %collective-permute-done.1.refs_2_, ...), custom_call_target="tpu_custom_call" | custom-call | tf_op jit(solution)/shard_map/mix/pallas_call | solution.py:139
  95.4 2.3 %collective-permute-start.9 = (f32[1024,128]{1,0:T(8,128)S(1)}, f32[1024,128]{1,0:T(8,128)S(1)}, u32[]{:S(2)}, u32[]{:S(2)}) collective-permute-start(f32[1024,128]{1,0:T(8,128)S(1)} %mix.13), channel_id=1, source_target_pairs={{0,8},{8,0},{16,24},{24,16},{1,9},{9,1},{17,25},{25,17},{2,10},{10... | collective-permute-start | bytes 1572872 | tf_op jit(solution)/shard_map/ppermute | solution.py:164
  97.7 1.5 %mix.14 = f32[1024,128]{1,0:T(8,128)S(1)} custom-call(s32[1]{0:T(128)} %bitcast.me_ref, f32[16,16]{1,0:T(8,128)S(1)} %copy-done.1, f32[1024,128]{1,0:T(8,128)S(1)} %get-tuple-element.9.refs_0_, f32[1024,128]{1,0:T(8,128)S(1)} %collective-permute-done.refs_1_, f32[1024,128]{1,0:T(8,128)S(1)} %collective-permute-done.1.refs_2_, ...), custom_call_target="tpu_custom_call" | custom-call | tf_op jit(solution)/shard_map/mix/pallas_call | solution.py:139
  99.3 1.0 collective-permute-start.10
  100.2 1.5 %mix.15 = f32[1024,128]{1,0:T(8,128)S(1)} custom-call(s32[1]{0:T(128)} %bitcast.me_ref, f32[16,16]{1,0:T(8,128)S(1)} %copy-done.1, f32[1024,128]{1,0:T(8,128)S(1)} %get-tuple-element.9.refs_0_, f32[1024,128]{1,0:T(8,128)S(1)} %collective-permute-done.refs_1_, f32[1024,128]{1,0:T(8,128)S(1)} %collective-permute-done.1.refs_2_, ...), custom_call_target="tpu_custom_call" | custom-call | tf_op jit(solution)/shard_map/mix/pallas_call | solution.py:139
  101.8 0.9 collective-permute-start.11
  102.7 2.1 %mix.9 = f32[1024,128]{1,0:T(8,128)S(1)} custom-call(s32[1]{0:T(128)} %bitcast.me_ref, f32[16,16]{1,0:T(8,128)S(1)} %copy-done, f32[1024,128]{1,0:T(8,128)S(1)} %get-tuple-element.19.refs_0_, f32[1024,128]{1,0:T(8,128)} %collective-permute-done.3.refs_1_, f32[1024,128]{1,0:T(8,128)} %collective-permute-done.4.refs_2_, ...), custom_call_target="tpu_custom_call" | custom-call | tf_op jit(solution)/shard_map/mix/pallas_call | solution.py:139
  104.8 1.8 %collective-permute-start.6 = (f32[1024,128]{1,0:T(8,128)S(1)}, f32[1024,128]{1,0:T(8,128)S(1)}, u32[]{:S(2)}, u32[]{:S(2)}) collective-permute-start(f32[1024,128]{1,0:T(8,128)S(1)} %mix.9), channel_id=1, source_target_pairs={{0,8},{8,0},{16,24},{24,16},{1,9},{9,1},{17,25},{25,17},{2,10},{10... | collective-permute-start | bytes 1572872 | tf_op jit(solution)/shard_map/ppermute | solution.py:164
  106.6 2.1 %mix.10 = f32[1024,128]{1,0:T(8,128)S(1)} custom-call(s32[1]{0:T(128)} %bitcast.me_ref, f32[16,16]{1,0:T(8,128)S(1)} %copy-done, f32[1024,128]{1,0:T(8,128)S(1)} %get-tuple-element.19.refs_0_, f32[1024,128]{1,0:T(8,128)} %collective-permute-done.3.refs_1_, f32[1024,128]{1,0:T(8,128)} %collective-permute-done.4.refs_2_, ...), custom_call_target="tpu_custom_call" | custom-call | tf_op jit(solution)/shard_map/mix/pallas_call | solution.py:139
  108.7 1.0 collective-permute-start.7
  109.7 2.3 %mix.12 = f32[4096,128]{1,0:T(8,128)} custom-call(s32[1]{0:T(128)} %bitcast.me_ref, f32[16,16]{1,0:T(8,128)S(1)} %copy-done.1, f32[1024,128]{1,0:T(8,128)S(1)} %get-tuple-element.9.refs_0_, f32[1024,128]{1,0:T(8,128)S(1)} %collective-permute-done.refs_1_, f32[1024,128]{1,0:T(8,128)S(1)} %collective-permute-done.1.refs_2_, ...), custom_call_target="tpu_custom_call" | custom-call | tf_op jit(solution)/shard_map/mix/pallas_call | solution.py:139
  112.0 2.2 %mix.11 = f32[1024,128]{1,0:T(8,128)S(1)} custom-call(s32[1]{0:T(128)} %bitcast.me_ref, f32[16,16]{1,0:T(8,128)S(1)} %copy-done, f32[1024,128]{1,0:T(8,128)S(1)} %get-tuple-element.19.refs_0_, f32[1024,128]{1,0:T(8,128)} %collective-permute-done.3.refs_1_, f32[1024,128]{1,0:T(8,128)} %collective-permute-done.4.refs_2_, ...), custom_call_target="tpu_custom_call" | custom-call | tf_op jit(solution)/shard_map/mix/pallas_call | solution.py:139
  114.3 0.9 collective-permute-start.8
  115.2 2.9 %mix.8 = f32[4096,128]{1,0:T(8,128)} custom-call(s32[1]{0:T(128)} %bitcast.me_ref, f32[16,16]{1,0:T(8,128)S(1)} %copy-done, f32[1024,128]{1,0:T(8,128)S(1)} %get-tuple-element.19.refs_0_, f32[1024,128]{1,0:T(8,128)} %collective-permute-done.3.refs_1_, f32[1024,128]{1,0:T(8,128)} %collective-permute-done.4.refs_2_, f32[1024,128]{1,0:T(8,128)S(1)} %collective-permute-done.5.refs_3_), custom_call_target="tpu_custom_call" | custom-call | tf_op jit(solution)/shard_map/mix/pallas_call | solution.py:139
  118.1 7.3 %collective-permute-done.10 = f32[1024,128]{1,0:T(8,128)S(1)} collective-permute-done((f32[1024,128]{1,0:T(8,128)S(1)}, f32[1024,128]{1,0:T(8,128)S(1)}, u32[]{:S(2)}, u32[]{:S(2)}) %collective-permute-start.10) | collective-permute-done | bytes 524320 | tf_op jit(solution)/shard_map/ppermute | solution.py:164
  125.5 7.5 %collective-permute-done.6 = f32[1024,128]{1,0:T(8,128)S(1)} collective-permute-done((f32[1024,128]{1,0:T(8,128)S(1)}, f32[1024,128]{1,0:T(8,128)S(1)}, u32[]{:S(2)}, u32[]{:S(2)}) %collective-permute-start.6) | collective-permute-done | bytes 524320 | tf_op jit(solution)/shard_map/ppermute | solution.py:164
  133.1 11.9 %collective-permute-done.7 = f32[1024,128]{1,0:T(8,128)S(1)} collective-permute-done((f32[1024,128]{1,0:T(8,128)S(1)}, f32[1024,128]{1,0:T(8,128)S(1)}, u32[]{:S(2)}, u32[]{:S(2)}) %collective-permute-start.7) | collective-permute-done | bytes 524320 | tf_op jit(solution)/shard_map/ppermute | solution.py:164
  145.2 1.3 copy-done.3
  (28 shorter events, 1.3 us)
Async XLA Ops:
  0.7 29.2 %copy-start.6 = (f32[4,131072]{1,0:T(4,128)S(1)}, f32[4,131072]{1,0:T(4,128)}, u32[]{:S(2)}) copy-start(f32[4,131072]{1,0:T(4,128)} %param.4) | copy-start | bytes 6291460
  2.5 16.8 %collective-permute-start.2 = (f32[1024,128]{1,0:T(8,128)S(1)}, f32[1024,128]{1,0:T(8,128)S(1)}, u32[]{:S(2)}, u32[]{:S(2)}) collective-permute-start(f32[1024,128]{1,0:T(8,128)S(1)} %get-tuple-element.20), channel_id=1, source_target_pairs={{0,24},{8,16},{16,8},{24,0},{1,25},{9,17},{17,9},{25,1},{2,26},{10... | collective-permute-start | bytes 1572872 | tf_op jit(solution)/shard_map/ppermute | solution.py:164
  6.4 23.2 %collective-permute-start.1 = (f32[1024,128]{1,0:T(8,128)S(1)}, f32[1024,128]{1,0:T(8,128)S(1)}, u32[]{:S(2)}, u32[]{:S(2)}) collective-permute-start(f32[1024,128]{1,0:T(8,128)S(1)} %get-tuple-element.21), channel_id=1, source_target_pairs={{0,16},{8,24},{16,0},{24,8},{1,17},{9,25},{17,1},{25,9},{2,18},{10... | collective-permute-start | bytes 1572872 | tf_op jit(solution)/shard_map/ppermute | solution.py:164
  6.9 22.9 %collective-permute-start = (f32[1024,128]{1,0:T(8,128)S(1)}, f32[1024,128]{1,0:T(8,128)S(1)}, u32[]{:S(2)}, u32[]{:S(2)}) collective-permute-start(f32[1024,128]{1,0:T(8,128)S(1)} %get-tuple-element.22), channel_id=1, source_target_pairs={{0,8},{8,0},{16,24},{24,16},{1,9},{9,1},{17,25},{25,17},{2,10},{10... | collective-permute-start | bytes 1572872 | tf_op jit(solution)/shard_map/ppermute | solution.py:164
  31.1 70.7 %collective-permute-start.5 = (f32[1024,128]{1,0:T(8,128)}, f32[1024,128]{1,0:T(8,128)S(1)}, u32[]{:S(2)}, u32[]{:S(2)}) collective-permute-start(f32[1024,128]{1,0:T(8,128)} %get-tuple-element.16), channel_id=1, source_target_pairs={{0,24},{8,16},{16,8},{24,0},{1,25},{9,17},{17,9},{25,1},{2,26},{10... | collective-permute-start | bytes 1572872 | tf_op jit(solution)/shard_map/ppermute | solution.py:164
  32.6 70.1 %collective-permute-start.4 = (f32[1024,128]{1,0:T(8,128)}, f32[1024,128]{1,0:T(8,128)}, u32[]{:S(2)}, u32[]{:S(2)}) collective-permute-start(f32[1024,128]{1,0:T(8,128)} %get-tuple-element.17), channel_id=1, source_target_pairs={{0,16},{8,24},{16,0},{24,8},{1,17},{9,25},{17,1},{25,9},{2,18},{10... | collective-permute-start | bytes 1572872 | tf_op jit(solution)/shard_map/ppermute | solution.py:164
  34.0 68.7 %collective-permute-start.3 = (f32[1024,128]{1,0:T(8,128)}, f32[1024,128]{1,0:T(8,128)}, u32[]{:S(2)}, u32[]{:S(2)}) collective-permute-start(f32[1024,128]{1,0:T(8,128)} %get-tuple-element.18), channel_id=1, source_target_pairs={{0,8},{8,0},{16,24},{24,16},{1,9},{9,1},{17,25},{25,17},{2,10},{10... | collective-permute-start | bytes 1572872 | tf_op jit(solution)/shard_map/ppermute | solution.py:164
  93.1 0.7 copy-start.1
  95.4 7.4 %copy-start = (f32[16,16]{1,0:T(8,128)S(1)}, f32[16,16]{1,0:T(8,128)}, u32[]{:S(2)}) copy-start(f32[16,16]{1,0:T(8,128)} %get-tuple-element.13.coef_ref) | copy-start | bytes 3076
  95.4 18.9 %collective-permute-start.9 = (f32[1024,128]{1,0:T(8,128)S(1)}, f32[1024,128]{1,0:T(8,128)S(1)}, u32[]{:S(2)}, u32[]{:S(2)}) collective-permute-start(f32[1024,128]{1,0:T(8,128)S(1)} %mix.13), channel_id=1, source_target_pairs={{0,8},{8,0},{16,24},{24,16},{1,9},{9,1},{17,25},{25,17},{2,10},{10... | collective-permute-start | bytes 1572872 | tf_op jit(solution)/shard_map/ppermute | solution.py:164
  99.3 26.2 %collective-permute-start.10 = (f32[1024,128]{1,0:T(8,128)S(1)}, f32[1024,128]{1,0:T(8,128)S(1)}, u32[]{:S(2)}, u32[]{:S(2)}) collective-permute-start(f32[1024,128]{1,0:T(8,128)S(1)} %mix.14), channel_id=1, source_target_pairs={{0,16},{8,24},{16,0},{24,8},{1,17},{9,25},{17,1},{25,9},{2,18},{10... | collective-permute-start | bytes 1572872 | tf_op jit(solution)/shard_map/ppermute | solution.py:164
  101.8 23.7 %collective-permute-start.11 = (f32[1024,128]{1,0:T(8,128)S(1)}, f32[1024,128]{1,0:T(8,128)S(1)}, u32[]{:S(2)}, u32[]{:S(2)}) collective-permute-start(f32[1024,128]{1,0:T(8,128)S(1)} %mix.15), channel_id=1, source_target_pairs={{0,24},{8,16},{16,8},{24,0},{1,25},{9,17},{17,9},{25,1},{2,26},{10... | collective-permute-start | bytes 1572872 | tf_op jit(solution)/shard_map/ppermute | solution.py:164
  104.8 28.2 %collective-permute-start.6 = (f32[1024,128]{1,0:T(8,128)S(1)}, f32[1024,128]{1,0:T(8,128)S(1)}, u32[]{:S(2)}, u32[]{:S(2)}) collective-permute-start(f32[1024,128]{1,0:T(8,128)S(1)} %mix.9), channel_id=1, source_target_pairs={{0,8},{8,0},{16,24},{24,16},{1,9},{9,1},{17,25},{25,17},{2,10},{10... | collective-permute-start | bytes 1572872 | tf_op jit(solution)/shard_map/ppermute | solution.py:164
  108.7 36.4 %collective-permute-start.7 = (f32[1024,128]{1,0:T(8,128)S(1)}, f32[1024,128]{1,0:T(8,128)S(1)}, u32[]{:S(2)}, u32[]{:S(2)}) collective-permute-start(f32[1024,128]{1,0:T(8,128)S(1)} %mix.10), channel_id=1, source_target_pairs={{0,16},{8,24},{16,0},{24,8},{1,17},{9,25},{17,1},{25,9},{2,18},{10... | collective-permute-start | bytes 1572872 | tf_op jit(solution)/shard_map/ppermute | solution.py:164
  112.0 3.2 %copy-start.4 = (f32[4096,128]{1,0:T(8,128)S(1)}, f32[4096,128]{1,0:T(8,128)}, u32[]{:S(2)}) copy-start(f32[4096,128]{1,0:T(8,128)} %mix.12) | copy-start | bytes 6291460
  114.3 30.8 %collective-permute-start.8 = (f32[1024,128]{1,0:T(8,128)S(1)}, f32[1024,128]{1,0:T(8,128)S(1)}, u32[]{:S(2)}, u32[]{:S(2)}) collective-permute-start(f32[1024,128]{1,0:T(8,128)S(1)} %mix.11), channel_id=1, source_target_pairs={{0,24},{8,16},{16,8},{24,0},{1,25},{9,17},{17,9},{25,1},{2,26},{10... | collective-permute-start | bytes 1572872 | tf_op jit(solution)/shard_map/ppermute | solution.py:164
  118.1 14.9 %copy-start.2 = (f32[4096,128]{1,0:T(8,128)S(1)}, f32[4096,128]{1,0:T(8,128)}, u32[]{:S(2)}) copy-start(f32[4096,128]{1,0:T(8,128)} %mix.8) | copy-start | bytes 6291460
  125.5 19.6 %copy-start.5 = (f32[4096,128]{1,0:T(8,128)}, f32[4096,128]{1,0:T(8,128)S(1)}, u32[]{:S(2)}) copy-start(f32[4096,128]{1,0:T(8,128)S(1)} %constant_dynamic-update-slice_fusion) | copy-start | bytes 6291460
  145.2 1.3 copy-start.3

commit v2 on v1

v2 whole, which is shorter than its diff:
```python
import functools

import jax
import jax.numpy as jnp
from jax import lax
from jax.experimental import pallas as pl
from jax.experimental.pallas import tpu as pltpu
from jax.sharding import PartitionSpec as P

P_SIZE = 1048576
LANES = 128
SUB = 8
VMEM_LIMIT = 16 * 2**20

SMEM_SPEC = pl.BlockSpec(memory_space=pltpu.SMEM)
VMEM_SPEC = pl.BlockSpec(memory_space=pltpu.VMEM)
HBM_SPEC = pl.BlockSpec(memory_space=pltpu.HBM)
SHORT = pl.CostEstimate(flops=1, bytes_accessed=1, transcendentals=0)


def dense(block):
    rows, columns = block.shape
    return block.reshape(rows, columns // LANES, LANES).transpose(1, 0, 2).reshape(-1, LANES)


def undense(block, rows):
    return block.reshape(-1, rows, LANES).transpose(1, 0, 2).reshape(rows, -1)


def gram_kernel(rows, groups, me_ref, *refs):
    xs, out_ref, acc_ref = refs[:groups], refs[groups], refs[groups + 1]
    me = me_ref[0]
    count = rows * groups
    step = SUB * rows
    steps = xs[0].shape[0] // step

    def load(ref, t, i):
        return ref[pl.ds(t * step + i, SUB, stride=rows), :]

    for a in range(groups):
        for b in range(a, groups):
            pairs = [(i, j) for i in range(rows) for j in range(rows) if a != b or i <= j]

            def body(t, sums):
                left = [load(xs[a], t, i) for i in range(rows)]
                right = left if a == b else [load(xs[b], t, j) for j in range(rows)]
                return tuple(s + left[i] * right[j] for s, (i, j) in zip(sums, pairs))

            zero = jnp.zeros((SUB, LANES), jnp.float32)
            sums = lax.fori_loop(0, steps, body, (zero,) * len(pairs), unroll=2)
            for s, (i, j) in zip(sums, pairs):
                row = jnp.sum(s, axis=0, keepdims=True)
                left, right = (me ^ a) * rows + i, (me ^ b) * rows + j
                acc_ref[pl.ds(left * count + right, 1), :] = row
                if a != b or i != j:
                    acc_ref[pl.ds(right * count + left, 1), :] = row
    total = lax.dot_general(
        jnp.ones((SUB, LANES), jnp.float32),
        acc_ref[...],
        (((1,), (1,)), ((), ())),
        precision=lax.Precision.HIGHEST,
        preferred_element_type=jnp.float32,
    )
    for n in range(count * count // LANES):
        row = total[:1, n * LANES : (n + 1) * LANES]
        out_ref[:, n : n + 1, :] = jnp.broadcast_to(row[None], (out_ref.shape[0], 1, LANES))


def gram(me, xs, rows, copies):
    groups = len(xs)
    count = rows * groups
    return pl.pallas_call(
        functools.partial(gram_kernel, rows, groups),
        out_shape=jax.ShapeDtypeStruct((copies, count * count // LANES, LANES), jnp.float32),
        in_specs=[SMEM_SPEC] + [VMEM_SPEC] * groups,
        out_specs=VMEM_SPEC,
        scratch_shapes=[pltpu.VMEM((count * count, LANES), jnp.float32)],
        compiler_params=pltpu.CompilerParams(vmem_limit_bytes=VMEM_LIMIT),
        cost_estimate=SHORT,
        name="gram",
    )(me, *xs)


def relay_kernel(grams_ref, token_ref, out_ref):
    total = jnp.sum(grams_ref[...], axis=0, keepdims=True)
    out_ref[...] = jnp.broadcast_to(total, out_ref.shape)


def relay(grams, token, copies):
    return pl.pallas_call(
        relay_kernel,
        out_shape=jax.ShapeDtypeStruct((copies, *grams.shape[1:]), jnp.float32),
        in_specs=[VMEM_SPEC, VMEM_SPEC],
        out_specs=VMEM_SPEC,
        compiler_params=pltpu.CompilerParams(vmem_limit_bytes=2**21),
        cost_estimate=SHORT,
        name="relay",
    )(grams, token)


def exact(left, right):
    return jnp.dot(left, right, precision=lax.Precision.HIGHEST, preferred_element_type=jnp.float32)


def weights_kernel(rows, count, me_ref, width_ref, grams_ref, drive_ref, repel_ref):
    def iota(shape, axis):
        return lax.broadcasted_iota(jnp.int32, shape, axis)

    def mask(condition):
        return jnp.where(condition, 1.0, 0.0)

    flat = jnp.sum(grams_ref[...], axis=0)
    lines = flat.shape[0]
    per = LANES // count
    held = exact(mask(iota((count, lines), 0) // per == iota((count, lines), 1)), flat)
    held = jnp.where(iota((count, LANES), 1) // count == iota((count, LANES), 0) % per, held, 0.0)
    inner = exact(held, mask(iota((LANES, count), 0) % count == iota((LANES, count), 1)))
    square = (count, count)
    r, c = iota(square, 0), iota(square, 1)
    order = mask(((me_ref[0] ^ (r // rows)) * rows + r % rows) == c)
    inner = exact(exact(order, inner), order)

    width = width_ref[0]
    diagonal = r == c
    norms = jnp.where(diagonal, inner, 0.0)
    dist = jnp.sum(norms, axis=1, keepdims=True) + jnp.sum(norms, axis=0, keepdims=True) - 2.0 * inner
    kern = jnp.exp(-dist / (width * P_SIZE))
    others = jnp.where(diagonal, 0.0, kern)
    to_drive = kern / count
    to_repel = jnp.where(diagonal, jnp.sum(others, axis=1, keepdims=True), -others) / (count * width)
    for j in range(count):
        drive_ref[j * count : (j + 1) * count, :] = jnp.broadcast_to(to_drive[:, j : j + 1], (count, LANES))
        repel_ref[j * count : (j + 1) * count, :] = jnp.broadcast_to(to_repel[:, j : j + 1], (count, LANES))


def weights(me, width, grams, rows, count):
    shape = jax.ShapeDtypeStruct((count * count, LANES), jnp.float32)
    return pl.pallas_call(
        functools.partial(weights_kernel, rows, count),
        out_shape=(shape, shape),
        in_specs=[SMEM_SPEC, SMEM_SPEC, VMEM_SPEC],
        out_specs=(VMEM_SPEC, VMEM_SPEC),
        compiler_params=pltpu.CompilerParams(vmem_limit_bytes=VMEM_LIMIT),
        cost_estimate=SHORT,
        name="weights",
    )(me, width, grams)


def mix_kernel(rows, count, jobs, drive_ref, repel_ref, *refs):
    out_ref = refs[-1]
    step = SUB * rows
    start = used = 0
    for coef_ref, dest, sources in ((repel_ref if repel else drive_ref, dest, sources) for repel, dest, sources in jobs):
        xs = refs[used : used + len(sources)]
        used += len(sources)
        steps = xs[0].shape[0] // step
        wide = next(w for w in (8, 4, 2, 1) if steps % w == 0)

        def body(t, carry):
            base = pl.multiple_of(t * step * wide, step)
            sums = [[None] * rows for _ in range(wide)]
            for b, source in enumerate(sources):
                for j in range(rows):
                    x = [xs[b][pl.ds(base + u * step + j, SUB, stride=rows), :] for u in range(wide)]
                    for i in range(rows):
                        row = (source * rows + j) * count + dest * rows + i
                        c = jnp.broadcast_to(coef_ref[row : row + 1, :], (SUB, LANES))
                        for u in range(wide):
                            term = c * x[u]
                            sums[u][i] = term if sums[u][i] is None else sums[u][i] + term
            for u in range(wide):
                for i in range(rows):
                    out_ref[pl.ds(start + base + u * step + i, SUB, stride=rows), :] = sums[u][i]
            return carry

        lax.fori_loop(0, steps // wide, body, 0)
        start += steps * step


def mix(coefs, rows, count, jobs, tokens=()):
    blocks = [block for job in jobs for block in job[3]]
    size = sum(job[3][0].shape[0] for job in jobs)
    return pl.pallas_call(
        functools.partial(mix_kernel, rows, count, [job[:3] for job in jobs]),
        out_shape=jax.ShapeDtypeStruct((size, LANES), jnp.float32),
        in_specs=[VMEM_SPEC] * (2 + len(blocks) + len(tokens)),
        out_specs=VMEM_SPEC,
        compiler_params=pltpu.CompilerParams(vmem_limit_bytes=VMEM_LIMIT),
        cost_estimate=SHORT,
        name="mix",
    )(*coefs, *blocks, *tokens)


def put_kernel(entries, blocks, me_ref, *refs):
    blocks, (out_ref, sum_ref, sems) = refs[:blocks], refs[-3:]
    copies = []
    used = 0
    for n, (parts, size, place) in enumerate(entries):
        block, start = parts[0]
        source = blocks[block].at[pl.ds(start, size), :]
        if len(parts) > 1:
            total = source[...]
            for block, start in parts[1:]:
                total = total + blocks[block][pl.ds(start, size), :]
            source = sum_ref.at[pl.ds(used, size), :]
            source[...] = total
            used += size
        offset = place[1] if place[0] else (me_ref[0] ^ place[1]) * size
        copy = pltpu.make_async_copy(source, out_ref.at[pl.ds(offset, size), :], sems.at[n])
        copy.start()
        copies.append(copy)
    for copy in copies:
        copy.wait()


def put(me, entries, blocks, size, base=None):
    extra = [] if base is None else [base]
    moved = sum(entry[1] for entry in entries)
    scratch = sum(entry[1] for entry in entries if len(entry[0]) > 1)
    return pl.pallas_call(
        functools.partial(put_kernel, entries, len(blocks)),
        out_shape=jax.ShapeDtypeStruct((size, LANES), jnp.float32),
        in_specs=[SMEM_SPEC] + [VMEM_SPEC] * len(blocks) + [HBM_SPEC] * len(extra),
        out_specs=HBM_SPEC,
        scratch_shapes=[pltpu.VMEM((max(scratch, SUB), LANES), jnp.float32), pltpu.SemaphoreType.DMA((len(entries),))],
        input_output_aliases={1 + len(blocks): 0} if extra else {},
        compiler_params=pltpu.CompilerParams(vmem_limit_bytes=VMEM_LIMIT),
        cost_estimate=pl.CostEstimate(flops=0, bytes_accessed=8 * LANES * moved, transcendentals=0),
        name="put",
    )(me, *blocks, *extra)


def cut_kernel(places, me_ref, block_ref, *refs):
    outs, sems = refs[:-1], refs[-1]
    size = outs[0].shape[0]
    copies = [
        pltpu.make_async_copy(block_ref.at[pl.ds((me_ref[0] ^ place) * size, size), :], out, sems.at[n])
        for n, (out, place) in enumerate(zip(outs, places))
    ]
    for copy in copies:
        copy.start()
    for copy in copies:
        copy.wait()


def cut(me, block, places, groups):
    part = jax.ShapeDtypeStruct((block.shape[0] // groups, LANES), jnp.float32)
    return pl.pallas_call(
        functools.partial(cut_kernel, places),
        out_shape=[part] * len(places),
        in_specs=[SMEM_SPEC, HBM_SPEC],
        out_specs=[VMEM_SPEC] * len(places),
        scratch_shapes=[pltpu.SemaphoreType.DMA((len(places),))],
        compiler_params=pltpu.CompilerParams(vmem_limit_bytes=60 * 2**20),
        cost_estimate=SHORT,
        name="cut",
    )(me, block)


def arrived_kernel(*refs):
    refs[-1][...] = jnp.zeros_like(refs[-1])


def arrived(blocks):
    return pl.pallas_call(
        arrived_kernel,
        out_shape=jax.ShapeDtypeStruct((SUB, LANES), jnp.float32),
        in_specs=[pl.BlockSpec(memory_space=pl.ANY)] * len(blocks),
        out_specs=VMEM_SPEC,
        compiler_params=pltpu.CompilerParams(vmem_limit_bytes=2**21),
        cost_estimate=pl.CostEstimate(flops=0, bytes_accessed=10**9, transcendentals=0),
        name="arrived",
    )(*blocks)


def shards(particles, scores, kernel_width):
    groups = lax.axis_size("grp")
    rows = particles.shape[0]
    count = rows * groups
    me = lax.axis_index("grp")
    place = me.astype(jnp.int32).reshape(1)
    x, s = dense(particles), dense(scores)
    part, half = x.shape[0] // groups, x.shape[0] // 2
    near = 2 ** ((groups.bit_length() - 1) // 2)
    lows, highs = list(range(near)), list(range(0, groups, near))

    def swap(block, k):
        return lax.ppermute(block, "grp", [(i, i ^ k) for i in range(groups)]) if k else block

    everyone, others = list(range(groups)), list(range(groups - 1, 0, -1))
    size, step = x.shape[0], SUB * rows
    first = max(1, half // step * 5 // 16) * step
    second = half - first

    sent = cut(place, x, others, groups)
    (x, s), sent = lax.optimization_barrier(((x, s), sent))
    s_own = [s[:first], s[first:half], s[half : half + first], s[half + first :]]
    xs = {k: swap(block, k) for k, block in zip(others, sent)}
    xs[0] = lax.dynamic_slice_in_dim(x, me * part, part, axis=0)
    xs = [xs[k] for k in everyone]

    def exchange(low, high):
        return [swap(low, k) for k in lows], [swap(high, k) for k in highs]

    def gather(grams, axis):
        return lax.all_to_all(grams, axis, 0, 0, tiled=True)

    xs, s_own = lax.optimization_barrier((xs, s_own))
    early = exchange(s_own[0], s_own[2])
    grams = gather(gram(place, xs, rows, groups), "grp")
    early, pair, grams = lax.optimization_barrier((early, (s_own[1], s_own[3]), grams))
    late = exchange(*pair)
    grams = gather(relay(grams, arrived(early[0][1:] + early[1][1:]), lax.axis_size("par")), "par")
    coefs = weights(place, kernel_width, grams, rows, count)
    token = arrived(late[0][1:] + late[1][1:])

    def send(dest, jobs, coefs, tokens=()):
        mixed = mix(coefs, rows, count, jobs, tokens)
        return swap(mixed, dest), lax.optimization_barrier((coefs, mixed))[0]

    def score_jobs(dest, sources, n):
        return [(False, dest, sources, early[n]), (False, dest, sources, late[n])]

    back, sums = {}, {}
    for n, (sources, dests) in enumerate(((lows, highs), (highs, lows))):
        for k in dests[1:]:
            sums[k], coefs = send(k, score_jobs(k, sources, n), coefs, [token])
    for k in others:
        back[k], coefs = send(k, [(True, k, everyone, xs)], coefs)
    own = mix(coefs, rows, count, [(True, 0, everyone, xs)] + score_jobs(0, lows, 0) + score_jobs(0, highs, 1))

    repel = put(place, [([(0, 0)], part, (False, 0))], [own], size)
    drive = None
    for n, dests in enumerate((highs[1:], lows[1:])):
        got = [sums[k] for k in dests]
        if drive is not None:
            drive, got = lax.optimization_barrier((drive, got))
        parts = [(0, part + n * half)] + [(1 + m, 0) for m in range(len(got))]
        drive = put(place, [(parts, half, (True, n * half))], [own] + got, size, base=drive)
    for dests in (others[:1], others[1:]):
        if dests:
            got = [back[k] for k in dests]
            (drive, repel), got = lax.optimization_barrier(((drive, repel), got))
            repel = put(place, [([(m, 0)], part, (False, k)) for m, k in enumerate(dests)], got, size, base=repel)
    return (undense(drive, rows), undense(repel, rows))


def solution(mesh):
    return jax.shard_map(
        shards,
        mesh=mesh,
        in_specs=(P("grp", "par"), P("grp", "par"), P()),
        out_specs=(P("grp", "par"), P("grp", "par")),
        check_vma=False,
    )
```

time: 147 us -> 112 us (0.76)
  blocking collectives: 52.7 us -> 7.27 us
  waiting for transfers between devices: 49.6 us -> 57.9 us
  starting transfers between devices: 16 us -> 18.4 us
    psum x1 -> x0, blocking collectives: 52.7 us -> none  [shards(): lax.psum(gram(place, xs, rows), ('grp', 'par')).reshape(count, count)]
    all_to_all x0 -> x1, blocking collectives: none -> 7.27 us  [gather(): return lax.all_to_all(grams, axis, 0, 0, tiled=True)]
    all_to_all x0 -> x1, waiting for transfers between devices: none -> 4.95 us  [gather(): return lax.all_to_all(grams, axis, 0, 0, tiled=True)]
    all_to_all x0 -> x1, starting transfers between devices: none -> 4.88 us  [gather(): return lax.all_to_all(grams, axis, 0, 0, tiled=True)]
    ppermute x12, waiting for transfers between devices: 49.6 us -> 53 us  [swap(): lax.ppermute(block, 'grp', [(i, i ^ k) for i in range(groups)])]
    slice x0 -> x2, local copies, waits for them, and re-layouts: none -> 3.37 us  [shards(): s_own = [s[:first], s[first:half], s[half:half + first], s[half + first:]]]
    ppermute x12, starting transfers between devices: 16 us -> 13.5 us  [swap(): lax.ppermute(block, 'grp', [(i, i ^ k) for i in range(groups)])]
    dynamic_slice x2 -> x1, local copies, waits for them, and re-layouts: 3.01 us -> 1.14 us  [shards(): xs[0] = lax.dynamic_slice_in_dim(x, me * part, part, axis=0)]
  transfers between devices with their start and end apart: 12 -> 13, of which waited for: 6 -> 8; matrix products, arithmetic and copies ran while one was open for 1% -> 4% of each run, Pallas kernels for 14% -> 13%
where the time goes in v2:
time: 112 us
  waiting for transfers between devices  57.9 us (52%)
  Pallas kernels  19.6 us (18%)
  starting transfers between devices  18.4 us (16%)
  blocking collectives  7.27 us (6%)
  local copies, waits for them, and re-layouts  7.21 us (6%)
  between operations  1.42 us (1%)
    ppermute x12, waiting for transfers between devices, swap(): lax.ppermute(block, 'grp', [(i, i ^ k) for i in range(groups)])  53 us
    ppermute x12, starting transfers between devices, swap(): lax.ppermute(block, 'grp', [(i, i ^ k) for i in range(groups)])  13.5 us
    pallas_call x6, Pallas kernels, mix(): pl.pallas_call(functools.partial(mix_kernel, rows, count, [job[:3] for jo...  8.52 us
    all_to_all x1, blocking collectives, gather(): return lax.all_to_all(grams, axis, 0, 0, tiled=True)  7.27 us
    all_to_all x1, waiting for transfers between devices, gather(): return lax.all_to_all(grams, axis, 0, 0, tiled=True)  4.95 us
    all_to_all x1, starting transfers between devices, gather(): return lax.all_to_all(grams, axis, 0, 0, tiled=True)  4.88 us
    pallas_call x5, Pallas kernels, put(): pl.pallas_call(functools.partial(put_kernel, entries, len(blocks)), out_s...  4.76 us
    slice x2, local copies, waits for them, and re-layouts, shards(): s_own = [s[:first], s[first:half], s[half:half + first], s[half + first:]]  3.37 us
  transfers between devices with their start and end apart: 13, of which 8 were waited for; matrix products, arithmetic and copies ran while one was open for 4% of the time, Pallas kernels for 13%

profile of v2, /device:TPU:0, one launch (start us, length us, event | category | flops | bytes accessed | tf_op | source)
XLA Modules:
  0.0 111.8 jit_solution(972525166843622729)
XLA Ops:
  0.6 2.5 %cut.1 = (f32[1024,128]{1,0:T(8,128)}, f32[1024,128]{1,0:T(8,128)}, f32[1024,128]{1,0:T(8,128)}) custom-call(s32[1]{0:T(128)} %bitcast.me_ref, f32[4096,128]{1,0:T(8,128)} %bitcast.23), custom_call_target="tpu_custom_call" | custom-call | flops 1 | bytes 1 | tf_op jit(solution)/shard_map/cut/pallas_call | solution.py:248
  3.2 3.0 %collective-permute-start = (f32[1024,128]{1,0:T(8,128)}, f32[1024,128]{1,0:T(8,128)S(1)}, u32[]{:S(2)}, u32[]{:S(2)}) collective-permute-start(f32[1024,128]{1,0:T(8,128)} %get-tuple-element.50), channel_id=1, source_target_pairs={{0,8},{8,0},{16,24},{24,16},{1,9},{9,1},{17,25},{25,17},{2,10},{10... | collective-permute-start | bytes 1572872 | tf_op jit(solution)/shard_map/ppermute | solution.py:288
  6.2 1.5 %collective-permute-start.1 = (f32[1024,128]{1,0:T(8,128)}, f32[1024,128]{1,0:T(8,128)S(1)}, u32[]{:S(2)}, u32[]{:S(2)}) collective-permute-start(f32[1024,128]{1,0:T(8,128)} %get-tuple-element.51), channel_id=1, source_target_pairs={{0,16},{8,24},{16,0},{24,8},{1,17},{9,25},{17,1},{25,9},{2,18},{10... | collective-permute-start | bytes 1572872 | tf_op jit(solution)/shard_map/ppermute | solution.py:288
  7.7 1.9 %fusion.1 = (f32[640,128]{1,0:T(8,128)}, f32[640,128]{1,0:T(8,128)}) fusion(f32[4096,128]{1,0:T(8,128)} %bitcast.25), kind=kLoop, calls=%fused_computation.2 | loop fusion | bytes 1310720 | tf_op jit(solution)/shard_map/slice | solution.py:297
  9.7 1.1 %constant_dynamic-slice_fusion.refs_0_ = f32[1024,128]{1,0:T(8,128)S(1)} fusion(f32[4096,128]{1,0:T(8,128)} %bitcast.24, s32[]{:T(128)S(6)} %select_n.3), kind=kLoop, calls=%fused_computation | loop fusion | bytes 1048580 | tf_op jit(solution)/shard_map/dynamic_slice | solution.py:299
  10.8 1.4 %fusion = (f32[1408,128]{1,0:T(8,128)S(1)}, f32[1408,128]{1,0:T(8,128)S(1)}) fusion(f32[4096,128]{1,0:T(8,128)} %bitcast.26), kind=kLoop, calls=%fused_computation.1 | loop fusion | bytes 2883584 | tf_op jit(solution)/shard_map/slice | solution.py:297
  12.2 6.9 %collective-permute-done.refs_1_ = f32[1024,128]{1,0:T(8,128)S(1)} collective-permute-done((f32[1024,128]{1,0:T(8,128)}, f32[1024,128]{1,0:T(8,128)S(1)}, u32[]{:S(2)}, u32[]{:S(2)}) %collective-permute-start) | collective-permute-done | bytes 524320 | tf_op jit(solution)/shard_map/ppermute | solution.py:288
  19.1 11.9 %collective-permute-done.1.refs_2_ = f32[1024,128]{1,0:T(8,128)S(1)} collective-permute-done((f32[1024,128]{1,0:T(8,128)}, f32[1024,128]{1,0:T(8,128)S(1)}, u32[]{:S(2)}, u32[]{:S(2)}) %collective-permute-start.1) | collective-permute-done | bytes 524320 | tf_op jit(solution)/shard_map/ppermute | solution.py:288
  31.0 1.2 %collective-permute-start.3 = (f32[640,128]{1,0:T(8,128)S(1)}, f32[640,128]{1,0:T(8,128)S(1)}, u32[]{:S(2)}, u32[]{:S(2)}) collective-permute-start(f32[640,128]{1,0:T(8,128)S(1)} %copy-done.2), channel_id=1, source_target_pairs={{0,8},{8,0},{16,24},{24,16},{1,9},{9,1},{17,25},{25,17},{2,10},{10... | collective-permute-start | bytes 983048 | tf_op jit(solution)/shard_map/ppermute | solution.py:288
  32.2 0.8 collective-permute-start.4
  33.1 2.3 %gram.1 = f32[4,2,128]{2,1,0:T(2,128)S(1)} custom-call(s32[1]{0:T(128)} %bitcast.me_ref, f32[1024,128]{1,0:T(8,128)S(1)} %constant_dynamic-slice_fusion.refs_0_, f32[1024,128]{1,0:T(8,128)S(1)} %collective-permute-done.refs_1_, f32[1024,128]{1,0:T(8,128)S(1)} %collective-permute-done.1.refs_2_, f32[1024,128]{1,0:T(8,128)S(1)} %collective-permute-done.2.refs_3_), custom_call_target="tpu_custom_call" | custom-call | flops 1 | bytes 1 | tf_op jit(solution)/shard_map/gram/pallas_call | solution.py:72
  35.4 7.3 %all_to_all.10.grams_ref = f32[4,2,128]{2,1,0:T(2,128)S(1)} all-to-all(f32[4,2,128]{2,1,0:T(2,128)S(1)} %gram.1), channel_id=1, replica_groups=mesh['grp'=4,'par'=8] {'grp'}, dimensions={0} | all-to-all | bytes 8192 | tf_op jit(solution)/shard_map/all_to_all | solution.py:306
  45.2 4.9 %all-to-all-start.1 = ((f32[8,2,128]{2,1,0:T(2,128)}), f32[8,2,128]{2,1,0:T(2,128)S(1)}, u32[]{:S(2)}, u32[]{:S(2)}) async-start(f32[8,2,128]{2,1,0:T(2,128)} %relay.1), calls=%async_computation.1 | async-start | bytes 16384 | tf_op jit(solution)/shard_map/all_to_all | solution.py:306
  50.7 5.0 %all-to-all-done.1.grams_ref = f32[8,2,128]{2,1,0:T(2,128)S(1)} async-done(((f32[8,2,128]{2,1,0:T(2,128)}), f32[8,2,128]{2,1,0:T(2,128)S(1)}, u32[]{:S(2)}, u32[]{:S(2)}) %all-to-all-start.1) | async-done | bytes 8224 | tf_op jit(solution)/shard_map/all_to_all | solution.py:306
  55.6 0.9 weights.1
  56.6 1.0 collective-permute-done.5.refs_0_.refs_3_.refs_7_
  58.3 1.0 copy-done.3
  59.2 1.0 copy-done.5
  60.2 1.7 %mix.6 = f32[2048,128]{1,0:T(8,128)S(1)} custom-call(f32[256,128]{1,0:T(8,128)S(1)} %get-tuple-element.79.drive_ref, f32[256,128]{1,0:T(8,128)S(1)} %get-tuple-element.80.repel_ref, f32[640,128]{1,0:T(8,128)S(1)} %copy-done.3, f32[640,128]{1,0:T(8,128)S(1)} %copy-done.5, f32[1408,128]{1,0:T(8,128)S(1)} %get-tuple-element.68.refs_2_.refs_6_, ...), custom_call_target="tpu_custom_call" | custom-call | flops 1 | bytes 1 | tf_op jit(solution)/shard_map/mix/pallas_call | solution.py:183
  62.6 1.7 %mix.7 = f32[2048,128]{1,0:T(8,128)S(1)} custom-call(f32[256,128]{1,0:T(8,128)S(1)} %get-tuple-element.79.drive_ref, f32[256,128]{1,0:T(8,128)S(1)} %get-tuple-element.80.repel_ref, f32[640,128]{1,0:T(8,128)S(1)} %copy-done.1, f32[640,128]{1,0:T(8,128)S(1)} %copy-done.8, f32[1408,128]{1,0:T(8,128)S(1)} %get-tuple-element.69.refs_2_.refs_10_, ...), custom_call_target="tpu_custom_call" | custom-call | flops 1 | bytes 1 | tf_op jit(solution)/shard_map/mix/pallas_call | solution.py:183
  64.3 1.5 %collective-permute-start.8 = (f32[2048,128]{1,0:T(8,128)S(1)}, f32[2048,128]{1,0:T(8,128)S(1)}, u32[]{:S(2)}, u32[]{:S(2)}) collective-permute-start(f32[2048,128]{1,0:T(8,128)S(1)} %mix.7), channel_id=1, source_target_pairs={{0,8},{8,0},{16,24},{24,16},{1,9},{9,1},{17,25},{25,17},{2,10},{10... | collective-permute-start | bytes 3145736 | tf_op jit(solution)/shard_map/ppermute | solution.py:288
  66.4 1.6 %collective-permute-start.9 = (f32[1024,128]{1,0:T(8,128)S(1)}, f32[1024,128]{1,0:T(8,128)S(1)}, u32[]{:S(2)}, u32[]{:S(2)}) collective-permute-start(f32[1024,128]{1,0:T(8,128)S(1)} %mix.8), channel_id=1, source_target_pairs={{0,24},{8,16},{16,8},{24,0},{1,25},{9,17},{17,9},{25,1},{2,26},{10... | collective-permute-start | bytes 1572872 | tf_op jit(solution)/shard_map/ppermute | solution.py:288
  69.2 1.2 %collective-permute-start.11 = (f32[1024,128]{1,0:T(8,128)S(1)}, f32[1024,128]{1,0:T(8,128)S(1)}, u32[]{:S(2)}, u32[]{:S(2)}) collective-permute-start(f32[1024,128]{1,0:T(8,128)S(1)} %mix.10), channel_id=1, source_target_pairs={{0,8},{8,0},{16,24},{24,16},{1,9},{9,1},{17,25},{25,17},{2,10},{10... | collective-permute-start | bytes 1572872 | tf_op jit(solution)/shard_map/ppermute | solution.py:288
  70.4 0.9 collective-permute-start.10
  71.3 3.2 %mix.11.refs_0_ = f32[5120,128]{1,0:T(8,128)S(1)} custom-call(f32[256,128]{1,0:T(8,128)S(1)} %get-tuple-element.79.drive_ref, f32[256,128]{1,0:T(8,128)S(1)} %get-tuple-element.80.repel_ref, f32[1024,128]{1,0:T(8,128)S(1)} %constant_dynamic-slice_fusion.refs_0_, f32[1024,128]{1,0:T(8,128)S(1)} %collective-permute-done.refs_1_, ...), custom_call_target="tpu_custom_call" | custom-call | flops 1 | bytes 1 | tf_op jit(solution)/shard_map/mix/pallas_call | solution.py:183
  74.5 0.8 put.7.refs_1_
  75.3 15.8 %collective-permute-done.7.refs_1_ = f32[2048,128]{1,0:T(8,128)S(1)} collective-permute-done((f32[2048,128]{1,0:T(8,128)S(1)}, f32[2048,128]{1,0:T(8,128)S(1)}, u32[]{:S(2)}, u32[]{:S(2)}) %collective-permute-start.7) | collective-permute-done | bytes 1048608 | tf_op jit(solution)/shard_map/ppermute | solution.py:288
  91.0 1.1 put.5.refs_2_
  92.1 1.1 put.6
  93.2 9.4 %collective-permute-done.9.refs_0_ = f32[1024,128]{1,0:T(8,128)S(1)} collective-permute-done((f32[1024,128]{1,0:T(8,128)S(1)}, f32[1024,128]{1,0:T(8,128)S(1)}, u32[]{:S(2)}, u32[]{:S(2)}) %collective-permute-start.9) | collective-permute-done | bytes 524320 | tf_op jit(solution)/shard_map/ppermute | solution.py:288
  103.5 7.3 %collective-permute-done.11.refs_1_ = f32[1024,128]{1,0:T(8,128)S(1)} collective-permute-done((f32[1024,128]{1,0:T(8,128)S(1)}, f32[1024,128]{1,0:T(8,128)S(1)}, u32[]{:S(2)}, u32[]{:S(2)}) %collective-permute-start.11) | collective-permute-done | bytes 524320 | tf_op jit(solution)/shard_map/ppermute | solution.py:288
  110.8 1.0 put.9
  (33 shorter events, 6.5 us)
Async XLA Ops:
  3.2 16.0 %collective-permute-start = (f32[1024,128]{1,0:T(8,128)}, f32[1024,128]{1,0:T(8,128)S(1)}, u32[]{:S(2)}, u32[]{:S(2)}) collective-permute-start(f32[1024,128]{1,0:T(8,128)} %get-tuple-element.50), channel_id=1, source_target_pairs={{0,8},{8,0},{16,24},{24,16},{1,9},{9,1},{17,25},{25,17},{2,10},{10... | collective-permute-start | bytes 1572872 | tf_op jit(solution)/shard_map/ppermute | solution.py:288
  6.2 24.8 %collective-permute-start.1 = (f32[1024,128]{1,0:T(8,128)}, f32[1024,128]{1,0:T(8,128)S(1)}, u32[]{:S(2)}, u32[]{:S(2)}) collective-permute-start(f32[1024,128]{1,0:T(8,128)} %get-tuple-element.51), channel_id=1, source_target_pairs={{0,16},{8,24},{16,0},{24,8},{1,17},{9,25},{17,1},{25,9},{2,18},{10... | collective-permute-start | bytes 1572872 | tf_op jit(solution)/shard_map/ppermute | solution.py:288
  7.7 23.3 %collective-permute-start.2 = (f32[1024,128]{1,0:T(8,128)}, f32[1024,128]{1,0:T(8,128)S(1)}, u32[]{:S(2)}, u32[]{:S(2)}) collective-permute-start(f32[1024,128]{1,0:T(8,128)} %get-tuple-element.52), channel_id=1, source_target_pairs={{0,24},{8,16},{16,8},{24,0},{1,25},{9,17},{17,9},{25,1},{2,26},{10... | collective-permute-start | bytes 1572872 | tf_op jit(solution)/shard_map/ppermute | solution.py:288
  9.7 21.3 %copy-start.2 = (f32[640,128]{1,0:T(8,128)S(1)}, f32[640,128]{1,0:T(8,128)}, u32[]{:S(2)}) copy-start(f32[640,128]{1,0:T(8,128)} %get-tuple-element.67.refs_0_.refs_4_) | copy-start | bytes 983044
  9.7 22.6 %copy-start = (f32[640,128]{1,0:T(8,128)S(1)}, f32[640,128]{1,0:T(8,128)}, u32[]{:S(2)}) copy-start(f32[640,128]{1,0:T(8,128)} %get-tuple-element.72.refs_0_.refs_8_) | copy-start | bytes 983044
  31.0 11.6 %collective-permute-start.3 = (f32[640,128]{1,0:T(8,128)S(1)}, f32[640,128]{1,0:T(8,128)S(1)}, u32[]{:S(2)}, u32[]{:S(2)}) collective-permute-start(f32[640,128]{1,0:T(8,128)S(1)} %copy-done.2), channel_id=1, source_target_pairs={{0,8},{8,0},{16,24},{24,16},{1,9},{9,1},{17,25},{25,17},{2,10},{10... | collective-permute-start | bytes 983048 | tf_op jit(solution)/shard_map/ppermute | solution.py:288
  32.2 10.4 %collective-permute-start.4 = (f32[640,128]{1,0:T(8,128)S(1)}, f32[640,128]{1,0:T(8,128)S(1)}, u32[]{:S(2)}, u32[]{:S(2)}) collective-permute-start(f32[640,128]{1,0:T(8,128)S(1)} %copy-done), channel_id=1, source_target_pairs={{0,16},{8,24},{16,0},{24,8},{1,17},{9,25},{17,1},{25,9},{2,18},{10... | collective-permute-start | bytes 983048 | tf_op jit(solution)/shard_map/ppermute | solution.py:288
  42.6 1.2 %copy-start.7 = (f32[640,128]{1,0:T(8,128)}, f32[640,128]{1,0:T(8,128)S(1)}, u32[]{:S(2)}) copy-start(f32[640,128]{1,0:T(8,128)S(1)} %collective-permute-done.4.refs_1_.refs_9_) | copy-start | bytes 983044
  42.6 15.0 %collective-permute-start.5 = (f32[1408,128]{1,0:T(8,128)S(1)}, f32[1408,128]{1,0:T(8,128)}, u32[]{:S(2)}, u32[]{:S(2)}) collective-permute-start(f32[1408,128]{1,0:T(8,128)S(1)} %get-tuple-element.68.refs_2_.refs_6_), channel_id=1, source_target_pairs={{0,8},{8,0},{16,24},{24,16},{1,9},{9,1},{17,25},{25,17},{2,10},{10... | collective-permute-start | bytes 2162696 | tf_op jit(solution)/shard_map/ppermute | solution.py:288
  43.3 15.0 %collective-permute-start.6 = (f32[1408,128]{1,0:T(8,128)S(1)}, f32[1408,128]{1,0:T(8,128)}, u32[]{:S(2)}, u32[]{:S(2)}) collective-permute-start(f32[1408,128]{1,0:T(8,128)S(1)} %get-tuple-element.69.refs_2_.refs_10_), channel_id=1, source_target_pairs={{0,16},{8,24},{16,0},{24,8},{1,17},{9,25},{17,1},{25,9},{2,18},{10... | collective-permute-start | bytes 2162696 | tf_op jit(solution)/shard_map/ppermute | solution.py:288
  43.8 0.7 copy-start.4
  45.2 10.5 %all-to-all-start.1 = ((f32[8,2,128]{2,1,0:T(2,128)}), f32[8,2,128]{2,1,0:T(2,128)S(1)}, u32[]{:S(2)}, u32[]{:S(2)}) async-start(f32[8,2,128]{2,1,0:T(2,128)} %relay.1), calls=%async_computation.1 | async-start | bytes 16384 | tf_op jit(solution)/shard_map/all_to_all | solution.py:306
  56.6 6.0 %copy-start.1 = (f32[640,128]{1,0:T(8,128)S(1)}, f32[640,128]{1,0:T(8,128)}, u32[]{:S(2)}) copy-start(f32[640,128]{1,0:T(8,128)} %get-tuple-element.72.refs_0_.refs_8_) | copy-start | bytes 983044
  56.6 6.0 %copy-start.8 = (f32[640,128]{1,0:T(8,128)S(1)}, f32[640,128]{1,0:T(8,128)}, u32[]{:S(2)}) copy-start(f32[640,128]{1,0:T(8,128)} %copy-done.7) | copy-start | bytes 983044
  58.3 1.0 copy-start.3
  59.2 1.0 copy-start.5
  61.9 29.1 %collective-permute-start.7 = (f32[2048,128]{1,0:T(8,128)S(1)}, f32[2048,128]{1,0:T(8,128)S(1)}, u32[]{:S(2)}, u32[]{:S(2)}) collective-permute-start(f32[2048,128]{1,0:T(8,128)S(1)} %mix.6), channel_id=1, source_target_pairs={{0,16},{8,24},{16,0},{24,8},{1,17},{9,25},{17,1},{25,9},{2,18},{10... | collective-permute-start | bytes 3145736 | tf_op jit(solution)/shard_map/ppermute | solution.py:288
  64.3 27.8 %collective-permute-start.8 = (f32[2048,128]{1,0:T(8,128)S(1)}, f32[2048,128]{1,0:T(8,128)S(1)}, u32[]{:S(2)}, u32[]{:S(2)}) collective-permute-start(f32[2048,128]{1,0:T(8,128)S(1)} %mix.7), channel_id=1, source_target_pairs={{0,8},{8,0},{16,24},{24,16},{1,9},{9,1},{17,25},{25,17},{2,10},{10... | collective-permute-start | bytes 3145736 | tf_op jit(solution)/shard_map/ppermute | solution.py:288
  66.4 36.3 %collective-permute-start.9 = (f32[1024,128]{1,0:T(8,128)S(1)}, f32[1024,128]{1,0:T(8,128)S(1)}, u32[]{:S(2)}, u32[]{:S(2)}) collective-permute-start(f32[1024,128]{1,0:T(8,128)S(1)} %mix.8), channel_id=1, source_target_pairs={{0,24},{8,16},{16,8},{24,0},{1,25},{9,17},{17,9},{25,1},{2,26},{10... | collective-permute-start | bytes 1572872 | tf_op jit(solution)/shard_map/ppermute | solution.py:288
  68.6 2.7 %copy-start.6 = (f32[640,128]{1,0:T(8,128)S(1)}, f32[640,128]{1,0:T(8,128)}, u32[]{:S(2)}) copy-start(f32[640,128]{1,0:T(8,128)} %copy-done.4) | copy-start | bytes 983044
  69.2 41.6 %collective-permute-start.11 = (f32[1024,128]{1,0:T(8,128)S(1)}, f32[1024,128]{1,0:T(8,128)S(1)}, u32[]{:S(2)}, u32[]{:S(2)}) collective-permute-start(f32[1024,128]{1,0:T(8,128)S(1)} %mix.10), channel_id=1, source_target_pairs={{0,8},{8,0},{16,24},{24,16},{1,9},{9,1},{17,25},{25,17},{2,10},{10... | collective-permute-start | bytes 1572872 | tf_op jit(solution)/shard_map/ppermute | solution.py:288
  70.4 40.4 %collective-permute-start.10 = (f32[1024,128]{1,0:T(8,128)S(1)}, f32[1024,128]{1,0:T(8,128)S(1)}, u32[]{:S(2)}, u32[]{:S(2)}) collective-permute-start(f32[1024,128]{1,0:T(8,128)S(1)} %mix.9), channel_id=1, source_target_pairs={{0,16},{8,24},{16,0},{24,8},{1,17},{9,25},{17,1},{25,9},{2,18},{10... | collective-permute-start | bytes 1572872 | tf_op jit(solution)/shard_map/ppermute | solution.py:288

commit v3 on v2

--- a/solution.py
+++ b/solution.py
@@ -14,6 +14,7 @@
 
 SMEM_SPEC = pl.BlockSpec(memory_space=pltpu.SMEM)
 VMEM_SPEC = pl.BlockSpec(memory_space=pltpu.VMEM)
+ANY_SPEC = pl.BlockSpec(memory_space=pl.ANY)
 HBM_SPEC = pl.BlockSpec(memory_space=pltpu.HBM)
 SHORT = pl.CostEstimate(flops=1, bytes_accessed=1, transcendentals=0)
 
@@ -81,23 +82,6 @@
     )(me, *xs)
 
 
-def relay_kernel(grams_ref, token_ref, out_ref):
-    total = jnp.sum(grams_ref[...], axis=0, keepdims=True)
-    out_ref[...] = jnp.broadcast_to(total, out_ref.shape)
-
-
-def relay(grams, token, copies):
-    return pl.pallas_call(
-        relay_kernel,
-        out_shape=jax.ShapeDtypeStruct((copies, *grams.shape[1:]), jnp.float32),
-        in_specs=[VMEM_SPEC, VMEM_SPEC],
-        out_specs=VMEM_SPEC,
-        compiler_params=pltpu.CompilerParams(vmem_limit_bytes=2**21),
-        cost_estimate=SHORT,
-        name="relay",
-    )(grams, token)
-
-
 def exact(left, right):
     return jnp.dot(left, right, precision=lax.Precision.HIGHEST, preferred_element_type=jnp.float32)
 
@@ -147,13 +131,26 @@
 
 
 def mix_kernel(rows, count, jobs, drive_ref, repel_ref, *refs):
-    out_ref = refs[-1]
+    blocks = sum(len(spans) for _, _, _, spans in jobs)
+    xs, out_ref, scratch = list(refs[:blocks]), refs[blocks], refs[blocks + 1 :]
+    streams = [n for n, span in enumerate(span for job in jobs for span in job[3]) if span is not None]
+    spans = [span for job in jobs for span in job[3]]
+    copies = {}
+    for m, n in enumerate(streams):
+        start, size = spans[n]
+        copies[n] = pltpu.make_async_copy(xs[n].at[pl.ds(start, size), :], scratch[m], scratch[-1].at[m])
+        copies[n].start()
+        xs[n] = scratch[m]
     step = SUB * rows
     start = used = 0
-    for coef_ref, dest, sources in ((repel_ref if repel else drive_ref, dest, sources) for repel, dest, sources in jobs):
-        xs = refs[used : used + len(sources)]
+    for repel, dest, sources, spans in jobs:
+        coef_ref = repel_ref if repel else drive_ref
+        held = xs[used : used + len(sources)]
+        for n in range(used, used + len(sources)):
+            if n in copies:
+                copies[n].wait()
         used += len(sources)
-        steps = xs[0].shape[0] // step
+        steps = held[0].shape[0] // step
         wide = next(w for w in (8, 4, 2, 1) if steps % w == 0)
 
         def body(t, carry):
@@ -161,7 +158,7 @@
             sums = [[None] * rows for _ in range(wide)]
             for b, source in enumerate(sources):
                 for j in range(rows):
-                    x = [xs[b][pl.ds(base + u * step + j, SUB, stride=rows), :] for u in range(wide)]
+                    x = [held[b][pl.ds(base + u * step + j, SUB, stride=rows), :] for u in range(wide)]
                     for i in range(rows):
                         row = (source * rows + j) * count + dest * rows + i
                         c = jnp.broadcast_to(coef_ref[row : row + 1, :], (SUB, LANES))
@@ -177,18 +174,22 @@
         start += steps * step
 
 
-def mix(coefs, rows, count, jobs, tokens=()):
+def mix(coefs, rows, count, jobs):
     blocks = [block for job in jobs for block in job[3]]
-    size = sum(job[3][0].shape[0] for job in jobs)
+    streams = [block for block in blocks if isinstance(block, tuple)]
+    spans = [(*job[:3], [b[1:] if isinstance(b, tuple) else None for b in job[3]]) for job in jobs]
+    size = sum(b[2] if isinstance(b, tuple) else b.shape[0] for b in (job[3][0] for job in jobs))
+    scratch = [pltpu.VMEM((block[2], LANES), jnp.float32) for block in streams]
     return pl.pallas_call(
-        functools.partial(mix_kernel, rows, count, [job[:3] for job in jobs]),
+        functools.partial(mix_kernel, rows, count, spans),
         out_shape=jax.ShapeDtypeStruct((size, LANES), jnp.float32),
-        in_specs=[VMEM_SPEC] * (2 + len(blocks) + len(tokens)),
+        in_specs=[VMEM_SPEC] * 2 + [ANY_SPEC if isinstance(block, tuple) else VMEM_SPEC for block in blocks],
         out_specs=VMEM_SPEC,
+        scratch_shapes=scratch + ([pltpu.SemaphoreType.DMA((len(streams),))] if streams else []),
         compiler_params=pltpu.CompilerParams(vmem_limit_bytes=VMEM_LIMIT),
         cost_estimate=SHORT,
         name="mix",
-    )(*coefs, *blocks, *tokens)
+    )(*coefs, *[block[0] if isinstance(block, tuple) else block for block in blocks])
 
 
 def put_kernel(entries, blocks, me_ref, *refs):
@@ -230,49 +231,6 @@
     )(me, *blocks, *extra)
 
 
-def cut_kernel(places, me_ref, block_ref, *refs):
-    outs, sems = refs[:-1], refs[-1]
-    size = outs[0].shape[0]
-    copies = [
-        pltpu.make_async_copy(block_ref.at[pl.ds((me_ref[0] ^ place) * size, size), :], out, sems.at[n])
-        for n, (out, place) in enumerate(zip(outs, places))
-    ]
-    for copy in copies:
-        copy.start()
-    for copy in copies:
-        copy.wait()
-
-
-def cut(me, block, places, groups):
-    part = jax.ShapeDtypeStruct((block.shape[0] // groups, LANES), jnp.float32)
-    return pl.pallas_call(
-        functools.partial(cut_kernel, places),
-        out_shape=[part] * len(places),
-        in_specs=[SMEM_SPEC, HBM_SPEC],
-        out_specs=[VMEM_SPEC] * len(places),
-        scratch_shapes=[pltpu.SemaphoreType.DMA((len(places),))],
-        compiler_params=pltpu.CompilerParams(vmem_limit_bytes=60 * 2**20),
-        cost_estimate=SHORT,
-        name="cut",
-    )(me, block)
-
-
-def arrived_kernel(*refs):
-    refs[-1][...] = jnp.zeros_like(refs[-1])
-
-
-def arrived(blocks):
-    return pl.pallas_call(
-        arrived_kernel,
-        out_shape=jax.ShapeDtypeStruct((SUB, LANES), jnp.float32),
-        in_specs=[pl.BlockSpec(memory_space=pl.ANY)] * len(blocks),
-        out_specs=VMEM_SPEC,
-        compiler_params=pltpu.CompilerParams(vmem_limit_bytes=2**21),
-        cost_estimate=pl.CostEstimate(flops=0, bytes_accessed=10**9, transcendentals=0),
-        name="arrived",
-    )(*blocks)
-
-
 def shards(particles, scores, kernel_width):
     groups = lax.axis_size("grp")
     rows = particles.shape[0]
@@ -289,59 +247,64 @@
 
     everyone, others = list(range(groups)), list(range(groups - 1, 0, -1))
     size, step = x.shape[0], SUB * rows
-    first = max(1, half // step * 5 // 16) * step
+    first = max(1, half // step * 3 // 8) * step
     second = half - first
 
-    sent = cut(place, x, others, groups)
-    (x, s), sent = lax.optimization_barrier(((x, s), sent))
+    def cut(block, k):
+        return lax.dynamic_slice_in_dim(block, (me ^ k) * part, part, axis=0)
+
+    sent = [cut(x, k) for k in others + [0]]
+    s, sent = lax.optimization_barrier((s, sent))
     s_own = [s[:first], s[first:half], s[half : half + first], s[half + first :]]
-    xs = {k: swap(block, k) for k, block in zip(others, sent)}
-    xs[0] = lax.dynamic_slice_in_dim(x, me * part, part, axis=0)
+    xs = {k: swap(block, k) for k, block in zip(others + [0], sent)}
     xs = [xs[k] for k in everyone]
 
     def exchange(low, high):
         return [swap(low, k) for k in lows], [swap(high, k) for k in highs]
 
-    def gather(grams, axis):
-        return lax.all_to_all(grams, axis, 0, 0, tiled=True)
-
-    xs, s_own = lax.optimization_barrier((xs, s_own))
+    xs[-1], s_own = lax.optimization_barrier((xs[-1], s_own))
     early = exchange(s_own[0], s_own[2])
-    grams = gather(gram(place, xs, rows, groups), "grp")
+    inner = gram(place, xs, rows, 1)
+    grams = [swap(inner, k) for k in everyone]
     early, pair, grams = lax.optimization_barrier((early, (s_own[1], s_own[3]), grams))
     late = exchange(*pair)
-    grams = gather(relay(grams, arrived(early[0][1:] + early[1][1:]), lax.axis_size("par")), "par")
-    coefs = weights(place, kernel_width, grams, rows, count)
-    token = arrived(late[0][1:] + late[1][1:])
-
-    def send(dest, jobs, coefs, tokens=()):
-        mixed = mix(coefs, rows, count, jobs, tokens)
+    coefs = weights(place, kernel_width, lax.psum(sum(grams[1:], grams[0]), "par"), rows, count)
+
+    def send(dest, jobs, coefs):
+        mixed = mix(coefs, rows, count, jobs)
         return swap(mixed, dest), lax.optimization_barrier((coefs, mixed))[0]
 
-    def score_jobs(dest, sources, n):
-        return [(False, dest, sources, early[n]), (False, dest, sources, late[n])]
-
+    def score_job(dest, n, held, start, size):
+        own = (s, n * half + start, size)
+        return (False, dest, (lows, highs)[n], [own] + [(block, 0, size) for block in held[n][1:]])
+
+    near_by = [k for k in others if k in lows or k in highs]
     back, sums = {}, {}
-    for n, (sources, dests) in enumerate(((lows, highs), (highs, lows))):
-        for k in dests[1:]:
-            sums[k], coefs = send(k, score_jobs(k, sources, n), coefs, [token])
-    for k in others:
+    for k in near_by + [k for k in others if k not in near_by]:
         back[k], coefs = send(k, [(True, k, everyone, xs)], coefs)
-    own = mix(coefs, rows, count, [(True, 0, everyone, xs)] + score_jobs(0, lows, 0) + score_jobs(0, highs, 1))
+    pieces = ((late, first, second), (early, 0, first))
+    for p, piece in enumerate(pieces):
+        for n, dests in enumerate((highs[1:], lows[1:])):
+            for k in dests:
+                sums[p, k], coefs = send(k, [score_job(k, n, *piece)], coefs)
+    own = mix(coefs, rows, count, [(True, 0, everyone, xs)] + [score_job(0, n, *piece) for piece in pieces for n in (0, 1)])
 
     repel = put(place, [([(0, 0)], part, (False, 0))], [own], size)
+    for k in back:
+        repel, back[k] = lax.optimization_barrier((repel, back[k]))
+        repel = put(place, [([(0, 0)], part, (False, k))], [back[k]], size, base=repel)
     drive = None
-    for n, dests in enumerate((highs[1:], lows[1:])):
-        got = [sums[k] for k in dests]
-        if drive is not None:
-            drive, got = lax.optimization_barrier((drive, got))
-        parts = [(0, part + n * half)] + [(1 + m, 0) for m in range(len(got))]
-        drive = put(place, [(parts, half, (True, n * half))], [own] + got, size, base=drive)
-    for dests in (others[:1], others[1:]):
-        if dests:
-            got = [back[k] for k in dests]
-            (drive, repel), got = lax.optimization_barrier(((drive, repel), got))
-            repel = put(place, [([(m, 0)], part, (False, k)) for m, k in enumerate(dests)], got, size, base=repel)
+    begin = part
+    for p, (held, row, length) in enumerate(pieces):
+        entries, blocks = [], [own]
+        for n, dests in enumerate((highs[1:], lows[1:])):
+            entries.append(([(0, begin)] + [(len(blocks) + m, 0) for m in range(len(dests))], length, (True, n * half + row)))
+            blocks += [sums[p, k] for k in dests]
+            begin += length
+        held = repel if drive is None else (drive, repel)
+        held, blocks = lax.optimization_barrier((held, blocks))
+        drive, repel = (None, held) if drive is None else held
+        drive = put(place, entries, blocks, size, base=drive)
     return (undense(drive, rows), undense(repel, rows))
 
 

time: 112 us -> 111 us (level)
  blocking collectives: 7.27 us -> 15.9 us
  waiting for transfers between devices: 57.9 us -> 50.6 us
  Pallas kernels: 19.6 us -> 17.8 us
    psum x0 -> x1, blocking collectives: none -> 15.9 us  [shards(): lax.psum(sum(grams[1:], grams[0]), 'par')]
    all_to_all x1 -> x0, blocking collectives: 7.27 us -> none  [gather(): return lax.all_to_all(grams, axis, 0, 0, tiled=True)]
    all_to_all x1 -> x0, waiting for transfers between devices: 4.95 us -> none  [gather(): return lax.all_to_all(grams, axis, 0, 0, tiled=True)]
    all_to_all x1 -> x0, starting transfers between devices: 4.88 us -> none  [gather(): return lax.all_to_all(grams, axis, 0, 0, tiled=True)]
    ppermute x12 -> x17, starting transfers between devices: 13.5 us -> 18.3 us  [swap(): lax.ppermute(block, 'grp', [(i, i ^ k) for i in range(groups)])]
    ppermute x12 -> x17, waiting for transfers between devices: 53 us -> 50.6 us  [swap(): lax.ppermute(block, 'grp', [(i, i ^ k) for i in range(groups)])]
    pallas_call x10 -> x8, Pallas kernels: 11.7 us -> 9.35 us  [mix(): pl.pallas_call(functools.partial(mix_kernel, rows, count, spans), out_sha...]
    slice x2, local copies, waits for them, and re-layouts: 3.37 us -> 1.19 us  [shards(): s_own = [s[:first], s[first:half], s[half:half + first], s[half + first:]]]
  transfers between devices with their start and end apart: 13 -> 17, of which waited for: 8 -> 9; matrix products, arithmetic and copies ran while one was open for 4% -> 1% of each run, Pallas kernels for 13% -> 15%
where the time goes in v3:
time: 111 us
  waiting for transfers between devices  50.6 us (46%)
  starting transfers between devices  18.3 us (16%)
  Pallas kernels  17.8 us (16%)
  blocking collectives  15.9 us (14%)
  local copies, waits for them, and re-layouts  6.69 us (6%)
  between operations  1.51 us (1%)
    ppermute x17, waiting for transfers between devices, swap(): lax.ppermute(block, 'grp', [(i, i ^ k) for i in range(groups)])  50.6 us
    ppermute x17, starting transfers between devices, swap(): lax.ppermute(block, 'grp', [(i, i ^ k) for i in range(groups)])  18.3 us
    psum x1, blocking collectives, shards(): lax.psum(sum(grams[1:], grams[0]), 'par')  15.9 us
    pallas_call x8, Pallas kernels, mix(): pl.pallas_call(functools.partial(mix_kernel, rows, count, spans), out_sha...  9.35 us
    pallas_call x6, Pallas kernels, put(): pl.pallas_call(functools.partial(put_kernel, entries, len(blocks)), out_s...  5.29 us
    unnamed x16, local copies, waits for them, and re-layouts  3.7 us
    pallas_call x1, Pallas kernels, gram(): pl.pallas_call(functools.partial(gram_kernel, rows, groups), out_shape=ja...  2.28 us
  transfers between devices with their start and end apart: 17, of which 9 were waited for; matrix products, arithmetic and copies ran while one was open for 1% of the time, Pallas kernels for 15%

profile of v3, /device:TPU:0, one launch (start us, length us, event | category | flops | bytes accessed | tf_op | source)
XLA Modules:
  0.0 110.8 jit_solution(3394154823180289878)
XLA Ops:
  0.7 1.8 %constant_dynamic-slice_fusion = (f32[1024,128]{1,0:T(8,128)S(1)}, f32[1024,128]{1,0:T(8,128)S(1)}, f32[1024,128]{1,0:T(8,128)S(1)}, f32[1024,128]{1,0:T(8,128)S(1)}) fusion(f32[4096,128]{1,0:T(8,128)} %bitcast.33, s32[]{:T(128)S(6)} %select_n.15, s32[]{:T(128)S(6)} %select_n.14, s32[]{:T(128)S(6)} %select_n.13, s32[]{:T(128)S(6)} %select_n.12), kind=kLoop, calls=%fused_computation.1 | loop fusion | bytes 4194320 | tf_op jit(solution)/shard_map/dynamic_slice | solution.py:254
  2.5 4.0 %collective-permute-start = (f32[1024,128]{1,0:T(8,128)S(1)}, f32[1024,128]{1,0:T(8,128)S(1)}, u32[]{:S(2)}, u32[]{:S(2)}) collective-permute-start(f32[1024,128]{1,0:T(8,128)S(1)} %get-tuple-element.51), channel_id=1, source_target_pairs={{0,24},{8,16},{16,8},{24,0},{1,25},{9,17},{17,9},{25,1},{2,26},{10... | collective-permute-start | bytes 1572872 | tf_op jit(solution)/shard_map/ppermute | solution.py:246
  7.1 1.1 %fusion = (f32[1280,128]{1,0:T(8,128)}, f32[1280,128]{1,0:T(8,128)}) fusion(f32[4096,128]{1,0:T(8,128)S(1)} %bitcast.21), kind=kLoop, calls=%fused_computation.5 | loop fusion | bytes 2621440 | tf_op jit(solution)/shard_map/slice | solution.py:258
  8.3 11.0 %collective-permute-done.refs_3_ = f32[1024,128]{1,0:T(8,128)S(1)} collective-permute-done((f32[1024,128]{1,0:T(8,128)S(1)}, f32[1024,128]{1,0:T(8,128)S(1)}, u32[]{:S(2)}, u32[]{:S(2)}) %collective-permute-start) | collective-permute-done | bytes 524320 | tf_op jit(solution)/shard_map/ppermute | solution.py:246
  19.2 2.0 %collective-permute-start.1 = (f32[768,128]{1,0:T(8,128)S(1)}, f32[768,128]{1,0:T(8,128)S(1)}, u32[]{:S(2)}, u32[]{:S(2)}) collective-permute-start(f32[768,128]{1,0:T(8,128)S(1)} %get-tuple-element.53), channel_id=1, source_target_pairs={{0,8},{8,0},{16,24},{24,16},{1,9},{9,1},{17,25},{25,17},{2,10},{10... | collective-permute-start | bytes 1179656 | tf_op jit(solution)/shard_map/ppermute | solution.py:246
  21.2 1.5 %collective-permute-start.2 = (f32[768,128]{1,0:T(8,128)S(1)}, f32[768,128]{1,0:T(8,128)S(1)}, u32[]{:S(2)}, u32[]{:S(2)}) collective-permute-start(f32[768,128]{1,0:T(8,128)S(1)} %get-tuple-element.54), channel_id=1, source_target_pairs={{0,16},{8,24},{16,0},{24,8},{1,17},{9,25},{17,1},{25,9},{2,18},{10... | collective-permute-start | bytes 1179656 | tf_op jit(solution)/shard_map/ppermute | solution.py:246
  22.8 8.3 %collective-permute-done.3.refs_1_ = f32[1024,128]{1,0:T(8,128)S(1)} collective-permute-done((f32[1024,128]{1,0:T(8,128)S(1)}, f32[1024,128]{1,0:T(8,128)S(1)}, u32[]{:S(2)}, u32[]{:S(2)}) %collective-permute-start.3) | collective-permute-done | bytes 524320 | tf_op jit(solution)/shard_map/ppermute | solution.py:246
  31.0 2.3 %gram.1 = f32[1,2,128]{2,1,0:T(2,128)S(1)} custom-call(s32[1]{0:T(128)} %bitcast.me_ref, f32[1024,128]{1,0:T(8,128)S(1)} %get-tuple-element.57.refs_0_, f32[1024,128]{1,0:T(8,128)S(1)} %collective-permute-done.3.refs_1_, f32[1024,128]{1,0:T(8,128)S(1)} %collective-permute-done.4.refs_2_, f32[1024,128]{1,0:T(8,128)S(1)} %collective-permute-done.refs_3_), custom_call_target="tpu_custom_call" | custom-call | flops 1 | bytes 1 | tf_op jit(solution)/shard_map/gram/pallas_call | solution.py:73
  33.3 0.8 copy-done.1
  34.2 1.4 %collective-permute-start.7 = (f32[1,2,128]{2,1,0:T(2,128)S(1)}, f32[1,2,128]{2,1,0:T(2,128)S(1)}, u32[]{:S(2)}, u32[]{:S(2)}) collective-permute-start(f32[1,2,128]{2,1,0:T(2,128)S(1)} %gram.1), channel_id=1, source_target_pairs={{0,24},{8,16},{16,8},{24,0},{1,25},{9,17},{17,9},{25,1},{2,26},{10... | collective-permute-start | bytes 3080 | tf_op jit(solution)/shard_map/ppermute | solution.py:246
  35.6 1.5 %collective-permute-start.6 = (f32[1,2,128]{2,1,0:T(2,128)S(1)}, f32[1,2,128]{2,1,0:T(2,128)S(1)}, u32[]{:S(2)}, u32[]{:S(2)}) collective-permute-start(f32[1,2,128]{2,1,0:T(2,128)S(1)} %gram.1), channel_id=1, source_target_pairs={{0,16},{8,24},{16,0},{24,8},{1,17},{9,25},{17,1},{25,9},{2,18},{10... | collective-permute-start | bytes 3080 | tf_op jit(solution)/shard_map/ppermute | solution.py:246
  37.7 1.0 collective-permute-done.7
  39.2 1.5 %collective-permute-done.5 = f32[1,2,128]{2,1,0:T(2,128)S(1)} collective-permute-done((f32[1,2,128]{2,1,0:T(2,128)S(1)}, f32[1,2,128]{2,1,0:T(2,128)S(1)}, u32[]{:S(2)}, u32[]{:S(2)}) %collective-permute-start.5) | collective-permute-done | bytes 1056 | tf_op jit(solution)/shard_map/ppermute | solution.py:246
  43.0 15.9 %psum.7.grams_ref = f32[1,2,128]{2,1,0:T(2,128)S(1)} all-reduce(f32[1,2,128]{2,1,0:T(2,128)S(1)} %add_add_fusion), channel_id=1, replica_groups=mesh['grp'=4,'par'=8] {'par'}, use_global_device_ids=true, to_apply=%region_0.0 | all-reduce | flops 256 | bytes 2048 | tf_op jit(solution)/shard_map/psum | solution.py:271
  58.9 0.9 weights.1
  59.9 1.0 copy-done.2
  60.9 1.0 copy-done.4
  64.9 1.7 %mix.11 = f32[1280,128]{1,0:T(8,128)S(1)} custom-call(f32[256,128]{1,0:T(8,128)S(1)} %get-tuple-element.83.drive_ref, f32[256,128]{1,0:T(8,128)S(1)} %get-tuple-element.84.repel_ref, f32[4096,128]{1,0:T(8,128)S(1)} %bitcast.23, f32[1280,128]{1,0:T(8,128)} %collective-permute-done.8.refs_1_.refs_5_), custom_call_target="tpu_custom_call" | custom-call | flops 1 | bytes 1 | tf_op jit(solution)/shard_map/mix/pallas_call | solution.py:183
  66.6 1.6 %collective-permute-start.13 = (f32[1280,128]{1,0:T(8,128)S(1)}, f32[1280,128]{1,0:T(8,128)S(1)}, u32[]{:S(2)}, u32[]{:S(2)}) collective-permute-start(f32[1280,128]{1,0:T(8,128)S(1)} %mix.11), channel_id=1, source_target_pairs={{0,16},{8,24},{16,0},{24,8},{1,17},{9,25},{17,1},{25,9},{2,18},{10... | collective-permute-start | bytes 1966088 | tf_op jit(solution)/shard_map/ppermute | solution.py:246
  68.2 1.7 %mix.12 = f32[1280,128]{1,0:T(8,128)S(1)} custom-call(f32[256,128]{1,0:T(8,128)S(1)} %get-tuple-element.83.drive_ref, f32[256,128]{1,0:T(8,128)S(1)} %get-tuple-element.84.repel_ref, f32[4096,128]{1,0:T(8,128)S(1)} %bitcast.24, f32[1280,128]{1,0:T(8,128)} %collective-permute-done.9.refs_1_.refs_7_), custom_call_target="tpu_custom_call" | custom-call | flops 1 | bytes 1 | tf_op jit(solution)/shard_map/mix/pallas_call | solution.py:183
  69.8 1.6 %collective-permute-start.14 = (f32[1280,128]{1,0:T(8,128)S(1)}, f32[1280,128]{1,0:T(8,128)S(1)}, u32[]{:S(2)}, u32[]{:S(2)}) collective-permute-start(f32[1280,128]{1,0:T(8,128)S(1)} %mix.12), channel_id=1, source_target_pairs={{0,8},{8,0},{16,24},{24,16},{1,9},{9,1},{17,25},{25,17},{2,10},{10... | collective-permute-start | bytes 1966088 | tf_op jit(solution)/shard_map/ppermute | solution.py:246
  73.1 5.0 %collective-permute-done.11.refs_0_ = f32[1024,128]{1,0:T(8,128)S(1)} collective-permute-done((f32[1024,128]{1,0:T(8,128)S(1)}, f32[1024,128]{1,0:T(8,128)S(1)}, u32[]{:S(2)}, u32[]{:S(2)}) %collective-permute-start.11) | collective-permute-done | bytes 524320 | tf_op jit(solution)/shard_map/ppermute | solution.py:246
  79.1 3.0 %mix.15.refs_0_ = f32[5120,128]{1,0:T(8,128)S(1)} custom-call(f32[256,128]{1,0:T(8,128)S(1)} %get-tuple-element.83.drive_ref, f32[256,128]{1,0:T(8,128)S(1)} %get-tuple-element.84.repel_ref, f32[1024,128]{1,0:T(8,128)S(1)} %get-tuple-element.57.refs_0_, f32[1024,128]{1,0:T(8,128)S(1)} %copy-done.2, f32[1024,128]{1,0:T(8,128)S(1)} %copy-done.5, ...), custom_call_target="tpu_custom_call" | custom-call | flops 1 | bytes 1 | tf_op jit(solution)/shard_map/mix/pallas_call | solution.py:183
  82.1 0.8 put.6.refs_1_
  82.9 0.8 put.7.refs_1_
  83.7 0.8 put.8.refs_1_
  84.6 18.8 %collective-permute-done.12.refs_0_ = f32[1024,128]{1,0:T(8,128)S(1)} collective-permute-done((f32[1024,128]{1,0:T(8,128)S(1)}, f32[1024,128]{1,0:T(8,128)S(1)}, u32[]{:S(2)}, u32[]{:S(2)}) %collective-permute-start.12) | collective-permute-done | bytes 524320 | tf_op jit(solution)/shard_map/ppermute | solution.py:246
  103.4 0.8 put.9
  104.2 1.1 %put.10.refs_3_ = f32[4096,128]{1,0:T(8,128)} custom-call(s32[1]{0:T(128)} %bitcast.me_ref, f32[5120,128]{1,0:T(8,128)S(1)} %mix.15.refs_0_, f32[1280,128]{1,0:T(8,128)S(1)} %collective-permute-done.13.refs_1_, f32[1280,128]{1,0:T(8,128)S(1)} %collective-permute-done.14.refs_2_), custom_call_target="tpu_custom_call" | custom-call | bytes 2621440 | tf_op jit(solution)/shard_map/put/pallas_call | solution.py:221
  105.3 3.3 %collective-permute-done.16.refs_2_ = f32[768,128]{1,0:T(8,128)S(1)} collective-permute-done((f32[768,128]{1,0:T(8,128)S(1)}, f32[768,128]{1,0:T(8,128)S(1)}, u32[]{:S(2)}, u32[]{:S(2)}) %collective-permute-start.16) | collective-permute-done | bytes 393248 | tf_op jit(solution)/shard_map/ppermute | solution.py:246
  108.7 1.2 %collective-permute-done.15.refs_1_ = f32[768,128]{1,0:T(8,128)S(1)} collective-permute-done((f32[768,128]{1,0:T(8,128)S(1)}, f32[768,128]{1,0:T(8,128)S(1)}, u32[]{:S(2)}, u32[]{:S(2)}) %collective-permute-start.15) | collective-permute-done | bytes 393248 | tf_op jit(solution)/shard_map/ppermute | solution.py:246
  109.8 0.9 put.11
  (39 shorter events, 9.1 us)
Async XLA Ops:
  0.7 6.4 %copy-start = (f32[4,131072]{1,0:T(4,128)S(1)}, f32[4,131072]{1,0:T(4,128)}, u32[]{:S(2)}) copy-start(f32[4,131072]{1,0:T(4,128)} %param.4) | copy-start | bytes 6291460
  2.5 16.8 %collective-permute-start = (f32[1024,128]{1,0:T(8,128)S(1)}, f32[1024,128]{1,0:T(8,128)S(1)}, u32[]{:S(2)}, u32[]{:S(2)}) collective-permute-start(f32[1024,128]{1,0:T(8,128)S(1)} %get-tuple-element.51), channel_id=1, source_target_pairs={{0,24},{8,16},{16,8},{24,0},{1,25},{9,17},{17,9},{25,1},{2,26},{10... | collective-permute-start | bytes 1572872 | tf_op jit(solution)/shard_map/ppermute | solution.py:246
  6.4 24.6 %collective-permute-start.3 = (f32[1024,128]{1,0:T(8,128)S(1)}, f32[1024,128]{1,0:T(8,128)S(1)}, u32[]{:S(2)}, u32[]{:S(2)}) collective-permute-start(f32[1024,128]{1,0:T(8,128)S(1)} %get-tuple-element.58), channel_id=1, source_target_pairs={{0,8},{8,0},{16,24},{24,16},{1,9},{9,1},{17,25},{25,17},{2,10},{10... | collective-permute-start | bytes 1572872 | tf_op jit(solution)/shard_map/ppermute | solution.py:246
  7.0 24.1 %collective-permute-start.4 = (f32[1024,128]{1,0:T(8,128)S(1)}, f32[1024,128]{1,0:T(8,128)S(1)}, u32[]{:S(2)}, u32[]{:S(2)}) collective-permute-start(f32[1024,128]{1,0:T(8,128)S(1)} %get-tuple-element.59), channel_id=1, source_target_pairs={{0,16},{8,24},{16,0},{24,8},{1,17},{9,25},{17,1},{25,9},{2,18},{10... | collective-permute-start | bytes 1572872 | tf_op jit(solution)/shard_map/ppermute | solution.py:246
  19.2 21.5 %collective-permute-start.1 = (f32[768,128]{1,0:T(8,128)S(1)}, f32[768,128]{1,0:T(8,128)S(1)}, u32[]{:S(2)}, u32[]{:S(2)}) collective-permute-start(f32[768,128]{1,0:T(8,128)S(1)} %get-tuple-element.53), channel_id=1, source_target_pairs={{0,8},{8,0},{16,24},{24,16},{1,9},{9,1},{17,25},{25,17},{2,10},{10... | collective-permute-start | bytes 1179656 | tf_op jit(solution)/shard_map/ppermute | solution.py:246
  21.2 19.5 %collective-permute-start.2 = (f32[768,128]{1,0:T(8,128)S(1)}, f32[768,128]{1,0:T(8,128)S(1)}, u32[]{:S(2)}, u32[]{:S(2)}) collective-permute-start(f32[768,128]{1,0:T(8,128)S(1)} %get-tuple-element.54), channel_id=1, source_target_pairs={{0,16},{8,24},{16,0},{24,8},{1,17},{9,25},{17,1},{25,9},{2,18},{10... | collective-permute-start | bytes 1179656 | tf_op jit(solution)/shard_map/ppermute | solution.py:246
  31.0 2.3 %copy-start.3 = (f32[1024,128]{1,0:T(8,128)}, f32[1024,128]{1,0:T(8,128)S(1)}, u32[]{:S(2)}) copy-start(f32[1024,128]{1,0:T(8,128)S(1)} %collective-permute-done.4.refs_2_) | copy-start | bytes 1572868
  33.3 0.8 copy-start.1
  34.2 4.5 %collective-permute-start.7 = (f32[1,2,128]{2,1,0:T(2,128)S(1)}, f32[1,2,128]{2,1,0:T(2,128)S(1)}, u32[]{:S(2)}, u32[]{:S(2)}) collective-permute-start(f32[1,2,128]{2,1,0:T(2,128)S(1)} %gram.1), channel_id=1, source_target_pairs={{0,24},{8,16},{16,8},{24,0},{1,25},{9,17},{17,9},{25,1},{2,26},{10... | collective-permute-start | bytes 3080 | tf_op jit(solution)/shard_map/ppermute | solution.py:246
  35.6 3.6 %collective-permute-start.6 = (f32[1,2,128]{2,1,0:T(2,128)S(1)}, f32[1,2,128]{2,1,0:T(2,128)S(1)}, u32[]{:S(2)}, u32[]{:S(2)}) collective-permute-start(f32[1,2,128]{2,1,0:T(2,128)S(1)} %gram.1), channel_id=1, source_target_pairs={{0,16},{8,24},{16,0},{24,8},{1,17},{9,25},{17,1},{25,9},{2,18},{10... | collective-permute-start | bytes 3080 | tf_op jit(solution)/shard_map/ppermute | solution.py:246
  37.1 3.6 %collective-permute-start.5 = (f32[1,2,128]{2,1,0:T(2,128)S(1)}, f32[1,2,128]{2,1,0:T(2,128)S(1)}, u32[]{:S(2)}, u32[]{:S(2)}) collective-permute-start(f32[1,2,128]{2,1,0:T(2,128)S(1)} %gram.1), channel_id=1, source_target_pairs={{0,8},{8,0},{16,24},{24,16},{1,9},{9,1},{17,25},{25,17},{2,10},{10... | collective-permute-start | bytes 3080 | tf_op jit(solution)/shard_map/ppermute | solution.py:246
  40.7 0.8 copy-start.6
  41.5 23.4 %collective-permute-start.8 = (f32[1280,128]{1,0:T(8,128)}, f32[1280,128]{1,0:T(8,128)}, u32[]{:S(2)}, u32[]{:S(2)}) collective-permute-start(f32[1280,128]{1,0:T(8,128)} %get-tuple-element.73), channel_id=1, source_target_pairs={{0,8},{8,0},{16,24},{24,16},{1,9},{9,1},{17,25},{25,17},{2,10},{10... | collective-permute-start | bytes 1966088 | tf_op jit(solution)/shard_map/ppermute | solution.py:246
  42.0 26.2 %collective-permute-start.9 = (f32[1280,128]{1,0:T(8,128)}, f32[1280,128]{1,0:T(8,128)}, u32[]{:S(2)}, u32[]{:S(2)}) collective-permute-start(f32[1280,128]{1,0:T(8,128)} %get-tuple-element.76), channel_id=1, source_target_pairs={{0,16},{8,24},{16,0},{24,8},{1,17},{9,25},{17,1},{25,9},{2,18},{10... | collective-permute-start | bytes 1966088 | tf_op jit(solution)/shard_map/ppermute | solution.py:246
  59.8 1.1 copy-start.2
  60.9 1.0 copy-start.4
  63.2 14.9 %collective-permute-start.11 = (f32[1024,128]{1,0:T(8,128)S(1)}, f32[1024,128]{1,0:T(8,128)S(1)}, u32[]{:S(2)}, u32[]{:S(2)}) collective-permute-start(f32[1024,128]{1,0:T(8,128)S(1)} %mix.9), channel_id=1, source_target_pairs={{0,8},{8,0},{16,24},{24,16},{1,9},{9,1},{17,25},{25,17},{2,10},{10... | collective-permute-start | bytes 1572872 | tf_op jit(solution)/shard_map/ppermute | solution.py:246
  63.8 14.9 %collective-permute-start.10 = (f32[1024,128]{1,0:T(8,128)S(1)}, f32[1024,128]{1,0:T(8,128)S(1)}, u32[]{:S(2)}, u32[]{:S(2)}) collective-permute-start(f32[1024,128]{1,0:T(8,128)S(1)} %mix.8), channel_id=1, source_target_pairs={{0,16},{8,24},{16,0},{24,8},{1,17},{9,25},{17,1},{25,9},{2,18},{10... | collective-permute-start | bytes 1572872 | tf_op jit(solution)/shard_map/ppermute | solution.py:246
  66.6 37.6 %collective-permute-start.13 = (f32[1280,128]{1,0:T(8,128)S(1)}, f32[1280,128]{1,0:T(8,128)S(1)}, u32[]{:S(2)}, u32[]{:S(2)}) collective-permute-start(f32[1280,128]{1,0:T(8,128)S(1)} %mix.11), channel_id=1, source_target_pairs={{0,16},{8,24},{16,0},{24,8},{1,17},{9,25},{17,1},{25,9},{2,18},{10... | collective-permute-start | bytes 1966088 | tf_op jit(solution)/shard_map/ppermute | solution.py:246
  69.8 2.7 %copy-start.7 = (f32[768,128]{1,0:T(8,128)S(1)}, f32[768,128]{1,0:T(8,128)}, u32[]{:S(2)}) copy-start(f32[768,128]{1,0:T(8,128)} %copy-done.6) | copy-start | bytes 1179652
  69.8 34.3 %collective-permute-start.14 = (f32[1280,128]{1,0:T(8,128)S(1)}, f32[1280,128]{1,0:T(8,128)S(1)}, u32[]{:S(2)}, u32[]{:S(2)}) collective-permute-start(f32[1280,128]{1,0:T(8,128)S(1)} %mix.12), channel_id=1, source_target_pairs={{0,8},{8,0},{16,24},{24,16},{1,9},{9,1},{17,25},{25,17},{2,10},{10... | collective-permute-start | bytes 1966088 | tf_op jit(solution)/shard_map/ppermute | solution.py:246
  71.4 32.0 %collective-permute-start.12 = (f32[1024,128]{1,0:T(8,128)S(1)}, f32[1024,128]{1,0:T(8,128)S(1)}, u32[]{:S(2)}, u32[]{:S(2)}) collective-permute-start(f32[1024,128]{1,0:T(8,128)S(1)} %mix.10), channel_id=1, source_target_pairs={{0,24},{8,16},{16,8},{24,0},{1,25},{9,17},{17,9},{25,1},{2,26},{10... | collective-permute-start | bytes 1572872 | tf_op jit(solution)/shard_map/ppermute | solution.py:246
  72.5 6.6 %copy-start.5 = (f32[1024,128]{1,0:T(8,128)S(1)}, f32[1024,128]{1,0:T(8,128)}, u32[]{:S(2)}) copy-start(f32[1024,128]{1,0:T(8,128)} %copy-done.3) | copy-start | bytes 1572868
  78.1 30.6 %collective-permute-start.16 = (f32[768,128]{1,0:T(8,128)S(1)}, f32[768,128]{1,0:T(8,128)S(1)}, u32[]{:S(2)}, u32[]{:S(2)}) collective-permute-start(f32[768,128]{1,0:T(8,128)S(1)} %mix.14), channel_id=1, source_target_pairs={{0,8},{8,0},{16,24},{24,16},{1,9},{9,1},{17,25},{25,17},{2,10},{10... | collective-permute-start | bytes 1179656 | tf_op jit(solution)/shard_map/ppermute | solution.py:246
  78.6 31.2 %collective-permute-start.15 = (f32[768,128]{1,0:T(8,128)S(1)}, f32[768,128]{1,0:T(8,128)S(1)}, u32[]{:S(2)}, u32[]{:S(2)}) collective-permute-start(f32[768,128]{1,0:T(8,128)S(1)} %mix.13), channel_id=1, source_target_pairs={{0,16},{8,24},{16,0},{24,8},{1,17},{9,25},{17,1},{25,9},{2,18},{10... | collective-permute-start | bytes 1179656 | tf_op jit(solution)/shard_map/ppermute | solution.py:246

commit v4 on v3

--- a/solution.py
+++ b/solution.py
@@ -17,6 +17,14 @@
 ANY_SPEC = pl.BlockSpec(memory_space=pl.ANY)
 HBM_SPEC = pl.BlockSpec(memory_space=pltpu.HBM)
 SHORT = pl.CostEstimate(flops=1, bytes_accessed=1, transcendentals=0)
+
+
+def in_hbm(array):
+    return pltpu.with_memory_space_constraint(array, pltpu.HBM)
+
+
+def in_vmem(array):
+    return pltpu.with_memory_space_constraint(array, pltpu.VMEM)
 
 
 def dense(block):
@@ -79,21 +87,39 @@
         compiler_params=pltpu.CompilerParams(vmem_limit_bytes=VMEM_LIMIT),
         cost_estimate=SHORT,
         name="gram",
-    )(me, *xs)
+    )(me, *map(in_vmem, xs))
+
+
+def add_kernel(*refs):
+    refs[-1][...] = sum((ref[...] for ref in refs[1:-1]), refs[0][...])
+
+
+def add(blocks):
+    return pl.pallas_call(
+        add_kernel,
+        out_shape=jax.ShapeDtypeStruct(blocks[0].shape, blocks[0].dtype),
+        in_specs=[VMEM_SPEC] * len(blocks),
+        out_specs=VMEM_SPEC,
+        compiler_params=pltpu.CompilerParams(vmem_limit_bytes=2**21),
+        cost_estimate=SHORT,
+        name="add",
+    )(*blocks)
 
 
 def exact(left, right):
     return jnp.dot(left, right, precision=lax.Precision.HIGHEST, preferred_element_type=jnp.float32)
 
 
-def weights_kernel(rows, count, me_ref, width_ref, grams_ref, drive_ref, repel_ref):
+def weights_kernel(rows, count, me_ref, width_ref, *refs):
+    grams, drive_ref, repel_ref = refs[:-2], refs[-2], refs[-1]
+
     def iota(shape, axis):
         return lax.broadcasted_iota(jnp.int32, shape, axis)
 
     def mask(condition):
         return jnp.where(condition, 1.0, 0.0)
 
-    flat = jnp.sum(grams_ref[...], axis=0)
+    flat = sum((ref[0] for ref in grams[1:]), grams[0][0])
     lines = flat.shape[0]
     per = LANES // count
     held = exact(mask(iota((count, lines), 0) // per == iota((count, lines), 1)), flat)
@@ -122,12 +148,12 @@
     return pl.pallas_call(
         functools.partial(weights_kernel, rows, count),
         out_shape=(shape, shape),
-        in_specs=[SMEM_SPEC, SMEM_SPEC, VMEM_SPEC],
+        in_specs=[SMEM_SPEC, SMEM_SPEC] + [VMEM_SPEC] * len(grams),
         out_specs=(VMEM_SPEC, VMEM_SPEC),
         compiler_params=pltpu.CompilerParams(vmem_limit_bytes=VMEM_LIMIT),
         cost_estimate=SHORT,
         name="weights",
-    )(me, width, grams)
+    )(me, width, *grams)
 
 
 def mix_kernel(rows, count, jobs, drive_ref, repel_ref, *refs):
@@ -189,7 +215,7 @@
         compiler_params=pltpu.CompilerParams(vmem_limit_bytes=VMEM_LIMIT),
         cost_estimate=SHORT,
         name="mix",
-    )(*coefs, *[block[0] if isinstance(block, tuple) else block for block in blocks])
+    )(*coefs, *[block[0] if isinstance(block, tuple) else in_vmem(block) for block in blocks])
 
 
 def put_kernel(entries, blocks, me_ref, *refs):
@@ -231,6 +257,41 @@
     )(me, *blocks, *extra)
 
 
+def cut_kernel(places, sizes, me_ref, block_ref, *refs):
+    outs, (in_sems, out_sems) = refs[: len(sizes)], refs[-2:]
+    through = refs[len(sizes) : -2]
+    copies = []
+    start = 0
+    for n, size in enumerate(sizes):
+        offset = (me_ref[0] ^ places[n]) * size if places else start
+        held = through[n] if through else outs[n]
+        copies.append(pltpu.make_async_copy(block_ref.at[pl.ds(offset, size), :], held, in_sems.at[n]))
+        copies[n].start()
+        start += size
+    for copy in copies:
+        copy.wait()
+    moves = [pltpu.make_async_copy(held, out, out_sems.at[n]) for n, (held, out) in enumerate(zip(through, outs))]
+    for move in moves:
+        move.start()
+    for move in moves:
+        move.wait()
+
+
+def cut(me, block, sizes, places=None):
+    out = pltpu.VMEM if places else pltpu.HBM
+    through = [] if places else [pltpu.VMEM((size, LANES), jnp.float32) for size in sizes]
+    return pl.pallas_call(
+        functools.partial(cut_kernel, places, sizes),
+        out_shape=[out((size, LANES), jnp.float32) for size in sizes],
+        in_specs=[SMEM_SPEC, HBM_SPEC],
+        out_specs=[VMEM_SPEC if places else HBM_SPEC] * len(sizes),
+        scratch_shapes=through + [pltpu.SemaphoreType.DMA((len(sizes),))] * 2,
+        compiler_params=pltpu.CompilerParams(vmem_limit_bytes=VMEM_LIMIT),
+        cost_estimate=SHORT,
+        name="cut",
+    )(me, in_hbm(block))
+
+
 def shards(particles, scores, kernel_width):
     groups = lax.axis_size("grp")
     rows = particles.shape[0]
@@ -242,20 +303,24 @@
     near = 2 ** ((groups.bit_length() - 1) // 2)
     lows, highs = list(range(near)), list(range(0, groups, near))
 
-    def swap(block, k):
-        return lax.ppermute(block, "grp", [(i, i ^ k) for i in range(groups)]) if k else block
+    def swap(block, k, axis="grp"):
+        return lax.ppermute(block, axis, [(i, i ^ k) for i in range(lax.axis_size(axis))]) if k else block
+
+    def stages(axis):
+        left, step = lax.axis_size(axis), 1
+        while left > 1:
+            radix = 4 if left % 4 == 0 else 2
+            yield [step * k for k in range(radix)]
+            left, step = left // radix, step * radix
 
     everyone, others = list(range(groups)), list(range(groups - 1, 0, -1))
     size, step = x.shape[0], SUB * rows
     first = max(1, half // step * 3 // 8) * step
     second = half - first
 
-    def cut(block, k):
-        return lax.dynamic_slice_in_dim(block, (me ^ k) * part, part, axis=0)
-
-    sent = [cut(x, k) for k in others + [0]]
+    sent = cut(place, x, [part] * groups, others + [0])
     s, sent = lax.optimization_barrier((s, sent))
-    s_own = [s[:first], s[first:half], s[half : half + first], s[half + first :]]
+    s_own = cut(place, s, [first, second] * 2)
     xs = {k: swap(block, k) for k, block in zip(others + [0], sent)}
     xs = [xs[k] for k in everyone]
 
@@ -264,18 +329,21 @@
 
     xs[-1], s_own = lax.optimization_barrier((xs[-1], s_own))
     early = exchange(s_own[0], s_own[2])
-    inner = gram(place, xs, rows, 1)
-    grams = [swap(inner, k) for k in everyone]
+    grams = [gram(place, xs, rows, 1)]
+    for partners in stages("grp"):
+        grams = [swap(add(grams) if len(grams) > 1 else grams[0], k) for k in partners]
     early, pair, grams = lax.optimization_barrier((early, (s_own[1], s_own[3]), grams))
     late = exchange(*pair)
-    coefs = weights(place, kernel_width, lax.psum(sum(grams[1:], grams[0]), "par"), rows, count)
+    for partners in stages("par"):
+        grams = [swap(add(grams), k, "par") for k in partners]
+    coefs = weights(place, kernel_width, grams, rows, count)
 
     def send(dest, jobs, coefs):
         mixed = mix(coefs, rows, count, jobs)
         return swap(mixed, dest), lax.optimization_barrier((coefs, mixed))[0]
 
     def score_job(dest, n, held, start, size):
-        own = (s, n * half + start, size)
+        own = (in_hbm(s), n * half + start, size)
         return (False, dest, (lows, highs)[n], [own] + [(block, 0, size) for block in held[n][1:]])
 
     near_by = [k for k in others if k in lows or k in highs]

time: 111 us -> 102 us (0.919)
  blocking collectives: 15.9 us -> 0 us
  starting transfers between devices: 18.3 us -> 26.9 us
  local copies, waits for them, and re-layouts: 6.69 us -> 0.01 us
  Pallas kernels: 17.8 us -> 22.8 us
    psum x1 -> x0, blocking collectives: 15.9 us -> none  [shards(): lax.psum(sum(grams[1:], grams[0]), 'par')]
    ppermute x17 -> x21, starting transfers between devices: 18.3 us -> 26.9 us  [swap(): lax.ppermute(block, axis, [(i, i ^ k) for i in range(lax.axis_size(axis))])]
    pallas_call x0 -> x4, Pallas kernels: none -> 4.5 us  [the longest x2 4.49 us: cut(): pl.pallas_call(functools.partial(cut_kernel, places, sizes), out_shape=[o...]
    unnamed x16 -> x4, local copies, waits for them, and re-layouts: 3.7 us -> 0.01 us
    dynamic_slice x1 -> x0, local copies, waits for them, and re-layouts: 1.81 us -> none  [cut(): return lax.dynamic_slice_in_dim(block, (me ^ k) * part, part, axis=0)]
    slice x2 -> x0, local copies, waits for them, and re-layouts: 1.19 us -> none  [shards(): s_own = [s[:first], s[first:half], s[half:half + first], s[half + first:]]]
    ppermute x17 -> x21, waiting for transfers between devices: 50.6 us -> 50.7 us  [swap(): lax.ppermute(block, axis, [(i, i ^ k) for i in range(lax.axis_size(axis))])]
  transfers between devices with their start and end apart: 17 -> 21, of which waited for: 9 -> 13; matrix products, arithmetic and copies ran while one was open for 1% -> 0% of each run, Pallas kernels for 15% -> 20%
where the time goes in v4:
time: 102 us
  waiting for transfers between devices  50.7 us (50%)
  starting transfers between devices  26.9 us (26%)
  Pallas kernels  22.8 us (22%)
  between operations  1.46 us (1%)
    ppermute x21, waiting for transfers between devices, swap(): lax.ppermute(block, axis, [(i, i ^ k) for i in range(lax.axis_size(axis))])  50.7 us
    ppermute x21, starting transfers between devices, swap(): lax.ppermute(block, axis, [(i, i ^ k) for i in range(lax.axis_size(axis))])  26.9 us
    pallas_call x8, Pallas kernels, mix(): pl.pallas_call(functools.partial(mix_kernel, rows, count, spans), out_sha...  9.83 us
    pallas_call x6, Pallas kernels, put(): pl.pallas_call(functools.partial(put_kernel, entries, len(blocks)), out_s...  5.29 us
    pallas_call x2, Pallas kernels, cut(): pl.pallas_call(functools.partial(cut_kernel, places, sizes), out_shape=[o...  4.49 us
    pallas_call x1, Pallas kernels, gram(): pl.pallas_call(functools.partial(gram_kernel, rows, groups), out_shape=ja...  2.28 us
  transfers between devices with their start and end apart: 21, of which 13 were waited for; matrix products, arithmetic and copies ran while one was open for 0% of the time, Pallas kernels for 20%

profile of v4, /device:TPU:0, one launch (start us, length us, event | category | flops | bytes accessed | tf_op | source)
XLA Modules:
  0.0 101.8 jit_solution(8961614252941745209)
XLA Ops:
  0.6 1.6 %cut.2 = (f32[1024,128]{1,0:T(8,128)S(1)}, f32[1024,128]{1,0:T(8,128)S(1)}, f32[1024,128]{1,0:T(8,128)S(1)}, f32[1024,128]{1,0:T(8,128)S(1)}) custom-call(s32[1]{0:T(128)} %bitcast.me_ref, f32[4096,128]{1,0:T(8,128)} %bitcast.32), custom_call_target="tpu_custom_call" | custom-call | flops 1 | bytes 1 | tf_op jit(solution)/shard_map/cut/pallas_call | solution.py:283
  2.2 4.0 %collective-permute-start = (f32[1024,128]{1,0:T(8,128)S(1)}, f32[1024,128]{1,0:T(8,128)S(1)}, u32[]{:S(2)}, u32[]{:S(2)}) collective-permute-start(f32[1024,128]{1,0:T(8,128)S(1)} %get-tuple-element.63), channel_id=1, source_target_pairs={{0,24},{8,16},{16,8},{24,0},{1,25},{9,17},{17,9},{25,1},{2,26},{10... | collective-permute-start | bytes 1572872 | tf_op jit(solution)/shard_map/ppermute | solution.py:307
  6.8 2.9 %cut.3 = (f32[768,128]{1,0:T(8,128)}, f32[1280,128]{1,0:T(8,128)}, f32[768,128]{1,0:T(8,128)}, f32[1280,128]{1,0:T(8,128)}) custom-call(s32[1]{0:T(128)} %bitcast.me_ref, f32[4096,128]{1,0:T(8,128)} %bitcast.21), custom_call_target="tpu_custom_call" | custom-call | flops 1 | bytes 1 | tf_op jit(solution)/shard_map/cut/pallas_call | solution.py:283
  9.8 9.2 %collective-permute-done.refs_3_ = f32[1024,128]{1,0:T(8,128)S(1)} collective-permute-done((f32[1024,128]{1,0:T(8,128)S(1)}, f32[1024,128]{1,0:T(8,128)S(1)}, u32[]{:S(2)}, u32[]{:S(2)}) %collective-permute-start) | collective-permute-done | bytes 524320 | tf_op jit(solution)/shard_map/ppermute | solution.py:307
  19.0 2.0 %collective-permute-start.1 = (f32[768,128]{1,0:T(8,128)}, f32[768,128]{1,0:T(8,128)S(1)}, u32[]{:S(2)}, u32[]{:S(2)}) collective-permute-start(f32[768,128]{1,0:T(8,128)} %get-tuple-element.69), channel_id=1, source_target_pairs={{0,8},{8,0},{16,24},{24,16},{1,9},{9,1},{17,25},{25,17},{2,10},{10... | collective-permute-start | bytes 1179656 | tf_op jit(solution)/shard_map/ppermute | solution.py:307
  21.0 1.5 %collective-permute-start.2 = (f32[768,128]{1,0:T(8,128)}, f32[768,128]{1,0:T(8,128)S(1)}, u32[]{:S(2)}, u32[]{:S(2)}) collective-permute-start(f32[768,128]{1,0:T(8,128)} %get-tuple-element.70), channel_id=1, source_target_pairs={{0,16},{8,24},{16,0},{24,8},{1,17},{9,25},{17,1},{25,9},{2,18},{10... | collective-permute-start | bytes 1179656 | tf_op jit(solution)/shard_map/ppermute | solution.py:307
  22.5 8.3 %collective-permute-done.3.refs_1_ = f32[1024,128]{1,0:T(8,128)S(1)} collective-permute-done((f32[1024,128]{1,0:T(8,128)S(1)}, f32[1024,128]{1,0:T(8,128)S(1)}, u32[]{:S(2)}, u32[]{:S(2)}) %collective-permute-start.3) | collective-permute-done | bytes 524320 | tf_op jit(solution)/shard_map/ppermute | solution.py:307
  30.8 2.3 %gram.1.refs_0_ = f32[1,2,128]{2,1,0:T(2,128)S(1)} custom-call(s32[1]{0:T(128)} %bitcast.me_ref, f32[1024,128]{1,0:T(8,128)S(1)} %get-tuple-element.73.refs_0_, f32[1024,128]{1,0:T(8,128)S(1)} %collective-permute-done.3.refs_1_, f32[1024,128]{1,0:T(8,128)S(1)} %collective-permute-done.4.refs_2_, f32[1024,128]{1,0:T(8,128)S(1)} %collective-permute-done.refs_3_), custom_call_target="tpu_custom_call" | custom-call | flops 1 | bytes 1 | tf_op jit(solution)/shard_map/gram/pallas_call | solution.py:81
  33.1 1.5 %collective-permute-start.7 = (f32[1,2,128]{2,1,0:T(2,128)S(1)}, f32[1,2,128]{2,1,0:T(2,128)S(1)}, u32[]{:S(2)}, u32[]{:S(2)}) collective-permute-start(f32[1,2,128]{2,1,0:T(2,128)S(1)} %gram.1.refs_0_), channel_id=1, source_target_pairs={{0,24},{8,16},{16,8},{24,0},{1,25},{9,17},{17,9},{25,1},{2,26},{10... | collective-permute-start | bytes 3080 | tf_op jit(solution)/shard_map/ppermute | solution.py:307
  34.5 1.5 %collective-permute-start.6 = (f32[1,2,128]{2,1,0:T(2,128)S(1)}, f32[1,2,128]{2,1,0:T(2,128)S(1)}, u32[]{:S(2)}, u32[]{:S(2)}) collective-permute-start(f32[1,2,128]{2,1,0:T(2,128)S(1)} %gram.1.refs_0_), channel_id=1, source_target_pairs={{0,16},{8,24},{16,0},{24,8},{1,17},{9,25},{17,1},{25,9},{2,18},{10... | collective-permute-start | bytes 3080 | tf_op jit(solution)/shard_map/ppermute | solution.py:307
  36.6 1.2 %collective-permute-done.7.refs_3_ = f32[1,2,128]{2,1,0:T(2,128)S(1)} collective-permute-done((f32[1,2,128]{2,1,0:T(2,128)S(1)}, f32[1,2,128]{2,1,0:T(2,128)S(1)}, u32[]{:S(2)}, u32[]{:S(2)}) %collective-permute-start.7) | collective-permute-done | bytes 1056 | tf_op jit(solution)/shard_map/ppermute | solution.py:307
  38.1 1.5 %collective-permute-done.5.refs_1_ = f32[1,2,128]{2,1,0:T(2,128)S(1)} collective-permute-done((f32[1,2,128]{2,1,0:T(2,128)S(1)}, f32[1,2,128]{2,1,0:T(2,128)S(1)}, u32[]{:S(2)}, u32[]{:S(2)}) %collective-permute-start.5) | collective-permute-done | bytes 1056 | tf_op jit(solution)/shard_map/ppermute | solution.py:307
  41.7 1.1 %collective-permute-start.9 = (f32[1,2,128]{2,1,0:T(2,128)S(1)}, f32[1,2,128]{2,1,0:T(2,128)S(1)}, u32[]{:S(2)}, u32[]{:S(2)}) collective-permute-start(f32[1,2,128]{2,1,0:T(2,128)S(1)} %add.2.refs_0_), channel_id=1, source_target_pairs={{0,2},{1,3},{2,0},{3,1},{4,6},{5,7},{6,4},{7,5},{8,10},{9,11},{10,... | collective-permute-start | bytes 3080 | tf_op jit(solution)/shard_map/ppermute | solution.py:307
  43.0 1.1 %collective-permute-done.10.refs_3_ = f32[1,2,128]{2,1,0:T(2,128)S(1)} collective-permute-done((f32[1,2,128]{2,1,0:T(2,128)S(1)}, f32[1,2,128]{2,1,0:T(2,128)S(1)}, u32[]{:S(2)}, u32[]{:S(2)}) %collective-permute-start.10) | collective-permute-done | bytes 1056 | tf_op jit(solution)/shard_map/ppermute | solution.py:307
  44.2 1.2 %collective-permute-done.9.refs_2_ = f32[1,2,128]{2,1,0:T(2,128)S(1)} collective-permute-done((f32[1,2,128]{2,1,0:T(2,128)S(1)}, f32[1,2,128]{2,1,0:T(2,128)S(1)}, u32[]{:S(2)}, u32[]{:S(2)}) %collective-permute-start.9) | collective-permute-done | bytes 1056 | tf_op jit(solution)/shard_map/ppermute | solution.py:307
  45.3 2.7 %collective-permute-start.11 = (f32[1,2,128]{2,1,0:T(2,128)S(1)}, f32[1,2,128]{2,1,0:T(2,128)S(1)}, u32[]{:S(2)}, u32[]{:S(2)}) collective-permute-start(f32[1,2,128]{2,1,0:T(2,128)S(1)} %add.3.refs_0_), channel_id=1, source_target_pairs={{0,4},{1,5},{2,6},{3,7},{4,0},{5,1},{6,2},{7,3},{8,12},{9,13},{10,... | collective-permute-start | bytes 3080 | tf_op jit(solution)/shard_map/ppermute | solution.py:307
  48.6 1.2 %collective-permute-done.11.refs_1_ = f32[1,2,128]{2,1,0:T(2,128)S(1)} collective-permute-done((f32[1,2,128]{2,1,0:T(2,128)S(1)}, f32[1,2,128]{2,1,0:T(2,128)S(1)}, u32[]{:S(2)}, u32[]{:S(2)}) %collective-permute-start.11) | collective-permute-done | bytes 1056 | tf_op jit(solution)/shard_map/ppermute | solution.py:307
  52.6 1.5 %collective-permute-start.14 = (f32[1024,128]{1,0:T(8,128)S(1)}, f32[1024,128]{1,0:T(8,128)S(1)}, u32[]{:S(2)}, u32[]{:S(2)}) collective-permute-start(f32[1024,128]{1,0:T(8,128)S(1)} %mix.8), channel_id=1, source_target_pairs={{0,16},{8,24},{16,0},{24,8},{1,17},{9,25},{17,1},{25,9},{2,18},{10... | collective-permute-start | bytes 1572872 | tf_op jit(solution)/shard_map/ppermute | solution.py:307
  55.3 1.5 %mix.11 = f32[1280,128]{1,0:T(8,128)S(1)} custom-call(f32[256,128]{1,0:T(8,128)S(1)} %get-tuple-element.99.drive_ref, f32[256,128]{1,0:T(8,128)S(1)} %get-tuple-element.100.repel_ref, f32[4096,128]{1,0:T(8,128)} %bitcast.22, f32[1280,128]{1,0:T(8,128)S(1)} %collective-permute-done.12.refs_1_.refs_5_), custom_call_target="tpu_custom_call" | custom-call | flops 1 | bytes 1 | tf_op jit(solution)/shard_map/mix/pallas_call | solution.py:209
  56.7 2.4 %collective-permute-start.17 = (f32[1280,128]{1,0:T(8,128)S(1)}, f32[1280,128]{1,0:T(8,128)S(1)}, u32[]{:S(2)}, u32[]{:S(2)}) collective-permute-start(f32[1280,128]{1,0:T(8,128)S(1)} %mix.11), channel_id=1, source_target_pairs={{0,16},{8,24},{16,0},{24,8},{1,17},{9,25},{17,1},{25,9},{2,18},{10... | collective-permute-start | bytes 1966088 | tf_op jit(solution)/shard_map/ppermute | solution.py:307
  59.1 1.5 %mix.12 = f32[1280,128]{1,0:T(8,128)S(1)} custom-call(f32[256,128]{1,0:T(8,128)S(1)} %get-tuple-element.99.drive_ref, f32[256,128]{1,0:T(8,128)S(1)} %get-tuple-element.100.repel_ref, f32[4096,128]{1,0:T(8,128)} %bitcast.23, f32[1280,128]{1,0:T(8,128)S(1)} %collective-permute-done.13.refs_1_.refs_7_), custom_call_target="tpu_custom_call" | custom-call | flops 1 | bytes 1 | tf_op jit(solution)/shard_map/mix/pallas_call | solution.py:209
  60.6 1.3 %collective-permute-start.18 = (f32[1280,128]{1,0:T(8,128)S(1)}, f32[1280,128]{1,0:T(8,128)S(1)}, u32[]{:S(2)}, u32[]{:S(2)}) collective-permute-start(f32[1280,128]{1,0:T(8,128)S(1)} %mix.12), channel_id=1, source_target_pairs={{0,8},{8,0},{16,24},{24,16},{1,9},{9,1},{17,25},{25,17},{2,10},{10... | collective-permute-start | bytes 1966088 | tf_op jit(solution)/shard_map/ppermute | solution.py:307
  62.1 1.2 %mix.13 = f32[768,128]{1,0:T(8,128)S(1)} custom-call(f32[256,128]{1,0:T(8,128)S(1)} %get-tuple-element.99.drive_ref, f32[256,128]{1,0:T(8,128)S(1)} %get-tuple-element.100.repel_ref, f32[4096,128]{1,0:T(8,128)} %bitcast.24, f32[768,128]{1,0:T(8,128)S(1)} %collective-permute-done.1.refs_1_.refs_9_), custom_call_target="tpu_custom_call" | custom-call | flops 1 | bytes 1 | tf_op jit(solution)/shard_map/mix/pallas_call | solution.py:209
  63.4 1.2 %mix.14 = f32[768,128]{1,0:T(8,128)S(1)} custom-call(f32[256,128]{1,0:T(8,128)S(1)} %get-tuple-element.99.drive_ref, f32[256,128]{1,0:T(8,128)S(1)} %get-tuple-element.100.repel_ref, f32[4096,128]{1,0:T(8,128)} %bitcast.25, f32[768,128]{1,0:T(8,128)S(1)} %collective-permute-done.2.refs_1_.refs_11_), custom_call_target="tpu_custom_call" | custom-call | flops 1 | bytes 1 | tf_op jit(solution)/shard_map/mix/pallas_call | solution.py:209
  64.6 2.3 %collective-permute-done.15.refs_0_ = f32[1024,128]{1,0:T(8,128)S(1)} collective-permute-done((f32[1024,128]{1,0:T(8,128)S(1)}, f32[1024,128]{1,0:T(8,128)S(1)}, u32[]{:S(2)}, u32[]{:S(2)}) %collective-permute-start.15) | collective-permute-done | bytes 524320 | tf_op jit(solution)/shard_map/ppermute | solution.py:307
  66.9 1.8 %collective-permute-start.20 = (f32[768,128]{1,0:T(8,128)S(1)}, f32[768,128]{1,0:T(8,128)S(1)}, u32[]{:S(2)}, u32[]{:S(2)}) collective-permute-start(f32[768,128]{1,0:T(8,128)S(1)} %mix.14), channel_id=1, source_target_pairs={{0,8},{8,0},{16,24},{24,16},{1,9},{9,1},{17,25},{25,17},{2,10},{10... | collective-permute-start | bytes 1179656 | tf_op jit(solution)/shard_map/ppermute | solution.py:307
  68.8 1.3 %collective-permute-start.19 = (f32[768,128]{1,0:T(8,128)S(1)}, f32[768,128]{1,0:T(8,128)S(1)}, u32[]{:S(2)}, u32[]{:S(2)}) collective-permute-start(f32[768,128]{1,0:T(8,128)S(1)} %mix.13), channel_id=1, source_target_pairs={{0,16},{8,24},{16,0},{24,8},{1,17},{9,25},{17,1},{25,9},{2,18},{10... | collective-permute-start | bytes 1179656 | tf_op jit(solution)/shard_map/ppermute | solution.py:307
  70.0 2.6 %mix.15.refs_0_ = f32[5120,128]{1,0:T(8,128)S(1)} custom-call(f32[256,128]{1,0:T(8,128)S(1)} %get-tuple-element.99.drive_ref, f32[256,128]{1,0:T(8,128)S(1)} %get-tuple-element.100.repel_ref, f32[1024,128]{1,0:T(8,128)S(1)} %get-tuple-element.73.refs_0_, f32[1024,128]{1,0:T(8,128)S(1)} %collective-permute-done.3.refs_1_, ...), custom_call_target="tpu_custom_call" | custom-call | flops 1 | bytes 1 | tf_op jit(solution)/shard_map/mix/pallas_call | solution.py:209
  75.1 18.5 %collective-permute-done.16.refs_0_ = f32[1024,128]{1,0:T(8,128)S(1)} collective-permute-done((f32[1024,128]{1,0:T(8,128)S(1)}, f32[1024,128]{1,0:T(8,128)S(1)}, u32[]{:S(2)}, u32[]{:S(2)}) %collective-permute-start.16) | collective-permute-done | bytes 524320 | tf_op jit(solution)/shard_map/ppermute | solution.py:307
  94.4 1.1 %put.10.refs_3_ = f32[4096,128]{1,0:T(8,128)} custom-call(s32[1]{0:T(128)} %bitcast.me_ref, f32[5120,128]{1,0:T(8,128)S(1)} %mix.15.refs_0_, f32[1280,128]{1,0:T(8,128)S(1)} %collective-permute-done.17.refs_1_, f32[1280,128]{1,0:T(8,128)S(1)} %collective-permute-done.18.refs_2_), custom_call_target="tpu_custom_call" | custom-call | bytes 2621440 | tf_op jit(solution)/shard_map/put/pallas_call | solution.py:247
  95.5 4.0 %collective-permute-done.20.refs_2_ = f32[768,128]{1,0:T(8,128)S(1)} collective-permute-done((f32[768,128]{1,0:T(8,128)S(1)}, f32[768,128]{1,0:T(8,128)S(1)}, u32[]{:S(2)}, u32[]{:S(2)}) %collective-permute-start.20) | collective-permute-done | bytes 393248 | tf_op jit(solution)/shard_map/ppermute | solution.py:307
  99.5 1.4 %collective-permute-done.19.refs_1_ = f32[768,128]{1,0:T(8,128)S(1)} collective-permute-done((f32[768,128]{1,0:T(8,128)S(1)}, f32[768,128]{1,0:T(8,128)S(1)}, u32[]{:S(2)}, u32[]{:S(2)}) %collective-permute-start.19) | collective-permute-done | bytes 393248 | tf_op jit(solution)/shard_map/ppermute | solution.py:307
  (34 shorter events, 12.1 us)
Async XLA Ops:
  2.2 16.8 %collective-permute-start = (f32[1024,128]{1,0:T(8,128)S(1)}, f32[1024,128]{1,0:T(8,128)S(1)}, u32[]{:S(2)}, u32[]{:S(2)}) collective-permute-start(f32[1024,128]{1,0:T(8,128)S(1)} %get-tuple-element.63), channel_id=1, source_target_pairs={{0,24},{8,16},{16,8},{24,0},{1,25},{9,17},{17,9},{25,1},{2,26},{10... | collective-permute-start | bytes 1572872 | tf_op jit(solution)/shard_map/ppermute | solution.py:307
  6.2 24.6 %collective-permute-start.3 = (f32[1024,128]{1,0:T(8,128)S(1)}, f32[1024,128]{1,0:T(8,128)S(1)}, u32[]{:S(2)}, u32[]{:S(2)}) collective-permute-start(f32[1024,128]{1,0:T(8,128)S(1)} %get-tuple-element.74), channel_id=1, source_target_pairs={{0,8},{8,0},{16,24},{24,16},{1,9},{9,1},{17,25},{25,17},{2,10},{10... | collective-permute-start | bytes 1572872 | tf_op jit(solution)/shard_map/ppermute | solution.py:307
  6.7 24.1 %collective-permute-start.4 = (f32[1024,128]{1,0:T(8,128)S(1)}, f32[1024,128]{1,0:T(8,128)S(1)}, u32[]{:S(2)}, u32[]{:S(2)}) collective-permute-start(f32[1024,128]{1,0:T(8,128)S(1)} %get-tuple-element.75), channel_id=1, source_target_pairs={{0,16},{8,24},{16,0},{24,8},{1,17},{9,25},{17,1},{25,9},{2,18},{10... | collective-permute-start | bytes 1572872 | tf_op jit(solution)/shard_map/ppermute | solution.py:307
  9.7 29.9 %copy-start.1 = (f32[1280,128]{1,0:T(8,128)S(1)}, f32[1280,128]{1,0:T(8,128)}, u32[]{:S(2)}) copy-start(f32[1280,128]{1,0:T(8,128)} %get-tuple-element.89) | copy-start | bytes 1966084
  9.8 30.5 %copy-start = (f32[1280,128]{1,0:T(8,128)S(1)}, f32[1280,128]{1,0:T(8,128)}, u32[]{:S(2)}) copy-start(f32[1280,128]{1,0:T(8,128)} %get-tuple-element.92) | copy-start | bytes 1966084
  19.0 20.6 %collective-permute-start.1 = (f32[768,128]{1,0:T(8,128)}, f32[768,128]{1,0:T(8,128)S(1)}, u32[]{:S(2)}, u32[]{:S(2)}) collective-permute-start(f32[768,128]{1,0:T(8,128)} %get-tuple-element.69), channel_id=1, source_target_pairs={{0,8},{8,0},{16,24},{24,16},{1,9},{9,1},{17,25},{25,17},{2,10},{10... | collective-permute-start | bytes 1179656 | tf_op jit(solution)/shard_map/ppermute | solution.py:307
  21.0 18.7 %collective-permute-start.2 = (f32[768,128]{1,0:T(8,128)}, f32[768,128]{1,0:T(8,128)S(1)}, u32[]{:S(2)}, u32[]{:S(2)}) collective-permute-start(f32[768,128]{1,0:T(8,128)} %get-tuple-element.70), channel_id=1, source_target_pairs={{0,16},{8,24},{16,0},{24,8},{1,17},{9,25},{17,1},{25,9},{2,18},{10... | collective-permute-start | bytes 1179656 | tf_op jit(solution)/shard_map/ppermute | solution.py:307
  33.1 4.8 %collective-permute-start.7 = (f32[1,2,128]{2,1,0:T(2,128)S(1)}, f32[1,2,128]{2,1,0:T(2,128)S(1)}, u32[]{:S(2)}, u32[]{:S(2)}) collective-permute-start(f32[1,2,128]{2,1,0:T(2,128)S(1)} %gram.1.refs_0_), channel_id=1, source_target_pairs={{0,24},{8,16},{16,8},{24,0},{1,25},{9,17},{17,9},{25,1},{2,26},{10... | collective-permute-start | bytes 3080 | tf_op jit(solution)/shard_map/ppermute | solution.py:307
  34.5 3.6 %collective-permute-start.6 = (f32[1,2,128]{2,1,0:T(2,128)S(1)}, f32[1,2,128]{2,1,0:T(2,128)S(1)}, u32[]{:S(2)}, u32[]{:S(2)}) collective-permute-start(f32[1,2,128]{2,1,0:T(2,128)S(1)} %gram.1.refs_0_), channel_id=1, source_target_pairs={{0,16},{8,24},{16,0},{24,8},{1,17},{9,25},{17,1},{25,9},{2,18},{10... | collective-permute-start | bytes 3080 | tf_op jit(solution)/shard_map/ppermute | solution.py:307
  36.1 3.6 %collective-permute-start.5 = (f32[1,2,128]{2,1,0:T(2,128)S(1)}, f32[1,2,128]{2,1,0:T(2,128)S(1)}, u32[]{:S(2)}, u32[]{:S(2)}) collective-permute-start(f32[1,2,128]{2,1,0:T(2,128)S(1)} %gram.1.refs_0_), channel_id=1, source_target_pairs={{0,8},{8,0},{16,24},{24,16},{1,9},{9,1},{17,25},{25,17},{2,10},{10... | collective-permute-start | bytes 3080 | tf_op jit(solution)/shard_map/ppermute | solution.py:307
  39.6 15.6 %collective-permute-start.12 = (f32[1280,128]{1,0:T(8,128)S(1)}, f32[1280,128]{1,0:T(8,128)S(1)}, u32[]{:S(2)}, u32[]{:S(2)}) collective-permute-start(f32[1280,128]{1,0:T(8,128)S(1)} %copy-done.1), channel_id=1, source_target_pairs={{0,8},{8,0},{16,24},{24,16},{1,9},{9,1},{17,25},{25,17},{2,10},{10... | collective-permute-start | bytes 1966088 | tf_op jit(solution)/shard_map/ppermute | solution.py:307
  40.2 18.9 %collective-permute-start.13 = (f32[1280,128]{1,0:T(8,128)S(1)}, f32[1280,128]{1,0:T(8,128)S(1)}, u32[]{:S(2)}, u32[]{:S(2)}) collective-permute-start(f32[1280,128]{1,0:T(8,128)S(1)} %copy-done), channel_id=1, source_target_pairs={{0,16},{8,24},{16,0},{24,8},{1,17},{9,25},{17,1},{25,9},{2,18},{10... | collective-permute-start | bytes 1966088 | tf_op jit(solution)/shard_map/ppermute | solution.py:307
  41.2 3.0 %collective-permute-start.10 = (f32[1,2,128]{2,1,0:T(2,128)S(1)}, f32[1,2,128]{2,1,0:T(2,128)S(1)}, u32[]{:S(2)}, u32[]{:S(2)}) collective-permute-start(f32[1,2,128]{2,1,0:T(2,128)S(1)} %add.2.refs_0_), channel_id=1, source_target_pairs={{0,3},{1,2},{2,1},{3,0},{4,7},{5,6},{6,5},{7,4},{8,11},{9,10},{10,... | collective-permute-start | bytes 3080 | tf_op jit(solution)/shard_map/ppermute | solution.py:307
  41.7 3.6 %collective-permute-start.9 = (f32[1,2,128]{2,1,0:T(2,128)S(1)}, f32[1,2,128]{2,1,0:T(2,128)S(1)}, u32[]{:S(2)}, u32[]{:S(2)}) collective-permute-start(f32[1,2,128]{2,1,0:T(2,128)S(1)} %add.2.refs_0_), channel_id=1, source_target_pairs={{0,2},{1,3},{2,0},{3,1},{4,6},{5,7},{6,4},{7,5},{8,10},{9,11},{10,... | collective-permute-start | bytes 3080 | tf_op jit(solution)/shard_map/ppermute | solution.py:307
  42.8 2.5 %collective-permute-start.8 = (f32[1,2,128]{2,1,0:T(2,128)S(1)}, f32[1,2,128]{2,1,0:T(2,128)S(1)}, u32[]{:S(2)}, u32[]{:S(2)}) collective-permute-start(f32[1,2,128]{2,1,0:T(2,128)S(1)} %add.2.refs_0_), channel_id=1, source_target_pairs={{0,1},{1,0},{2,3},{3,2},{4,5},{5,4},{6,7},{7,6},{8,9},{9,8},{10,11... | collective-permute-start | bytes 3080 | tf_op jit(solution)/shard_map/ppermute | solution.py:307
  45.3 4.5 %collective-permute-start.11 = (f32[1,2,128]{2,1,0:T(2,128)S(1)}, f32[1,2,128]{2,1,0:T(2,128)S(1)}, u32[]{:S(2)}, u32[]{:S(2)}) collective-permute-start(f32[1,2,128]{2,1,0:T(2,128)S(1)} %add.3.refs_0_), channel_id=1, source_target_pairs={{0,4},{1,5},{2,6},{3,7},{4,0},{5,1},{6,2},{7,3},{8,12},{9,13},{10,... | collective-permute-start | bytes 3080 | tf_op jit(solution)/shard_map/ppermute | solution.py:307
  52.0 14.9 %collective-permute-start.15 = (f32[1024,128]{1,0:T(8,128)S(1)}, f32[1024,128]{1,0:T(8,128)S(1)}, u32[]{:S(2)}, u32[]{:S(2)}) collective-permute-start(f32[1024,128]{1,0:T(8,128)S(1)} %mix.9), channel_id=1, source_target_pairs={{0,8},{8,0},{16,24},{24,16},{1,9},{9,1},{17,25},{25,17},{2,10},{10... | collective-permute-start | bytes 1572872 | tf_op jit(solution)/shard_map/ppermute | solution.py:307
  52.6 16.1 %collective-permute-start.14 = (f32[1024,128]{1,0:T(8,128)S(1)}, f32[1024,128]{1,0:T(8,128)S(1)}, u32[]{:S(2)}, u32[]{:S(2)}) collective-permute-start(f32[1024,128]{1,0:T(8,128)S(1)} %mix.8), channel_id=1, source_target_pairs={{0,16},{8,24},{16,0},{24,8},{1,17},{9,25},{17,1},{25,9},{2,18},{10... | collective-permute-start | bytes 1572872 | tf_op jit(solution)/shard_map/ppermute | solution.py:307
  56.7 37.6 %collective-permute-start.17 = (f32[1280,128]{1,0:T(8,128)S(1)}, f32[1280,128]{1,0:T(8,128)S(1)}, u32[]{:S(2)}, u32[]{:S(2)}) collective-permute-start(f32[1280,128]{1,0:T(8,128)S(1)} %mix.11), channel_id=1, source_target_pairs={{0,16},{8,24},{16,0},{24,8},{1,17},{9,25},{17,1},{25,9},{2,18},{10... | collective-permute-start | bytes 1966088 | tf_op jit(solution)/shard_map/ppermute | solution.py:307
  60.6 33.8 %collective-permute-start.18 = (f32[1280,128]{1,0:T(8,128)S(1)}, f32[1280,128]{1,0:T(8,128)S(1)}, u32[]{:S(2)}, u32[]{:S(2)}) collective-permute-start(f32[1280,128]{1,0:T(8,128)S(1)} %mix.12), channel_id=1, source_target_pairs={{0,8},{8,0},{16,24},{24,16},{1,9},{9,1},{17,25},{25,17},{2,10},{10... | collective-permute-start | bytes 1966088 | tf_op jit(solution)/shard_map/ppermute | solution.py:307
  61.8 31.7 %collective-permute-start.16 = (f32[1024,128]{1,0:T(8,128)S(1)}, f32[1024,128]{1,0:T(8,128)S(1)}, u32[]{:S(2)}, u32[]{:S(2)}) collective-permute-start(f32[1024,128]{1,0:T(8,128)S(1)} %mix.10), channel_id=1, source_target_pairs={{0,24},{8,16},{16,8},{24,0},{1,25},{9,17},{17,9},{25,1},{2,26},{10... | collective-permute-start | bytes 1572872 | tf_op jit(solution)/shard_map/ppermute | solution.py:307
  66.9 32.6 %collective-permute-start.20 = (f32[768,128]{1,0:T(8,128)S(1)}, f32[768,128]{1,0:T(8,128)S(1)}, u32[]{:S(2)}, u32[]{:S(2)}) collective-permute-start(f32[768,128]{1,0:T(8,128)S(1)} %mix.14), channel_id=1, source_target_pairs={{0,8},{8,0},{16,24},{24,16},{1,9},{9,1},{17,25},{25,17},{2,10},{10... | collective-permute-start | bytes 1179656 | tf_op jit(solution)/shard_map/ppermute | solution.py:307
  68.8 32.1 %collective-permute-start.19 = (f32[768,128]{1,0:T(8,128)S(1)}, f32[768,128]{1,0:T(8,128)S(1)}, u32[]{:S(2)}, u32[]{:S(2)}) collective-permute-start(f32[768,128]{1,0:T(8,128)S(1)} %mix.13), channel_id=1, source_target_pairs={{0,16},{8,24},{16,0},{24,8},{1,17},{9,25},{17,1},{25,9},{2,18},{10... | collective-permute-start | bytes 1179656 | tf_op jit(solution)/shard_map/ppermute | solution.py:307

commit v5 on v4

--- a/solution.py
+++ b/solution.py
@@ -36,9 +36,9 @@
     return block.reshape(-1, rows, LANES).transpose(1, 0, 2).reshape(rows, -1)
 
 
-def gram_kernel(rows, groups, me_ref, *refs):
+def gram_kernel(rows, groups, *refs):
     xs, out_ref, acc_ref = refs[:groups], refs[groups], refs[groups + 1]
-    me = me_ref[0]
+    me = lax.axis_index("grp")
     count = rows * groups
     step = SUB * rows
     steps = xs[0].shape[0] // step
@@ -75,19 +75,19 @@
         out_ref[:, n : n + 1, :] = jnp.broadcast_to(row[None], (out_ref.shape[0], 1, LANES))
 
 
-def gram(me, xs, rows, copies):
+def gram(xs, rows, copies):
     groups = len(xs)
     count = rows * groups
     return pl.pallas_call(
         functools.partial(gram_kernel, rows, groups),
         out_shape=jax.ShapeDtypeStruct((copies, count * count // LANES, LANES), jnp.float32),
-        in_specs=[SMEM_SPEC] + [VMEM_SPEC] * groups,
+        in_specs=[VMEM_SPEC] * groups,
         out_specs=VMEM_SPEC,
         scratch_shapes=[pltpu.VMEM((count * count, LANES), jnp.float32)],
         compiler_params=pltpu.CompilerParams(vmem_limit_bytes=VMEM_LIMIT),
         cost_estimate=SHORT,
         name="gram",
-    )(me, *map(in_vmem, xs))
+    )(*map(in_vmem, xs))
 
 
 def add_kernel(*refs):
@@ -110,7 +110,8 @@
     return jnp.dot(left, right, precision=lax.Precision.HIGHEST, preferred_element_type=jnp.float32)
 
 
-def weights_kernel(rows, count, me_ref, width_ref, *refs):
+def weights_kernel(rows, count, width_ref, *refs):
+    me = lax.axis_index("grp")
     grams, drive_ref, repel_ref = refs[:-2], refs[-2], refs[-1]
 
     def iota(shape, axis):
@@ -127,7 +128,7 @@
     inner = exact(held, mask(iota((LANES, count), 0) % count == iota((LANES, count), 1)))
     square = (count, count)
     r, c = iota(square, 0), iota(square, 1)
-    order = mask(((me_ref[0] ^ (r // rows)) * rows + r % rows) == c)
+    order = mask(((me ^ (r // rows)) * rows + r % rows) == c)
     inner = exact(exact(order, inner), order)
 
     width = width_ref[0]
@@ -143,17 +144,17 @@
         repel_ref[j * count : (j + 1) * count, :] = jnp.broadcast_to(to_repel[:, j : j + 1], (count, LANES))
 
 
-def weights(me, width, grams, rows, count):
+def weights(width, grams, rows, count):
     shape = jax.ShapeDtypeStruct((count * count, LANES), jnp.float32)
     return pl.pallas_call(
         functools.partial(weights_kernel, rows, count),
         out_shape=(shape, shape),
-        in_specs=[SMEM_SPEC, SMEM_SPEC] + [VMEM_SPEC] * len(grams),
+        in_specs=[SMEM_SPEC] + [VMEM_SPEC] * len(grams),
         out_specs=(VMEM_SPEC, VMEM_SPEC),
         compiler_params=pltpu.CompilerParams(vmem_limit_bytes=VMEM_LIMIT),
         cost_estimate=SHORT,
         name="weights",
-    )(me, width, *grams)
+    )(width, *grams)
 
 
 def mix_kernel(rows, count, jobs, drive_ref, repel_ref, *refs):
@@ -218,7 +219,8 @@
     )(*coefs, *[block[0] if isinstance(block, tuple) else in_vmem(block) for block in blocks])
 
 
-def put_kernel(entries, blocks, me_ref, *refs):
+def put_kernel(entries, blocks, *refs):
+    me = lax.axis_index("grp")
     blocks, (out_ref, sum_ref, sems) = refs[:blocks], refs[-3:]
     copies = []
     used = 0
@@ -232,7 +234,7 @@
             source = sum_ref.at[pl.ds(used, size), :]
             source[...] = total
             used += size
-        offset = place[1] if place[0] else (me_ref[0] ^ place[1]) * size
+        offset = place[1] if place[0] else (me ^ place[1]) * size
         copy = pltpu.make_async_copy(source, out_ref.at[pl.ds(offset, size), :], sems.at[n])
         copy.start()
         copies.append(copy)
@@ -240,30 +242,31 @@
         copy.wait()
 
 
-def put(me, entries, blocks, size, base=None):
+def put(entries, blocks, size, base=None):
     extra = [] if base is None else [base]
     moved = sum(entry[1] for entry in entries)
     scratch = sum(entry[1] for entry in entries if len(entry[0]) > 1)
     return pl.pallas_call(
         functools.partial(put_kernel, entries, len(blocks)),
         out_shape=jax.ShapeDtypeStruct((size, LANES), jnp.float32),
-        in_specs=[SMEM_SPEC] + [VMEM_SPEC] * len(blocks) + [HBM_SPEC] * len(extra),
+        in_specs=[VMEM_SPEC] * len(blocks) + [HBM_SPEC] * len(extra),
         out_specs=HBM_SPEC,
         scratch_shapes=[pltpu.VMEM((max(scratch, SUB), LANES), jnp.float32), pltpu.SemaphoreType.DMA((len(entries),))],
-        input_output_aliases={1 + len(blocks): 0} if extra else {},
+        input_output_aliases={len(blocks): 0} if extra else {},
         compiler_params=pltpu.CompilerParams(vmem_limit_bytes=VMEM_LIMIT),
         cost_estimate=pl.CostEstimate(flops=0, bytes_accessed=8 * LANES * moved, transcendentals=0),
         name="put",
-    )(me, *blocks, *extra)
-
-
-def cut_kernel(places, sizes, me_ref, block_ref, *refs):
+    )(*blocks, *extra)
+
+
+def cut_kernel(places, sizes, block_ref, *refs):
+    me = lax.axis_index("grp")
     outs, (in_sems, out_sems) = refs[: len(sizes)], refs[-2:]
     through = refs[len(sizes) : -2]
     copies = []
     start = 0
     for n, size in enumerate(sizes):
-        offset = (me_ref[0] ^ places[n]) * size if places else start
+        offset = (me ^ places[n]) * size if places else start
         held = through[n] if through else outs[n]
         copies.append(pltpu.make_async_copy(block_ref.at[pl.ds(offset, size), :], held, in_sems.at[n]))
         copies[n].start()
@@ -277,27 +280,25 @@
         move.wait()
 
 
-def cut(me, block, sizes, places=None):
+def cut(block, sizes, places=None):
     out = pltpu.VMEM if places else pltpu.HBM
     through = [] if places else [pltpu.VMEM((size, LANES), jnp.float32) for size in sizes]
     return pl.pallas_call(
         functools.partial(cut_kernel, places, sizes),
         out_shape=[out((size, LANES), jnp.float32) for size in sizes],
-        in_specs=[SMEM_SPEC, HBM_SPEC],
+        in_specs=[HBM_SPEC],
         out_specs=[VMEM_SPEC if places else HBM_SPEC] * len(sizes),
         scratch_shapes=through + [pltpu.SemaphoreType.DMA((len(sizes),))] * 2,
         compiler_params=pltpu.CompilerParams(vmem_limit_bytes=VMEM_LIMIT),
         cost_estimate=SHORT,
         name="cut",
-    )(me, in_hbm(block))
+    )(in_hbm(block))
 
 
 def shards(particles, scores, kernel_width):
     groups = lax.axis_size("grp")
     rows = particles.shape[0]
     count = rows * groups
-    me = lax.axis_index("grp")
-    place = me.astype(jnp.int32).reshape(1)
     x, s = dense(particles), dense(scores)
     part, half = x.shape[0] // groups, x.shape[0] // 2
     near = 2 ** ((groups.bit_length() - 1) // 2)
@@ -318,10 +319,12 @@
     first = max(1, half // step * 3 // 8) * step
     second = half - first
 
-    sent = cut(place, x, [part] * groups, others + [0])
+    sent = cut(x, [part] * len(others), others)
     s, sent = lax.optimization_barrier((s, sent))
-    s_own = cut(place, s, [first, second] * 2)
-    xs = {k: swap(block, k) for k, block in zip(others + [0], sent)}
+    s_own = cut(s, [first, second] * 2)
+    xs = {k: swap(block, k) for k, block in zip(others, sent)}
+    xs[others[0]], x = lax.optimization_barrier((xs[others[0]], x))
+    xs[0] = cut(x, [part], [0])[0]
     xs = [xs[k] for k in everyone]
 
     def exchange(low, high):
@@ -329,50 +332,60 @@
 
     xs[-1], s_own = lax.optimization_barrier((xs[-1], s_own))
     early = exchange(s_own[0], s_own[2])
-    grams = [gram(place, xs, rows, 1)]
+    grams = [gram(xs, rows, 1)]
     for partners in stages("grp"):
         grams = [swap(add(grams) if len(grams) > 1 else grams[0], k) for k in partners]
     early, pair, grams = lax.optimization_barrier((early, (s_own[1], s_own[3]), grams))
     late = exchange(*pair)
     for partners in stages("par"):
         grams = [swap(add(grams), k, "par") for k in partners]
-    coefs = weights(place, kernel_width, grams, rows, count)
+    coefs = weights(kernel_width, grams, rows, count)
+
+    s = in_hbm(s)
 
     def send(dest, jobs, coefs):
         mixed = mix(coefs, rows, count, jobs)
         return swap(mixed, dest), lax.optimization_barrier((coefs, mixed))[0]
 
-    def score_job(dest, n, held, start, size):
-        own = (in_hbm(s), n * half + start, size)
-        return (False, dest, (lows, highs)[n], [own] + [(block, 0, size) for block in held[n][1:]])
-
-    near_by = [k for k in others if k in lows or k in highs]
+    def score_jobs(dest, n, low, high):
+        jobs = []
+        for held, start, end in ((early, 0, first), (late, first, half)):
+            begin, size = max(low, start), min(high, end) - max(low, start)
+            if size > 0:
+                blocks = [(s, n * half + begin, size)] + [(block, begin - start, size) for block in held[n][1:]]
+                jobs.append((False, dest, (lows, highs)[n], blocks))
+        return jobs
+
     back, sums = {}, {}
-    for k in near_by + [k for k in others if k not in near_by]:
+    for k in others:
         back[k], coefs = send(k, [(True, k, everyone, xs)], coefs)
-    pieces = ((late, first, second), (early, 0, first))
-    for p, piece in enumerate(pieces):
+    middle = half // step // 2 * step
+    spans = [span for span in ((0, middle), (middle, half)) if span[0] < span[1]]
+    for span in spans:
         for n, dests in enumerate((highs[1:], lows[1:])):
             for k in dests:
-                sums[p, k], coefs = send(k, [score_job(k, n, *piece)], coefs)
-    own = mix(coefs, rows, count, [(True, 0, everyone, xs)] + [score_job(0, n, *piece) for piece in pieces for n in (0, 1)])
-
-    repel = put(place, [([(0, 0)], part, (False, 0))], [own], size)
-    for k in back:
+                sums[span, k], coefs = send(k, score_jobs(k, n, *span), coefs)
+    own_jobs = [(True, 0, everyone, xs)]
+    for span in spans:
+        own_jobs += score_jobs(0, 0, *span) + score_jobs(0, 1, *span)
+    own = mix(coefs, rows, count, own_jobs)
+
+    repel = put([([(0, 0)], part, (False, 0))], [own], size)
+    for k in others:
         repel, back[k] = lax.optimization_barrier((repel, back[k]))
-        repel = put(place, [([(0, 0)], part, (False, k))], [back[k]], size, base=repel)
+        repel = put([([(0, 0)], part, (False, k))], [back[k]], size, base=repel)
     drive = None
     begin = part
-    for p, (held, row, length) in enumerate(pieces):
-        entries, blocks = [], [own]
+    for span in spans:
+        length = span[1] - span[0]
         for n, dests in enumerate((highs[1:], lows[1:])):
-            entries.append(([(0, begin)] + [(len(blocks) + m, 0) for m in range(len(dests))], length, (True, n * half + row)))
-            blocks += [sums[p, k] for k in dests]
+            got = [sums[span, k] for k in dests]
+            held = repel if drive is None else (drive, repel)
+            held, got = lax.optimization_barrier((held, got))
+            drive, repel = (None, held) if drive is None else held
+            entry = ([(0, begin)] + [(1 + m, 0) for m in range(len(got))], length, (True, n * half + span[0]))
+            drive = put([entry], [own, *got], size, base=drive)
             begin += length
-        held = repel if drive is None else (drive, repel)
-        held, blocks = lax.optimization_barrier((held, blocks))
-        drive, repel = (None, held) if drive is None else held
-        drive = put(place, entries, blocks, size, base=drive)
     return (undense(drive, rows), undense(repel, rows))
 
 

time: 102 us -> 103 us (level)
  starting transfers between devices: 26.9 us -> 23.7 us
  Pallas kernels: 22.8 us -> 25.1 us
  waiting for transfers between devices: 50.7 us -> 52.1 us
    ppermute x21, starting transfers between devices: 26.9 us -> 23.7 us  [swap(): lax.ppermute(block, axis, [(i, i ^ k) for i in range(lax.axis_size(axis))])]
    ppermute x21, waiting for transfers between devices: 50.7 us -> 52.1 us  [swap(): lax.ppermute(block, axis, [(i, i ^ k) for i in range(lax.axis_size(axis))])]
    pallas_call x6 -> x8, Pallas kernels: 5.29 us -> 6.69 us  [put(): pl.pallas_call(functools.partial(put_kernel, entries, len(blocks)), out_s...]
    pallas_call x2 -> x3, Pallas kernels: 4.49 us -> 5.38 us  [cut(): pl.pallas_call(functools.partial(cut_kernel, places, sizes), out_shape=[o...]
  transfers between devices with their start and end apart: 21 -> 21, of which waited for: 13 -> 12; matrix products, arithmetic and copies ran while one was open for 0% -> 0% of each run, Pallas kernels for 20% -> 22%
where the time goes in v5:
time: 103 us; the launch traced here: 102 us
  waiting for transfers between devices  52.1 us (51%)
  Pallas kernels  25.1 us (24%)
  starting transfers between devices  23.7 us (23%)
  between operations  1.49 us (1%)
    ppermute x21, waiting for transfers between devices, swap(): lax.ppermute(block, axis, [(i, i ^ k) for i in range(lax.axis_size(axis))])  52.1 us
    ppermute x21, starting transfers between devices, swap(): lax.ppermute(block, axis, [(i, i ^ k) for i in range(lax.axis_size(axis))])  23.7 us
    pallas_call x8, Pallas kernels, mix(): pl.pallas_call(functools.partial(mix_kernel, rows, count, spans), out_sha...  9.85 us
    pallas_call x8, Pallas kernels, put(): pl.pallas_call(functools.partial(put_kernel, entries, len(blocks)), out_s...  6.69 us
    pallas_call x3, Pallas kernels, cut(): pl.pallas_call(functools.partial(cut_kernel, places, sizes), out_shape=[o...  5.38 us
    pallas_call x1, Pallas kernels, gram(): pl.pallas_call(functools.partial(gram_kernel, rows, groups), out_shape=ja...  2.28 us
  transfers between devices with their start and end apart: 21, of which 12 were waited for; matrix products, arithmetic and copies ran while one was open for 0% of the time, Pallas kernels for 22%

profile of v5, /device:TPU:0, one launch (start us, length us, event | category | flops | bytes accessed | tf_op | source)
XLA Modules:
  0.0 102.5 jit_solution(17681944374548008292)
XLA Ops:
  0.6 1.4 %cut.3 = (f32[1024,128]{1,0:T(8,128)S(1)}, f32[1024,128]{1,0:T(8,128)S(1)}, f32[1024,128]{1,0:T(8,128)S(1)}) custom-call(f32[4096,128]{1,0:T(8,128)} %bitcast.35), custom_call_target="tpu_custom_call" | custom-call | flops 1 | bytes 1 | tf_op jit(solution)/shard_map/cut/pallas_call | solution.py:286
  2.1 4.0 %collective-permute-start = (f32[1024,128]{1,0:T(8,128)S(1)}, f32[1024,128]{1,0:T(8,128)S(1)}, u32[]{:S(2)}, u32[]{:S(2)}) collective-permute-start(f32[1024,128]{1,0:T(8,128)S(1)} %get-tuple-element.64), channel_id=1, source_target_pairs={{0,24},{8,16},{16,8},{24,0},{1,25},{9,17},{17,9},{25,1},{2,26},{10... | collective-permute-start | bytes 1572872 | tf_op jit(solution)/shard_map/ppermute | solution.py:308
  6.7 2.9 %cut.4 = (f32[768,128]{1,0:T(8,128)}, f32[1280,128]{1,0:T(8,128)}, f32[768,128]{1,0:T(8,128)}, f32[1280,128]{1,0:T(8,128)}) custom-call(f32[4096,128]{1,0:T(8,128)} %bitcast.20), custom_call_target="tpu_custom_call" | custom-call | flops 1 | bytes 1 | tf_op jit(solution)/shard_map/cut/pallas_call | solution.py:286
  9.6 9.2 %collective-permute-done.refs_3_ = f32[1024,128]{1,0:T(8,128)S(1)} collective-permute-done((f32[1024,128]{1,0:T(8,128)S(1)}, f32[1024,128]{1,0:T(8,128)S(1)}, u32[]{:S(2)}, u32[]{:S(2)}) %collective-permute-start) | collective-permute-done | bytes 524320 | tf_op jit(solution)/shard_map/ppermute | solution.py:308
  18.8 2.0 %collective-permute-start.1 = (f32[768,128]{1,0:T(8,128)}, f32[768,128]{1,0:T(8,128)S(1)}, u32[]{:S(2)}, u32[]{:S(2)}) collective-permute-start(f32[768,128]{1,0:T(8,128)} %get-tuple-element.71), channel_id=1, source_target_pairs={{0,8},{8,0},{16,24},{24,16},{1,9},{9,1},{17,25},{25,17},{2,10},{10... | collective-permute-start | bytes 1179656 | tf_op jit(solution)/shard_map/ppermute | solution.py:308
  20.8 1.5 %collective-permute-start.2 = (f32[768,128]{1,0:T(8,128)}, f32[768,128]{1,0:T(8,128)S(1)}, u32[]{:S(2)}, u32[]{:S(2)}) collective-permute-start(f32[768,128]{1,0:T(8,128)} %get-tuple-element.72), channel_id=1, source_target_pairs={{0,16},{8,24},{16,0},{24,8},{1,17},{9,25},{17,1},{25,9},{2,18},{10... | collective-permute-start | bytes 1179656 | tf_op jit(solution)/shard_map/ppermute | solution.py:308
  22.3 1.1 %cut.5.refs_0_ = f32[1024,128]{1,0:T(8,128)S(1)} custom-call(f32[4096,128]{1,0:T(8,128)} %bitcast.36), custom_call_target="tpu_custom_call" | custom-call | flops 1 | bytes 1 | tf_op jit(solution)/shard_map/cut/pallas_call | solution.py:286
  23.4 7.2 %collective-permute-done.3.refs_1_ = f32[1024,128]{1,0:T(8,128)S(1)} collective-permute-done((f32[1024,128]{1,0:T(8,128)S(1)}, f32[1024,128]{1,0:T(8,128)S(1)}, u32[]{:S(2)}, u32[]{:S(2)}) %collective-permute-start.3) | collective-permute-done | bytes 524320 | tf_op jit(solution)/shard_map/ppermute | solution.py:308
  30.6 2.3 %gram.1.refs_0_ = f32[1,2,128]{2,1,0:T(2,128)S(1)} custom-call(f32[1024,128]{1,0:T(8,128)S(1)} %cut.5.refs_0_, f32[1024,128]{1,0:T(8,128)S(1)} %collective-permute-done.3.refs_1_, f32[1024,128]{1,0:T(8,128)S(1)} %collective-permute-done.4.refs_2_, f32[1024,128]{1,0:T(8,128)S(1)} %collective-permute-done.refs_3_), custom_call_target="tpu_custom_call" | custom-call | flops 1 | bytes 1 | tf_op jit(solution)/shard_map/gram/pallas_call | solution.py:81
  32.9 1.5 %collective-permute-start.7 = (f32[1,2,128]{2,1,0:T(2,128)S(1)}, f32[1,2,128]{2,1,0:T(2,128)S(1)}, u32[]{:S(2)}, u32[]{:S(2)}) collective-permute-start(f32[1,2,128]{2,1,0:T(2,128)S(1)} %gram.1.refs_0_), channel_id=1, source_target_pairs={{0,24},{8,16},{16,8},{24,0},{1,25},{9,17},{17,9},{25,1},{2,26},{10... | collective-permute-start | bytes 3080 | tf_op jit(solution)/shard_map/ppermute | solution.py:308
  34.4 1.5 %collective-permute-start.6 = (f32[1,2,128]{2,1,0:T(2,128)S(1)}, f32[1,2,128]{2,1,0:T(2,128)S(1)}, u32[]{:S(2)}, u32[]{:S(2)}) collective-permute-start(f32[1,2,128]{2,1,0:T(2,128)S(1)} %gram.1.refs_0_), channel_id=1, source_target_pairs={{0,16},{8,24},{16,0},{24,8},{1,17},{9,25},{17,1},{25,9},{2,18},{10... | collective-permute-start | bytes 3080 | tf_op jit(solution)/shard_map/ppermute | solution.py:308
  36.4 1.2 %collective-permute-done.7.refs_3_ = f32[1,2,128]{2,1,0:T(2,128)S(1)} collective-permute-done((f32[1,2,128]{2,1,0:T(2,128)S(1)}, f32[1,2,128]{2,1,0:T(2,128)S(1)}, u32[]{:S(2)}, u32[]{:S(2)}) %collective-permute-start.7) | collective-permute-done | bytes 1056 | tf_op jit(solution)/shard_map/ppermute | solution.py:308
  37.9 1.5 %collective-permute-done.5.refs_1_ = f32[1,2,128]{2,1,0:T(2,128)S(1)} collective-permute-done((f32[1,2,128]{2,1,0:T(2,128)S(1)}, f32[1,2,128]{2,1,0:T(2,128)S(1)}, u32[]{:S(2)}, u32[]{:S(2)}) %collective-permute-start.5) | collective-permute-done | bytes 1056 | tf_op jit(solution)/shard_map/ppermute | solution.py:308
  40.1 0.9 collective-permute-start.13
  41.6 1.1 %collective-permute-start.9 = (f32[1,2,128]{2,1,0:T(2,128)S(1)}, f32[1,2,128]{2,1,0:T(2,128)S(1)}, u32[]{:S(2)}, u32[]{:S(2)}) collective-permute-start(f32[1,2,128]{2,1,0:T(2,128)S(1)} %add.2.refs_0_), channel_id=1, source_target_pairs={{0,2},{1,3},{2,0},{3,1},{4,6},{5,7},{6,4},{7,5},{8,10},{9,11},{10,... | collective-permute-start | bytes 3080 | tf_op jit(solution)/shard_map/ppermute | solution.py:308
  42.8 1.1 %collective-permute-done.10.refs_3_ = f32[1,2,128]{2,1,0:T(2,128)S(1)} collective-permute-done((f32[1,2,128]{2,1,0:T(2,128)S(1)}, f32[1,2,128]{2,1,0:T(2,128)S(1)}, u32[]{:S(2)}, u32[]{:S(2)}) %collective-permute-start.10) | collective-permute-done | bytes 1056 | tf_op jit(solution)/shard_map/ppermute | solution.py:308
  44.0 1.2 %collective-permute-done.9.refs_2_ = f32[1,2,128]{2,1,0:T(2,128)S(1)} collective-permute-done((f32[1,2,128]{2,1,0:T(2,128)S(1)}, f32[1,2,128]{2,1,0:T(2,128)S(1)}, u32[]{:S(2)}, u32[]{:S(2)}) %collective-permute-start.9) | collective-permute-done | bytes 1056 | tf_op jit(solution)/shard_map/ppermute | solution.py:308
  45.1 2.7 %collective-permute-start.11 = (f32[1,2,128]{2,1,0:T(2,128)S(1)}, f32[1,2,128]{2,1,0:T(2,128)S(1)}, u32[]{:S(2)}, u32[]{:S(2)}) collective-permute-start(f32[1,2,128]{2,1,0:T(2,128)S(1)} %add.3.refs_0_), channel_id=1, source_target_pairs={{0,4},{1,5},{2,6},{3,7},{4,0},{5,1},{6,2},{7,3},{8,12},{9,13},{10,... | collective-permute-start | bytes 3080 | tf_op jit(solution)/shard_map/ppermute | solution.py:308
  48.5 1.2 %collective-permute-done.11.refs_1_ = f32[1,2,128]{2,1,0:T(2,128)S(1)} collective-permute-done((f32[1,2,128]{2,1,0:T(2,128)S(1)}, f32[1,2,128]{2,1,0:T(2,128)S(1)}, u32[]{:S(2)}, u32[]{:S(2)}) %collective-permute-start.11) | collective-permute-done | bytes 1056 | tf_op jit(solution)/shard_map/ppermute | solution.py:308
  49.7 0.9 weights.1
  52.5 1.4 %collective-permute-start.14 = (f32[1024,128]{1,0:T(8,128)S(1)}, f32[1024,128]{1,0:T(8,128)S(1)}, u32[]{:S(2)}, u32[]{:S(2)}) collective-permute-start(f32[1024,128]{1,0:T(8,128)S(1)} %mix.8), channel_id=1, source_target_pairs={{0,24},{8,16},{16,8},{24,0},{1,25},{9,17},{17,9},{25,1},{2,26},{10... | collective-permute-start | bytes 1572872 | tf_op jit(solution)/shard_map/ppermute | solution.py:308
  54.5 1.5 %collective-permute-start.16 = (f32[1024,128]{1,0:T(8,128)S(1)}, f32[1024,128]{1,0:T(8,128)S(1)}, u32[]{:S(2)}, u32[]{:S(2)}) collective-permute-start(f32[1024,128]{1,0:T(8,128)S(1)} %mix.10), channel_id=1, source_target_pairs={{0,8},{8,0},{16,24},{24,16},{1,9},{9,1},{17,25},{25,17},{2,10},{10... | collective-permute-start | bytes 1572872 | tf_op jit(solution)/shard_map/ppermute | solution.py:308
  56.1 1.3 %mix.11 = f32[1024,128]{1,0:T(8,128)S(1)} custom-call(f32[256,128]{1,0:T(8,128)S(1)} %get-tuple-element.101.drive_ref, f32[256,128]{1,0:T(8,128)S(1)} %get-tuple-element.102.repel_ref, f32[4096,128]{1,0:T(8,128)} %bitcast.21, f32[768,128]{1,0:T(8,128)S(1)} %collective-permute-done.1.refs_1_.refs_5_, f32[4096,128]{1,0:T(8,128)} %bitcast.22, ...), custom_call_target="tpu_custom_call" | custom-call | flops 1 | bytes 1 | tf_op jit(solution)/shard_map/mix/pallas_call | solution.py:210
  58.1 10.9 %collective-permute-done.13.refs_3_.refs_1_.refs_11_.refs_15_ = f32[1280,128]{1,0:T(8,128)S(1)} collective-permute-done((f32[1280,128]{1,0:T(8,128)S(1)}, f32[1280,128]{1,0:T(8,128)S(1)}, u32[]{:S(2)}, u32[]{:S(2)}) %collective-permute-start.13) | collective-permute-done | bytes 655392 | tf_op jit(solution)/shard_map/ppermute | solution.py:308
  69.0 1.3 %mix.12 = f32[1024,128]{1,0:T(8,128)S(1)} custom-call(f32[256,128]{1,0:T(8,128)S(1)} %get-tuple-element.101.drive_ref, f32[256,128]{1,0:T(8,128)S(1)} %get-tuple-element.102.repel_ref, f32[4096,128]{1,0:T(8,128)} %bitcast.23, f32[768,128]{1,0:T(8,128)S(1)} %collective-permute-done.2.refs_1_.refs_9_, f32[4096,128]{1,0:T(8,128)} %bitcast.24, ...), custom_call_target="tpu_custom_call" | custom-call | flops 1 | bytes 1 | tf_op jit(solution)/shard_map/mix/pallas_call | solution.py:210
  70.4 1.3 %mix.13 = f32[1024,128]{1,0:T(8,128)S(1)} custom-call(f32[256,128]{1,0:T(8,128)S(1)} %get-tuple-element.101.drive_ref, f32[256,128]{1,0:T(8,128)S(1)} %get-tuple-element.102.repel_ref, f32[4096,128]{1,0:T(8,128)} %bitcast.25, f32[1280,128]{1,0:T(8,128)S(1)} %collective-permute-done.12.refs_3_.refs_1_.refs_7_.refs_13_), custom_call_target="tpu_custom_call" | custom-call | flops 1 | bytes 1 | tf_op jit(solution)/shard_map/mix/pallas_call | solution.py:210
  71.7 8.5 %collective-permute-done.15.refs_0_ = f32[1024,128]{1,0:T(8,128)S(1)} collective-permute-done((f32[1024,128]{1,0:T(8,128)S(1)}, f32[1024,128]{1,0:T(8,128)S(1)}, u32[]{:S(2)}, u32[]{:S(2)}) %collective-permute-start.15) | collective-permute-done | bytes 524320 | tf_op jit(solution)/shard_map/ppermute | solution.py:308
  80.2 0.9 collective-permute-start.19
  81.1 1.3 %mix.14 = f32[1024,128]{1,0:T(8,128)S(1)} custom-call(f32[256,128]{1,0:T(8,128)S(1)} %get-tuple-element.101.drive_ref, f32[256,128]{1,0:T(8,128)S(1)} %get-tuple-element.102.repel_ref, f32[4096,128]{1,0:T(8,128)} %bitcast.26, f32[1280,128]{1,0:T(8,128)S(1)} %collective-permute-done.13.refs_3_.refs_1_.refs_11_.refs_15_), custom_call_target="tpu_custom_call" | custom-call | flops 1 | bytes 1 | tf_op jit(solution)/shard_map/mix/pallas_call | solution.py:210
  83.3 2.7 %mix.15.refs_0_ = f32[5120,128]{1,0:T(8,128)S(1)} custom-call(f32[256,128]{1,0:T(8,128)S(1)} %get-tuple-element.101.drive_ref, f32[256,128]{1,0:T(8,128)S(1)} %get-tuple-element.102.repel_ref, f32[1024,128]{1,0:T(8,128)S(1)} %cut.5.refs_0_, f32[1024,128]{1,0:T(8,128)S(1)} %collective-permute-done.3.refs_1_, f32[1024,128]{1,0:T(8,128)S(1)} %collective-permute-done.4.refs_2_, ...), custom_call_target="tpu_custom_call" | custom-call | flops 1 | bytes 1 | tf_op jit(solution)/shard_map/mix/pallas_call | solution.py:210
  89.3 2.2 %collective-permute-done.17.refs_1_ = f32[1024,128]{1,0:T(8,128)S(1)} collective-permute-done((f32[1024,128]{1,0:T(8,128)S(1)}, f32[1024,128]{1,0:T(8,128)S(1)}, u32[]{:S(2)}, u32[]{:S(2)}) %collective-permute-start.17) | collective-permute-done | bytes 524320 | tf_op jit(solution)/shard_map/ppermute | solution.py:308
  93.2 7.5 %collective-permute-done.19.refs_1_ = f32[1024,128]{1,0:T(8,128)S(1)} collective-permute-done((f32[1024,128]{1,0:T(8,128)S(1)}, f32[1024,128]{1,0:T(8,128)S(1)}, u32[]{:S(2)}, u32[]{:S(2)}) %collective-permute-start.19) | collective-permute-done | bytes 524320 | tf_op jit(solution)/shard_map/ppermute | solution.py:308
  (37 shorter events, 13.7 us)
Async XLA Ops:
  2.1 16.8 %collective-permute-start = (f32[1024,128]{1,0:T(8,128)S(1)}, f32[1024,128]{1,0:T(8,128)S(1)}, u32[]{:S(2)}, u32[]{:S(2)}) collective-permute-start(f32[1024,128]{1,0:T(8,128)S(1)} %get-tuple-element.64), channel_id=1, source_target_pairs={{0,24},{8,16},{16,8},{24,0},{1,25},{9,17},{17,9},{25,1},{2,26},{10... | collective-permute-start | bytes 1572872 | tf_op jit(solution)/shard_map/ppermute | solution.py:308
  6.0 24.6 %collective-permute-start.3 = (f32[1024,128]{1,0:T(8,128)S(1)}, f32[1024,128]{1,0:T(8,128)S(1)}, u32[]{:S(2)}, u32[]{:S(2)}) collective-permute-start(f32[1024,128]{1,0:T(8,128)S(1)} %get-tuple-element.76), channel_id=1, source_target_pairs={{0,8},{8,0},{16,24},{24,16},{1,9},{9,1},{17,25},{25,17},{2,10},{10... | collective-permute-start | bytes 1572872 | tf_op jit(solution)/shard_map/ppermute | solution.py:308
  6.6 24.1 %collective-permute-start.4 = (f32[1024,128]{1,0:T(8,128)S(1)}, f32[1024,128]{1,0:T(8,128)S(1)}, u32[]{:S(2)}, u32[]{:S(2)}) collective-permute-start(f32[1024,128]{1,0:T(8,128)S(1)} %get-tuple-element.77), channel_id=1, source_target_pairs={{0,16},{8,24},{16,0},{24,8},{1,17},{9,25},{17,1},{25,9},{2,18},{10... | collective-permute-start | bytes 1572872 | tf_op jit(solution)/shard_map/ppermute | solution.py:308
  18.8 20.7 %copy-start.1 = (f32[1280,128]{1,0:T(8,128)S(1)}, f32[1280,128]{1,0:T(8,128)}, u32[]{:S(2)}) copy-start(f32[1280,128]{1,0:T(8,128)} %get-tuple-element.92) | copy-start | bytes 1966084
  18.8 21.3 %copy-start = (f32[1280,128]{1,0:T(8,128)S(1)}, f32[1280,128]{1,0:T(8,128)}, u32[]{:S(2)}) copy-start(f32[1280,128]{1,0:T(8,128)} %get-tuple-element.96) | copy-start | bytes 1966084
  18.8 20.6 %collective-permute-start.1 = (f32[768,128]{1,0:T(8,128)}, f32[768,128]{1,0:T(8,128)S(1)}, u32[]{:S(2)}, u32[]{:S(2)}) collective-permute-start(f32[768,128]{1,0:T(8,128)} %get-tuple-element.71), channel_id=1, source_target_pairs={{0,8},{8,0},{16,24},{24,16},{1,9},{9,1},{17,25},{25,17},{2,10},{10... | collective-permute-start | bytes 1179656 | tf_op jit(solution)/shard_map/ppermute | solution.py:308
  20.8 18.6 %collective-permute-start.2 = (f32[768,128]{1,0:T(8,128)}, f32[768,128]{1,0:T(8,128)S(1)}, u32[]{:S(2)}, u32[]{:S(2)}) collective-permute-start(f32[768,128]{1,0:T(8,128)} %get-tuple-element.72), channel_id=1, source_target_pairs={{0,16},{8,24},{16,0},{24,8},{1,17},{9,25},{17,1},{25,9},{2,18},{10... | collective-permute-start | bytes 1179656 | tf_op jit(solution)/shard_map/ppermute | solution.py:308
  32.9 4.8 %collective-permute-start.7 = (f32[1,2,128]{2,1,0:T(2,128)S(1)}, f32[1,2,128]{2,1,0:T(2,128)S(1)}, u32[]{:S(2)}, u32[]{:S(2)}) collective-permute-start(f32[1,2,128]{2,1,0:T(2,128)S(1)} %gram.1.refs_0_), channel_id=1, source_target_pairs={{0,24},{8,16},{16,8},{24,0},{1,25},{9,17},{17,9},{25,1},{2,26},{10... | collective-permute-start | bytes 3080 | tf_op jit(solution)/shard_map/ppermute | solution.py:308
  34.4 3.6 %collective-permute-start.6 = (f32[1,2,128]{2,1,0:T(2,128)S(1)}, f32[1,2,128]{2,1,0:T(2,128)S(1)}, u32[]{:S(2)}, u32[]{:S(2)}) collective-permute-start(f32[1,2,128]{2,1,0:T(2,128)S(1)} %gram.1.refs_0_), channel_id=1, source_target_pairs={{0,16},{8,24},{16,0},{24,8},{1,17},{9,25},{17,1},{25,9},{2,18},{10... | collective-permute-start | bytes 3080 | tf_op jit(solution)/shard_map/ppermute | solution.py:308
  35.9 3.6 %collective-permute-start.5 = (f32[1,2,128]{2,1,0:T(2,128)S(1)}, f32[1,2,128]{2,1,0:T(2,128)S(1)}, u32[]{:S(2)}, u32[]{:S(2)}) collective-permute-start(f32[1,2,128]{2,1,0:T(2,128)S(1)} %gram.1.refs_0_), channel_id=1, source_target_pairs={{0,8},{8,0},{16,24},{24,16},{1,9},{9,1},{17,25},{25,17},{2,10},{10... | collective-permute-start | bytes 3080 | tf_op jit(solution)/shard_map/ppermute | solution.py:308
  39.5 16.6 %collective-permute-start.12 = (f32[1280,128]{1,0:T(8,128)S(1)}, f32[1280,128]{1,0:T(8,128)S(1)}, u32[]{:S(2)}, u32[]{:S(2)}) collective-permute-start(f32[1280,128]{1,0:T(8,128)S(1)} %copy-done.1), channel_id=1, source_target_pairs={{0,8},{8,0},{16,24},{24,16},{1,9},{9,1},{17,25},{25,17},{2,10},{10... | collective-permute-start | bytes 1966088 | tf_op jit(solution)/shard_map/ppermute | solution.py:308
  40.1 28.9 %collective-permute-start.13 = (f32[1280,128]{1,0:T(8,128)S(1)}, f32[1280,128]{1,0:T(8,128)S(1)}, u32[]{:S(2)}, u32[]{:S(2)}) collective-permute-start(f32[1280,128]{1,0:T(8,128)S(1)} %copy-done), channel_id=1, source_target_pairs={{0,16},{8,24},{16,0},{24,8},{1,17},{9,25},{17,1},{25,9},{2,18},{10... | collective-permute-start | bytes 1966088 | tf_op jit(solution)/shard_map/ppermute | solution.py:308
  41.0 3.0 %collective-permute-start.10 = (f32[1,2,128]{2,1,0:T(2,128)S(1)}, f32[1,2,128]{2,1,0:T(2,128)S(1)}, u32[]{:S(2)}, u32[]{:S(2)}) collective-permute-start(f32[1,2,128]{2,1,0:T(2,128)S(1)} %add.2.refs_0_), channel_id=1, source_target_pairs={{0,3},{1,2},{2,1},{3,0},{4,7},{5,6},{6,5},{7,4},{8,11},{9,10},{10,... | collective-permute-start | bytes 3080 | tf_op jit(solution)/shard_map/ppermute | solution.py:308
  41.6 3.6 %collective-permute-start.9 = (f32[1,2,128]{2,1,0:T(2,128)S(1)}, f32[1,2,128]{2,1,0:T(2,128)S(1)}, u32[]{:S(2)}, u32[]{:S(2)}) collective-permute-start(f32[1,2,128]{2,1,0:T(2,128)S(1)} %add.2.refs_0_), channel_id=1, source_target_pairs={{0,2},{1,3},{2,0},{3,1},{4,6},{5,7},{6,4},{7,5},{8,10},{9,11},{10,... | collective-permute-start | bytes 3080 | tf_op jit(solution)/shard_map/ppermute | solution.py:308
  42.6 2.5 %collective-permute-start.8 = (f32[1,2,128]{2,1,0:T(2,128)S(1)}, f32[1,2,128]{2,1,0:T(2,128)S(1)}, u32[]{:S(2)}, u32[]{:S(2)}) collective-permute-start(f32[1,2,128]{2,1,0:T(2,128)S(1)} %add.2.refs_0_), channel_id=1, source_target_pairs={{0,1},{1,0},{2,3},{3,2},{4,5},{5,4},{6,7},{7,6},{8,9},{9,8},{10,11... | collective-permute-start | bytes 3080 | tf_op jit(solution)/shard_map/ppermute | solution.py:308
  45.1 4.5 %collective-permute-start.11 = (f32[1,2,128]{2,1,0:T(2,128)S(1)}, f32[1,2,128]{2,1,0:T(2,128)S(1)}, u32[]{:S(2)}, u32[]{:S(2)}) collective-permute-start(f32[1,2,128]{2,1,0:T(2,128)S(1)} %add.3.refs_0_), channel_id=1, source_target_pairs={{0,4},{1,5},{2,6},{3,7},{4,0},{5,1},{6,2},{7,3},{8,12},{9,13},{10,... | collective-permute-start | bytes 3080 | tf_op jit(solution)/shard_map/ppermute | solution.py:308
  51.8 28.4 %collective-permute-start.15 = (f32[1024,128]{1,0:T(8,128)S(1)}, f32[1024,128]{1,0:T(8,128)S(1)}, u32[]{:S(2)}, u32[]{:S(2)}) collective-permute-start(f32[1024,128]{1,0:T(8,128)S(1)} %mix.9), channel_id=1, source_target_pairs={{0,16},{8,24},{16,0},{24,8},{1,17},{9,25},{17,1},{25,9},{2,18},{10... | collective-permute-start | bytes 1572872 | tf_op jit(solution)/shard_map/ppermute | solution.py:308
  52.5 30.0 %collective-permute-start.14 = (f32[1024,128]{1,0:T(8,128)S(1)}, f32[1024,128]{1,0:T(8,128)S(1)}, u32[]{:S(2)}, u32[]{:S(2)}) collective-permute-start(f32[1024,128]{1,0:T(8,128)S(1)} %mix.8), channel_id=1, source_target_pairs={{0,24},{8,16},{16,8},{24,0},{1,25},{9,17},{17,9},{25,1},{2,26},{10... | collective-permute-start | bytes 1572872 | tf_op jit(solution)/shard_map/ppermute | solution.py:308
  54.5 33.9 %collective-permute-start.16 = (f32[1024,128]{1,0:T(8,128)S(1)}, f32[1024,128]{1,0:T(8,128)S(1)}, u32[]{:S(2)}, u32[]{:S(2)}) collective-permute-start(f32[1024,128]{1,0:T(8,128)S(1)} %mix.10), channel_id=1, source_target_pairs={{0,8},{8,0},{16,24},{24,16},{1,9},{9,1},{17,25},{25,17},{2,10},{10... | collective-permute-start | bytes 1572872 | tf_op jit(solution)/shard_map/ppermute | solution.py:308
  57.4 34.1 %collective-permute-start.17 = (f32[1024,128]{1,0:T(8,128)S(1)}, f32[1024,128]{1,0:T(8,128)S(1)}, u32[]{:S(2)}, u32[]{:S(2)}) collective-permute-start(f32[1024,128]{1,0:T(8,128)S(1)} %mix.11), channel_id=1, source_target_pairs={{0,16},{8,24},{16,0},{24,8},{1,17},{9,25},{17,1},{25,9},{2,18},{10... | collective-permute-start | bytes 1572872 | tf_op jit(solution)/shard_map/ppermute | solution.py:308
  70.3 22.0 %collective-permute-start.18 = (f32[1024,128]{1,0:T(8,128)S(1)}, f32[1024,128]{1,0:T(8,128)S(1)}, u32[]{:S(2)}, u32[]{:S(2)}) collective-permute-start(f32[1024,128]{1,0:T(8,128)S(1)} %mix.12), channel_id=1, source_target_pairs={{0,8},{8,0},{16,24},{24,16},{1,9},{9,1},{17,25},{25,17},{2,10},{10... | collective-permute-start | bytes 1572872 | tf_op jit(solution)/shard_map/ppermute | solution.py:308
  80.2 20.5 %collective-permute-start.19 = (f32[1024,128]{1,0:T(8,128)S(1)}, f32[1024,128]{1,0:T(8,128)S(1)}, u32[]{:S(2)}, u32[]{:S(2)}) collective-permute-start(f32[1024,128]{1,0:T(8,128)S(1)} %mix.13), channel_id=1, source_target_pairs={{0,16},{8,24},{16,0},{24,8},{1,17},{9,25},{17,1},{25,9},{2,18},{10... | collective-permute-start | bytes 1572872 | tf_op jit(solution)/shard_map/ppermute | solution.py:308
  82.5 19.1 %collective-permute-start.20 = (f32[1024,128]{1,0:T(8,128)S(1)}, f32[1024,128]{1,0:T(8,128)S(1)}, u32[]{:S(2)}, u32[]{:S(2)}) collective-permute-start(f32[1024,128]{1,0:T(8,128)S(1)} %mix.14), channel_id=1, source_target_pairs={{0,8},{8,0},{16,24},{24,16},{1,9},{9,1},{17,25},{25,17},{2,10},{10... | collective-permute-start | bytes 1572872 | tf_op jit(solution)/shard_map/ppermute | solution.py:308

commit v6 on v5

--- a/solution.py
+++ b/solution.py
@@ -36,27 +36,31 @@
     return block.reshape(-1, rows, LANES).transpose(1, 0, 2).reshape(rows, -1)
 
 
-def gram_kernel(rows, groups, *refs):
-    xs, out_ref, acc_ref = refs[:groups], refs[groups], refs[groups + 1]
+def gram_kernel(rows, pieces, *refs):
+    out_ref, acc_ref = refs[-2], refs[-1]
     me = lax.axis_index("grp")
-    count = rows * groups
+    groups, count = len(pieces), rows * len(pieces)
     step = SUB * rows
-    steps = xs[0].shape[0] // step
-
-    def load(ref, t, i):
-        return ref[pl.ds(t * step + i, SUB, stride=rows), :]
+    xs = [refs[sum(pieces[:k]) : sum(pieces[: k + 1])] for k in range(groups)]
+    cuts = max(pieces)
+    steps = sum(x.shape[0] for x in xs[0]) // step // cuts
+
+    def load(x, cut, t, i):
+        ref, base = (x[cut], 0) if len(x) > 1 else (x[0], cut * steps * step)
+        return ref[pl.ds(base + t * step + i, SUB, stride=rows), :]
 
     for a in range(groups):
         for b in range(a, groups):
             pairs = [(i, j) for i in range(rows) for j in range(rows) if a != b or i <= j]
-
-            def body(t, sums):
-                left = [load(xs[a], t, i) for i in range(rows)]
-                right = left if a == b else [load(xs[b], t, j) for j in range(rows)]
-                return tuple(s + left[i] * right[j] for s, (i, j) in zip(sums, pairs))
-
-            zero = jnp.zeros((SUB, LANES), jnp.float32)
-            sums = lax.fori_loop(0, steps, body, (zero,) * len(pairs), unroll=2)
+            sums = (jnp.zeros((SUB, LANES), jnp.float32),) * len(pairs)
+            for cut in range(cuts):
+
+                def body(t, sums):
+                    left = [load(xs[a], cut, t, i) for i in range(rows)]
+                    right = left if a == b else [load(xs[b], cut, t, j) for j in range(rows)]
+                    return tuple(s + left[i] * right[j] for s, (i, j) in zip(sums, pairs))
+
+                sums = lax.fori_loop(0, steps, body, sums, unroll=2)
             for s, (i, j) in zip(sums, pairs):
                 row = jnp.sum(s, axis=0, keepdims=True)
                 left, right = (me ^ a) * rows + i, (me ^ b) * rows + j
@@ -72,22 +76,22 @@
     )
     for n in range(count * count // LANES):
         row = total[:1, n * LANES : (n + 1) * LANES]
-        out_ref[:, n : n + 1, :] = jnp.broadcast_to(row[None], (out_ref.shape[0], 1, LANES))
-
-
-def gram(xs, rows, copies):
-    groups = len(xs)
-    count = rows * groups
-    return pl.pallas_call(
-        functools.partial(gram_kernel, rows, groups),
-        out_shape=jax.ShapeDtypeStruct((copies, count * count // LANES, LANES), jnp.float32),
-        in_specs=[VMEM_SPEC] * groups,
+        out_ref[:, n : n + 1, :] = row[None]
+
+
+def gram(xs, rows):
+    blocks = [block for x in xs for block in x]
+    count = rows * len(xs)
+    return pl.pallas_call(
+        functools.partial(gram_kernel, rows, [len(x) for x in xs]),
+        out_shape=jax.ShapeDtypeStruct((1, count * count // LANES, LANES), jnp.float32),
+        in_specs=[VMEM_SPEC] * len(blocks),
         out_specs=VMEM_SPEC,
         scratch_shapes=[pltpu.VMEM((count * count, LANES), jnp.float32)],
         compiler_params=pltpu.CompilerParams(vmem_limit_bytes=VMEM_LIMIT),
         cost_estimate=SHORT,
         name="gram",
-    )(*map(in_vmem, xs))
+    )(*map(in_vmem, blocks))
 
 
 def add_kernel(*refs):
@@ -158,34 +162,34 @@
 
 
 def mix_kernel(rows, count, jobs, drive_ref, repel_ref, *refs):
-    blocks = sum(len(spans) for _, _, _, spans in jobs)
-    xs, out_ref, scratch = list(refs[:blocks]), refs[blocks], refs[blocks + 1 :]
-    streams = [n for n, span in enumerate(span for job in jobs for span in job[3]) if span is not None]
     spans = [span for job in jobs for span in job[3]]
+    xs, out_ref, scratch = list(refs[: len(spans)]), refs[len(spans)], refs[len(spans) + 1 :]
+    offsets = [start for start, _, _ in spans]
     copies = {}
-    for m, n in enumerate(streams):
-        start, size = spans[n]
-        copies[n] = pltpu.make_async_copy(xs[n].at[pl.ds(start, size), :], scratch[m], scratch[-1].at[m])
-        copies[n].start()
-        xs[n] = scratch[m]
+    for n, (start, size, stream) in enumerate(spans):
+        if stream:
+            m = len(copies)
+            copies[n] = pltpu.make_async_copy(xs[n].at[pl.ds(start, size), :], scratch[m], scratch[-1].at[m])
+            copies[n].start()
+            xs[n], offsets[n] = scratch[m], 0
     step = SUB * rows
-    start = used = 0
+    done = used = 0
     for repel, dest, sources, spans in jobs:
         coef_ref = repel_ref if repel else drive_ref
-        held = xs[used : used + len(sources)]
+        held = [(xs[n], offsets[n]) for n in range(used, used + len(sources))]
         for n in range(used, used + len(sources)):
             if n in copies:
                 copies[n].wait()
         used += len(sources)
-        steps = held[0].shape[0] // step
+        steps = spans[0][1] // step
         wide = next(w for w in (8, 4, 2, 1) if steps % w == 0)
 
         def body(t, carry):
             base = pl.multiple_of(t * step * wide, step)
             sums = [[None] * rows for _ in range(wide)]
-            for b, source in enumerate(sources):
+            for (ref, offset), source in zip(held, sources):
                 for j in range(rows):
-                    x = [held[b][pl.ds(base + u * step + j, SUB, stride=rows), :] for u in range(wide)]
+                    x = [ref[pl.ds(offset + base + u * step + j, SUB, stride=rows), :] for u in range(wide)]
                     for i in range(rows):
                         row = (source * rows + j) * count + dest * rows + i
                         c = jnp.broadcast_to(coef_ref[row : row + 1, :], (SUB, LANES))
@@ -194,37 +198,35 @@
                             sums[u][i] = term if sums[u][i] is None else sums[u][i] + term
             for u in range(wide):
                 for i in range(rows):
-                    out_ref[pl.ds(start + base + u * step + i, SUB, stride=rows), :] = sums[u][i]
+                    out_ref[pl.ds(done + base + u * step + i, SUB, stride=rows), :] = sums[u][i]
             return carry
 
         lax.fori_loop(0, steps // wide, body, 0)
-        start += steps * step
+        done += steps * step
 
 
 def mix(coefs, rows, count, jobs):
     blocks = [block for job in jobs for block in job[3]]
-    streams = [block for block in blocks if isinstance(block, tuple)]
-    spans = [(*job[:3], [b[1:] if isinstance(b, tuple) else None for b in job[3]]) for job in jobs]
-    size = sum(b[2] if isinstance(b, tuple) else b.shape[0] for b in (job[3][0] for job in jobs))
-    scratch = [pltpu.VMEM((block[2], LANES), jnp.float32) for block in streams]
-    return pl.pallas_call(
-        functools.partial(mix_kernel, rows, count, spans),
-        out_shape=jax.ShapeDtypeStruct((size, LANES), jnp.float32),
-        in_specs=[VMEM_SPEC] * 2 + [ANY_SPEC if isinstance(block, tuple) else VMEM_SPEC for block in blocks],
+    streams = [block for block in blocks if block[3]]
+    return pl.pallas_call(
+        functools.partial(mix_kernel, rows, count, [(*job[:3], [block[1:] for block in job[3]]) for job in jobs]),
+        out_shape=jax.ShapeDtypeStruct((sum(job[3][0][2] for job in jobs), LANES), jnp.float32),
+        in_specs=[VMEM_SPEC] * 2 + [ANY_SPEC if block[3] else VMEM_SPEC for block in blocks],
         out_specs=VMEM_SPEC,
-        scratch_shapes=scratch + ([pltpu.SemaphoreType.DMA((len(streams),))] if streams else []),
+        scratch_shapes=[pltpu.VMEM((block[2], LANES), jnp.float32) for block in streams]
+        + ([pltpu.SemaphoreType.DMA((len(streams),))] if streams else []),
         compiler_params=pltpu.CompilerParams(vmem_limit_bytes=VMEM_LIMIT),
         cost_estimate=SHORT,
         name="mix",
-    )(*coefs, *[block[0] if isinstance(block, tuple) else in_vmem(block) for block in blocks])
-
-
-def put_kernel(entries, blocks, *refs):
+    )(*coefs, *[block[0] if block[3] else in_vmem(block[0]) for block in blocks])
+
+
+def put_kernel(entries, part, blocks, *refs):
     me = lax.axis_index("grp")
     blocks, (out_ref, sum_ref, sems) = refs[:blocks], refs[-3:]
     copies = []
     used = 0
-    for n, (parts, size, place) in enumerate(entries):
+    for n, (parts, size, (k, row)) in enumerate(entries):
         block, start = parts[0]
         source = blocks[block].at[pl.ds(start, size), :]
         if len(parts) > 1:
@@ -234,7 +236,7 @@
             source = sum_ref.at[pl.ds(used, size), :]
             source[...] = total
             used += size
-        offset = place[1] if place[0] else (me ^ place[1]) * size
+        offset = row if k is None else (me ^ k) * part + row
         copy = pltpu.make_async_copy(source, out_ref.at[pl.ds(offset, size), :], sems.at[n])
         copy.start()
         copies.append(copy)
@@ -242,12 +244,12 @@
         copy.wait()
 
 
-def put(entries, blocks, size, base=None):
+def put(entries, blocks, part, size, base=None):
     extra = [] if base is None else [base]
     moved = sum(entry[1] for entry in entries)
     scratch = sum(entry[1] for entry in entries if len(entry[0]) > 1)
     return pl.pallas_call(
-        functools.partial(put_kernel, entries, len(blocks)),
+        functools.partial(put_kernel, entries, part, len(blocks)),
         out_shape=jax.ShapeDtypeStruct((size, LANES), jnp.float32),
         in_specs=[VMEM_SPEC] * len(blocks) + [HBM_SPEC] * len(extra),
         out_specs=HBM_SPEC,
@@ -259,18 +261,16 @@
     )(*blocks, *extra)
 
 
-def cut_kernel(places, sizes, block_ref, *refs):
+def cut_kernel(places, part, block_ref, *refs):
     me = lax.axis_index("grp")
-    outs, (in_sems, out_sems) = refs[: len(sizes)], refs[-2:]
-    through = refs[len(sizes) : -2]
+    outs, (in_sems, out_sems) = refs[: len(places)], refs[-2:]
+    through = refs[len(places) : -2]
     copies = []
-    start = 0
-    for n, size in enumerate(sizes):
-        offset = (me ^ places[n]) * size if places else start
+    for n, (k, row, size) in enumerate(places):
+        offset = row if k is None else (me ^ k) * part + row
         held = through[n] if through else outs[n]
         copies.append(pltpu.make_async_copy(block_ref.at[pl.ds(offset, size), :], held, in_sems.at[n]))
         copies[n].start()
-        start += size
     for copy in copies:
         copy.wait()
     moves = [pltpu.make_async_copy(held, out, out_sems.at[n]) for n, (held, out) in enumerate(zip(through, outs))]
@@ -280,15 +280,15 @@
         move.wait()
 
 
-def cut(block, sizes, places=None):
-    out = pltpu.VMEM if places else pltpu.HBM
-    through = [] if places else [pltpu.VMEM((size, LANES), jnp.float32) for size in sizes]
-    return pl.pallas_call(
-        functools.partial(cut_kernel, places, sizes),
-        out_shape=[out((size, LANES), jnp.float32) for size in sizes],
+def cut(block, places, part, fast):
+    out = pltpu.VMEM if fast else pltpu.HBM
+    through = [] if fast else [pltpu.VMEM((size, LANES), jnp.float32) for _, _, size in places]
+    return pl.pallas_call(
+        functools.partial(cut_kernel, places, part),
+        out_shape=[out((size, LANES), jnp.float32) for _, _, size in places],
         in_specs=[HBM_SPEC],
-        out_specs=[VMEM_SPEC if places else HBM_SPEC] * len(sizes),
-        scratch_shapes=through + [pltpu.SemaphoreType.DMA((len(sizes),))] * 2,
+        out_specs=[VMEM_SPEC if fast else HBM_SPEC] * len(places),
+        scratch_shapes=through + [pltpu.SemaphoreType.DMA((len(places),))] * 2,
         compiler_params=pltpu.CompilerParams(vmem_limit_bytes=VMEM_LIMIT),
         cost_estimate=SHORT,
         name="cut",
@@ -314,25 +314,36 @@
             yield [step * k for k in range(radix)]
             left, step = left // radix, step * radix
 
-    everyone, others = list(range(groups)), list(range(groups - 1, 0, -1))
+    everyone = list(range(groups))
+    direct = [k for k in everyone[1:] if k in lows or k in highs]
+    distant = [k for k in everyone[1:] if k not in direct]
     size, step = x.shape[0], SUB * rows
     first = max(1, half // step * 3 // 8) * step
-    second = half - first
-
-    sent = cut(x, [part] * len(others), others)
+    split = part // step // 2 * step
+    halves = [(0, split), (split, part - split)]
+
+    def legs(k, n):
+        low, high = k % near, k - k % near
+        return (low, high) if n == 0 else (high, low)
+
+    def pieces(k):
+        return halves if k in distant else [(0, part)]
+
+    order = distant + direct
+    sent = cut(x, [(k, 0, part) for k in order], part, True)
     s, sent = lax.optimization_barrier((s, sent))
-    s_own = cut(s, [first, second] * 2)
-    xs = {k: swap(block, k) for k, block in zip(others, sent)}
-    xs[others[0]], x = lax.optimization_barrier((xs[others[0]], x))
-    xs[0] = cut(x, [part], [0])[0]
-    xs = [xs[k] for k in everyone]
+    bounds = [(n * half + row, length) for n in (0, 1) for row, length in ((0, first), (first, half - first))]
+    s_own = cut(s, [(None, *bound) for bound in bounds], part, False)
+    xs = {k: swap(block, k) for k, block in zip(order, sent)}
+    xs[order[0]], x, s_own = lax.optimization_barrier((xs[order[0]], x, s_own))
+    xs[0] = cut(x, [(0, 0, part)], part, True)[0]
+    xs = [[xs[k]] for k in everyone]
 
     def exchange(low, high):
         return [swap(low, k) for k in lows], [swap(high, k) for k in highs]
 
-    xs[-1], s_own = lax.optimization_barrier((xs[-1], s_own))
     early = exchange(s_own[0], s_own[2])
-    grams = [gram(xs, rows, 1)]
+    grams = [gram(xs, rows)]
     for partners in stages("grp"):
         grams = [swap(add(grams) if len(grams) > 1 else grams[0], k) for k in partners]
     early, pair, grams = lax.optimization_barrier((early, (s_own[1], s_own[3]), grams))
@@ -347,33 +358,49 @@
         mixed = mix(coefs, rows, count, jobs)
         return swap(mixed, dest), lax.optimization_barrier((coefs, mixed))[0]
 
+    def particle_jobs(dest, start, length):
+        jobs = []
+        for n, (row, piece) in enumerate(halves):
+            begin, extent = max(start, row), min(start + length, row + piece) - max(start, row)
+            if extent > 0:
+                blocks = [(xs[k][n], begin - row, extent, False) if len(xs[k]) > 1 else (xs[k][0], begin, extent, False) for k in everyone]
+                jobs.append((True, dest, everyone, blocks))
+        return jobs
+
     def score_jobs(dest, n, low, high):
         jobs = []
         for held, start, end in ((early, 0, first), (late, first, half)):
-            begin, size = max(low, start), min(high, end) - max(low, start)
-            if size > 0:
-                blocks = [(s, n * half + begin, size)] + [(block, begin - start, size) for block in held[n][1:]]
+            begin, extent = max(low, start), min(high, end) - max(low, start)
+            if extent > 0:
+                blocks = [(s, n * half + begin, extent, True)] + [(block, begin - start, extent, True) for block in held[n][1:]]
                 jobs.append((False, dest, (lows, highs)[n], blocks))
         return jobs
 
     back, sums = {}, {}
-    for k in others:
-        back[k], coefs = send(k, [(True, k, everyone, xs)], coefs)
+    for k in direct:
+        back[k, 0], coefs = send(k, particle_jobs(k, 0, part), coefs)
+    for k in distant:
+        for n in (0, 1):
+            hop, coefs = send(legs(k, n)[0], particle_jobs(k, *halves[n]), coefs)
+            back[k, n] = swap(hop, legs(k, n)[1])
     middle = half // step // 2 * step
     spans = [span for span in ((0, middle), (middle, half)) if span[0] < span[1]]
     for span in spans:
         for n, dests in enumerate((highs[1:], lows[1:])):
             for k in dests:
                 sums[span, k], coefs = send(k, score_jobs(k, n, *span), coefs)
-    own_jobs = [(True, 0, everyone, xs)]
+    own_jobs = particle_jobs(0, 0, part)
     for span in spans:
         own_jobs += score_jobs(0, 0, *span) + score_jobs(0, 1, *span)
     own = mix(coefs, rows, count, own_jobs)
 
-    repel = put([([(0, 0)], part, (False, 0))], [own], size)
-    for k in others:
-        repel, back[k] = lax.optimization_barrier((repel, back[k]))
-        repel = put([([(0, 0)], part, (False, k))], [back[k]], size, base=repel)
+    def place(k):
+        return [([(n, 0)], length, (k, row)) for n, (row, length) in enumerate(pieces(k))]
+
+    repel = put([([(0, 0)], part, (0, 0))], [own], part, size)
+    for k in direct:
+        repel, got = lax.optimization_barrier((repel, back[k, 0]))
+        repel = put(place(k), [got], part, size, base=repel)
     drive = None
     begin = part
     for span in spans:
@@ -383,9 +410,13 @@
             held = repel if drive is None else (drive, repel)
             held, got = lax.optimization_barrier((held, got))
             drive, repel = (None, held) if drive is None else held
-            entry = ([(0, begin)] + [(1 + m, 0) for m in range(len(got))], length, (True, n * half + span[0]))
-            drive = put([entry], [own, *got], size, base=drive)
+            entry = ([(0, begin)] + [(1 + m, 0) for m in range(len(got))], length, (None, n * half + span[0]))
+            drive = put([entry], [own, *got], part, size, base=drive)
             begin += length
+    for k in distant:
+        got = [back[k, n] for n in (0, 1)]
+        (drive, repel), got = lax.optimization_barrier(((drive, repel), got))
+        repel = put(place(k), got, part, size, base=repel)
     return (undense(drive, rows), undense(repel, rows))
 
 

time: 103 us -> 103 us (level)
  waiting for transfers between devices: 52.1 us -> 48.2 us
  starting transfers between devices: 23.7 us -> 27.5 us
    ppermute x21 -> x24, waiting for transfers between devices: 52.1 us -> 48.2 us  [swap(): lax.ppermute(block, axis, [(i, i ^ k) for i in range(lax.axis_size(axis))])]
    ppermute x21 -> x24, starting transfers between devices: 23.7 us -> 27.5 us  [swap(): lax.ppermute(block, axis, [(i, i ^ k) for i in range(lax.axis_size(axis))])]
    pallas_call x20 -> x21, Pallas kernels: 24.2 us -> 24.2 us  [the longest x9 9.85 us: mix(): pl.pallas_call(functools.partial(mix_kernel, rows, count, [(*job[:3], [bl...]
  transfers between devices with their start and end apart: 21 -> 24, of which waited for: 12 -> 13; matrix products, arithmetic and copies ran while one was open for 0% -> 0% of each run, Pallas kernels for 22% -> 22%
where the time goes in v6:
time: 103 us; the launch traced here: 102 us
  waiting for transfers between devices  48.2 us (47%)
  starting transfers between devices  27.5 us (27%)
  Pallas kernels  25.1 us (24%)
  between operations  1.49 us (1%)
    ppermute x24, waiting for transfers between devices, swap(): lax.ppermute(block, axis, [(i, i ^ k) for i in range(lax.axis_size(axis))])  48.2 us
    ppermute x24, starting transfers between devices, swap(): lax.ppermute(block, axis, [(i, i ^ k) for i in range(lax.axis_size(axis))])  27.5 us
    pallas_call x9, Pallas kernels, mix(): pl.pallas_call(functools.partial(mix_kernel, rows, count, [(*job[:3], [bl...  9.85 us
    pallas_call x8, Pallas kernels, put(): pl.pallas_call(functools.partial(put_kernel, entries, part, len(blocks)),...  6.67 us
    pallas_call x3, Pallas kernels, cut(): pl.pallas_call(functools.partial(cut_kernel, places, part), out_shape=[ou...  5.38 us
    pallas_call x1, Pallas kernels, gram(): pl.pallas_call(functools.partial(gram_kernel, rows, [len(x) for x in xs])...  2.28 us
  transfers between devices with their start and end apart: 24, of which 13 were waited for; matrix products, arithmetic and copies ran while one was open for 0% of the time, Pallas kernels for 22%

profile of v6, /device:TPU:0, one launch (start us, length us, event | category | flops | bytes accessed | tf_op | source)
XLA Modules:
  0.0 102.3 jit_solution(479189730904531920)
XLA Ops:
  0.6 1.4 %cut.3 = (f32[1024,128]{1,0:T(8,128)S(1)}, f32[1024,128]{1,0:T(8,128)S(1)}, f32[1024,128]{1,0:T(8,128)S(1)}) custom-call(f32[4096,128]{1,0:T(8,128)} %bitcast.35), custom_call_target="tpu_custom_call" | custom-call | flops 1 | bytes 1 | tf_op jit(solution)/shard_map/cut/pallas_call | solution.py:286
  2.1 4.0 %collective-permute-start = (f32[1024,128]{1,0:T(8,128)S(1)}, f32[1024,128]{1,0:T(8,128)S(1)}, u32[]{:S(2)}, u32[]{:S(2)}) collective-permute-start(f32[1024,128]{1,0:T(8,128)S(1)} %get-tuple-element.67), channel_id=1, source_target_pairs={{0,24},{8,16},{16,8},{24,0},{1,25},{9,17},{17,9},{25,1},{2,26},{10... | collective-permute-start | bytes 1572872 | tf_op jit(solution)/shard_map/ppermute | solution.py:308
  6.7 2.9 %cut.4 = (f32[768,128]{1,0:T(8,128)}, f32[1280,128]{1,0:T(8,128)}, f32[768,128]{1,0:T(8,128)}, f32[1280,128]{1,0:T(8,128)}) custom-call(f32[4096,128]{1,0:T(8,128)} %bitcast.20), custom_call_target="tpu_custom_call" | custom-call | flops 1 | bytes 1 | tf_op jit(solution)/shard_map/cut/pallas_call | solution.py:286
  9.6 9.2 %collective-permute-done.refs_3_.refs_7_ = f32[1024,128]{1,0:T(8,128)S(1)} collective-permute-done((f32[1024,128]{1,0:T(8,128)S(1)}, f32[1024,128]{1,0:T(8,128)S(1)}, u32[]{:S(2)}, u32[]{:S(2)}) %collective-permute-start) | collective-permute-done | bytes 524320 | tf_op jit(solution)/shard_map/ppermute | solution.py:308
  18.8 2.0 %collective-permute-start.1 = (f32[768,128]{1,0:T(8,128)}, f32[768,128]{1,0:T(8,128)S(1)}, u32[]{:S(2)}, u32[]{:S(2)}) collective-permute-start(f32[768,128]{1,0:T(8,128)} %get-tuple-element.73), channel_id=1, source_target_pairs={{0,8},{8,0},{16,24},{24,16},{1,9},{9,1},{17,25},{25,17},{2,10},{10... | collective-permute-start | bytes 1179656 | tf_op jit(solution)/shard_map/ppermute | solution.py:308
  20.8 1.5 %collective-permute-start.2 = (f32[768,128]{1,0:T(8,128)}, f32[768,128]{1,0:T(8,128)S(1)}, u32[]{:S(2)}, u32[]{:S(2)}) collective-permute-start(f32[768,128]{1,0:T(8,128)} %get-tuple-element.74), channel_id=1, source_target_pairs={{0,16},{8,24},{16,0},{24,8},{1,17},{9,25},{17,1},{25,9},{2,18},{10... | collective-permute-start | bytes 1179656 | tf_op jit(solution)/shard_map/ppermute | solution.py:308
  22.3 1.1 %cut.5.refs_0_.refs_4_ = f32[1024,128]{1,0:T(8,128)S(1)} custom-call(f32[4096,128]{1,0:T(8,128)} %bitcast.36), custom_call_target="tpu_custom_call" | custom-call | flops 1 | bytes 1 | tf_op jit(solution)/shard_map/cut/pallas_call | solution.py:286
  23.4 7.2 %collective-permute-done.3.refs_1_.refs_5_ = f32[1024,128]{1,0:T(8,128)S(1)} collective-permute-done((f32[1024,128]{1,0:T(8,128)S(1)}, f32[1024,128]{1,0:T(8,128)S(1)}, u32[]{:S(2)}, u32[]{:S(2)}) %collective-permute-start.3) | collective-permute-done | bytes 524320 | tf_op jit(solution)/shard_map/ppermute | solution.py:308
  30.6 2.3 %gram.1.refs_0_ = f32[1,2,128]{2,1,0:T(2,128)S(1)} custom-call(f32[1024,128]{1,0:T(8,128)S(1)} %cut.5.refs_0_.refs_4_, f32[1024,128]{1,0:T(8,128)S(1)} %collective-permute-done.3.refs_1_.refs_5_, f32[1024,128]{1,0:T(8,128)S(1)} %collective-permute-done.4.refs_2_.refs_6_, f32[1024,128]{1,0:T(8,128)S(1)} %collective-permute-done.refs_3_.refs_7_), custom_call_target="tpu_custom_call" | custom-call | flops 1 | bytes 1 | tf_op jit(solution)/shard_map/gram/pallas_call | solution.py:85
  32.9 1.5 %collective-permute-start.7 = (f32[1,2,128]{2,1,0:T(2,128)S(1)}, f32[1,2,128]{2,1,0:T(2,128)S(1)}, u32[]{:S(2)}, u32[]{:S(2)}) collective-permute-start(f32[1,2,128]{2,1,0:T(2,128)S(1)} %gram.1.refs_0_), channel_id=1, source_target_pairs={{0,24},{8,16},{16,8},{24,0},{1,25},{9,17},{17,9},{25,1},{2,26},{10... | collective-permute-start | bytes 3080 | tf_op jit(solution)/shard_map/ppermute | solution.py:308
  34.4 1.5 %collective-permute-start.6 = (f32[1,2,128]{2,1,0:T(2,128)S(1)}, f32[1,2,128]{2,1,0:T(2,128)S(1)}, u32[]{:S(2)}, u32[]{:S(2)}) collective-permute-start(f32[1,2,128]{2,1,0:T(2,128)S(1)} %gram.1.refs_0_), channel_id=1, source_target_pairs={{0,16},{8,24},{16,0},{24,8},{1,17},{9,25},{17,1},{25,9},{2,18},{10... | collective-permute-start | bytes 3080 | tf_op jit(solution)/shard_map/ppermute | solution.py:308
  36.4 1.2 %collective-permute-done.7.refs_3_ = f32[1,2,128]{2,1,0:T(2,128)S(1)} collective-permute-done((f32[1,2,128]{2,1,0:T(2,128)S(1)}, f32[1,2,128]{2,1,0:T(2,128)S(1)}, u32[]{:S(2)}, u32[]{:S(2)}) %collective-permute-start.7) | collective-permute-done | bytes 1056 | tf_op jit(solution)/shard_map/ppermute | solution.py:308
  37.9 1.5 %collective-permute-done.5.refs_1_ = f32[1,2,128]{2,1,0:T(2,128)S(1)} collective-permute-done((f32[1,2,128]{2,1,0:T(2,128)S(1)}, f32[1,2,128]{2,1,0:T(2,128)S(1)}, u32[]{:S(2)}, u32[]{:S(2)}) %collective-permute-start.5) | collective-permute-done | bytes 1056 | tf_op jit(solution)/shard_map/ppermute | solution.py:308
  41.6 1.1 %collective-permute-start.9 = (f32[1,2,128]{2,1,0:T(2,128)S(1)}, f32[1,2,128]{2,1,0:T(2,128)S(1)}, u32[]{:S(2)}, u32[]{:S(2)}) collective-permute-start(f32[1,2,128]{2,1,0:T(2,128)S(1)} %add.2.refs_0_), channel_id=1, source_target_pairs={{0,2},{1,3},{2,0},{3,1},{4,6},{5,7},{6,4},{7,5},{8,10},{9,11},{10,... | collective-permute-start | bytes 3080 | tf_op jit(solution)/shard_map/ppermute | solution.py:308
  42.8 1.1 %collective-permute-done.10.refs_3_ = f32[1,2,128]{2,1,0:T(2,128)S(1)} collective-permute-done((f32[1,2,128]{2,1,0:T(2,128)S(1)}, f32[1,2,128]{2,1,0:T(2,128)S(1)}, u32[]{:S(2)}, u32[]{:S(2)}) %collective-permute-start.10) | collective-permute-done | bytes 1056 | tf_op jit(solution)/shard_map/ppermute | solution.py:308
  44.0 1.2 %collective-permute-done.9.refs_2_ = f32[1,2,128]{2,1,0:T(2,128)S(1)} collective-permute-done((f32[1,2,128]{2,1,0:T(2,128)S(1)}, f32[1,2,128]{2,1,0:T(2,128)S(1)}, u32[]{:S(2)}, u32[]{:S(2)}) %collective-permute-start.9) | collective-permute-done | bytes 1056 | tf_op jit(solution)/shard_map/ppermute | solution.py:308
  45.1 2.7 %collective-permute-start.11 = (f32[1,2,128]{2,1,0:T(2,128)S(1)}, f32[1,2,128]{2,1,0:T(2,128)S(1)}, u32[]{:S(2)}, u32[]{:S(2)}) collective-permute-start(f32[1,2,128]{2,1,0:T(2,128)S(1)} %add.3.refs_0_), channel_id=1, source_target_pairs={{0,4},{1,5},{2,6},{3,7},{4,0},{5,1},{6,2},{7,3},{8,12},{9,13},{10,... | collective-permute-start | bytes 3080 | tf_op jit(solution)/shard_map/ppermute | solution.py:308
  48.5 1.2 %collective-permute-done.11.refs_1_ = f32[1,2,128]{2,1,0:T(2,128)S(1)} collective-permute-done((f32[1,2,128]{2,1,0:T(2,128)S(1)}, f32[1,2,128]{2,1,0:T(2,128)S(1)}, u32[]{:S(2)}, u32[]{:S(2)}) %collective-permute-start.11) | collective-permute-done | bytes 1056 | tf_op jit(solution)/shard_map/ppermute | solution.py:308
  53.1 1.5 %collective-permute-start.22 = (f32[512,128]{1,0:T(8,128)S(1)}, f32[512,128]{1,0:T(8,128)S(1)}, u32[]{:S(2)}, u32[]{:S(2)}) collective-permute-start(f32[512,128]{1,0:T(8,128)S(1)} %mix.12), channel_id=1, source_target_pairs={{0,16},{8,24},{16,0},{24,8},{1,17},{9,25},{17,1},{25,9},{2,18},{10... | collective-permute-start | bytes 786440 | tf_op jit(solution)/shard_map/ppermute | solution.py:308
  55.2 1.5 %collective-permute-start.14 = (f32[1024,128]{1,0:T(8,128)S(1)}, f32[1024,128]{1,0:T(8,128)S(1)}, u32[]{:S(2)}, u32[]{:S(2)}) collective-permute-start(f32[1024,128]{1,0:T(8,128)S(1)} %mix.9), channel_id=1, source_target_pairs={{0,8},{8,0},{16,24},{24,16},{1,9},{9,1},{17,25},{25,17},{2,10},{10... | collective-permute-start | bytes 1572872 | tf_op jit(solution)/shard_map/ppermute | solution.py:308
  56.6 1.3 %mix.13 = f32[1024,128]{1,0:T(8,128)S(1)} custom-call(f32[256,128]{1,0:T(8,128)S(1)} %get-tuple-element.105.drive_ref, f32[256,128]{1,0:T(8,128)S(1)} %get-tuple-element.106.repel_ref, f32[4096,128]{1,0:T(8,128)} %bitcast.21, f32[768,128]{1,0:T(8,128)S(1)} %collective-permute-done.1.refs_1_.refs_9_, f32[4096,128]{1,0:T(8,128)} %bitcast.22, ...), custom_call_target="tpu_custom_call" | custom-call | flops 1 | bytes 1 | tf_op jit(solution)/shard_map/mix/pallas_call | solution.py:211
  58.0 1.0 collective-permute-start.16
  59.0 1.3 %mix.14 = f32[1024,128]{1,0:T(8,128)S(1)} custom-call(f32[256,128]{1,0:T(8,128)S(1)} %get-tuple-element.105.drive_ref, f32[256,128]{1,0:T(8,128)S(1)} %get-tuple-element.106.repel_ref, f32[4096,128]{1,0:T(8,128)} %bitcast.23, f32[768,128]{1,0:T(8,128)S(1)} %collective-permute-done.2.refs_1_.refs_13_, f32[4096,128]{1,0:T(8,128)} %bitcast.24, ...), custom_call_target="tpu_custom_call" | custom-call | flops 1 | bytes 1 | tf_op jit(solution)/shard_map/mix/pallas_call | solution.py:211
  60.3 14.3 %collective-permute-done.22 = f32[512,128]{1,0:T(8,128)S(1)} collective-permute-done((f32[512,128]{1,0:T(8,128)S(1)}, f32[512,128]{1,0:T(8,128)S(1)}, u32[]{:S(2)}, u32[]{:S(2)}) %collective-permute-start.22) | collective-permute-done | bytes 262176 | tf_op jit(solution)/shard_map/ppermute | solution.py:308
  74.6 1.3 %mix.15 = f32[1024,128]{1,0:T(8,128)S(1)} custom-call(f32[256,128]{1,0:T(8,128)S(1)} %get-tuple-element.105.drive_ref, f32[256,128]{1,0:T(8,128)S(1)} %get-tuple-element.106.repel_ref, f32[4096,128]{1,0:T(8,128)} %bitcast.25, f32[1280,128]{1,0:T(8,128)S(1)} %collective-permute-done.12.refs_3_.refs_1_.refs_11_.refs_17_), custom_call_target="tpu_custom_call" | custom-call | flops 1 | bytes 1 | tf_op jit(solution)/shard_map/mix/pallas_call | solution.py:211
  76.0 1.7 %collective-permute-start.18 = (f32[1024,128]{1,0:T(8,128)S(1)}, f32[1024,128]{1,0:T(8,128)S(1)}, u32[]{:S(2)}, u32[]{:S(2)}) collective-permute-start(f32[1024,128]{1,0:T(8,128)S(1)} %mix.15), channel_id=1, source_target_pairs={{0,16},{8,24},{16,0},{24,8},{1,17},{9,25},{17,1},{25,9},{2,18},{10... | collective-permute-start | bytes 1572872 | tf_op jit(solution)/shard_map/ppermute | solution.py:308
  77.7 1.3 %mix.16 = f32[1024,128]{1,0:T(8,128)S(1)} custom-call(f32[256,128]{1,0:T(8,128)S(1)} %get-tuple-element.105.drive_ref, f32[256,128]{1,0:T(8,128)S(1)} %get-tuple-element.106.repel_ref, f32[4096,128]{1,0:T(8,128)} %bitcast.26, f32[1280,128]{1,0:T(8,128)S(1)} %collective-permute-done.13.refs_3_.refs_1_.refs_15_.refs_19_), custom_call_target="tpu_custom_call" | custom-call | flops 1 | bytes 1 | tf_op jit(solution)/shard_map/mix/pallas_call | solution.py:211
  79.0 1.3 %collective-permute-start.19 = (f32[1024,128]{1,0:T(8,128)S(1)}, f32[1024,128]{1,0:T(8,128)S(1)}, u32[]{:S(2)}, u32[]{:S(2)}) collective-permute-start(f32[1024,128]{1,0:T(8,128)S(1)} %mix.16), channel_id=1, source_target_pairs={{0,8},{8,0},{16,24},{24,16},{1,9},{9,1},{17,25},{25,17},{2,10},{10... | collective-permute-start | bytes 1572872 | tf_op jit(solution)/shard_map/ppermute | solution.py:308
  81.1 4.7 %collective-permute-done.16.refs_1_ = f32[1024,128]{1,0:T(8,128)S(1)} collective-permute-done((f32[1024,128]{1,0:T(8,128)S(1)}, f32[1024,128]{1,0:T(8,128)S(1)}, u32[]{:S(2)}, u32[]{:S(2)}) %collective-permute-start.16) | collective-permute-done | bytes 524320 | tf_op jit(solution)/shard_map/ppermute | solution.py:308
  86.7 2.7 %mix.17.refs_0_ = f32[5120,128]{1,0:T(8,128)S(1)} custom-call(f32[256,128]{1,0:T(8,128)S(1)} %get-tuple-element.105.drive_ref, f32[256,128]{1,0:T(8,128)S(1)} %get-tuple-element.106.repel_ref, f32[1024,128]{1,0:T(8,128)S(1)} %cut.5.refs_0_.refs_4_, f32[1024,128]{1,0:T(8,128)S(1)} %collective-permute-done.3.refs_1_.refs_5_, ...), custom_call_target="tpu_custom_call" | custom-call | flops 1 | bytes 1 | tf_op jit(solution)/shard_map/mix/pallas_call | solution.py:211
  93.6 3.5 %collective-permute-done.18.refs_1_ = f32[1024,128]{1,0:T(8,128)S(1)} collective-permute-done((f32[1024,128]{1,0:T(8,128)S(1)}, f32[1024,128]{1,0:T(8,128)S(1)}, u32[]{:S(2)}, u32[]{:S(2)}) %collective-permute-start.18) | collective-permute-done | bytes 524320 | tf_op jit(solution)/shard_map/ppermute | solution.py:308
  99.5 1.9 %collective-permute-done.23.refs_1_ = f32[512,128]{1,0:T(8,128)S(1)} collective-permute-done((f32[512,128]{1,0:T(8,128)S(1)}, f32[512,128]{1,0:T(8,128)S(1)}, u32[]{:S(2)}, u32[]{:S(2)}) %collective-permute-start.23) | collective-permute-done | bytes 262176 | tf_op jit(solution)/shard_map/ppermute | solution.py:308
  (44 shorter events, 16.8 us)
Async XLA Ops:
  2.1 16.8 %collective-permute-start = (f32[1024,128]{1,0:T(8,128)S(1)}, f32[1024,128]{1,0:T(8,128)S(1)}, u32[]{:S(2)}, u32[]{:S(2)}) collective-permute-start(f32[1024,128]{1,0:T(8,128)S(1)} %get-tuple-element.67), channel_id=1, source_target_pairs={{0,24},{8,16},{16,8},{24,0},{1,25},{9,17},{17,9},{25,1},{2,26},{10... | collective-permute-start | bytes 1572872 | tf_op jit(solution)/shard_map/ppermute | solution.py:308
  6.0 24.6 %collective-permute-start.3 = (f32[1024,128]{1,0:T(8,128)S(1)}, f32[1024,128]{1,0:T(8,128)S(1)}, u32[]{:S(2)}, u32[]{:S(2)}) collective-permute-start(f32[1024,128]{1,0:T(8,128)S(1)} %get-tuple-element.78), channel_id=1, source_target_pairs={{0,8},{8,0},{16,24},{24,16},{1,9},{9,1},{17,25},{25,17},{2,10},{10... | collective-permute-start | bytes 1572872 | tf_op jit(solution)/shard_map/ppermute | solution.py:308
  6.6 24.1 %collective-permute-start.4 = (f32[1024,128]{1,0:T(8,128)S(1)}, f32[1024,128]{1,0:T(8,128)S(1)}, u32[]{:S(2)}, u32[]{:S(2)}) collective-permute-start(f32[1024,128]{1,0:T(8,128)S(1)} %get-tuple-element.79), channel_id=1, source_target_pairs={{0,16},{8,24},{16,0},{24,8},{1,17},{9,25},{17,1},{25,9},{2,18},{10... | collective-permute-start | bytes 1572872 | tf_op jit(solution)/shard_map/ppermute | solution.py:308
  18.8 20.7 %copy-start.1 = (f32[1280,128]{1,0:T(8,128)S(1)}, f32[1280,128]{1,0:T(8,128)}, u32[]{:S(2)}) copy-start(f32[1280,128]{1,0:T(8,128)} %get-tuple-element.96) | copy-start | bytes 1966084
  18.8 21.3 %copy-start = (f32[1280,128]{1,0:T(8,128)S(1)}, f32[1280,128]{1,0:T(8,128)}, u32[]{:S(2)}) copy-start(f32[1280,128]{1,0:T(8,128)} %get-tuple-element.100) | copy-start | bytes 1966084
  18.8 20.6 %collective-permute-start.1 = (f32[768,128]{1,0:T(8,128)}, f32[768,128]{1,0:T(8,128)S(1)}, u32[]{:S(2)}, u32[]{:S(2)}) collective-permute-start(f32[768,128]{1,0:T(8,128)} %get-tuple-element.73), channel_id=1, source_target_pairs={{0,8},{8,0},{16,24},{24,16},{1,9},{9,1},{17,25},{25,17},{2,10},{10... | collective-permute-start | bytes 1179656 | tf_op jit(solution)/shard_map/ppermute | solution.py:308
  20.8 18.6 %collective-permute-start.2 = (f32[768,128]{1,0:T(8,128)}, f32[768,128]{1,0:T(8,128)S(1)}, u32[]{:S(2)}, u32[]{:S(2)}) collective-permute-start(f32[768,128]{1,0:T(8,128)} %get-tuple-element.74), channel_id=1, source_target_pairs={{0,16},{8,24},{16,0},{24,8},{1,17},{9,25},{17,1},{25,9},{2,18},{10... | collective-permute-start | bytes 1179656 | tf_op jit(solution)/shard_map/ppermute | solution.py:308
  32.9 4.8 %collective-permute-start.7 = (f32[1,2,128]{2,1,0:T(2,128)S(1)}, f32[1,2,128]{2,1,0:T(2,128)S(1)}, u32[]{:S(2)}, u32[]{:S(2)}) collective-permute-start(f32[1,2,128]{2,1,0:T(2,128)S(1)} %gram.1.refs_0_), channel_id=1, source_target_pairs={{0,24},{8,16},{16,8},{24,0},{1,25},{9,17},{17,9},{25,1},{2,26},{10... | collective-permute-start | bytes 3080 | tf_op jit(solution)/shard_map/ppermute | solution.py:308
  34.4 3.6 %collective-permute-start.6 = (f32[1,2,128]{2,1,0:T(2,128)S(1)}, f32[1,2,128]{2,1,0:T(2,128)S(1)}, u32[]{:S(2)}, u32[]{:S(2)}) collective-permute-start(f32[1,2,128]{2,1,0:T(2,128)S(1)} %gram.1.refs_0_), channel_id=1, source_target_pairs={{0,16},{8,24},{16,0},{24,8},{1,17},{9,25},{17,1},{25,9},{2,18},{10... | collective-permute-start | bytes 3080 | tf_op jit(solution)/shard_map/ppermute | solution.py:308
  35.9 3.6 %collective-permute-start.5 = (f32[1,2,128]{2,1,0:T(2,128)S(1)}, f32[1,2,128]{2,1,0:T(2,128)S(1)}, u32[]{:S(2)}, u32[]{:S(2)}) collective-permute-start(f32[1,2,128]{2,1,0:T(2,128)S(1)} %gram.1.refs_0_), channel_id=1, source_target_pairs={{0,8},{8,0},{16,24},{24,16},{1,9},{9,1},{17,25},{25,17},{2,10},{10... | collective-permute-start | bytes 3080 | tf_op jit(solution)/shard_map/ppermute | solution.py:308
  39.5 15.7 %collective-permute-start.12 = (f32[1280,128]{1,0:T(8,128)S(1)}, f32[1280,128]{1,0:T(8,128)S(1)}, u32[]{:S(2)}, u32[]{:S(2)}) collective-permute-start(f32[1280,128]{1,0:T(8,128)S(1)} %copy-done.1), channel_id=1, source_target_pairs={{0,8},{8,0},{16,24},{24,16},{1,9},{9,1},{17,25},{25,17},{2,10},{10... | collective-permute-start | bytes 1966088 | tf_op jit(solution)/shard_map/ppermute | solution.py:308
  40.1 17.9 %collective-permute-start.13 = (f32[1280,128]{1,0:T(8,128)S(1)}, f32[1280,128]{1,0:T(8,128)S(1)}, u32[]{:S(2)}, u32[]{:S(2)}) collective-permute-start(f32[1280,128]{1,0:T(8,128)S(1)} %copy-done), channel_id=1, source_target_pairs={{0,16},{8,24},{16,0},{24,8},{1,17},{9,25},{17,1},{25,9},{2,18},{10... | collective-permute-start | bytes 1966088 | tf_op jit(solution)/shard_map/ppermute | solution.py:308
  41.0 3.0 %collective-permute-start.10 = (f32[1,2,128]{2,1,0:T(2,128)S(1)}, f32[1,2,128]{2,1,0:T(2,128)S(1)}, u32[]{:S(2)}, u32[]{:S(2)}) collective-permute-start(f32[1,2,128]{2,1,0:T(2,128)S(1)} %add.2.refs_0_), channel_id=1, source_target_pairs={{0,3},{1,2},{2,1},{3,0},{4,7},{5,6},{6,5},{7,4},{8,11},{9,10},{10,... | collective-permute-start | bytes 3080 | tf_op jit(solution)/shard_map/ppermute | solution.py:308
  41.6 3.6 %collective-permute-start.9 = (f32[1,2,128]{2,1,0:T(2,128)S(1)}, f32[1,2,128]{2,1,0:T(2,128)S(1)}, u32[]{:S(2)}, u32[]{:S(2)}) collective-permute-start(f32[1,2,128]{2,1,0:T(2,128)S(1)} %add.2.refs_0_), channel_id=1, source_target_pairs={{0,2},{1,3},{2,0},{3,1},{4,6},{5,7},{6,4},{7,5},{8,10},{9,11},{10,... | collective-permute-start | bytes 3080 | tf_op jit(solution)/shard_map/ppermute | solution.py:308
  42.6 2.5 %collective-permute-start.8 = (f32[1,2,128]{2,1,0:T(2,128)S(1)}, f32[1,2,128]{2,1,0:T(2,128)S(1)}, u32[]{:S(2)}, u32[]{:S(2)}) collective-permute-start(f32[1,2,128]{2,1,0:T(2,128)S(1)} %add.2.refs_0_), channel_id=1, source_target_pairs={{0,1},{1,0},{2,3},{3,2},{4,5},{5,4},{6,7},{7,6},{8,9},{9,8},{10,11... | collective-permute-start | bytes 3080 | tf_op jit(solution)/shard_map/ppermute | solution.py:308
  45.1 4.5 %collective-permute-start.11 = (f32[1,2,128]{2,1,0:T(2,128)S(1)}, f32[1,2,128]{2,1,0:T(2,128)S(1)}, u32[]{:S(2)}, u32[]{:S(2)}) collective-permute-start(f32[1,2,128]{2,1,0:T(2,128)S(1)} %add.3.refs_0_), channel_id=1, source_target_pairs={{0,4},{1,5},{2,6},{3,7},{4,0},{5,1},{6,2},{7,3},{8,12},{9,13},{10,... | collective-permute-start | bytes 3080 | tf_op jit(solution)/shard_map/ppermute | solution.py:308
  51.8 27.2 %collective-permute-start.15 = (f32[1024,128]{1,0:T(8,128)S(1)}, f32[1024,128]{1,0:T(8,128)S(1)}, u32[]{:S(2)}, u32[]{:S(2)}) collective-permute-start(f32[1024,128]{1,0:T(8,128)S(1)} %mix.10), channel_id=1, source_target_pairs={{0,16},{8,24},{16,0},{24,8},{1,17},{9,25},{17,1},{25,9},{2,18},{10... | collective-permute-start | bytes 1572872 | tf_op jit(solution)/shard_map/ppermute | solution.py:308
  53.1 21.5 %collective-permute-start.22 = (f32[512,128]{1,0:T(8,128)S(1)}, f32[512,128]{1,0:T(8,128)S(1)}, u32[]{:S(2)}, u32[]{:S(2)}) collective-permute-start(f32[512,128]{1,0:T(8,128)S(1)} %mix.12), channel_id=1, source_target_pairs={{0,16},{8,24},{16,0},{24,8},{1,17},{9,25},{17,1},{25,9},{2,18},{10... | collective-permute-start | bytes 786440 | tf_op jit(solution)/shard_map/ppermute | solution.py:308
  54.6 21.3 %collective-permute-start.20 = (f32[512,128]{1,0:T(8,128)S(1)}, f32[512,128]{1,0:T(8,128)S(1)}, u32[]{:S(2)}, u32[]{:S(2)}) collective-permute-start(f32[512,128]{1,0:T(8,128)S(1)} %mix.11), channel_id=1, source_target_pairs={{0,8},{8,0},{16,24},{24,16},{1,9},{9,1},{17,25},{25,17},{2,10},{10... | collective-permute-start | bytes 786440 | tf_op jit(solution)/shard_map/ppermute | solution.py:308
  55.2 25.2 %collective-permute-start.14 = (f32[1024,128]{1,0:T(8,128)S(1)}, f32[1024,128]{1,0:T(8,128)S(1)}, u32[]{:S(2)}, u32[]{:S(2)}) collective-permute-start(f32[1024,128]{1,0:T(8,128)S(1)} %mix.9), channel_id=1, source_target_pairs={{0,8},{8,0},{16,24},{24,16},{1,9},{9,1},{17,25},{25,17},{2,10},{10... | collective-permute-start | bytes 1572872 | tf_op jit(solution)/shard_map/ppermute | solution.py:308
  58.0 27.9 %collective-permute-start.16 = (f32[1024,128]{1,0:T(8,128)S(1)}, f32[1024,128]{1,0:T(8,128)S(1)}, u32[]{:S(2)}, u32[]{:S(2)}) collective-permute-start(f32[1024,128]{1,0:T(8,128)S(1)} %mix.13), channel_id=1, source_target_pairs={{0,16},{8,24},{16,0},{24,8},{1,17},{9,25},{17,1},{25,9},{2,18},{10... | collective-permute-start | bytes 1572872 | tf_op jit(solution)/shard_map/ppermute | solution.py:308
  74.6 18.1 %collective-permute-start.17 = (f32[1024,128]{1,0:T(8,128)S(1)}, f32[1024,128]{1,0:T(8,128)S(1)}, u32[]{:S(2)}, u32[]{:S(2)}) collective-permute-start(f32[1024,128]{1,0:T(8,128)S(1)} %mix.14), channel_id=1, source_target_pairs={{0,8},{8,0},{16,24},{24,16},{1,9},{9,1},{17,25},{25,17},{2,10},{10... | collective-permute-start | bytes 1572872 | tf_op jit(solution)/shard_map/ppermute | solution.py:308
  76.0 21.1 %collective-permute-start.18 = (f32[1024,128]{1,0:T(8,128)S(1)}, f32[1024,128]{1,0:T(8,128)S(1)}, u32[]{:S(2)}, u32[]{:S(2)}) collective-permute-start(f32[1024,128]{1,0:T(8,128)S(1)} %mix.15), channel_id=1, source_target_pairs={{0,16},{8,24},{16,0},{24,8},{1,17},{9,25},{17,1},{25,9},{2,18},{10... | collective-permute-start | bytes 1572872 | tf_op jit(solution)/shard_map/ppermute | solution.py:308
  79.0 19.6 %collective-permute-start.19 = (f32[1024,128]{1,0:T(8,128)S(1)}, f32[1024,128]{1,0:T(8,128)S(1)}, u32[]{:S(2)}, u32[]{:S(2)}) collective-permute-start(f32[1024,128]{1,0:T(8,128)S(1)} %mix.16), channel_id=1, source_target_pairs={{0,8},{8,0},{16,24},{24,16},{1,9},{9,1},{17,25},{25,17},{2,10},{10... | collective-permute-start | bytes 1572872 | tf_op jit(solution)/shard_map/ppermute | solution.py:308
  80.4 21.1 %collective-permute-start.23 = (f32[512,128]{1,0:T(8,128)S(1)}, f32[512,128]{1,0:T(8,128)S(1)}, u32[]{:S(2)}, u32[]{:S(2)}) collective-permute-start(f32[512,128]{1,0:T(8,128)S(1)} %collective-permute-done.22), channel_id=1, source_target_pairs={{0,8},{8,0},{16,24},{24,16},{1,9},{9,1},{17,25},{25,17},{2,10},{10... | collective-permute-start | bytes 786440 | tf_op jit(solution)/shard_map/ppermute | solution.py:308
  85.8 15.6 %collective-permute-start.21 = (f32[512,128]{1,0:T(8,128)S(1)}, f32[512,128]{1,0:T(8,128)S(1)}, u32[]{:S(2)}, u32[]{:S(2)}) collective-permute-start(f32[512,128]{1,0:T(8,128)S(1)} %collective-permute-done.20), channel_id=1, source_target_pairs={{0,16},{8,24},{16,0},{24,8},{1,17},{9,25},{17,1},{25,9},{2,18},{10... | collective-permute-start | bytes 786440 | tf_op jit(solution)/shard_map/ppermute | solution.py:308

commit v7 on v6

--- a/solution.py
+++ b/solution.py
@@ -339,15 +339,17 @@
     xs[0] = cut(x, [(0, 0, part)], part, True)[0]
     xs = [[xs[k]] for k in everyone]
 
-    def exchange(low, high):
-        return [swap(low, k) for k in lows], [swap(high, k) for k in highs]
-
-    early = exchange(s_own[0], s_own[2])
+    def exchange(block, partners):
+        return [swap(block, k) for k in partners]
+
+    early = [exchange(s_own[0], lows), exchange(s_own[2], highs)]
     grams = [gram(xs, rows)]
+    pair = [s_own[1], s_own[3]]
     for partners in stages("grp"):
-        grams = [swap(add(grams) if len(grams) > 1 else grams[0], k) for k in partners]
-    early, pair, grams = lax.optimization_barrier((early, (s_own[1], s_own[3]), grams))
-    late = exchange(*pair)
+        total = add(grams) if len(grams) > 1 else grams[0]
+        grams = [swap(total, k) for k in partners]
+    early, pair, grams = lax.optimization_barrier((early, pair, grams))
+    late = [exchange(pair[0], lows), exchange(pair[1], highs)]
     for partners in stages("par"):
         grams = [swap(add(grams), k, "par") for k in partners]
     coefs = weights(kernel_width, grams, rows, count)
@@ -380,7 +382,7 @@
     for k in direct:
         back[k, 0], coefs = send(k, particle_jobs(k, 0, part), coefs)
     for k in distant:
-        for n in (0, 1):
+        for n in (1, 0):
             hop, coefs = send(legs(k, n)[0], particle_jobs(k, *halves[n]), coefs)
             back[k, n] = swap(hop, legs(k, n)[1])
     middle = half // step // 2 * step

time: 103 us -> 102 us (level)
  transfers between devices with their start and end apart: 24 -> 24, of which waited for: 13 -> 13; matrix products, arithmetic and copies ran while one was open for 0% -> 0% of each run, Pallas kernels for 22% -> 23%
where the time goes in v7:
time: 102 us
  waiting for transfers between devices  48 us (47%)
  starting transfers between devices  26.9 us (26%)
  Pallas kernels  25.1 us (25%)
  between operations  1.49 us (1%)
    ppermute x24, waiting for transfers between devices, swap(): lax.ppermute(block, axis, [(i, i ^ k) for i in range(lax.axis_size(axis))])  48 us
    ppermute x24, starting transfers between devices, swap(): lax.ppermute(block, axis, [(i, i ^ k) for i in range(lax.axis_size(axis))])  26.9 us
    pallas_call x9, Pallas kernels, mix(): pl.pallas_call(functools.partial(mix_kernel, rows, count, [(*job[:3], [bl...  9.85 us
    pallas_call x8, Pallas kernels, put(): pl.pallas_call(functools.partial(put_kernel, entries, part, len(blocks)),...  6.68 us
    pallas_call x3, Pallas kernels, cut(): pl.pallas_call(functools.partial(cut_kernel, places, part), out_shape=[ou...  5.38 us
    pallas_call x1, Pallas kernels, gram(): pl.pallas_call(functools.partial(gram_kernel, rows, [len(x) for x in xs])...  2.28 us
  transfers between devices with their start and end apart: 24, of which 13 were waited for; matrix products, arithmetic and copies ran while one was open for 0% of the time, Pallas kernels for 23%

profile of v7, /device:TPU:0, one launch (start us, length us, event | category | flops | bytes accessed | tf_op | source)
XLA Modules:
  0.0 101.5 jit_solution(6456589561948043145)
XLA Ops:
  0.6 1.4 %cut.3 = (f32[1024,128]{1,0:T(8,128)S(1)}, f32[1024,128]{1,0:T(8,128)S(1)}, f32[1024,128]{1,0:T(8,128)S(1)}) custom-call(f32[4096,128]{1,0:T(8,128)} %bitcast.35), custom_call_target="tpu_custom_call" | custom-call | flops 1 | bytes 1 | tf_op jit(solution)/shard_map/cut/pallas_call | solution.py:286
  2.1 4.0 %collective-permute-start = (f32[1024,128]{1,0:T(8,128)S(1)}, f32[1024,128]{1,0:T(8,128)S(1)}, u32[]{:S(2)}, u32[]{:S(2)}) collective-permute-start(f32[1024,128]{1,0:T(8,128)S(1)} %get-tuple-element.67), channel_id=1, source_target_pairs={{0,24},{8,16},{16,8},{24,0},{1,25},{9,17},{17,9},{25,1},{2,26},{10... | collective-permute-start | bytes 1572872 | tf_op jit(solution)/shard_map/ppermute | solution.py:308
  6.7 2.9 %cut.4 = (f32[768,128]{1,0:T(8,128)}, f32[1280,128]{1,0:T(8,128)}, f32[768,128]{1,0:T(8,128)}, f32[1280,128]{1,0:T(8,128)}) custom-call(f32[4096,128]{1,0:T(8,128)} %bitcast.20), custom_call_target="tpu_custom_call" | custom-call | flops 1 | bytes 1 | tf_op jit(solution)/shard_map/cut/pallas_call | solution.py:286
  9.6 9.2 %collective-permute-done.refs_3_.refs_7_ = f32[1024,128]{1,0:T(8,128)S(1)} collective-permute-done((f32[1024,128]{1,0:T(8,128)S(1)}, f32[1024,128]{1,0:T(8,128)S(1)}, u32[]{:S(2)}, u32[]{:S(2)}) %collective-permute-start) | collective-permute-done | bytes 524320 | tf_op jit(solution)/shard_map/ppermute | solution.py:308
  18.8 2.0 %collective-permute-start.1 = (f32[768,128]{1,0:T(8,128)}, f32[768,128]{1,0:T(8,128)S(1)}, u32[]{:S(2)}, u32[]{:S(2)}) collective-permute-start(f32[768,128]{1,0:T(8,128)} %get-tuple-element.73), channel_id=1, source_target_pairs={{0,8},{8,0},{16,24},{24,16},{1,9},{9,1},{17,25},{25,17},{2,10},{10... | collective-permute-start | bytes 1179656 | tf_op jit(solution)/shard_map/ppermute | solution.py:308
  20.8 1.5 %collective-permute-start.2 = (f32[768,128]{1,0:T(8,128)}, f32[768,128]{1,0:T(8,128)S(1)}, u32[]{:S(2)}, u32[]{:S(2)}) collective-permute-start(f32[768,128]{1,0:T(8,128)} %get-tuple-element.74), channel_id=1, source_target_pairs={{0,16},{8,24},{16,0},{24,8},{1,17},{9,25},{17,1},{25,9},{2,18},{10... | collective-permute-start | bytes 1179656 | tf_op jit(solution)/shard_map/ppermute | solution.py:308
  22.3 1.1 %cut.5.refs_0_.refs_4_ = f32[1024,128]{1,0:T(8,128)S(1)} custom-call(f32[4096,128]{1,0:T(8,128)} %bitcast.36), custom_call_target="tpu_custom_call" | custom-call | flops 1 | bytes 1 | tf_op jit(solution)/shard_map/cut/pallas_call | solution.py:286
  23.4 7.2 %collective-permute-done.3.refs_1_.refs_5_ = f32[1024,128]{1,0:T(8,128)S(1)} collective-permute-done((f32[1024,128]{1,0:T(8,128)S(1)}, f32[1024,128]{1,0:T(8,128)S(1)}, u32[]{:S(2)}, u32[]{:S(2)}) %collective-permute-start.3) | collective-permute-done | bytes 524320 | tf_op jit(solution)/shard_map/ppermute | solution.py:308
  30.6 2.3 %gram.1.refs_0_ = f32[1,2,128]{2,1,0:T(2,128)S(1)} custom-call(f32[1024,128]{1,0:T(8,128)S(1)} %cut.5.refs_0_.refs_4_, f32[1024,128]{1,0:T(8,128)S(1)} %collective-permute-done.3.refs_1_.refs_5_, f32[1024,128]{1,0:T(8,128)S(1)} %collective-permute-done.4.refs_2_.refs_6_, f32[1024,128]{1,0:T(8,128)S(1)} %collective-permute-done.refs_3_.refs_7_), custom_call_target="tpu_custom_call" | custom-call | flops 1 | bytes 1 | tf_op jit(solution)/shard_map/gram/pallas_call | solution.py:85
  32.9 1.5 %collective-permute-start.7 = (f32[1,2,128]{2,1,0:T(2,128)S(1)}, f32[1,2,128]{2,1,0:T(2,128)S(1)}, u32[]{:S(2)}, u32[]{:S(2)}) collective-permute-start(f32[1,2,128]{2,1,0:T(2,128)S(1)} %gram.1.refs_0_), channel_id=1, source_target_pairs={{0,24},{8,16},{16,8},{24,0},{1,25},{9,17},{17,9},{25,1},{2,26},{10... | collective-permute-start | bytes 3080 | tf_op jit(solution)/shard_map/ppermute | solution.py:308
  34.4 1.5 %collective-permute-start.6 = (f32[1,2,128]{2,1,0:T(2,128)S(1)}, f32[1,2,128]{2,1,0:T(2,128)S(1)}, u32[]{:S(2)}, u32[]{:S(2)}) collective-permute-start(f32[1,2,128]{2,1,0:T(2,128)S(1)} %gram.1.refs_0_), channel_id=1, source_target_pairs={{0,16},{8,24},{16,0},{24,8},{1,17},{9,25},{17,1},{25,9},{2,18},{10... | collective-permute-start | bytes 3080 | tf_op jit(solution)/shard_map/ppermute | solution.py:308
  36.4 1.2 %collective-permute-done.7.refs_3_ = f32[1,2,128]{2,1,0:T(2,128)S(1)} collective-permute-done((f32[1,2,128]{2,1,0:T(2,128)S(1)}, f32[1,2,128]{2,1,0:T(2,128)S(1)}, u32[]{:S(2)}, u32[]{:S(2)}) %collective-permute-start.7) | collective-permute-done | bytes 1056 | tf_op jit(solution)/shard_map/ppermute | solution.py:308
  37.9 1.5 %collective-permute-done.5.refs_1_ = f32[1,2,128]{2,1,0:T(2,128)S(1)} collective-permute-done((f32[1,2,128]{2,1,0:T(2,128)S(1)}, f32[1,2,128]{2,1,0:T(2,128)S(1)}, u32[]{:S(2)}, u32[]{:S(2)}) %collective-permute-start.5) | collective-permute-done | bytes 1056 | tf_op jit(solution)/shard_map/ppermute | solution.py:308
  41.6 1.1 %collective-permute-start.9 = (f32[1,2,128]{2,1,0:T(2,128)S(1)}, f32[1,2,128]{2,1,0:T(2,128)S(1)}, u32[]{:S(2)}, u32[]{:S(2)}) collective-permute-start(f32[1,2,128]{2,1,0:T(2,128)S(1)} %add.2.refs_0_), channel_id=1, source_target_pairs={{0,2},{1,3},{2,0},{3,1},{4,6},{5,7},{6,4},{7,5},{8,10},{9,11},{10,... | collective-permute-start | bytes 3080 | tf_op jit(solution)/shard_map/ppermute | solution.py:308
  42.8 1.1 %collective-permute-done.10.refs_3_ = f32[1,2,128]{2,1,0:T(2,128)S(1)} collective-permute-done((f32[1,2,128]{2,1,0:T(2,128)S(1)}, f32[1,2,128]{2,1,0:T(2,128)S(1)}, u32[]{:S(2)}, u32[]{:S(2)}) %collective-permute-start.10) | collective-permute-done | bytes 1056 | tf_op jit(solution)/shard_map/ppermute | solution.py:308
  44.0 1.2 %collective-permute-done.9.refs_2_ = f32[1,2,128]{2,1,0:T(2,128)S(1)} collective-permute-done((f32[1,2,128]{2,1,0:T(2,128)S(1)}, f32[1,2,128]{2,1,0:T(2,128)S(1)}, u32[]{:S(2)}, u32[]{:S(2)}) %collective-permute-start.9) | collective-permute-done | bytes 1056 | tf_op jit(solution)/shard_map/ppermute | solution.py:308
  45.1 2.7 %collective-permute-start.11 = (f32[1,2,128]{2,1,0:T(2,128)S(1)}, f32[1,2,128]{2,1,0:T(2,128)S(1)}, u32[]{:S(2)}, u32[]{:S(2)}) collective-permute-start(f32[1,2,128]{2,1,0:T(2,128)S(1)} %add.3.refs_0_), channel_id=1, source_target_pairs={{0,4},{1,5},{2,6},{3,7},{4,0},{5,1},{6,2},{7,3},{8,12},{9,13},{10,... | collective-permute-start | bytes 3080 | tf_op jit(solution)/shard_map/ppermute | solution.py:308
  48.5 1.2 %collective-permute-done.11.refs_1_ = f32[1,2,128]{2,1,0:T(2,128)S(1)} collective-permute-done((f32[1,2,128]{2,1,0:T(2,128)S(1)}, f32[1,2,128]{2,1,0:T(2,128)S(1)}, u32[]{:S(2)}, u32[]{:S(2)}) %collective-permute-start.11) | collective-permute-done | bytes 1056 | tf_op jit(solution)/shard_map/ppermute | solution.py:308
  53.1 1.6 %collective-permute-start.20 = (f32[512,128]{1,0:T(8,128)S(1)}, f32[512,128]{1,0:T(8,128)S(1)}, u32[]{:S(2)}, u32[]{:S(2)}) collective-permute-start(f32[512,128]{1,0:T(8,128)S(1)} %mix.12), channel_id=1, source_target_pairs={{0,8},{8,0},{16,24},{24,16},{1,9},{9,1},{17,25},{25,17},{2,10},{10... | collective-permute-start | bytes 786440 | tf_op jit(solution)/shard_map/ppermute | solution.py:308
  55.2 1.5 %collective-permute-start.14 = (f32[1024,128]{1,0:T(8,128)S(1)}, f32[1024,128]{1,0:T(8,128)S(1)}, u32[]{:S(2)}, u32[]{:S(2)}) collective-permute-start(f32[1024,128]{1,0:T(8,128)S(1)} %mix.9), channel_id=1, source_target_pairs={{0,8},{8,0},{16,24},{24,16},{1,9},{9,1},{17,25},{25,17},{2,10},{10... | collective-permute-start | bytes 1572872 | tf_op jit(solution)/shard_map/ppermute | solution.py:308
  56.6 1.3 %mix.13 = f32[1024,128]{1,0:T(8,128)S(1)} custom-call(f32[256,128]{1,0:T(8,128)S(1)} %get-tuple-element.105.drive_ref, f32[256,128]{1,0:T(8,128)S(1)} %get-tuple-element.106.repel_ref, f32[4096,128]{1,0:T(8,128)} %bitcast.21, f32[768,128]{1,0:T(8,128)S(1)} %collective-permute-done.1.refs_1_.refs_9_, f32[4096,128]{1,0:T(8,128)} %bitcast.22, ...), custom_call_target="tpu_custom_call" | custom-call | flops 1 | bytes 1 | tf_op jit(solution)/shard_map/mix/pallas_call | solution.py:211
  58.0 1.4 %collective-permute-start.16 = (f32[1024,128]{1,0:T(8,128)S(1)}, f32[1024,128]{1,0:T(8,128)S(1)}, u32[]{:S(2)}, u32[]{:S(2)}) collective-permute-start(f32[1024,128]{1,0:T(8,128)S(1)} %mix.13), channel_id=1, source_target_pairs={{0,16},{8,24},{16,0},{24,8},{1,17},{9,25},{17,1},{25,9},{2,18},{10... | collective-permute-start | bytes 1572872 | tf_op jit(solution)/shard_map/ppermute | solution.py:308
  59.4 1.3 %mix.14 = f32[1024,128]{1,0:T(8,128)S(1)} custom-call(f32[256,128]{1,0:T(8,128)S(1)} %get-tuple-element.105.drive_ref, f32[256,128]{1,0:T(8,128)S(1)} %get-tuple-element.106.repel_ref, f32[4096,128]{1,0:T(8,128)} %bitcast.23, f32[768,128]{1,0:T(8,128)S(1)} %collective-permute-done.2.refs_1_.refs_13_, f32[4096,128]{1,0:T(8,128)} %bitcast.24, ...), custom_call_target="tpu_custom_call" | custom-call | flops 1 | bytes 1 | tf_op jit(solution)/shard_map/mix/pallas_call | solution.py:211
  60.7 1.7 %collective-permute-done.20 = f32[512,128]{1,0:T(8,128)S(1)} collective-permute-done((f32[512,128]{1,0:T(8,128)S(1)}, f32[512,128]{1,0:T(8,128)S(1)}, u32[]{:S(2)}, u32[]{:S(2)}) %collective-permute-start.20) | collective-permute-done | bytes 262176 | tf_op jit(solution)/shard_map/ppermute | solution.py:308
  62.4 1.5 %collective-permute-start.17 = (f32[1024,128]{1,0:T(8,128)S(1)}, f32[1024,128]{1,0:T(8,128)S(1)}, u32[]{:S(2)}, u32[]{:S(2)}) collective-permute-start(f32[1024,128]{1,0:T(8,128)S(1)} %mix.14), channel_id=1, source_target_pairs={{0,8},{8,0},{16,24},{24,16},{1,9},{9,1},{17,25},{25,17},{2,10},{10... | collective-permute-start | bytes 1572872 | tf_op jit(solution)/shard_map/ppermute | solution.py:308
  63.9 1.3 %mix.15 = f32[1024,128]{1,0:T(8,128)S(1)} custom-call(f32[256,128]{1,0:T(8,128)S(1)} %get-tuple-element.105.drive_ref, f32[256,128]{1,0:T(8,128)S(1)} %get-tuple-element.106.repel_ref, f32[4096,128]{1,0:T(8,128)} %bitcast.25, f32[1280,128]{1,0:T(8,128)S(1)} %collective-permute-done.12.refs_3_.refs_1_.refs_11_.refs_17_), custom_call_target="tpu_custom_call" | custom-call | flops 1 | bytes 1 | tf_op jit(solution)/shard_map/mix/pallas_call | solution.py:211
  65.3 9.3 %collective-permute-done.22 = f32[512,128]{1,0:T(8,128)S(1)} collective-permute-done((f32[512,128]{1,0:T(8,128)S(1)}, f32[512,128]{1,0:T(8,128)S(1)}, u32[]{:S(2)}, u32[]{:S(2)}) %collective-permute-start.22) | collective-permute-done | bytes 262176 | tf_op jit(solution)/shard_map/ppermute | solution.py:308
  75.5 1.3 %mix.16 = f32[1024,128]{1,0:T(8,128)S(1)} custom-call(f32[256,128]{1,0:T(8,128)S(1)} %get-tuple-element.105.drive_ref, f32[256,128]{1,0:T(8,128)S(1)} %get-tuple-element.106.repel_ref, f32[4096,128]{1,0:T(8,128)} %bitcast.26, f32[1280,128]{1,0:T(8,128)S(1)} %collective-permute-done.13.refs_3_.refs_1_.refs_15_.refs_19_), custom_call_target="tpu_custom_call" | custom-call | flops 1 | bytes 1 | tf_op jit(solution)/shard_map/mix/pallas_call | solution.py:211
  78.1 7.7 %collective-permute-done.16.refs_1_ = f32[1024,128]{1,0:T(8,128)S(1)} collective-permute-done((f32[1024,128]{1,0:T(8,128)S(1)}, f32[1024,128]{1,0:T(8,128)S(1)}, u32[]{:S(2)}, u32[]{:S(2)}) %collective-permute-start.16) | collective-permute-done | bytes 524320 | tf_op jit(solution)/shard_map/ppermute | solution.py:308
  85.8 2.7 %mix.17.refs_0_ = f32[5120,128]{1,0:T(8,128)S(1)} custom-call(f32[256,128]{1,0:T(8,128)S(1)} %get-tuple-element.105.drive_ref, f32[256,128]{1,0:T(8,128)S(1)} %get-tuple-element.106.repel_ref, f32[1024,128]{1,0:T(8,128)S(1)} %cut.5.refs_0_.refs_4_, f32[1024,128]{1,0:T(8,128)S(1)} %collective-permute-done.3.refs_1_.refs_5_, ...), custom_call_target="tpu_custom_call" | custom-call | flops 1 | bytes 1 | tf_op jit(solution)/shard_map/mix/pallas_call | solution.py:211
  92.7 4.3 %collective-permute-done.18.refs_1_ = f32[1024,128]{1,0:T(8,128)S(1)} collective-permute-done((f32[1024,128]{1,0:T(8,128)S(1)}, f32[1024,128]{1,0:T(8,128)S(1)}, u32[]{:S(2)}, u32[]{:S(2)}) %collective-permute-start.18) | collective-permute-done | bytes 524320 | tf_op jit(solution)/shard_map/ppermute | solution.py:308
  98.8 1.9 %collective-permute-done.21.refs_0_ = f32[512,128]{1,0:T(8,128)S(1)} collective-permute-done((f32[512,128]{1,0:T(8,128)S(1)}, f32[512,128]{1,0:T(8,128)S(1)}, u32[]{:S(2)}, u32[]{:S(2)}) %collective-permute-start.21) | collective-permute-done | bytes 262176 | tf_op jit(solution)/shard_map/ppermute | solution.py:308
  (44 shorter events, 16.6 us)
Async XLA Ops:
  2.1 16.8 %collective-permute-start = (f32[1024,128]{1,0:T(8,128)S(1)}, f32[1024,128]{1,0:T(8,128)S(1)}, u32[]{:S(2)}, u32[]{:S(2)}) collective-permute-start(f32[1024,128]{1,0:T(8,128)S(1)} %get-tuple-element.67), channel_id=1, source_target_pairs={{0,24},{8,16},{16,8},{24,0},{1,25},{9,17},{17,9},{25,1},{2,26},{10... | collective-permute-start | bytes 1572872 | tf_op jit(solution)/shard_map/ppermute | solution.py:308
  6.0 24.6 %collective-permute-start.3 = (f32[1024,128]{1,0:T(8,128)S(1)}, f32[1024,128]{1,0:T(8,128)S(1)}, u32[]{:S(2)}, u32[]{:S(2)}) collective-permute-start(f32[1024,128]{1,0:T(8,128)S(1)} %get-tuple-element.78), channel_id=1, source_target_pairs={{0,8},{8,0},{16,24},{24,16},{1,9},{9,1},{17,25},{25,17},{2,10},{10... | collective-permute-start | bytes 1572872 | tf_op jit(solution)/shard_map/ppermute | solution.py:308
  6.6 24.1 %collective-permute-start.4 = (f32[1024,128]{1,0:T(8,128)S(1)}, f32[1024,128]{1,0:T(8,128)S(1)}, u32[]{:S(2)}, u32[]{:S(2)}) collective-permute-start(f32[1024,128]{1,0:T(8,128)S(1)} %get-tuple-element.79), channel_id=1, source_target_pairs={{0,16},{8,24},{16,0},{24,8},{1,17},{9,25},{17,1},{25,9},{2,18},{10... | collective-permute-start | bytes 1572872 | tf_op jit(solution)/shard_map/ppermute | solution.py:308
  18.8 20.7 %copy-start.1 = (f32[1280,128]{1,0:T(8,128)S(1)}, f32[1280,128]{1,0:T(8,128)}, u32[]{:S(2)}) copy-start(f32[1280,128]{1,0:T(8,128)} %get-tuple-element.96) | copy-start | bytes 1966084
  18.8 21.3 %copy-start = (f32[1280,128]{1,0:T(8,128)S(1)}, f32[1280,128]{1,0:T(8,128)}, u32[]{:S(2)}) copy-start(f32[1280,128]{1,0:T(8,128)} %get-tuple-element.100) | copy-start | bytes 1966084
  18.8 20.6 %collective-permute-start.1 = (f32[768,128]{1,0:T(8,128)}, f32[768,128]{1,0:T(8,128)S(1)}, u32[]{:S(2)}, u32[]{:S(2)}) collective-permute-start(f32[768,128]{1,0:T(8,128)} %get-tuple-element.73), channel_id=1, source_target_pairs={{0,8},{8,0},{16,24},{24,16},{1,9},{9,1},{17,25},{25,17},{2,10},{10... | collective-permute-start | bytes 1179656 | tf_op jit(solution)/shard_map/ppermute | solution.py:308
  20.8 18.6 %collective-permute-start.2 = (f32[768,128]{1,0:T(8,128)}, f32[768,128]{1,0:T(8,128)S(1)}, u32[]{:S(2)}, u32[]{:S(2)}) collective-permute-start(f32[768,128]{1,0:T(8,128)} %get-tuple-element.74), channel_id=1, source_target_pairs={{0,16},{8,24},{16,0},{24,8},{1,17},{9,25},{17,1},{25,9},{2,18},{10... | collective-permute-start | bytes 1179656 | tf_op jit(solution)/shard_map/ppermute | solution.py:308
  32.9 4.8 %collective-permute-start.7 = (f32[1,2,128]{2,1,0:T(2,128)S(1)}, f32[1,2,128]{2,1,0:T(2,128)S(1)}, u32[]{:S(2)}, u32[]{:S(2)}) collective-permute-start(f32[1,2,128]{2,1,0:T(2,128)S(1)} %gram.1.refs_0_), channel_id=1, source_target_pairs={{0,24},{8,16},{16,8},{24,0},{1,25},{9,17},{17,9},{25,1},{2,26},{10... | collective-permute-start | bytes 3080 | tf_op jit(solution)/shard_map/ppermute | solution.py:308
  34.4 3.6 %collective-permute-start.6 = (f32[1,2,128]{2,1,0:T(2,128)S(1)}, f32[1,2,128]{2,1,0:T(2,128)S(1)}, u32[]{:S(2)}, u32[]{:S(2)}) collective-permute-start(f32[1,2,128]{2,1,0:T(2,128)S(1)} %gram.1.refs_0_), channel_id=1, source_target_pairs={{0,16},{8,24},{16,0},{24,8},{1,17},{9,25},{17,1},{25,9},{2,18},{10... | collective-permute-start | bytes 3080 | tf_op jit(solution)/shard_map/ppermute | solution.py:308
  35.9 3.6 %collective-permute-start.5 = (f32[1,2,128]{2,1,0:T(2,128)S(1)}, f32[1,2,128]{2,1,0:T(2,128)S(1)}, u32[]{:S(2)}, u32[]{:S(2)}) collective-permute-start(f32[1,2,128]{2,1,0:T(2,128)S(1)} %gram.1.refs_0_), channel_id=1, source_target_pairs={{0,8},{8,0},{16,24},{24,16},{1,9},{9,1},{17,25},{25,17},{2,10},{10... | collective-permute-start | bytes 3080 | tf_op jit(solution)/shard_map/ppermute | solution.py:308
  39.5 15.7 %collective-permute-start.12 = (f32[1280,128]{1,0:T(8,128)S(1)}, f32[1280,128]{1,0:T(8,128)S(1)}, u32[]{:S(2)}, u32[]{:S(2)}) collective-permute-start(f32[1280,128]{1,0:T(8,128)S(1)} %copy-done.1), channel_id=1, source_target_pairs={{0,8},{8,0},{16,24},{24,16},{1,9},{9,1},{17,25},{25,17},{2,10},{10... | collective-permute-start | bytes 1966088 | tf_op jit(solution)/shard_map/ppermute | solution.py:308
  40.1 17.9 %collective-permute-start.13 = (f32[1280,128]{1,0:T(8,128)S(1)}, f32[1280,128]{1,0:T(8,128)S(1)}, u32[]{:S(2)}, u32[]{:S(2)}) collective-permute-start(f32[1280,128]{1,0:T(8,128)S(1)} %copy-done), channel_id=1, source_target_pairs={{0,16},{8,24},{16,0},{24,8},{1,17},{9,25},{17,1},{25,9},{2,18},{10... | collective-permute-start | bytes 1966088 | tf_op jit(solution)/shard_map/ppermute | solution.py:308
  41.0 3.0 %collective-permute-start.10 = (f32[1,2,128]{2,1,0:T(2,128)S(1)}, f32[1,2,128]{2,1,0:T(2,128)S(1)}, u32[]{:S(2)}, u32[]{:S(2)}) collective-permute-start(f32[1,2,128]{2,1,0:T(2,128)S(1)} %add.2.refs_0_), channel_id=1, source_target_pairs={{0,3},{1,2},{2,1},{3,0},{4,7},{5,6},{6,5},{7,4},{8,11},{9,10},{10,... | collective-permute-start | bytes 3080 | tf_op jit(solution)/shard_map/ppermute | solution.py:308
  41.6 3.6 %collective-permute-start.9 = (f32[1,2,128]{2,1,0:T(2,128)S(1)}, f32[1,2,128]{2,1,0:T(2,128)S(1)}, u32[]{:S(2)}, u32[]{:S(2)}) collective-permute-start(f32[1,2,128]{2,1,0:T(2,128)S(1)} %add.2.refs_0_), channel_id=1, source_target_pairs={{0,2},{1,3},{2,0},{3,1},{4,6},{5,7},{6,4},{7,5},{8,10},{9,11},{10,... | collective-permute-start | bytes 3080 | tf_op jit(solution)/shard_map/ppermute | solution.py:308
  42.6 2.5 %collective-permute-start.8 = (f32[1,2,128]{2,1,0:T(2,128)S(1)}, f32[1,2,128]{2,1,0:T(2,128)S(1)}, u32[]{:S(2)}, u32[]{:S(2)}) collective-permute-start(f32[1,2,128]{2,1,0:T(2,128)S(1)} %add.2.refs_0_), channel_id=1, source_target_pairs={{0,1},{1,0},{2,3},{3,2},{4,5},{5,4},{6,7},{7,6},{8,9},{9,8},{10,11... | collective-permute-start | bytes 3080 | tf_op jit(solution)/shard_map/ppermute | solution.py:308
  45.1 4.5 %collective-permute-start.11 = (f32[1,2,128]{2,1,0:T(2,128)S(1)}, f32[1,2,128]{2,1,0:T(2,128)S(1)}, u32[]{:S(2)}, u32[]{:S(2)}) collective-permute-start(f32[1,2,128]{2,1,0:T(2,128)S(1)} %add.3.refs_0_), channel_id=1, source_target_pairs={{0,4},{1,5},{2,6},{3,7},{4,0},{5,1},{6,2},{7,3},{8,12},{9,13},{10,... | collective-permute-start | bytes 3080 | tf_op jit(solution)/shard_map/ppermute | solution.py:308
  51.8 25.0 %collective-permute-start.15 = (f32[1024,128]{1,0:T(8,128)S(1)}, f32[1024,128]{1,0:T(8,128)S(1)}, u32[]{:S(2)}, u32[]{:S(2)}) collective-permute-start(f32[1024,128]{1,0:T(8,128)S(1)} %mix.10), channel_id=1, source_target_pairs={{0,16},{8,24},{16,0},{24,8},{1,17},{9,25},{17,1},{25,9},{2,18},{10... | collective-permute-start | bytes 1572872 | tf_op jit(solution)/shard_map/ppermute | solution.py:308
  53.1 9.3 %collective-permute-start.20 = (f32[512,128]{1,0:T(8,128)S(1)}, f32[512,128]{1,0:T(8,128)S(1)}, u32[]{:S(2)}, u32[]{:S(2)}) collective-permute-start(f32[512,128]{1,0:T(8,128)S(1)} %mix.12), channel_id=1, source_target_pairs={{0,8},{8,0},{16,24},{24,16},{1,9},{9,1},{17,25},{25,17},{2,10},{10... | collective-permute-start | bytes 786440 | tf_op jit(solution)/shard_map/ppermute | solution.py:308
  54.7 19.9 %collective-permute-start.22 = (f32[512,128]{1,0:T(8,128)S(1)}, f32[512,128]{1,0:T(8,128)S(1)}, u32[]{:S(2)}, u32[]{:S(2)}) collective-permute-start(f32[512,128]{1,0:T(8,128)S(1)} %mix.11), channel_id=1, source_target_pairs={{0,16},{8,24},{16,0},{24,8},{1,17},{9,25},{17,1},{25,9},{2,18},{10... | collective-permute-start | bytes 786440 | tf_op jit(solution)/shard_map/ppermute | solution.py:308
  55.2 22.5 %collective-permute-start.14 = (f32[1024,128]{1,0:T(8,128)S(1)}, f32[1024,128]{1,0:T(8,128)S(1)}, u32[]{:S(2)}, u32[]{:S(2)}) collective-permute-start(f32[1024,128]{1,0:T(8,128)S(1)} %mix.9), channel_id=1, source_target_pairs={{0,8},{8,0},{16,24},{24,16},{1,9},{9,1},{17,25},{25,17},{2,10},{10... | collective-permute-start | bytes 1572872 | tf_op jit(solution)/shard_map/ppermute | solution.py:308
  58.0 27.9 %collective-permute-start.16 = (f32[1024,128]{1,0:T(8,128)S(1)}, f32[1024,128]{1,0:T(8,128)S(1)}, u32[]{:S(2)}, u32[]{:S(2)}) collective-permute-start(f32[1024,128]{1,0:T(8,128)S(1)} %mix.13), channel_id=1, source_target_pairs={{0,16},{8,24},{16,0},{24,8},{1,17},{9,25},{17,1},{25,9},{2,18},{10... | collective-permute-start | bytes 1572872 | tf_op jit(solution)/shard_map/ppermute | solution.py:308
  62.4 29.4 %collective-permute-start.17 = (f32[1024,128]{1,0:T(8,128)S(1)}, f32[1024,128]{1,0:T(8,128)S(1)}, u32[]{:S(2)}, u32[]{:S(2)}) collective-permute-start(f32[1024,128]{1,0:T(8,128)S(1)} %mix.14), channel_id=1, source_target_pairs={{0,8},{8,0},{16,24},{24,16},{1,9},{9,1},{17,25},{25,17},{2,10},{10... | collective-permute-start | bytes 1572872 | tf_op jit(solution)/shard_map/ppermute | solution.py:308
  74.6 22.5 %collective-permute-start.18 = (f32[1024,128]{1,0:T(8,128)S(1)}, f32[1024,128]{1,0:T(8,128)S(1)}, u32[]{:S(2)}, u32[]{:S(2)}) collective-permute-start(f32[1024,128]{1,0:T(8,128)S(1)} %mix.15), channel_id=1, source_target_pairs={{0,16},{8,24},{16,0},{24,8},{1,17},{9,25},{17,1},{25,9},{2,18},{10... | collective-permute-start | bytes 1572872 | tf_op jit(solution)/shard_map/ppermute | solution.py:308
  76.8 21.1 %collective-permute-start.19 = (f32[1024,128]{1,0:T(8,128)S(1)}, f32[1024,128]{1,0:T(8,128)S(1)}, u32[]{:S(2)}, u32[]{:S(2)}) collective-permute-start(f32[1024,128]{1,0:T(8,128)S(1)} %mix.16), channel_id=1, source_target_pairs={{0,8},{8,0},{16,24},{24,16},{1,9},{9,1},{17,25},{25,17},{2,10},{10... | collective-permute-start | bytes 1572872 | tf_op jit(solution)/shard_map/ppermute | solution.py:308
  77.7 23.0 %collective-permute-start.21 = (f32[512,128]{1,0:T(8,128)S(1)}, f32[512,128]{1,0:T(8,128)S(1)}, u32[]{:S(2)}, u32[]{:S(2)}) collective-permute-start(f32[512,128]{1,0:T(8,128)S(1)} %collective-permute-done.20), channel_id=1, source_target_pairs={{0,16},{8,24},{16,0},{24,8},{1,17},{9,25},{17,1},{25,9},{2,18},{10... | collective-permute-start | bytes 786440 | tf_op jit(solution)/shard_map/ppermute | solution.py:308
  85.8 14.9 %collective-permute-start.23 = (f32[512,128]{1,0:T(8,128)S(1)}, f32[512,128]{1,0:T(8,128)S(1)}, u32[]{:S(2)}, u32[]{:S(2)}) collective-permute-start(f32[512,128]{1,0:T(8,128)S(1)} %collective-permute-done.22), channel_id=1, source_target_pairs={{0,8},{8,0},{16,24},{24,16},{1,9},{9,1},{17,25},{25,17},{2,10},{10... | collective-permute-start | bytes 786440 | tf_op jit(solution)/shard_map/ppermute | solution.py:308

commit v8 on v7

--- a/solution.py
+++ b/solution.py
@@ -318,7 +318,7 @@
     direct = [k for k in everyone[1:] if k in lows or k in highs]
     distant = [k for k in everyone[1:] if k not in direct]
     size, step = x.shape[0], SUB * rows
-    first = max(1, half // step * 3 // 8) * step
+    first = max(1, half // step * 7 // 16) * step
     split = part // step // 2 * step
     halves = [(0, split), (split, part - split)]
 
@@ -329,7 +329,7 @@
     def pieces(k):
         return halves if k in distant else [(0, part)]
 
-    order = distant + direct
+    order = direct + distant
     sent = cut(x, [(k, 0, part) for k in order], part, True)
     s, sent = lax.optimization_barrier((s, sent))
     bounds = [(n * half + row, length) for n in (0, 1) for row, length in ((0, first), (first, half - first))]

time: 102 us -> 102 us (level)
  transfers between devices with their start and end apart: 24 -> 24, of which waited for: 13 -> 15; matrix products, arithmetic and copies ran while one was open for 0% -> 0% of each run, Pallas kernels for 23% -> 23%
where the time goes in v8:
time: 102 us
  waiting for transfers between devices  47.6 us (47%)
  starting transfers between devices  27.4 us (27%)
  Pallas kernels  25.3 us (25%)
  between operations  1.49 us (1%)
    ppermute x24, waiting for transfers between devices, swap(): lax.ppermute(block, axis, [(i, i ^ k) for i in range(lax.axis_size(axis))])  47.6 us
    ppermute x24, starting transfers between devices, swap(): lax.ppermute(block, axis, [(i, i ^ k) for i in range(lax.axis_size(axis))])  27.4 us
    pallas_call x9, Pallas kernels, mix(): pl.pallas_call(functools.partial(mix_kernel, rows, count, [(*job[:3], [bl...  10 us
    pallas_call x8, Pallas kernels, put(): pl.pallas_call(functools.partial(put_kernel, entries, part, len(blocks)),...  6.67 us
    pallas_call x3, Pallas kernels, cut(): pl.pallas_call(functools.partial(cut_kernel, places, part), out_shape=[ou...  5.38 us
    pallas_call x1, Pallas kernels, gram(): pl.pallas_call(functools.partial(gram_kernel, rows, [len(x) for x in xs])...  2.28 us
  transfers between devices with their start and end apart: 24, of which 15 were waited for; matrix products, arithmetic and copies ran while one was open for 0% of the time, Pallas kernels for 23%

profile of v8, /device:TPU:0, one launch (start us, length us, event | category | flops | bytes accessed | tf_op | source)
XLA Modules:
  0.0 101.7 jit_solution(6014439346686951133)
XLA Ops:
  0.6 1.4 %cut.3 = (f32[1024,128]{1,0:T(8,128)S(1)}, f32[1024,128]{1,0:T(8,128)S(1)}, f32[1024,128]{1,0:T(8,128)S(1)}) custom-call(f32[4096,128]{1,0:T(8,128)} %bitcast.35), custom_call_target="tpu_custom_call" | custom-call | flops 1 | bytes 1 | tf_op jit(solution)/shard_map/cut/pallas_call | solution.py:286
  2.1 3.0 %collective-permute-start = (f32[1024,128]{1,0:T(8,128)S(1)}, f32[1024,128]{1,0:T(8,128)S(1)}, u32[]{:S(2)}, u32[]{:S(2)}) collective-permute-start(f32[1024,128]{1,0:T(8,128)S(1)} %get-tuple-element.67), channel_id=1, source_target_pairs={{0,8},{8,0},{16,24},{24,16},{1,9},{9,1},{17,25},{25,17},{2,10},{10... | collective-permute-start | bytes 1572872 | tf_op jit(solution)/shard_map/ppermute | solution.py:308
  5.1 1.5 %collective-permute-start.3 = (f32[1024,128]{1,0:T(8,128)S(1)}, f32[1024,128]{1,0:T(8,128)S(1)}, u32[]{:S(2)}, u32[]{:S(2)}) collective-permute-start(f32[1024,128]{1,0:T(8,128)S(1)} %get-tuple-element.79), channel_id=1, source_target_pairs={{0,16},{8,24},{16,0},{24,8},{1,17},{9,25},{17,1},{25,9},{2,18},{10... | collective-permute-start | bytes 1572872 | tf_op jit(solution)/shard_map/ppermute | solution.py:308
  6.6 2.9 %cut.4 = (f32[896,128]{1,0:T(8,128)}, f32[1152,128]{1,0:T(8,128)}, f32[896,128]{1,0:T(8,128)}, f32[1152,128]{1,0:T(8,128)}) custom-call(f32[4096,128]{1,0:T(8,128)} %bitcast.20), custom_call_target="tpu_custom_call" | custom-call | flops 1 | bytes 1 | tf_op jit(solution)/shard_map/cut/pallas_call | solution.py:286
  9.5 8.3 %collective-permute-done.refs_1_.refs_5_ = f32[1024,128]{1,0:T(8,128)S(1)} collective-permute-done((f32[1024,128]{1,0:T(8,128)S(1)}, f32[1024,128]{1,0:T(8,128)S(1)}, u32[]{:S(2)}, u32[]{:S(2)}) %collective-permute-start) | collective-permute-done | bytes 524320 | tf_op jit(solution)/shard_map/ppermute | solution.py:308
  17.8 2.1 %collective-permute-start.1 = (f32[896,128]{1,0:T(8,128)}, f32[896,128]{1,0:T(8,128)S(1)}, u32[]{:S(2)}, u32[]{:S(2)}) collective-permute-start(f32[896,128]{1,0:T(8,128)} %get-tuple-element.73), channel_id=1, source_target_pairs={{0,8},{8,0},{16,24},{24,16},{1,9},{9,1},{17,25},{25,17},{2,10},{10... | collective-permute-start | bytes 1376264 | tf_op jit(solution)/shard_map/ppermute | solution.py:308
  19.9 1.5 %collective-permute-start.2 = (f32[896,128]{1,0:T(8,128)}, f32[896,128]{1,0:T(8,128)S(1)}, u32[]{:S(2)}, u32[]{:S(2)}) collective-permute-start(f32[896,128]{1,0:T(8,128)} %get-tuple-element.74), channel_id=1, source_target_pairs={{0,16},{8,24},{16,0},{24,8},{1,17},{9,25},{17,1},{25,9},{2,18},{10... | collective-permute-start | bytes 1376264 | tf_op jit(solution)/shard_map/ppermute | solution.py:308
  21.4 1.1 %cut.5.refs_0_.refs_4_ = f32[1024,128]{1,0:T(8,128)S(1)} custom-call(f32[4096,128]{1,0:T(8,128)} %bitcast.36), custom_call_target="tpu_custom_call" | custom-call | flops 1 | bytes 1 | tf_op jit(solution)/shard_map/cut/pallas_call | solution.py:286
  22.5 7.6 %collective-permute-done.3.refs_2_.refs_6_ = f32[1024,128]{1,0:T(8,128)S(1)} collective-permute-done((f32[1024,128]{1,0:T(8,128)S(1)}, f32[1024,128]{1,0:T(8,128)S(1)}, u32[]{:S(2)}, u32[]{:S(2)}) %collective-permute-start.3) | collective-permute-done | bytes 524320 | tf_op jit(solution)/shard_map/ppermute | solution.py:308
  30.6 2.3 %gram.1.refs_0_ = f32[1,2,128]{2,1,0:T(2,128)S(1)} custom-call(f32[1024,128]{1,0:T(8,128)S(1)} %cut.5.refs_0_.refs_4_, f32[1024,128]{1,0:T(8,128)S(1)} %collective-permute-done.refs_1_.refs_5_, f32[1024,128]{1,0:T(8,128)S(1)} %collective-permute-done.3.refs_2_.refs_6_, f32[1024,128]{1,0:T(8,128)S(1)} %collective-permute-done.4.refs_3_.refs_7_), custom_call_target="tpu_custom_call" | custom-call | flops 1 | bytes 1 | tf_op jit(solution)/shard_map/gram/pallas_call | solution.py:85
  32.9 1.5 %collective-permute-start.7 = (f32[1,2,128]{2,1,0:T(2,128)S(1)}, f32[1,2,128]{2,1,0:T(2,128)S(1)}, u32[]{:S(2)}, u32[]{:S(2)}) collective-permute-start(f32[1,2,128]{2,1,0:T(2,128)S(1)} %gram.1.refs_0_), channel_id=1, source_target_pairs={{0,24},{8,16},{16,8},{24,0},{1,25},{9,17},{17,9},{25,1},{2,26},{10... | collective-permute-start | bytes 3080 | tf_op jit(solution)/shard_map/ppermute | solution.py:308
  34.4 1.5 %collective-permute-start.6 = (f32[1,2,128]{2,1,0:T(2,128)S(1)}, f32[1,2,128]{2,1,0:T(2,128)S(1)}, u32[]{:S(2)}, u32[]{:S(2)}) collective-permute-start(f32[1,2,128]{2,1,0:T(2,128)S(1)} %gram.1.refs_0_), channel_id=1, source_target_pairs={{0,16},{8,24},{16,0},{24,8},{1,17},{9,25},{17,1},{25,9},{2,18},{10... | collective-permute-start | bytes 3080 | tf_op jit(solution)/shard_map/ppermute | solution.py:308
  36.4 2.9 %collective-permute-done.7.refs_3_ = f32[1,2,128]{2,1,0:T(2,128)S(1)} collective-permute-done((f32[1,2,128]{2,1,0:T(2,128)S(1)}, f32[1,2,128]{2,1,0:T(2,128)S(1)}, u32[]{:S(2)}, u32[]{:S(2)}) %collective-permute-start.7) | collective-permute-done | bytes 1056 | tf_op jit(solution)/shard_map/ppermute | solution.py:308
  39.6 1.3 %collective-permute-start.12 = (f32[1152,128]{1,0:T(8,128)S(1)}, f32[1152,128]{1,0:T(8,128)S(1)}, u32[]{:S(2)}, u32[]{:S(2)}) collective-permute-start(f32[1152,128]{1,0:T(8,128)S(1)} %copy-done.1), channel_id=1, source_target_pairs={{0,8},{8,0},{16,24},{24,16},{1,9},{9,1},{17,25},{25,17},{2,10},{10... | collective-permute-start | bytes 1769480 | tf_op jit(solution)/shard_map/ppermute | solution.py:308
  40.9 1.1 %collective-permute-start.13 = (f32[1152,128]{1,0:T(8,128)S(1)}, f32[1152,128]{1,0:T(8,128)S(1)}, u32[]{:S(2)}, u32[]{:S(2)}) collective-permute-start(f32[1152,128]{1,0:T(8,128)S(1)} %copy-done), channel_id=1, source_target_pairs={{0,16},{8,24},{16,0},{24,8},{1,17},{9,25},{17,1},{25,9},{2,18},{10... | collective-permute-start | bytes 1769480 | tf_op jit(solution)/shard_map/ppermute | solution.py:308
  42.3 1.1 %collective-permute-start.9 = (f32[1,2,128]{2,1,0:T(2,128)S(1)}, f32[1,2,128]{2,1,0:T(2,128)S(1)}, u32[]{:S(2)}, u32[]{:S(2)}) collective-permute-start(f32[1,2,128]{2,1,0:T(2,128)S(1)} %add.2.refs_0_), channel_id=1, source_target_pairs={{0,2},{1,3},{2,0},{3,1},{4,6},{5,7},{6,4},{7,5},{8,10},{9,11},{10,... | collective-permute-start | bytes 3080 | tf_op jit(solution)/shard_map/ppermute | solution.py:308
  43.9 1.1 %collective-permute-done.10.refs_3_ = f32[1,2,128]{2,1,0:T(2,128)S(1)} collective-permute-done((f32[1,2,128]{2,1,0:T(2,128)S(1)}, f32[1,2,128]{2,1,0:T(2,128)S(1)}, u32[]{:S(2)}, u32[]{:S(2)}) %collective-permute-start.10) | collective-permute-done | bytes 1056 | tf_op jit(solution)/shard_map/ppermute | solution.py:308
  45.9 2.7 %collective-permute-start.11 = (f32[1,2,128]{2,1,0:T(2,128)S(1)}, f32[1,2,128]{2,1,0:T(2,128)S(1)}, u32[]{:S(2)}, u32[]{:S(2)}) collective-permute-start(f32[1,2,128]{2,1,0:T(2,128)S(1)} %add.3.refs_0_), channel_id=1, source_target_pairs={{0,4},{1,5},{2,6},{3,7},{4,0},{5,1},{6,2},{7,3},{8,12},{9,13},{10,... | collective-permute-start | bytes 3080 | tf_op jit(solution)/shard_map/ppermute | solution.py:308
  49.2 1.2 %collective-permute-done.11.refs_1_ = f32[1,2,128]{2,1,0:T(2,128)S(1)} collective-permute-done((f32[1,2,128]{2,1,0:T(2,128)S(1)}, f32[1,2,128]{2,1,0:T(2,128)S(1)}, u32[]{:S(2)}, u32[]{:S(2)}) %collective-permute-start.11) | collective-permute-done | bytes 1056 | tf_op jit(solution)/shard_map/ppermute | solution.py:308
  52.6 1.2 %collective-permute-start.15 = (f32[1024,128]{1,0:T(8,128)S(1)}, f32[1024,128]{1,0:T(8,128)S(1)}, u32[]{:S(2)}, u32[]{:S(2)}) collective-permute-start(f32[1024,128]{1,0:T(8,128)S(1)} %mix.10), channel_id=1, source_target_pairs={{0,16},{8,24},{16,0},{24,8},{1,17},{9,25},{17,1},{25,9},{2,18},{10... | collective-permute-start | bytes 1572872 | tf_op jit(solution)/shard_map/ppermute | solution.py:308
  57.4 1.4 %mix.13 = f32[1024,128]{1,0:T(8,128)S(1)} custom-call(f32[256,128]{1,0:T(8,128)S(1)} %get-tuple-element.105.drive_ref, f32[256,128]{1,0:T(8,128)S(1)} %get-tuple-element.106.repel_ref, f32[4096,128]{1,0:T(8,128)} %bitcast.21, f32[896,128]{1,0:T(8,128)S(1)} %collective-permute-done.1.refs_1_.refs_9_, f32[4096,128]{1,0:T(8,128)} %bitcast.22, ...), custom_call_target="tpu_custom_call" | custom-call | flops 1 | bytes 1 | tf_op jit(solution)/shard_map/mix/pallas_call | solution.py:211
  58.8 1.2 %collective-permute-start.16 = (f32[1024,128]{1,0:T(8,128)S(1)}, f32[1024,128]{1,0:T(8,128)S(1)}, u32[]{:S(2)}, u32[]{:S(2)}) collective-permute-start(f32[1024,128]{1,0:T(8,128)S(1)} %mix.13), channel_id=1, source_target_pairs={{0,16},{8,24},{16,0},{24,8},{1,17},{9,25},{17,1},{25,9},{2,18},{10... | collective-permute-start | bytes 1572872 | tf_op jit(solution)/shard_map/ppermute | solution.py:308
  60.0 1.4 %mix.14 = f32[1024,128]{1,0:T(8,128)S(1)} custom-call(f32[256,128]{1,0:T(8,128)S(1)} %get-tuple-element.105.drive_ref, f32[256,128]{1,0:T(8,128)S(1)} %get-tuple-element.106.repel_ref, f32[4096,128]{1,0:T(8,128)} %bitcast.23, f32[896,128]{1,0:T(8,128)S(1)} %collective-permute-done.2.refs_1_.refs_13_, f32[4096,128]{1,0:T(8,128)} %bitcast.24, ...), custom_call_target="tpu_custom_call" | custom-call | flops 1 | bytes 1 | tf_op jit(solution)/shard_map/mix/pallas_call | solution.py:211
  61.4 2.4 %collective-permute-done.20 = f32[512,128]{1,0:T(8,128)S(1)} collective-permute-done((f32[512,128]{1,0:T(8,128)S(1)}, f32[512,128]{1,0:T(8,128)S(1)}, u32[]{:S(2)}, u32[]{:S(2)}) %collective-permute-start.20) | collective-permute-done | bytes 262176 | tf_op jit(solution)/shard_map/ppermute | solution.py:308
  64.6 1.3 %mix.15 = f32[1024,128]{1,0:T(8,128)S(1)} custom-call(f32[256,128]{1,0:T(8,128)S(1)} %get-tuple-element.105.drive_ref, f32[256,128]{1,0:T(8,128)S(1)} %get-tuple-element.106.repel_ref, f32[4096,128]{1,0:T(8,128)} %bitcast.25, f32[1152,128]{1,0:T(8,128)S(1)} %collective-permute-done.12.refs_3_.refs_1_.refs_11_.refs_17_), custom_call_target="tpu_custom_call" | custom-call | flops 1 | bytes 1 | tf_op jit(solution)/shard_map/mix/pallas_call | solution.py:211
  66.0 8.1 %collective-permute-done.22 = f32[512,128]{1,0:T(8,128)S(1)} collective-permute-done((f32[512,128]{1,0:T(8,128)S(1)}, f32[512,128]{1,0:T(8,128)S(1)}, u32[]{:S(2)}, u32[]{:S(2)}) %collective-permute-start.22) | collective-permute-done | bytes 262176 | tf_op jit(solution)/shard_map/ppermute | solution.py:308
  74.5 1.3 %mix.16 = f32[1024,128]{1,0:T(8,128)S(1)} custom-call(f32[256,128]{1,0:T(8,128)S(1)} %get-tuple-element.105.drive_ref, f32[256,128]{1,0:T(8,128)S(1)} %get-tuple-element.106.repel_ref, f32[4096,128]{1,0:T(8,128)} %bitcast.26, f32[1152,128]{1,0:T(8,128)S(1)} %collective-permute-done.13.refs_3_.refs_1_.refs_15_.refs_19_), custom_call_target="tpu_custom_call" | custom-call | flops 1 | bytes 1 | tf_op jit(solution)/shard_map/mix/pallas_call | solution.py:211
  76.6 1.1 %collective-permute-start.21 = (f32[512,128]{1,0:T(8,128)S(1)}, f32[512,128]{1,0:T(8,128)S(1)}, u32[]{:S(2)}, u32[]{:S(2)}) collective-permute-start(f32[512,128]{1,0:T(8,128)S(1)} %collective-permute-done.20), channel_id=1, source_target_pairs={{0,16},{8,24},{16,0},{24,8},{1,17},{9,25},{17,1},{25,9},{2,18},{10... | collective-permute-start | bytes 786440 | tf_op jit(solution)/shard_map/ppermute | solution.py:308
  77.7 7.6 %collective-permute-done.16.refs_1_ = f32[1024,128]{1,0:T(8,128)S(1)} collective-permute-done((f32[1024,128]{1,0:T(8,128)S(1)}, f32[1024,128]{1,0:T(8,128)S(1)}, u32[]{:S(2)}, u32[]{:S(2)}) %collective-permute-start.16) | collective-permute-done | bytes 524320 | tf_op jit(solution)/shard_map/ppermute | solution.py:308
  85.5 2.7 %mix.17.refs_0_ = f32[5120,128]{1,0:T(8,128)S(1)} custom-call(f32[256,128]{1,0:T(8,128)S(1)} %get-tuple-element.105.drive_ref, f32[256,128]{1,0:T(8,128)S(1)} %get-tuple-element.106.repel_ref, f32[1024,128]{1,0:T(8,128)S(1)} %cut.5.refs_0_.refs_4_, f32[1024,128]{1,0:T(8,128)S(1)} %collective-permute-done.refs_1_.refs_5_, ...), custom_call_target="tpu_custom_call" | custom-call | flops 1 | bytes 1 | tf_op jit(solution)/shard_map/mix/pallas_call | solution.py:211
  92.4 4.1 %collective-permute-done.18.refs_1_ = f32[1024,128]{1,0:T(8,128)S(1)} collective-permute-done((f32[1024,128]{1,0:T(8,128)S(1)}, f32[1024,128]{1,0:T(8,128)S(1)}, u32[]{:S(2)}, u32[]{:S(2)}) %collective-permute-start.18) | collective-permute-done | bytes 524320 | tf_op jit(solution)/shard_map/ppermute | solution.py:308
  98.3 2.5 %collective-permute-done.21.refs_0_ = f32[512,128]{1,0:T(8,128)S(1)} collective-permute-done((f32[512,128]{1,0:T(8,128)S(1)}, f32[512,128]{1,0:T(8,128)S(1)}, u32[]{:S(2)}, u32[]{:S(2)}) %collective-permute-start.21) | collective-permute-done | bytes 262176 | tf_op jit(solution)/shard_map/ppermute | solution.py:308
  (44 shorter events, 17.9 us)
Async XLA Ops:
  2.1 15.8 %collective-permute-start = (f32[1024,128]{1,0:T(8,128)S(1)}, f32[1024,128]{1,0:T(8,128)S(1)}, u32[]{:S(2)}, u32[]{:S(2)}) collective-permute-start(f32[1024,128]{1,0:T(8,128)S(1)} %get-tuple-element.67), channel_id=1, source_target_pairs={{0,8},{8,0},{16,24},{24,16},{1,9},{9,1},{17,25},{25,17},{2,10},{10... | collective-permute-start | bytes 1572872 | tf_op jit(solution)/shard_map/ppermute | solution.py:308
  5.1 25.0 %collective-permute-start.3 = (f32[1024,128]{1,0:T(8,128)S(1)}, f32[1024,128]{1,0:T(8,128)S(1)}, u32[]{:S(2)}, u32[]{:S(2)}) collective-permute-start(f32[1024,128]{1,0:T(8,128)S(1)} %get-tuple-element.79), channel_id=1, source_target_pairs={{0,16},{8,24},{16,0},{24,8},{1,17},{9,25},{17,1},{25,9},{2,18},{10... | collective-permute-start | bytes 1572872 | tf_op jit(solution)/shard_map/ppermute | solution.py:308
  6.6 24.0 %collective-permute-start.4 = (f32[1024,128]{1,0:T(8,128)S(1)}, f32[1024,128]{1,0:T(8,128)S(1)}, u32[]{:S(2)}, u32[]{:S(2)}) collective-permute-start(f32[1024,128]{1,0:T(8,128)S(1)} %get-tuple-element.80), channel_id=1, source_target_pairs={{0,24},{8,16},{16,8},{24,0},{1,25},{9,17},{17,9},{25,1},{2,26},{10... | collective-permute-start | bytes 1572872 | tf_op jit(solution)/shard_map/ppermute | solution.py:308
  17.8 21.8 %copy-start.1 = (f32[1152,128]{1,0:T(8,128)S(1)}, f32[1152,128]{1,0:T(8,128)}, u32[]{:S(2)}) copy-start(f32[1152,128]{1,0:T(8,128)} %get-tuple-element.96) | copy-start | bytes 1769476
  17.8 23.1 %copy-start = (f32[1152,128]{1,0:T(8,128)S(1)}, f32[1152,128]{1,0:T(8,128)}, u32[]{:S(2)}) copy-start(f32[1152,128]{1,0:T(8,128)} %get-tuple-element.100) | copy-start | bytes 1769476
  17.8 21.8 %collective-permute-start.1 = (f32[896,128]{1,0:T(8,128)}, f32[896,128]{1,0:T(8,128)S(1)}, u32[]{:S(2)}, u32[]{:S(2)}) collective-permute-start(f32[896,128]{1,0:T(8,128)} %get-tuple-element.73), channel_id=1, source_target_pairs={{0,8},{8,0},{16,24},{24,16},{1,9},{9,1},{17,25},{25,17},{2,10},{10... | collective-permute-start | bytes 1376264 | tf_op jit(solution)/shard_map/ppermute | solution.py:308
  19.9 19.7 %collective-permute-start.2 = (f32[896,128]{1,0:T(8,128)}, f32[896,128]{1,0:T(8,128)S(1)}, u32[]{:S(2)}, u32[]{:S(2)}) collective-permute-start(f32[896,128]{1,0:T(8,128)} %get-tuple-element.74), channel_id=1, source_target_pairs={{0,16},{8,24},{16,0},{24,8},{1,17},{9,25},{17,1},{25,9},{2,18},{10... | collective-permute-start | bytes 1376264 | tf_op jit(solution)/shard_map/ppermute | solution.py:308
  32.9 6.4 %collective-permute-start.7 = (f32[1,2,128]{2,1,0:T(2,128)S(1)}, f32[1,2,128]{2,1,0:T(2,128)S(1)}, u32[]{:S(2)}, u32[]{:S(2)}) collective-permute-start(f32[1,2,128]{2,1,0:T(2,128)S(1)} %gram.1.refs_0_), channel_id=1, source_target_pairs={{0,24},{8,16},{16,8},{24,0},{1,25},{9,17},{17,9},{25,1},{2,26},{10... | collective-permute-start | bytes 3080 | tf_op jit(solution)/shard_map/ppermute | solution.py:308
  34.4 5.2 %collective-permute-start.6 = (f32[1,2,128]{2,1,0:T(2,128)S(1)}, f32[1,2,128]{2,1,0:T(2,128)S(1)}, u32[]{:S(2)}, u32[]{:S(2)}) collective-permute-start(f32[1,2,128]{2,1,0:T(2,128)S(1)} %gram.1.refs_0_), channel_id=1, source_target_pairs={{0,16},{8,24},{16,0},{24,8},{1,17},{9,25},{17,1},{25,9},{2,18},{10... | collective-permute-start | bytes 3080 | tf_op jit(solution)/shard_map/ppermute | solution.py:308
  35.9 3.7 %collective-permute-start.5 = (f32[1,2,128]{2,1,0:T(2,128)S(1)}, f32[1,2,128]{2,1,0:T(2,128)S(1)}, u32[]{:S(2)}, u32[]{:S(2)}) collective-permute-start(f32[1,2,128]{2,1,0:T(2,128)S(1)} %gram.1.refs_0_), channel_id=1, source_target_pairs={{0,8},{8,0},{16,24},{24,16},{1,9},{9,1},{17,25},{25,17},{2,10},{10... | collective-permute-start | bytes 3080 | tf_op jit(solution)/shard_map/ppermute | solution.py:308
  39.6 16.7 %collective-permute-start.12 = (f32[1152,128]{1,0:T(8,128)S(1)}, f32[1152,128]{1,0:T(8,128)S(1)}, u32[]{:S(2)}, u32[]{:S(2)}) collective-permute-start(f32[1152,128]{1,0:T(8,128)S(1)} %copy-done.1), channel_id=1, source_target_pairs={{0,8},{8,0},{16,24},{24,16},{1,9},{9,1},{17,25},{25,17},{2,10},{10... | collective-permute-start | bytes 1769480 | tf_op jit(solution)/shard_map/ppermute | solution.py:308
  40.9 17.8 %collective-permute-start.13 = (f32[1152,128]{1,0:T(8,128)S(1)}, f32[1152,128]{1,0:T(8,128)S(1)}, u32[]{:S(2)}, u32[]{:S(2)}) collective-permute-start(f32[1152,128]{1,0:T(8,128)S(1)} %copy-done), channel_id=1, source_target_pairs={{0,16},{8,24},{16,0},{24,8},{1,17},{9,25},{17,1},{25,9},{2,18},{10... | collective-permute-start | bytes 1769480 | tf_op jit(solution)/shard_map/ppermute | solution.py:308
  42.0 3.0 %collective-permute-start.10 = (f32[1,2,128]{2,1,0:T(2,128)S(1)}, f32[1,2,128]{2,1,0:T(2,128)S(1)}, u32[]{:S(2)}, u32[]{:S(2)}) collective-permute-start(f32[1,2,128]{2,1,0:T(2,128)S(1)} %add.2.refs_0_), channel_id=1, source_target_pairs={{0,3},{1,2},{2,1},{3,0},{4,7},{5,6},{6,5},{7,4},{8,11},{9,10},{10,... | collective-permute-start | bytes 3080 | tf_op jit(solution)/shard_map/ppermute | solution.py:308
  42.3 3.6 %collective-permute-start.9 = (f32[1,2,128]{2,1,0:T(2,128)S(1)}, f32[1,2,128]{2,1,0:T(2,128)S(1)}, u32[]{:S(2)}, u32[]{:S(2)}) collective-permute-start(f32[1,2,128]{2,1,0:T(2,128)S(1)} %add.2.refs_0_), channel_id=1, source_target_pairs={{0,2},{1,3},{2,0},{3,1},{4,6},{5,7},{6,4},{7,5},{8,10},{9,11},{10,... | collective-permute-start | bytes 3080 | tf_op jit(solution)/shard_map/ppermute | solution.py:308
  43.4 2.5 %collective-permute-start.8 = (f32[1,2,128]{2,1,0:T(2,128)S(1)}, f32[1,2,128]{2,1,0:T(2,128)S(1)}, u32[]{:S(2)}, u32[]{:S(2)}) collective-permute-start(f32[1,2,128]{2,1,0:T(2,128)S(1)} %add.2.refs_0_), channel_id=1, source_target_pairs={{0,1},{1,0},{2,3},{3,2},{4,5},{5,4},{6,7},{7,6},{8,9},{9,8},{10,11... | collective-permute-start | bytes 3080 | tf_op jit(solution)/shard_map/ppermute | solution.py:308
  45.9 4.5 %collective-permute-start.11 = (f32[1,2,128]{2,1,0:T(2,128)S(1)}, f32[1,2,128]{2,1,0:T(2,128)S(1)}, u32[]{:S(2)}, u32[]{:S(2)}) collective-permute-start(f32[1,2,128]{2,1,0:T(2,128)S(1)} %add.3.refs_0_), channel_id=1, source_target_pairs={{0,4},{1,5},{2,6},{3,7},{4,0},{5,1},{6,2},{7,3},{8,12},{9,13},{10,... | collective-permute-start | bytes 3080 | tf_op jit(solution)/shard_map/ppermute | solution.py:308
  52.6 23.3 %collective-permute-start.15 = (f32[1024,128]{1,0:T(8,128)S(1)}, f32[1024,128]{1,0:T(8,128)S(1)}, u32[]{:S(2)}, u32[]{:S(2)}) collective-permute-start(f32[1024,128]{1,0:T(8,128)S(1)} %mix.10), channel_id=1, source_target_pairs={{0,16},{8,24},{16,0},{24,8},{1,17},{9,25},{17,1},{25,9},{2,18},{10... | collective-permute-start | bytes 1572872 | tf_op jit(solution)/shard_map/ppermute | solution.py:308
  54.4 9.3 %collective-permute-start.20 = (f32[512,128]{1,0:T(8,128)S(1)}, f32[512,128]{1,0:T(8,128)S(1)}, u32[]{:S(2)}, u32[]{:S(2)}) collective-permute-start(f32[512,128]{1,0:T(8,128)S(1)} %mix.12), channel_id=1, source_target_pairs={{0,8},{8,0},{16,24},{24,16},{1,9},{9,1},{17,25},{25,17},{2,10},{10... | collective-permute-start | bytes 786440 | tf_op jit(solution)/shard_map/ppermute | solution.py:308
  55.4 18.7 %collective-permute-start.22 = (f32[512,128]{1,0:T(8,128)S(1)}, f32[512,128]{1,0:T(8,128)S(1)}, u32[]{:S(2)}, u32[]{:S(2)}) collective-permute-start(f32[512,128]{1,0:T(8,128)S(1)} %mix.11), channel_id=1, source_target_pairs={{0,16},{8,24},{16,0},{24,8},{1,17},{9,25},{17,1},{25,9},{2,18},{10... | collective-permute-start | bytes 786440 | tf_op jit(solution)/shard_map/ppermute | solution.py:308
  56.3 20.2 %collective-permute-start.14 = (f32[1024,128]{1,0:T(8,128)S(1)}, f32[1024,128]{1,0:T(8,128)S(1)}, u32[]{:S(2)}, u32[]{:S(2)}) collective-permute-start(f32[1024,128]{1,0:T(8,128)S(1)} %mix.9), channel_id=1, source_target_pairs={{0,8},{8,0},{16,24},{24,16},{1,9},{9,1},{17,25},{25,17},{2,10},{10... | collective-permute-start | bytes 1572872 | tf_op jit(solution)/shard_map/ppermute | solution.py:308
  58.8 26.5 %collective-permute-start.16 = (f32[1024,128]{1,0:T(8,128)S(1)}, f32[1024,128]{1,0:T(8,128)S(1)}, u32[]{:S(2)}, u32[]{:S(2)}) collective-permute-start(f32[1024,128]{1,0:T(8,128)S(1)} %mix.13), channel_id=1, source_target_pairs={{0,16},{8,24},{16,0},{24,8},{1,17},{9,25},{17,1},{25,9},{2,18},{10... | collective-permute-start | bytes 1572872 | tf_op jit(solution)/shard_map/ppermute | solution.py:308
  63.7 27.8 %collective-permute-start.17 = (f32[1024,128]{1,0:T(8,128)S(1)}, f32[1024,128]{1,0:T(8,128)S(1)}, u32[]{:S(2)}, u32[]{:S(2)}) collective-permute-start(f32[1024,128]{1,0:T(8,128)S(1)} %mix.14), channel_id=1, source_target_pairs={{0,8},{8,0},{16,24},{24,16},{1,9},{9,1},{17,25},{25,17},{2,10},{10... | collective-permute-start | bytes 1572872 | tf_op jit(solution)/shard_map/ppermute | solution.py:308
  74.0 22.5 %collective-permute-start.18 = (f32[1024,128]{1,0:T(8,128)S(1)}, f32[1024,128]{1,0:T(8,128)S(1)}, u32[]{:S(2)}, u32[]{:S(2)}) collective-permute-start(f32[1024,128]{1,0:T(8,128)S(1)} %mix.15), channel_id=1, source_target_pairs={{0,16},{8,24},{16,0},{24,8},{1,17},{9,25},{17,1},{25,9},{2,18},{10... | collective-permute-start | bytes 1572872 | tf_op jit(solution)/shard_map/ppermute | solution.py:308
  75.8 21.6 %collective-permute-start.19 = (f32[1024,128]{1,0:T(8,128)S(1)}, f32[1024,128]{1,0:T(8,128)S(1)}, u32[]{:S(2)}, u32[]{:S(2)}) collective-permute-start(f32[1024,128]{1,0:T(8,128)S(1)} %mix.16), channel_id=1, source_target_pairs={{0,8},{8,0},{16,24},{24,16},{1,9},{9,1},{17,25},{25,17},{2,10},{10... | collective-permute-start | bytes 1572872 | tf_op jit(solution)/shard_map/ppermute | solution.py:308
  76.6 24.2 %collective-permute-start.21 = (f32[512,128]{1,0:T(8,128)S(1)}, f32[512,128]{1,0:T(8,128)S(1)}, u32[]{:S(2)}, u32[]{:S(2)}) collective-permute-start(f32[512,128]{1,0:T(8,128)S(1)} %collective-permute-done.20), channel_id=1, source_target_pairs={{0,16},{8,24},{16,0},{24,8},{1,17},{9,25},{17,1},{25,9},{2,18},{10... | collective-permute-start | bytes 786440 | tf_op jit(solution)/shard_map/ppermute | solution.py:308
  85.2 15.7 %collective-permute-start.23 = (f32[512,128]{1,0:T(8,128)S(1)}, f32[512,128]{1,0:T(8,128)S(1)}, u32[]{:S(2)}, u32[]{:S(2)}) collective-permute-start(f32[512,128]{1,0:T(8,128)S(1)} %collective-permute-done.22), channel_id=1, source_target_pairs={{0,8},{8,0},{16,24},{24,16},{1,9},{9,1},{17,25},{25,17},{2,10},{10... | collective-permute-start | bytes 786440 | tf_op jit(solution)/shard_map/ppermute | solution.py:308

commit v9 on v8

--- a/solution.py
+++ b/solution.py
@@ -36,37 +36,35 @@
     return block.reshape(-1, rows, LANES).transpose(1, 0, 2).reshape(rows, -1)
 
 
-def gram_kernel(rows, pieces, *refs):
-    out_ref, acc_ref = refs[-2], refs[-1]
+def gram_kernel(rows, groups, pairs, *refs):
+    xs, (out_ref, acc_ref) = refs[:groups], refs[-2:]
+    base = refs[groups : -2]
     me = lax.axis_index("grp")
-    groups, count = len(pieces), rows * len(pieces)
+    count = rows * groups
     step = SUB * rows
-    xs = [refs[sum(pieces[:k]) : sum(pieces[: k + 1])] for k in range(groups)]
-    cuts = max(pieces)
-    steps = sum(x.shape[0] for x in xs[0]) // step // cuts
-
-    def load(x, cut, t, i):
-        ref, base = (x[cut], 0) if len(x) > 1 else (x[0], cut * steps * step)
-        return ref[pl.ds(base + t * step + i, SUB, stride=rows), :]
-
-    for a in range(groups):
-        for b in range(a, groups):
-            pairs = [(i, j) for i in range(rows) for j in range(rows) if a != b or i <= j]
-            sums = (jnp.zeros((SUB, LANES), jnp.float32),) * len(pairs)
-            for cut in range(cuts):
-
-                def body(t, sums):
-                    left = [load(xs[a], cut, t, i) for i in range(rows)]
-                    right = left if a == b else [load(xs[b], cut, t, j) for j in range(rows)]
-                    return tuple(s + left[i] * right[j] for s, (i, j) in zip(sums, pairs))
-
-                sums = lax.fori_loop(0, steps, body, sums, unroll=2)
-            for s, (i, j) in zip(sums, pairs):
-                row = jnp.sum(s, axis=0, keepdims=True)
-                left, right = (me ^ a) * rows + i, (me ^ b) * rows + j
-                acc_ref[pl.ds(left * count + right, 1), :] = row
-                if a != b or i != j:
-                    acc_ref[pl.ds(right * count + left, 1), :] = row
+    steps = xs[0].shape[0] // step
+
+    def load(ref, t, i):
+        return ref[pl.ds(t * step + i, SUB, stride=rows), :]
+
+    if len(pairs) < groups * (groups + 1) // 2:
+        acc_ref[...] = jnp.zeros_like(acc_ref)
+    for a, b in pairs:
+        terms = [(i, j) for i in range(rows) for j in range(rows) if a != b or i <= j]
+
+        def body(t, sums):
+            left = [load(xs[a], t, i) for i in range(rows)]
+            right = left if a == b else [load(xs[b], t, j) for j in range(rows)]
+            return tuple(s + left[i] * right[j] for s, (i, j) in zip(sums, terms))
+
+        sums = (jnp.zeros((SUB, LANES), jnp.float32),) * len(terms)
+        sums = lax.fori_loop(0, steps, body, sums, unroll=2)
+        for s, (i, j) in zip(sums, terms):
+            row = jnp.sum(s, axis=0, keepdims=True)
+            left, right = (me ^ a) * rows + i, (me ^ b) * rows + j
+            acc_ref[pl.ds(left * count + right, 1), :] = row
+            if a != b or i != j:
+                acc_ref[pl.ds(right * count + left, 1), :] = row
     total = lax.dot_general(
         jnp.ones((SUB, LANES), jnp.float32),
         acc_ref[...],
@@ -76,22 +74,23 @@
     )
     for n in range(count * count // LANES):
         row = total[:1, n * LANES : (n + 1) * LANES]
-        out_ref[:, n : n + 1, :] = row[None]
-
-
-def gram(xs, rows):
-    blocks = [block for x in xs for block in x]
-    count = rows * len(xs)
-    return pl.pallas_call(
-        functools.partial(gram_kernel, rows, [len(x) for x in xs]),
+        out_ref[:, n : n + 1, :] = (row + base[0][0, n : n + 1, :] if base else row)[None]
+
+
+def gram(xs, rows, groups, pairs, base=None):
+    count = rows * groups
+    held = [xs.get(k, xs[0]) for k in range(groups)]
+    extra = [] if base is None else [base]
+    return pl.pallas_call(
+        functools.partial(gram_kernel, rows, groups, pairs),
         out_shape=jax.ShapeDtypeStruct((1, count * count // LANES, LANES), jnp.float32),
-        in_specs=[VMEM_SPEC] * len(blocks),
+        in_specs=[VMEM_SPEC] * (groups + len(extra)),
         out_specs=VMEM_SPEC,
         scratch_shapes=[pltpu.VMEM((count * count, LANES), jnp.float32)],
         compiler_params=pltpu.CompilerParams(vmem_limit_bytes=VMEM_LIMIT),
         cost_estimate=SHORT,
         name="gram",
-    )(*map(in_vmem, blocks))
+    )(*map(in_vmem, held + extra))
 
 
 def add_kernel(*refs):
@@ -337,13 +336,18 @@
     xs = {k: swap(block, k) for k, block in zip(order, sent)}
     xs[order[0]], x, s_own = lax.optimization_barrier((xs[order[0]], x, s_own))
     xs[0] = cut(x, [(0, 0, part)], part, True)[0]
+    pairs = [(a, b) for a in everyone for b in everyone if a <= b]
+    late_pairs = [pair for pair in pairs if pair[0] in distant or pair[1] in distant]
+    inner = gram({k: xs[k] for k in [0] + direct}, rows, groups, [pair for pair in pairs if pair not in late_pairs])
+    if late_pairs:
+        inner = gram(xs, rows, groups, late_pairs, inner)
     xs = [[xs[k]] for k in everyone]
 
     def exchange(block, partners):
         return [swap(block, k) for k in partners]
 
     early = [exchange(s_own[0], lows), exchange(s_own[2], highs)]
-    grams = [gram(xs, rows)]
+    grams = [inner]
     pair = [s_own[1], s_own[3]]
     for partners in stages("grp"):
         total = add(grams) if len(grams) > 1 else grams[0]

time: 102 us -> 102 us (level)
  waiting for transfers between devices: 47.6 us -> 46.3 us
    ppermute x24, waiting for transfers between devices: 47.6 us -> 46.3 us  [swap(): lax.ppermute(block, axis, [(i, i ^ k) for i in range(lax.axis_size(axis))])]
    ppermute x24, starting transfers between devices: 27.4 us -> 28.4 us  [swap(): lax.ppermute(block, axis, [(i, i ^ k) for i in range(lax.axis_size(axis))])]
    pallas_call x1 -> x2, Pallas kernels: 2.28 us -> 2.52 us  [gram(): pl.pallas_call(functools.partial(gram_kernel, rows, groups, pairs), out_s...]
  transfers between devices with their start and end apart: 24 -> 24, of which waited for: 15 -> 14; matrix products, arithmetic and copies ran while one was open for 0% -> 0% of each run, Pallas kernels for 23% -> 23%
where the time goes in v9:
time: 102 us
  waiting for transfers between devices  46.3 us (45%)
  starting transfers between devices  28.4 us (28%)
  Pallas kernels  25.5 us (25%)
  between operations  1.51 us (1%)
    ppermute x24, waiting for transfers between devices, swap(): lax.ppermute(block, axis, [(i, i ^ k) for i in range(lax.axis_size(axis))])  46.3 us
    ppermute x24, starting transfers between devices, swap(): lax.ppermute(block, axis, [(i, i ^ k) for i in range(lax.axis_size(axis))])  28.4 us
    pallas_call x9, Pallas kernels, mix(): pl.pallas_call(functools.partial(mix_kernel, rows, count, [(*job[:3], [bl...  10 us
    pallas_call x8, Pallas kernels, put(): pl.pallas_call(functools.partial(put_kernel, entries, part, len(blocks)),...  6.67 us
    pallas_call x3, Pallas kernels, cut(): pl.pallas_call(functools.partial(cut_kernel, places, part), out_shape=[ou...  5.38 us
    pallas_call x2, Pallas kernels, gram(): pl.pallas_call(functools.partial(gram_kernel, rows, groups, pairs), out_s...  2.52 us
  transfers between devices with their start and end apart: 24, of which 14 were waited for; matrix products, arithmetic and copies ran while one was open for 0% of the time, Pallas kernels for 23%

profile of v9, /device:TPU:0, one launch (start us, length us, event | category | flops | bytes accessed | tf_op | source)
XLA Modules:
  0.0 101.7 jit_solution(3804556217634961194)
XLA Ops:
  0.6 1.4 %cut.3 = (f32[1024,128]{1,0:T(8,128)S(1)}, f32[1024,128]{1,0:T(8,128)S(1)}, f32[1024,128]{1,0:T(8,128)S(1)}) custom-call(f32[4096,128]{1,0:T(8,128)} %bitcast.35), custom_call_target="tpu_custom_call" | custom-call | flops 1 | bytes 1 | tf_op jit(solution)/shard_map/cut/pallas_call | solution.py:285
  2.1 3.0 %collective-permute-start = (f32[1024,128]{1,0:T(8,128)S(1)}, f32[1024,128]{1,0:T(8,128)S(1)}, u32[]{:S(2)}, u32[]{:S(2)}) collective-permute-start(f32[1024,128]{1,0:T(8,128)S(1)} %get-tuple-element.67), channel_id=1, source_target_pairs={{0,8},{8,0},{16,24},{24,16},{1,9},{9,1},{17,25},{25,17},{2,10},{10... | collective-permute-start | bytes 1572872 | tf_op jit(solution)/shard_map/ppermute | solution.py:307
  5.1 1.5 %collective-permute-start.3 = (f32[1024,128]{1,0:T(8,128)S(1)}, f32[1024,128]{1,0:T(8,128)S(1)}, u32[]{:S(2)}, u32[]{:S(2)}) collective-permute-start(f32[1024,128]{1,0:T(8,128)S(1)} %get-tuple-element.79), channel_id=1, source_target_pairs={{0,16},{8,24},{16,0},{24,8},{1,17},{9,25},{17,1},{25,9},{2,18},{10... | collective-permute-start | bytes 1572872 | tf_op jit(solution)/shard_map/ppermute | solution.py:307
  6.6 2.9 %cut.4 = (f32[896,128]{1,0:T(8,128)}, f32[1152,128]{1,0:T(8,128)}, f32[896,128]{1,0:T(8,128)}, f32[1152,128]{1,0:T(8,128)}) custom-call(f32[4096,128]{1,0:T(8,128)} %bitcast.20), custom_call_target="tpu_custom_call" | custom-call | flops 1 | bytes 1 | tf_op jit(solution)/shard_map/cut/pallas_call | solution.py:285
  9.5 8.3 %collective-permute-done.refs_1_.refs_5_ = f32[1024,128]{1,0:T(8,128)S(1)} collective-permute-done((f32[1024,128]{1,0:T(8,128)S(1)}, f32[1024,128]{1,0:T(8,128)S(1)}, u32[]{:S(2)}, u32[]{:S(2)}) %collective-permute-start) | collective-permute-done | bytes 524320 | tf_op jit(solution)/shard_map/ppermute | solution.py:307
  17.8 2.1 %collective-permute-start.1 = (f32[896,128]{1,0:T(8,128)}, f32[896,128]{1,0:T(8,128)S(1)}, u32[]{:S(2)}, u32[]{:S(2)}) collective-permute-start(f32[896,128]{1,0:T(8,128)} %get-tuple-element.73), channel_id=1, source_target_pairs={{0,8},{8,0},{16,24},{24,16},{1,9},{9,1},{17,25},{25,17},{2,10},{10... | collective-permute-start | bytes 1376264 | tf_op jit(solution)/shard_map/ppermute | solution.py:307
  19.9 1.5 %collective-permute-start.2 = (f32[896,128]{1,0:T(8,128)}, f32[896,128]{1,0:T(8,128)S(1)}, u32[]{:S(2)}, u32[]{:S(2)}) collective-permute-start(f32[896,128]{1,0:T(8,128)} %get-tuple-element.74), channel_id=1, source_target_pairs={{0,16},{8,24},{16,0},{24,8},{1,17},{9,25},{17,1},{25,9},{2,18},{10... | collective-permute-start | bytes 1376264 | tf_op jit(solution)/shard_map/ppermute | solution.py:307
  22.5 7.6 %collective-permute-done.3.refs_2_.refs_6_ = f32[1024,128]{1,0:T(8,128)S(1)} collective-permute-done((f32[1024,128]{1,0:T(8,128)S(1)}, f32[1024,128]{1,0:T(8,128)S(1)}, u32[]{:S(2)}, u32[]{:S(2)}) %collective-permute-start.3) | collective-permute-done | bytes 524320 | tf_op jit(solution)/shard_map/ppermute | solution.py:307
  30.1 1.4 %gram.2.refs_4_ = f32[1,2,128]{2,1,0:T(2,128)S(1)} custom-call(f32[1024,128]{1,0:T(8,128)S(1)} %cut.5.refs_0_.refs_3_.refs_4_, f32[1024,128]{1,0:T(8,128)S(1)} %collective-permute-done.refs_1_.refs_5_, f32[1024,128]{1,0:T(8,128)S(1)} %collective-permute-done.3.refs_2_.refs_6_, f32[1024,128]{1,0:T(8,128)S(1)} %cut.5.refs_0_.refs_3_.refs_4_), custom_call_target="tpu_custom_call" | custom-call | flops 1 | bytes 1 | tf_op jit(solution)/shard_map/gram/pallas_call | solution.py:84
  31.5 1.1 %gram.3.refs_0_ = f32[1,2,128]{2,1,0:T(2,128)S(1)} custom-call(f32[1024,128]{1,0:T(8,128)S(1)} %cut.5.refs_0_.refs_3_.refs_4_, f32[1024,128]{1,0:T(8,128)S(1)} %collective-permute-done.refs_1_.refs_5_, f32[1024,128]{1,0:T(8,128)S(1)} %collective-permute-done.3.refs_2_.refs_6_, f32[1024,128]{1,0:T(8,128)S(1)} %collective-permute-done.4.refs_3_.refs_7_, ...), custom_call_target="tpu_custom_call" | custom-call | flops 1 | bytes 1 | tf_op jit(solution)/shard_map/gram/pallas_call | solution.py:84
  33.2 2.0 %collective-permute-start.6 = (f32[1,2,128]{2,1,0:T(2,128)S(1)}, f32[1,2,128]{2,1,0:T(2,128)S(1)}, u32[]{:S(2)}, u32[]{:S(2)}) collective-permute-start(f32[1,2,128]{2,1,0:T(2,128)S(1)} %gram.3.refs_0_), channel_id=1, source_target_pairs={{0,16},{8,24},{16,0},{24,8},{1,17},{9,25},{17,1},{25,9},{2,18},{10... | collective-permute-start | bytes 3080 | tf_op jit(solution)/shard_map/ppermute | solution.py:307
  35.1 1.4 %collective-permute-start.5 = (f32[1,2,128]{2,1,0:T(2,128)S(1)}, f32[1,2,128]{2,1,0:T(2,128)S(1)}, u32[]{:S(2)}, u32[]{:S(2)}) collective-permute-start(f32[1,2,128]{2,1,0:T(2,128)S(1)} %gram.3.refs_0_), channel_id=1, source_target_pairs={{0,8},{8,0},{16,24},{24,16},{1,9},{9,1},{17,25},{25,17},{2,10},{10... | collective-permute-start | bytes 3080 | tf_op jit(solution)/shard_map/ppermute | solution.py:307
  36.6 2.8 %collective-permute-done.7.refs_3_ = f32[1,2,128]{2,1,0:T(2,128)S(1)} collective-permute-done((f32[1,2,128]{2,1,0:T(2,128)S(1)}, f32[1,2,128]{2,1,0:T(2,128)S(1)}, u32[]{:S(2)}, u32[]{:S(2)}) %collective-permute-start.7) | collective-permute-done | bytes 1056 | tf_op jit(solution)/shard_map/ppermute | solution.py:307
  39.6 1.3 %collective-permute-start.12 = (f32[1152,128]{1,0:T(8,128)S(1)}, f32[1152,128]{1,0:T(8,128)S(1)}, u32[]{:S(2)}, u32[]{:S(2)}) collective-permute-start(f32[1152,128]{1,0:T(8,128)S(1)} %copy-done.1), channel_id=1, source_target_pairs={{0,8},{8,0},{16,24},{24,16},{1,9},{9,1},{17,25},{25,17},{2,10},{10... | collective-permute-start | bytes 1769480 | tf_op jit(solution)/shard_map/ppermute | solution.py:307
  40.9 1.3 %collective-permute-start.13 = (f32[1152,128]{1,0:T(8,128)S(1)}, f32[1152,128]{1,0:T(8,128)S(1)}, u32[]{:S(2)}, u32[]{:S(2)}) collective-permute-start(f32[1152,128]{1,0:T(8,128)S(1)} %copy-done), channel_id=1, source_target_pairs={{0,16},{8,24},{16,0},{24,8},{1,17},{9,25},{17,1},{25,9},{2,18},{10... | collective-permute-start | bytes 1769480 | tf_op jit(solution)/shard_map/ppermute | solution.py:307
  42.3 1.4 %collective-permute-start.9 = (f32[1,2,128]{2,1,0:T(2,128)S(1)}, f32[1,2,128]{2,1,0:T(2,128)S(1)}, u32[]{:S(2)}, u32[]{:S(2)}) collective-permute-start(f32[1,2,128]{2,1,0:T(2,128)S(1)} %add.2.refs_0_), channel_id=1, source_target_pairs={{0,2},{1,3},{2,0},{3,1},{4,6},{5,7},{6,4},{7,5},{8,10},{9,11},{10,... | collective-permute-start | bytes 3080 | tf_op jit(solution)/shard_map/ppermute | solution.py:307
  44.1 1.1 %collective-permute-done.10.refs_3_ = f32[1,2,128]{2,1,0:T(2,128)S(1)} collective-permute-done((f32[1,2,128]{2,1,0:T(2,128)S(1)}, f32[1,2,128]{2,1,0:T(2,128)S(1)}, u32[]{:S(2)}, u32[]{:S(2)}) %collective-permute-start.10) | collective-permute-done | bytes 1056 | tf_op jit(solution)/shard_map/ppermute | solution.py:307
  45.9 2.6 %collective-permute-start.11 = (f32[1,2,128]{2,1,0:T(2,128)S(1)}, f32[1,2,128]{2,1,0:T(2,128)S(1)}, u32[]{:S(2)}, u32[]{:S(2)}) collective-permute-start(f32[1,2,128]{2,1,0:T(2,128)S(1)} %add.3.refs_0_), channel_id=1, source_target_pairs={{0,4},{1,5},{2,6},{3,7},{4,0},{5,1},{6,2},{7,3},{8,12},{9,13},{10,... | collective-permute-start | bytes 3080 | tf_op jit(solution)/shard_map/ppermute | solution.py:307
  49.2 1.3 %collective-permute-done.11.refs_1_ = f32[1,2,128]{2,1,0:T(2,128)S(1)} collective-permute-done((f32[1,2,128]{2,1,0:T(2,128)S(1)}, f32[1,2,128]{2,1,0:T(2,128)S(1)}, u32[]{:S(2)}, u32[]{:S(2)}) %collective-permute-start.11) | collective-permute-done | bytes 1056 | tf_op jit(solution)/shard_map/ppermute | solution.py:307
  52.6 1.2 %collective-permute-start.15 = (f32[1024,128]{1,0:T(8,128)S(1)}, f32[1024,128]{1,0:T(8,128)S(1)}, u32[]{:S(2)}, u32[]{:S(2)}) collective-permute-start(f32[1024,128]{1,0:T(8,128)S(1)} %mix.10), channel_id=1, source_target_pairs={{0,16},{8,24},{16,0},{24,8},{1,17},{9,25},{17,1},{25,9},{2,18},{10... | collective-permute-start | bytes 1572872 | tf_op jit(solution)/shard_map/ppermute | solution.py:307
  57.4 1.4 %mix.13 = f32[1024,128]{1,0:T(8,128)S(1)} custom-call(f32[256,128]{1,0:T(8,128)S(1)} %get-tuple-element.105.drive_ref, f32[256,128]{1,0:T(8,128)S(1)} %get-tuple-element.106.repel_ref, f32[4096,128]{1,0:T(8,128)} %bitcast.21, f32[896,128]{1,0:T(8,128)S(1)} %collective-permute-done.1.refs_1_.refs_9_, f32[4096,128]{1,0:T(8,128)} %bitcast.22, ...), custom_call_target="tpu_custom_call" | custom-call | flops 1 | bytes 1 | tf_op jit(solution)/shard_map/mix/pallas_call | solution.py:210
  58.8 1.2 %collective-permute-start.16 = (f32[1024,128]{1,0:T(8,128)S(1)}, f32[1024,128]{1,0:T(8,128)S(1)}, u32[]{:S(2)}, u32[]{:S(2)}) collective-permute-start(f32[1024,128]{1,0:T(8,128)S(1)} %mix.13), channel_id=1, source_target_pairs={{0,16},{8,24},{16,0},{24,8},{1,17},{9,25},{17,1},{25,9},{2,18},{10... | collective-permute-start | bytes 1572872 | tf_op jit(solution)/shard_map/ppermute | solution.py:307
  60.0 1.4 %mix.14 = f32[1024,128]{1,0:T(8,128)S(1)} custom-call(f32[256,128]{1,0:T(8,128)S(1)} %get-tuple-element.105.drive_ref, f32[256,128]{1,0:T(8,128)S(1)} %get-tuple-element.106.repel_ref, f32[4096,128]{1,0:T(8,128)} %bitcast.23, f32[896,128]{1,0:T(8,128)S(1)} %collective-permute-done.2.refs_1_.refs_13_, f32[4096,128]{1,0:T(8,128)} %bitcast.24, ...), custom_call_target="tpu_custom_call" | custom-call | flops 1 | bytes 1 | tf_op jit(solution)/shard_map/mix/pallas_call | solution.py:210
  61.4 2.4 %collective-permute-done.20 = f32[512,128]{1,0:T(8,128)S(1)} collective-permute-done((f32[512,128]{1,0:T(8,128)S(1)}, f32[512,128]{1,0:T(8,128)S(1)}, u32[]{:S(2)}, u32[]{:S(2)}) %collective-permute-start.20) | collective-permute-done | bytes 262176 | tf_op jit(solution)/shard_map/ppermute | solution.py:307
  64.6 1.3 %mix.15 = f32[1024,128]{1,0:T(8,128)S(1)} custom-call(f32[256,128]{1,0:T(8,128)S(1)} %get-tuple-element.105.drive_ref, f32[256,128]{1,0:T(8,128)S(1)} %get-tuple-element.106.repel_ref, f32[4096,128]{1,0:T(8,128)} %bitcast.25, f32[1152,128]{1,0:T(8,128)S(1)} %collective-permute-done.12.refs_3_.refs_1_.refs_11_.refs_17_), custom_call_target="tpu_custom_call" | custom-call | flops 1 | bytes 1 | tf_op jit(solution)/shard_map/mix/pallas_call | solution.py:210
  66.0 7.9 %collective-permute-done.22 = f32[512,128]{1,0:T(8,128)S(1)} collective-permute-done((f32[512,128]{1,0:T(8,128)S(1)}, f32[512,128]{1,0:T(8,128)S(1)}, u32[]{:S(2)}, u32[]{:S(2)}) %collective-permute-start.22) | collective-permute-done | bytes 262176 | tf_op jit(solution)/shard_map/ppermute | solution.py:307
  74.5 1.3 %mix.16 = f32[1024,128]{1,0:T(8,128)S(1)} custom-call(f32[256,128]{1,0:T(8,128)S(1)} %get-tuple-element.105.drive_ref, f32[256,128]{1,0:T(8,128)S(1)} %get-tuple-element.106.repel_ref, f32[4096,128]{1,0:T(8,128)} %bitcast.26, f32[1152,128]{1,0:T(8,128)S(1)} %collective-permute-done.13.refs_3_.refs_1_.refs_15_.refs_19_), custom_call_target="tpu_custom_call" | custom-call | flops 1 | bytes 1 | tf_op jit(solution)/shard_map/mix/pallas_call | solution.py:210
  76.6 1.1 %collective-permute-start.21 = (f32[512,128]{1,0:T(8,128)S(1)}, f32[512,128]{1,0:T(8,128)S(1)}, u32[]{:S(2)}, u32[]{:S(2)}) collective-permute-start(f32[512,128]{1,0:T(8,128)S(1)} %collective-permute-done.20), channel_id=1, source_target_pairs={{0,16},{8,24},{16,0},{24,8},{1,17},{9,25},{17,1},{25,9},{2,18},{10... | collective-permute-start | bytes 786440 | tf_op jit(solution)/shard_map/ppermute | solution.py:307
  77.7 7.4 %collective-permute-done.16.refs_1_ = f32[1024,128]{1,0:T(8,128)S(1)} collective-permute-done((f32[1024,128]{1,0:T(8,128)S(1)}, f32[1024,128]{1,0:T(8,128)S(1)}, u32[]{:S(2)}, u32[]{:S(2)}) %collective-permute-start.16) | collective-permute-done | bytes 524320 | tf_op jit(solution)/shard_map/ppermute | solution.py:307
  85.5 2.7 %mix.17.refs_0_ = f32[5120,128]{1,0:T(8,128)S(1)} custom-call(f32[256,128]{1,0:T(8,128)S(1)} %get-tuple-element.105.drive_ref, f32[256,128]{1,0:T(8,128)S(1)} %get-tuple-element.106.repel_ref, f32[1024,128]{1,0:T(8,128)S(1)} %cut.5.refs_0_.refs_3_.refs_4_, f32[1024,128]{1,0:T(8,128)S(1)} %collective-permute-done.refs_1_.refs_5_, ...), custom_call_target="tpu_custom_call" | custom-call | flops 1 | bytes 1 | tf_op jit(solution)/shard_map/mix/pallas_call | solution.py:210
  92.4 3.9 %collective-permute-done.18.refs_1_ = f32[1024,128]{1,0:T(8,128)S(1)} collective-permute-done((f32[1024,128]{1,0:T(8,128)S(1)}, f32[1024,128]{1,0:T(8,128)S(1)}, u32[]{:S(2)}, u32[]{:S(2)}) %collective-permute-start.18) | collective-permute-done | bytes 524320 | tf_op jit(solution)/shard_map/ppermute | solution.py:307
  98.3 2.5 %collective-permute-done.21.refs_0_ = f32[512,128]{1,0:T(8,128)S(1)} collective-permute-done((f32[512,128]{1,0:T(8,128)S(1)}, f32[512,128]{1,0:T(8,128)S(1)}, u32[]{:S(2)}, u32[]{:S(2)}) %collective-permute-start.21) | collective-permute-done | bytes 262176 | tf_op jit(solution)/shard_map/ppermute | solution.py:307
  (45 shorter events, 18.6 us)
Async XLA Ops:
  2.1 15.8 %collective-permute-start = (f32[1024,128]{1,0:T(8,128)S(1)}, f32[1024,128]{1,0:T(8,128)S(1)}, u32[]{:S(2)}, u32[]{:S(2)}) collective-permute-start(f32[1024,128]{1,0:T(8,128)S(1)} %get-tuple-element.67), channel_id=1, source_target_pairs={{0,8},{8,0},{16,24},{24,16},{1,9},{9,1},{17,25},{25,17},{2,10},{10... | collective-permute-start | bytes 1572872 | tf_op jit(solution)/shard_map/ppermute | solution.py:307
  5.1 25.0 %collective-permute-start.3 = (f32[1024,128]{1,0:T(8,128)S(1)}, f32[1024,128]{1,0:T(8,128)S(1)}, u32[]{:S(2)}, u32[]{:S(2)}) collective-permute-start(f32[1024,128]{1,0:T(8,128)S(1)} %get-tuple-element.79), channel_id=1, source_target_pairs={{0,16},{8,24},{16,0},{24,8},{1,17},{9,25},{17,1},{25,9},{2,18},{10... | collective-permute-start | bytes 1572872 | tf_op jit(solution)/shard_map/ppermute | solution.py:307
  6.6 24.9 %collective-permute-start.4 = (f32[1024,128]{1,0:T(8,128)S(1)}, f32[1024,128]{1,0:T(8,128)S(1)}, u32[]{:S(2)}, u32[]{:S(2)}) collective-permute-start(f32[1024,128]{1,0:T(8,128)S(1)} %get-tuple-element.80), channel_id=1, source_target_pairs={{0,24},{8,16},{16,8},{24,0},{1,25},{9,17},{17,9},{25,1},{2,26},{10... | collective-permute-start | bytes 1572872 | tf_op jit(solution)/shard_map/ppermute | solution.py:307
  17.8 21.8 %collective-permute-start.1 = (f32[896,128]{1,0:T(8,128)}, f32[896,128]{1,0:T(8,128)S(1)}, u32[]{:S(2)}, u32[]{:S(2)}) collective-permute-start(f32[896,128]{1,0:T(8,128)} %get-tuple-element.73), channel_id=1, source_target_pairs={{0,8},{8,0},{16,24},{24,16},{1,9},{9,1},{17,25},{25,17},{2,10},{10... | collective-permute-start | bytes 1376264 | tf_op jit(solution)/shard_map/ppermute | solution.py:307
  19.9 19.7 %collective-permute-start.2 = (f32[896,128]{1,0:T(8,128)}, f32[896,128]{1,0:T(8,128)S(1)}, u32[]{:S(2)}, u32[]{:S(2)}) collective-permute-start(f32[896,128]{1,0:T(8,128)} %get-tuple-element.74), channel_id=1, source_target_pairs={{0,16},{8,24},{16,0},{24,8},{1,17},{9,25},{17,1},{25,9},{2,18},{10... | collective-permute-start | bytes 1376264 | tf_op jit(solution)/shard_map/ppermute | solution.py:307
  22.5 17.1 %copy-start.1 = (f32[1152,128]{1,0:T(8,128)S(1)}, f32[1152,128]{1,0:T(8,128)}, u32[]{:S(2)}) copy-start(f32[1152,128]{1,0:T(8,128)} %get-tuple-element.96) | copy-start | bytes 1769476
  22.5 18.4 %copy-start = (f32[1152,128]{1,0:T(8,128)S(1)}, f32[1152,128]{1,0:T(8,128)}, u32[]{:S(2)}) copy-start(f32[1152,128]{1,0:T(8,128)} %get-tuple-element.100) | copy-start | bytes 1769476
  32.6 6.7 %collective-permute-start.7 = (f32[1,2,128]{2,1,0:T(2,128)S(1)}, f32[1,2,128]{2,1,0:T(2,128)S(1)}, u32[]{:S(2)}, u32[]{:S(2)}) collective-permute-start(f32[1,2,128]{2,1,0:T(2,128)S(1)} %gram.3.refs_0_), channel_id=1, source_target_pairs={{0,24},{8,16},{16,8},{24,0},{1,25},{9,17},{17,9},{25,1},{2,26},{10... | collective-permute-start | bytes 3080 | tf_op jit(solution)/shard_map/ppermute | solution.py:307
  33.2 6.4 %collective-permute-start.6 = (f32[1,2,128]{2,1,0:T(2,128)S(1)}, f32[1,2,128]{2,1,0:T(2,128)S(1)}, u32[]{:S(2)}, u32[]{:S(2)}) collective-permute-start(f32[1,2,128]{2,1,0:T(2,128)S(1)} %gram.3.refs_0_), channel_id=1, source_target_pairs={{0,16},{8,24},{16,0},{24,8},{1,17},{9,25},{17,1},{25,9},{2,18},{10... | collective-permute-start | bytes 3080 | tf_op jit(solution)/shard_map/ppermute | solution.py:307
  35.1 4.5 %collective-permute-start.5 = (f32[1,2,128]{2,1,0:T(2,128)S(1)}, f32[1,2,128]{2,1,0:T(2,128)S(1)}, u32[]{:S(2)}, u32[]{:S(2)}) collective-permute-start(f32[1,2,128]{2,1,0:T(2,128)S(1)} %gram.3.refs_0_), channel_id=1, source_target_pairs={{0,8},{8,0},{16,24},{24,16},{1,9},{9,1},{17,25},{25,17},{2,10},{10... | collective-permute-start | bytes 3080 | tf_op jit(solution)/shard_map/ppermute | solution.py:307
  39.6 16.7 %collective-permute-start.12 = (f32[1152,128]{1,0:T(8,128)S(1)}, f32[1152,128]{1,0:T(8,128)S(1)}, u32[]{:S(2)}, u32[]{:S(2)}) collective-permute-start(f32[1152,128]{1,0:T(8,128)S(1)} %copy-done.1), channel_id=1, source_target_pairs={{0,8},{8,0},{16,24},{24,16},{1,9},{9,1},{17,25},{25,17},{2,10},{10... | collective-permute-start | bytes 1769480 | tf_op jit(solution)/shard_map/ppermute | solution.py:307
  40.9 17.9 %collective-permute-start.13 = (f32[1152,128]{1,0:T(8,128)S(1)}, f32[1152,128]{1,0:T(8,128)S(1)}, u32[]{:S(2)}, u32[]{:S(2)}) collective-permute-start(f32[1152,128]{1,0:T(8,128)S(1)} %copy-done), channel_id=1, source_target_pairs={{0,16},{8,24},{16,0},{24,8},{1,17},{9,25},{17,1},{25,9},{2,18},{10... | collective-permute-start | bytes 1769480 | tf_op jit(solution)/shard_map/ppermute | solution.py:307
  42.3 3.0 %collective-permute-start.10 = (f32[1,2,128]{2,1,0:T(2,128)S(1)}, f32[1,2,128]{2,1,0:T(2,128)S(1)}, u32[]{:S(2)}, u32[]{:S(2)}) collective-permute-start(f32[1,2,128]{2,1,0:T(2,128)S(1)} %add.2.refs_0_), channel_id=1, source_target_pairs={{0,3},{1,2},{2,1},{3,0},{4,7},{5,6},{6,5},{7,4},{8,11},{9,10},{10,... | collective-permute-start | bytes 3080 | tf_op jit(solution)/shard_map/ppermute | solution.py:307
  42.3 3.6 %collective-permute-start.9 = (f32[1,2,128]{2,1,0:T(2,128)S(1)}, f32[1,2,128]{2,1,0:T(2,128)S(1)}, u32[]{:S(2)}, u32[]{:S(2)}) collective-permute-start(f32[1,2,128]{2,1,0:T(2,128)S(1)} %add.2.refs_0_), channel_id=1, source_target_pairs={{0,2},{1,3},{2,0},{3,1},{4,6},{5,7},{6,4},{7,5},{8,10},{9,11},{10,... | collective-permute-start | bytes 3080 | tf_op jit(solution)/shard_map/ppermute | solution.py:307
  43.6 2.2 %collective-permute-start.8 = (f32[1,2,128]{2,1,0:T(2,128)S(1)}, f32[1,2,128]{2,1,0:T(2,128)S(1)}, u32[]{:S(2)}, u32[]{:S(2)}) collective-permute-start(f32[1,2,128]{2,1,0:T(2,128)S(1)} %add.2.refs_0_), channel_id=1, source_target_pairs={{0,1},{1,0},{2,3},{3,2},{4,5},{5,4},{6,7},{7,6},{8,9},{9,8},{10,11... | collective-permute-start | bytes 3080 | tf_op jit(solution)/shard_map/ppermute | solution.py:307
  45.9 4.5 %collective-permute-start.11 = (f32[1,2,128]{2,1,0:T(2,128)S(1)}, f32[1,2,128]{2,1,0:T(2,128)S(1)}, u32[]{:S(2)}, u32[]{:S(2)}) collective-permute-start(f32[1,2,128]{2,1,0:T(2,128)S(1)} %add.3.refs_0_), channel_id=1, source_target_pairs={{0,4},{1,5},{2,6},{3,7},{4,0},{5,1},{6,2},{7,3},{8,12},{9,13},{10,... | collective-permute-start | bytes 3080 | tf_op jit(solution)/shard_map/ppermute | solution.py:307
  52.6 23.2 %collective-permute-start.15 = (f32[1024,128]{1,0:T(8,128)S(1)}, f32[1024,128]{1,0:T(8,128)S(1)}, u32[]{:S(2)}, u32[]{:S(2)}) collective-permute-start(f32[1024,128]{1,0:T(8,128)S(1)} %mix.10), channel_id=1, source_target_pairs={{0,16},{8,24},{16,0},{24,8},{1,17},{9,25},{17,1},{25,9},{2,18},{10... | collective-permute-start | bytes 1572872 | tf_op jit(solution)/shard_map/ppermute | solution.py:307
  54.4 9.3 %collective-permute-start.20 = (f32[512,128]{1,0:T(8,128)S(1)}, f32[512,128]{1,0:T(8,128)S(1)}, u32[]{:S(2)}, u32[]{:S(2)}) collective-permute-start(f32[512,128]{1,0:T(8,128)S(1)} %mix.12), channel_id=1, source_target_pairs={{0,8},{8,0},{16,24},{24,16},{1,9},{9,1},{17,25},{25,17},{2,10},{10... | collective-permute-start | bytes 786440 | tf_op jit(solution)/shard_map/ppermute | solution.py:307
  55.4 18.5 %collective-permute-start.22 = (f32[512,128]{1,0:T(8,128)S(1)}, f32[512,128]{1,0:T(8,128)S(1)}, u32[]{:S(2)}, u32[]{:S(2)}) collective-permute-start(f32[512,128]{1,0:T(8,128)S(1)} %mix.11), channel_id=1, source_target_pairs={{0,16},{8,24},{16,0},{24,8},{1,17},{9,25},{17,1},{25,9},{2,18},{10... | collective-permute-start | bytes 786440 | tf_op jit(solution)/shard_map/ppermute | solution.py:307
  56.3 20.2 %collective-permute-start.14 = (f32[1024,128]{1,0:T(8,128)S(1)}, f32[1024,128]{1,0:T(8,128)S(1)}, u32[]{:S(2)}, u32[]{:S(2)}) collective-permute-start(f32[1024,128]{1,0:T(8,128)S(1)} %mix.9), channel_id=1, source_target_pairs={{0,8},{8,0},{16,24},{24,16},{1,9},{9,1},{17,25},{25,17},{2,10},{10... | collective-permute-start | bytes 1572872 | tf_op jit(solution)/shard_map/ppermute | solution.py:307
  58.8 26.3 %collective-permute-start.16 = (f32[1024,128]{1,0:T(8,128)S(1)}, f32[1024,128]{1,0:T(8,128)S(1)}, u32[]{:S(2)}, u32[]{:S(2)}) collective-permute-start(f32[1024,128]{1,0:T(8,128)S(1)} %mix.13), channel_id=1, source_target_pairs={{0,16},{8,24},{16,0},{24,8},{1,17},{9,25},{17,1},{25,9},{2,18},{10... | collective-permute-start | bytes 1572872 | tf_op jit(solution)/shard_map/ppermute | solution.py:307
  63.7 27.8 %collective-permute-start.17 = (f32[1024,128]{1,0:T(8,128)S(1)}, f32[1024,128]{1,0:T(8,128)S(1)}, u32[]{:S(2)}, u32[]{:S(2)}) collective-permute-start(f32[1024,128]{1,0:T(8,128)S(1)} %mix.14), channel_id=1, source_target_pairs={{0,8},{8,0},{16,24},{24,16},{1,9},{9,1},{17,25},{25,17},{2,10},{10... | collective-permute-start | bytes 1572872 | tf_op jit(solution)/shard_map/ppermute | solution.py:307
  73.8 22.5 %collective-permute-start.18 = (f32[1024,128]{1,0:T(8,128)S(1)}, f32[1024,128]{1,0:T(8,128)S(1)}, u32[]{:S(2)}, u32[]{:S(2)}) collective-permute-start(f32[1024,128]{1,0:T(8,128)S(1)} %mix.15), channel_id=1, source_target_pairs={{0,16},{8,24},{16,0},{24,8},{1,17},{9,25},{17,1},{25,9},{2,18},{10... | collective-permute-start | bytes 1572872 | tf_op jit(solution)/shard_map/ppermute | solution.py:307
  75.8 21.6 %collective-permute-start.19 = (f32[1024,128]{1,0:T(8,128)S(1)}, f32[1024,128]{1,0:T(8,128)S(1)}, u32[]{:S(2)}, u32[]{:S(2)}) collective-permute-start(f32[1024,128]{1,0:T(8,128)S(1)} %mix.16), channel_id=1, source_target_pairs={{0,8},{8,0},{16,24},{24,16},{1,9},{9,1},{17,25},{25,17},{2,10},{10... | collective-permute-start | bytes 1572872 | tf_op jit(solution)/shard_map/ppermute | solution.py:307
  76.6 24.2 %collective-permute-start.21 = (f32[512,128]{1,0:T(8,128)S(1)}, f32[512,128]{1,0:T(8,128)S(1)}, u32[]{:S(2)}, u32[]{:S(2)}) collective-permute-start(f32[512,128]{1,0:T(8,128)S(1)} %collective-permute-done.20), channel_id=1, source_target_pairs={{0,16},{8,24},{16,0},{24,8},{1,17},{9,25},{17,1},{25,9},{2,18},{10... | collective-permute-start | bytes 786440 | tf_op jit(solution)/shard_map/ppermute | solution.py:307
  85.1 15.9 %collective-permute-start.23 = (f32[512,128]{1,0:T(8,128)S(1)}, f32[512,128]{1,0:T(8,128)S(1)}, u32[]{:S(2)}, u32[]{:S(2)}) collective-permute-start(f32[512,128]{1,0:T(8,128)S(1)} %collective-permute-done.22), channel_id=1, source_target_pairs={{0,8},{8,0},{16,24},{24,16},{1,9},{9,1},{17,25},{25,17},{2,10},{10... | collective-permute-start | bytes 786440 | tf_op jit(solution)/shard_map/ppermute | solution.py:307

commit v10 on v8

--- a/solution.py
+++ b/solution.py
@@ -333,7 +333,7 @@
     sent = cut(x, [(k, 0, part) for k in order], part, True)
     s, sent = lax.optimization_barrier((s, sent))
     bounds = [(n * half + row, length) for n in (0, 1) for row, length in ((0, first), (first, half - first))]
-    s_own = cut(s, [(None, *bound) for bound in bounds], part, False)
+    s_own = cut(s, [(None, *bound) for bound in bounds], part, True)
     xs = {k: swap(block, k) for k, block in zip(order, sent)}
     xs[order[0]], x, s_own = lax.optimization_barrier((xs[order[0]], x, s_own))
     xs[0] = cut(x, [(0, 0, part)], part, True)[0]

time: 102 us -> 102 us (level)
  Pallas kernels: 25.3 us -> 23.9 us
    pallas_call x3, Pallas kernels: 5.38 us -> 4.07 us  [cut(): pl.pallas_call(functools.partial(cut_kernel, places, part), out_shape=[ou...]
  transfers between devices with their start and end apart: 24 -> 24, of which waited for: 15 -> 15; matrix products, arithmetic and copies ran while one was open for 0% -> 0% of each run, Pallas kernels for 23% -> 21%
where the time goes in v10:
time: 102 us
  waiting for transfers between devices  48.2 us (47%)
  starting transfers between devices  28 us (27%)
  Pallas kernels  23.9 us (23%)
  between operations  1.49 us (1%)
    ppermute x24, waiting for transfers between devices, swap(): lax.ppermute(block, axis, [(i, i ^ k) for i in range(lax.axis_size(axis))])  48.2 us
    ppermute x24, starting transfers between devices, swap(): lax.ppermute(block, axis, [(i, i ^ k) for i in range(lax.axis_size(axis))])  28 us
    pallas_call x9, Pallas kernels, mix(): pl.pallas_call(functools.partial(mix_kernel, rows, count, [(*job[:3], [bl...  10 us
    pallas_call x8, Pallas kernels, put(): pl.pallas_call(functools.partial(put_kernel, entries, part, len(blocks)),...  6.67 us
    pallas_call x3, Pallas kernels, cut(): pl.pallas_call(functools.partial(cut_kernel, places, part), out_shape=[ou...  4.07 us
    pallas_call x1, Pallas kernels, gram(): pl.pallas_call(functools.partial(gram_kernel, rows, [len(x) for x in xs])...  2.28 us
  transfers between devices with their start and end apart: 24, of which 15 were waited for; matrix products, arithmetic and copies ran while one was open for 0% of the time, Pallas kernels for 21%

profile of v10, /device:TPU:0, one launch (start us, length us, event | category | flops | bytes accessed | tf_op | source)
XLA Modules:
  0.0 101.7 jit_solution(8135495001107789339)
XLA Ops:
  0.6 1.4 %cut.3 = (f32[1024,128]{1,0:T(8,128)S(1)}, f32[1024,128]{1,0:T(8,128)S(1)}, f32[1024,128]{1,0:T(8,128)S(1)}) custom-call(f32[4096,128]{1,0:T(8,128)} %bitcast.35), custom_call_target="tpu_custom_call" | custom-call | flops 1 | bytes 1 | tf_op jit(solution)/shard_map/cut/pallas_call | solution.py:286
  2.1 3.0 %collective-permute-start = (f32[1024,128]{1,0:T(8,128)S(1)}, f32[1024,128]{1,0:T(8,128)S(1)}, u32[]{:S(2)}, u32[]{:S(2)}) collective-permute-start(f32[1024,128]{1,0:T(8,128)S(1)} %get-tuple-element.67), channel_id=1, source_target_pairs={{0,8},{8,0},{16,24},{24,16},{1,9},{9,1},{17,25},{25,17},{2,10},{10... | collective-permute-start | bytes 1572872 | tf_op jit(solution)/shard_map/ppermute | solution.py:308
  5.1 1.5 %collective-permute-start.3 = (f32[1024,128]{1,0:T(8,128)S(1)}, f32[1024,128]{1,0:T(8,128)S(1)}, u32[]{:S(2)}, u32[]{:S(2)}) collective-permute-start(f32[1024,128]{1,0:T(8,128)S(1)} %get-tuple-element.79), channel_id=1, source_target_pairs={{0,16},{8,24},{16,0},{24,8},{1,17},{9,25},{17,1},{25,9},{2,18},{10... | collective-permute-start | bytes 1572872 | tf_op jit(solution)/shard_map/ppermute | solution.py:308
  6.6 1.6 %cut.4 = (f32[896,128]{1,0:T(8,128)S(1)}, f32[1152,128]{1,0:T(8,128)S(1)}, f32[896,128]{1,0:T(8,128)S(1)}, f32[1152,128]{1,0:T(8,128)S(1)}) custom-call(f32[4096,128]{1,0:T(8,128)} %bitcast.20), custom_call_target="tpu_custom_call" | custom-call | flops 1 | bytes 1 | tf_op jit(solution)/shard_map/cut/pallas_call | solution.py:286
  8.2 9.6 %collective-permute-done.refs_1_.refs_5_ = f32[1024,128]{1,0:T(8,128)S(1)} collective-permute-done((f32[1024,128]{1,0:T(8,128)S(1)}, f32[1024,128]{1,0:T(8,128)S(1)}, u32[]{:S(2)}, u32[]{:S(2)}) %collective-permute-start) | collective-permute-done | bytes 524320 | tf_op jit(solution)/shard_map/ppermute | solution.py:308
  17.8 2.1 %collective-permute-start.1 = (f32[896,128]{1,0:T(8,128)S(1)}, f32[896,128]{1,0:T(8,128)S(1)}, u32[]{:S(2)}, u32[]{:S(2)}) collective-permute-start(f32[896,128]{1,0:T(8,128)S(1)} %get-tuple-element.73), channel_id=1, source_target_pairs={{0,8},{8,0},{16,24},{24,16},{1,9},{9,1},{17,25},{25,17},{2,10},{10... | collective-permute-start | bytes 1376264 | tf_op jit(solution)/shard_map/ppermute | solution.py:308
  19.9 1.5 %collective-permute-start.2 = (f32[896,128]{1,0:T(8,128)S(1)}, f32[896,128]{1,0:T(8,128)S(1)}, u32[]{:S(2)}, u32[]{:S(2)}) collective-permute-start(f32[896,128]{1,0:T(8,128)S(1)} %get-tuple-element.74), channel_id=1, source_target_pairs={{0,16},{8,24},{16,0},{24,8},{1,17},{9,25},{17,1},{25,9},{2,18},{10... | collective-permute-start | bytes 1376264 | tf_op jit(solution)/shard_map/ppermute | solution.py:308
  21.4 1.1 %cut.5.refs_0_.refs_4_ = f32[1024,128]{1,0:T(8,128)S(1)} custom-call(f32[4096,128]{1,0:T(8,128)} %bitcast.36), custom_call_target="tpu_custom_call" | custom-call | flops 1 | bytes 1 | tf_op jit(solution)/shard_map/cut/pallas_call | solution.py:286
  22.5 7.6 %collective-permute-done.3.refs_2_.refs_6_ = f32[1024,128]{1,0:T(8,128)S(1)} collective-permute-done((f32[1024,128]{1,0:T(8,128)S(1)}, f32[1024,128]{1,0:T(8,128)S(1)}, u32[]{:S(2)}, u32[]{:S(2)}) %collective-permute-start.3) | collective-permute-done | bytes 524320 | tf_op jit(solution)/shard_map/ppermute | solution.py:308
  30.6 2.3 %gram.1.refs_0_ = f32[1,2,128]{2,1,0:T(2,128)S(1)} custom-call(f32[1024,128]{1,0:T(8,128)S(1)} %cut.5.refs_0_.refs_4_, f32[1024,128]{1,0:T(8,128)S(1)} %collective-permute-done.refs_1_.refs_5_, f32[1024,128]{1,0:T(8,128)S(1)} %collective-permute-done.3.refs_2_.refs_6_, f32[1024,128]{1,0:T(8,128)S(1)} %collective-permute-done.4.refs_3_.refs_7_), custom_call_target="tpu_custom_call" | custom-call | flops 1 | bytes 1 | tf_op jit(solution)/shard_map/gram/pallas_call | solution.py:85
  32.9 1.5 %collective-permute-start.7 = (f32[1,2,128]{2,1,0:T(2,128)S(1)}, f32[1,2,128]{2,1,0:T(2,128)S(1)}, u32[]{:S(2)}, u32[]{:S(2)}) collective-permute-start(f32[1,2,128]{2,1,0:T(2,128)S(1)} %gram.1.refs_0_), channel_id=1, source_target_pairs={{0,24},{8,16},{16,8},{24,0},{1,25},{9,17},{17,9},{25,1},{2,26},{10... | collective-permute-start | bytes 3080 | tf_op jit(solution)/shard_map/ppermute | solution.py:308
  34.4 1.5 %collective-permute-start.6 = (f32[1,2,128]{2,1,0:T(2,128)S(1)}, f32[1,2,128]{2,1,0:T(2,128)S(1)}, u32[]{:S(2)}, u32[]{:S(2)}) collective-permute-start(f32[1,2,128]{2,1,0:T(2,128)S(1)} %gram.1.refs_0_), channel_id=1, source_target_pairs={{0,16},{8,24},{16,0},{24,8},{1,17},{9,25},{17,1},{25,9},{2,18},{10... | collective-permute-start | bytes 3080 | tf_op jit(solution)/shard_map/ppermute | solution.py:308
  36.4 2.9 %collective-permute-done.7.refs_3_ = f32[1,2,128]{2,1,0:T(2,128)S(1)} collective-permute-done((f32[1,2,128]{2,1,0:T(2,128)S(1)}, f32[1,2,128]{2,1,0:T(2,128)S(1)}, u32[]{:S(2)}, u32[]{:S(2)}) %collective-permute-start.7) | collective-permute-done | bytes 1056 | tf_op jit(solution)/shard_map/ppermute | solution.py:308
  39.6 1.3 %collective-permute-start.12 = (f32[1152,128]{1,0:T(8,128)S(1)}, f32[1152,128]{1,0:T(8,128)S(1)}, u32[]{:S(2)}, u32[]{:S(2)}) collective-permute-start(f32[1152,128]{1,0:T(8,128)S(1)} %get-tuple-element.96), channel_id=1, source_target_pairs={{0,8},{8,0},{16,24},{24,16},{1,9},{9,1},{17,25},{25,17},{2,10},{10... | collective-permute-start | bytes 1769480 | tf_op jit(solution)/shard_map/ppermute | solution.py:308
  40.9 1.0 %collective-permute-start.13 = (f32[1152,128]{1,0:T(8,128)S(1)}, f32[1152,128]{1,0:T(8,128)S(1)}, u32[]{:S(2)}, u32[]{:S(2)}) collective-permute-start(f32[1152,128]{1,0:T(8,128)S(1)} %get-tuple-element.100), channel_id=1, source_target_pairs={{0,16},{8,24},{16,0},{24,8},{1,17},{9,25},{17,1},{25,9},{2,18},{10... | collective-permute-start | bytes 1769480 | tf_op jit(solution)/shard_map/ppermute | solution.py:308
  42.3 1.1 %collective-permute-start.9 = (f32[1,2,128]{2,1,0:T(2,128)S(1)}, f32[1,2,128]{2,1,0:T(2,128)S(1)}, u32[]{:S(2)}, u32[]{:S(2)}) collective-permute-start(f32[1,2,128]{2,1,0:T(2,128)S(1)} %add.2.refs_0_), channel_id=1, source_target_pairs={{0,2},{1,3},{2,0},{3,1},{4,6},{5,7},{6,4},{7,5},{8,10},{9,11},{10,... | collective-permute-start | bytes 3080 | tf_op jit(solution)/shard_map/ppermute | solution.py:308
  43.8 1.1 %collective-permute-done.10.refs_3_ = f32[1,2,128]{2,1,0:T(2,128)S(1)} collective-permute-done((f32[1,2,128]{2,1,0:T(2,128)S(1)}, f32[1,2,128]{2,1,0:T(2,128)S(1)}, u32[]{:S(2)}, u32[]{:S(2)}) %collective-permute-start.10) | collective-permute-done | bytes 1056 | tf_op jit(solution)/shard_map/ppermute | solution.py:308
  45.9 2.7 %collective-permute-start.11 = (f32[1,2,128]{2,1,0:T(2,128)S(1)}, f32[1,2,128]{2,1,0:T(2,128)S(1)}, u32[]{:S(2)}, u32[]{:S(2)}) collective-permute-start(f32[1,2,128]{2,1,0:T(2,128)S(1)} %add.3.refs_0_), channel_id=1, source_target_pairs={{0,4},{1,5},{2,6},{3,7},{4,0},{5,1},{6,2},{7,3},{8,12},{9,13},{10,... | collective-permute-start | bytes 3080 | tf_op jit(solution)/shard_map/ppermute | solution.py:308
  49.2 1.2 %collective-permute-done.11.refs_1_ = f32[1,2,128]{2,1,0:T(2,128)S(1)} collective-permute-done((f32[1,2,128]{2,1,0:T(2,128)S(1)}, f32[1,2,128]{2,1,0:T(2,128)S(1)}, u32[]{:S(2)}, u32[]{:S(2)}) %collective-permute-start.11) | collective-permute-done | bytes 1056 | tf_op jit(solution)/shard_map/ppermute | solution.py:308
  54.2 1.2 %collective-permute-start.20 = (f32[512,128]{1,0:T(8,128)S(1)}, f32[512,128]{1,0:T(8,128)S(1)}, u32[]{:S(2)}, u32[]{:S(2)}) collective-permute-start(f32[512,128]{1,0:T(8,128)S(1)} %mix.12), channel_id=1, source_target_pairs={{0,8},{8,0},{16,24},{24,16},{1,9},{9,1},{17,25},{25,17},{2,10},{10... | collective-permute-start | bytes 786440 | tf_op jit(solution)/shard_map/ppermute | solution.py:308
  57.4 1.4 %mix.13 = f32[1024,128]{1,0:T(8,128)S(1)} custom-call(f32[256,128]{1,0:T(8,128)S(1)} %get-tuple-element.105.drive_ref, f32[256,128]{1,0:T(8,128)S(1)} %get-tuple-element.106.repel_ref, f32[4096,128]{1,0:T(8,128)} %bitcast.21, f32[896,128]{1,0:T(8,128)S(1)} %collective-permute-done.1.refs_1_.refs_9_, f32[4096,128]{1,0:T(8,128)} %bitcast.22, ...), custom_call_target="tpu_custom_call" | custom-call | flops 1 | bytes 1 | tf_op jit(solution)/shard_map/mix/pallas_call | solution.py:211
  59.8 1.4 %mix.14 = f32[1024,128]{1,0:T(8,128)S(1)} custom-call(f32[256,128]{1,0:T(8,128)S(1)} %get-tuple-element.105.drive_ref, f32[256,128]{1,0:T(8,128)S(1)} %get-tuple-element.106.repel_ref, f32[4096,128]{1,0:T(8,128)} %bitcast.23, f32[896,128]{1,0:T(8,128)S(1)} %collective-permute-done.2.refs_1_.refs_13_, f32[4096,128]{1,0:T(8,128)} %bitcast.24, ...), custom_call_target="tpu_custom_call" | custom-call | flops 1 | bytes 1 | tf_op jit(solution)/shard_map/mix/pallas_call | solution.py:211
  61.1 2.4 %collective-permute-done.20 = f32[512,128]{1,0:T(8,128)S(1)} collective-permute-done((f32[512,128]{1,0:T(8,128)S(1)}, f32[512,128]{1,0:T(8,128)S(1)}, u32[]{:S(2)}, u32[]{:S(2)}) %collective-permute-start.20) | collective-permute-done | bytes 262176 | tf_op jit(solution)/shard_map/ppermute | solution.py:308
  63.5 1.1 %collective-permute-start.17 = (f32[1024,128]{1,0:T(8,128)S(1)}, f32[1024,128]{1,0:T(8,128)S(1)}, u32[]{:S(2)}, u32[]{:S(2)}) collective-permute-start(f32[1024,128]{1,0:T(8,128)S(1)} %mix.14), channel_id=1, source_target_pairs={{0,8},{8,0},{16,24},{24,16},{1,9},{9,1},{17,25},{25,17},{2,10},{10... | collective-permute-start | bytes 1572872 | tf_op jit(solution)/shard_map/ppermute | solution.py:308
  64.6 1.3 %mix.15 = f32[1024,128]{1,0:T(8,128)S(1)} custom-call(f32[256,128]{1,0:T(8,128)S(1)} %get-tuple-element.105.drive_ref, f32[256,128]{1,0:T(8,128)S(1)} %get-tuple-element.106.repel_ref, f32[4096,128]{1,0:T(8,128)} %bitcast.25, f32[1152,128]{1,0:T(8,128)S(1)} %collective-permute-done.12.refs_3_.refs_1_.refs_11_.refs_17_), custom_call_target="tpu_custom_call" | custom-call | flops 1 | bytes 1 | tf_op jit(solution)/shard_map/mix/pallas_call | solution.py:211
  65.9 7.7 %collective-permute-done.22 = f32[512,128]{1,0:T(8,128)S(1)} collective-permute-done((f32[512,128]{1,0:T(8,128)S(1)}, f32[512,128]{1,0:T(8,128)S(1)}, u32[]{:S(2)}, u32[]{:S(2)}) %collective-permute-start.22) | collective-permute-done | bytes 262176 | tf_op jit(solution)/shard_map/ppermute | solution.py:308
  74.4 1.3 %mix.16 = f32[1024,128]{1,0:T(8,128)S(1)} custom-call(f32[256,128]{1,0:T(8,128)S(1)} %get-tuple-element.105.drive_ref, f32[256,128]{1,0:T(8,128)S(1)} %get-tuple-element.106.repel_ref, f32[4096,128]{1,0:T(8,128)} %bitcast.26, f32[1152,128]{1,0:T(8,128)S(1)} %collective-permute-done.13.refs_3_.refs_1_.refs_15_.refs_19_), custom_call_target="tpu_custom_call" | custom-call | flops 1 | bytes 1 | tf_op jit(solution)/shard_map/mix/pallas_call | solution.py:211
  76.6 1.1 %collective-permute-start.21 = (f32[512,128]{1,0:T(8,128)S(1)}, f32[512,128]{1,0:T(8,128)S(1)}, u32[]{:S(2)}, u32[]{:S(2)}) collective-permute-start(f32[512,128]{1,0:T(8,128)S(1)} %collective-permute-done.20), channel_id=1, source_target_pairs={{0,16},{8,24},{16,0},{24,8},{1,17},{9,25},{17,1},{25,9},{2,18},{10... | collective-permute-start | bytes 786440 | tf_op jit(solution)/shard_map/ppermute | solution.py:308
  77.7 7.2 %collective-permute-done.16.refs_1_ = f32[1024,128]{1,0:T(8,128)S(1)} collective-permute-done((f32[1024,128]{1,0:T(8,128)S(1)}, f32[1024,128]{1,0:T(8,128)S(1)}, u32[]{:S(2)}, u32[]{:S(2)}) %collective-permute-start.16) | collective-permute-done | bytes 524320 | tf_op jit(solution)/shard_map/ppermute | solution.py:308
  85.5 2.7 %mix.17.refs_0_ = f32[5120,128]{1,0:T(8,128)S(1)} custom-call(f32[256,128]{1,0:T(8,128)S(1)} %get-tuple-element.105.drive_ref, f32[256,128]{1,0:T(8,128)S(1)} %get-tuple-element.106.repel_ref, f32[1024,128]{1,0:T(8,128)S(1)} %cut.5.refs_0_.refs_4_, f32[1024,128]{1,0:T(8,128)S(1)} %collective-permute-done.refs_1_.refs_5_, ...), custom_call_target="tpu_custom_call" | custom-call | flops 1 | bytes 1 | tf_op jit(solution)/shard_map/mix/pallas_call | solution.py:211
  92.4 3.7 %collective-permute-done.18.refs_1_ = f32[1024,128]{1,0:T(8,128)S(1)} collective-permute-done((f32[1024,128]{1,0:T(8,128)S(1)}, f32[1024,128]{1,0:T(8,128)S(1)}, u32[]{:S(2)}, u32[]{:S(2)}) %collective-permute-start.18) | collective-permute-done | bytes 524320 | tf_op jit(solution)/shard_map/ppermute | solution.py:308
  98.1 2.5 %collective-permute-done.21.refs_0_ = f32[512,128]{1,0:T(8,128)S(1)} collective-permute-done((f32[512,128]{1,0:T(8,128)S(1)}, f32[512,128]{1,0:T(8,128)S(1)}, u32[]{:S(2)}, u32[]{:S(2)}) %collective-permute-start.21) | collective-permute-done | bytes 262176 | tf_op jit(solution)/shard_map/ppermute | solution.py:308
  (40 shorter events, 19.3 us)
Async XLA Ops:
  2.1 15.8 %collective-permute-start = (f32[1024,128]{1,0:T(8,128)S(1)}, f32[1024,128]{1,0:T(8,128)S(1)}, u32[]{:S(2)}, u32[]{:S(2)}) collective-permute-start(f32[1024,128]{1,0:T(8,128)S(1)} %get-tuple-element.67), channel_id=1, source_target_pairs={{0,8},{8,0},{16,24},{24,16},{1,9},{9,1},{17,25},{25,17},{2,10},{10... | collective-permute-start | bytes 1572872 | tf_op jit(solution)/shard_map/ppermute | solution.py:308
  5.1 25.0 %collective-permute-start.3 = (f32[1024,128]{1,0:T(8,128)S(1)}, f32[1024,128]{1,0:T(8,128)S(1)}, u32[]{:S(2)}, u32[]{:S(2)}) collective-permute-start(f32[1024,128]{1,0:T(8,128)S(1)} %get-tuple-element.79), channel_id=1, source_target_pairs={{0,16},{8,24},{16,0},{24,8},{1,17},{9,25},{17,1},{25,9},{2,18},{10... | collective-permute-start | bytes 1572872 | tf_op jit(solution)/shard_map/ppermute | solution.py:308
  6.6 24.0 %collective-permute-start.4 = (f32[1024,128]{1,0:T(8,128)S(1)}, f32[1024,128]{1,0:T(8,128)S(1)}, u32[]{:S(2)}, u32[]{:S(2)}) collective-permute-start(f32[1024,128]{1,0:T(8,128)S(1)} %get-tuple-element.80), channel_id=1, source_target_pairs={{0,24},{8,16},{16,8},{24,0},{1,25},{9,17},{17,9},{25,1},{2,26},{10... | collective-permute-start | bytes 1572872 | tf_op jit(solution)/shard_map/ppermute | solution.py:308
  17.8 21.8 %collective-permute-start.1 = (f32[896,128]{1,0:T(8,128)S(1)}, f32[896,128]{1,0:T(8,128)S(1)}, u32[]{:S(2)}, u32[]{:S(2)}) collective-permute-start(f32[896,128]{1,0:T(8,128)S(1)} %get-tuple-element.73), channel_id=1, source_target_pairs={{0,8},{8,0},{16,24},{24,16},{1,9},{9,1},{17,25},{25,17},{2,10},{10... | collective-permute-start | bytes 1376264 | tf_op jit(solution)/shard_map/ppermute | solution.py:308
  19.9 19.7 %collective-permute-start.2 = (f32[896,128]{1,0:T(8,128)S(1)}, f32[896,128]{1,0:T(8,128)S(1)}, u32[]{:S(2)}, u32[]{:S(2)}) collective-permute-start(f32[896,128]{1,0:T(8,128)S(1)} %get-tuple-element.74), channel_id=1, source_target_pairs={{0,16},{8,24},{16,0},{24,8},{1,17},{9,25},{17,1},{25,9},{2,18},{10... | collective-permute-start | bytes 1376264 | tf_op jit(solution)/shard_map/ppermute | solution.py:308
  32.9 6.4 %collective-permute-start.7 = (f32[1,2,128]{2,1,0:T(2,128)S(1)}, f32[1,2,128]{2,1,0:T(2,128)S(1)}, u32[]{:S(2)}, u32[]{:S(2)}) collective-permute-start(f32[1,2,128]{2,1,0:T(2,128)S(1)} %gram.1.refs_0_), channel_id=1, source_target_pairs={{0,24},{8,16},{16,8},{24,0},{1,25},{9,17},{17,9},{25,1},{2,26},{10... | collective-permute-start | bytes 3080 | tf_op jit(solution)/shard_map/ppermute | solution.py:308
  34.4 5.2 %collective-permute-start.6 = (f32[1,2,128]{2,1,0:T(2,128)S(1)}, f32[1,2,128]{2,1,0:T(2,128)S(1)}, u32[]{:S(2)}, u32[]{:S(2)}) collective-permute-start(f32[1,2,128]{2,1,0:T(2,128)S(1)} %gram.1.refs_0_), channel_id=1, source_target_pairs={{0,16},{8,24},{16,0},{24,8},{1,17},{9,25},{17,1},{25,9},{2,18},{10... | collective-permute-start | bytes 3080 | tf_op jit(solution)/shard_map/ppermute | solution.py:308
  35.9 3.7 %collective-permute-start.5 = (f32[1,2,128]{2,1,0:T(2,128)S(1)}, f32[1,2,128]{2,1,0:T(2,128)S(1)}, u32[]{:S(2)}, u32[]{:S(2)}) collective-permute-start(f32[1,2,128]{2,1,0:T(2,128)S(1)} %gram.1.refs_0_), channel_id=1, source_target_pairs={{0,8},{8,0},{16,24},{24,16},{1,9},{9,1},{17,25},{25,17},{2,10},{10... | collective-permute-start | bytes 3080 | tf_op jit(solution)/shard_map/ppermute | solution.py:308
  39.6 16.7 %collective-permute-start.12 = (f32[1152,128]{1,0:T(8,128)S(1)}, f32[1152,128]{1,0:T(8,128)S(1)}, u32[]{:S(2)}, u32[]{:S(2)}) collective-permute-start(f32[1152,128]{1,0:T(8,128)S(1)} %get-tuple-element.96), channel_id=1, source_target_pairs={{0,8},{8,0},{16,24},{24,16},{1,9},{9,1},{17,25},{25,17},{2,10},{10... | collective-permute-start | bytes 1769480 | tf_op jit(solution)/shard_map/ppermute | solution.py:308
  40.9 17.8 %collective-permute-start.13 = (f32[1152,128]{1,0:T(8,128)S(1)}, f32[1152,128]{1,0:T(8,128)S(1)}, u32[]{:S(2)}, u32[]{:S(2)}) collective-permute-start(f32[1152,128]{1,0:T(8,128)S(1)} %get-tuple-element.100), channel_id=1, source_target_pairs={{0,16},{8,24},{16,0},{24,8},{1,17},{9,25},{17,1},{25,9},{2,18},{10... | collective-permute-start | bytes 1769480 | tf_op jit(solution)/shard_map/ppermute | solution.py:308
  41.9 3.0 %collective-permute-start.10 = (f32[1,2,128]{2,1,0:T(2,128)S(1)}, f32[1,2,128]{2,1,0:T(2,128)S(1)}, u32[]{:S(2)}, u32[]{:S(2)}) collective-permute-start(f32[1,2,128]{2,1,0:T(2,128)S(1)} %add.2.refs_0_), channel_id=1, source_target_pairs={{0,3},{1,2},{2,1},{3,0},{4,7},{5,6},{6,5},{7,4},{8,11},{9,10},{10,... | collective-permute-start | bytes 3080 | tf_op jit(solution)/shard_map/ppermute | solution.py:308
  42.3 3.6 %collective-permute-start.9 = (f32[1,2,128]{2,1,0:T(2,128)S(1)}, f32[1,2,128]{2,1,0:T(2,128)S(1)}, u32[]{:S(2)}, u32[]{:S(2)}) collective-permute-start(f32[1,2,128]{2,1,0:T(2,128)S(1)} %add.2.refs_0_), channel_id=1, source_target_pairs={{0,2},{1,3},{2,0},{3,1},{4,6},{5,7},{6,4},{7,5},{8,10},{9,11},{10,... | collective-permute-start | bytes 3080 | tf_op jit(solution)/shard_map/ppermute | solution.py:308
  43.4 2.5 %collective-permute-start.8 = (f32[1,2,128]{2,1,0:T(2,128)S(1)}, f32[1,2,128]{2,1,0:T(2,128)S(1)}, u32[]{:S(2)}, u32[]{:S(2)}) collective-permute-start(f32[1,2,128]{2,1,0:T(2,128)S(1)} %add.2.refs_0_), channel_id=1, source_target_pairs={{0,1},{1,0},{2,3},{3,2},{4,5},{5,4},{6,7},{7,6},{8,9},{9,8},{10,11... | collective-permute-start | bytes 3080 | tf_op jit(solution)/shard_map/ppermute | solution.py:308
  45.9 4.5 %collective-permute-start.11 = (f32[1,2,128]{2,1,0:T(2,128)S(1)}, f32[1,2,128]{2,1,0:T(2,128)S(1)}, u32[]{:S(2)}, u32[]{:S(2)}) collective-permute-start(f32[1,2,128]{2,1,0:T(2,128)S(1)} %add.3.refs_0_), channel_id=1, source_target_pairs={{0,4},{1,5},{2,6},{3,7},{4,0},{5,1},{6,2},{7,3},{8,12},{9,13},{10,... | collective-permute-start | bytes 3080 | tf_op jit(solution)/shard_map/ppermute | solution.py:308
  52.5 23.3 %collective-permute-start.15 = (f32[1024,128]{1,0:T(8,128)S(1)}, f32[1024,128]{1,0:T(8,128)S(1)}, u32[]{:S(2)}, u32[]{:S(2)}) collective-permute-start(f32[1024,128]{1,0:T(8,128)S(1)} %mix.10), channel_id=1, source_target_pairs={{0,16},{8,24},{16,0},{24,8},{1,17},{9,25},{17,1},{25,9},{2,18},{10... | collective-permute-start | bytes 1572872 | tf_op jit(solution)/shard_map/ppermute | solution.py:308
  54.2 9.3 %collective-permute-start.20 = (f32[512,128]{1,0:T(8,128)S(1)}, f32[512,128]{1,0:T(8,128)S(1)}, u32[]{:S(2)}, u32[]{:S(2)}) collective-permute-start(f32[512,128]{1,0:T(8,128)S(1)} %mix.12), channel_id=1, source_target_pairs={{0,8},{8,0},{16,24},{24,16},{1,9},{9,1},{17,25},{25,17},{2,10},{10... | collective-permute-start | bytes 786440 | tf_op jit(solution)/shard_map/ppermute | solution.py:308
  55.3 18.3 %collective-permute-start.22 = (f32[512,128]{1,0:T(8,128)S(1)}, f32[512,128]{1,0:T(8,128)S(1)}, u32[]{:S(2)}, u32[]{:S(2)}) collective-permute-start(f32[512,128]{1,0:T(8,128)S(1)} %mix.11), channel_id=1, source_target_pairs={{0,16},{8,24},{16,0},{24,8},{1,17},{9,25},{17,1},{25,9},{2,18},{10... | collective-permute-start | bytes 786440 | tf_op jit(solution)/shard_map/ppermute | solution.py:308
  56.3 20.2 %collective-permute-start.14 = (f32[1024,128]{1,0:T(8,128)S(1)}, f32[1024,128]{1,0:T(8,128)S(1)}, u32[]{:S(2)}, u32[]{:S(2)}) collective-permute-start(f32[1024,128]{1,0:T(8,128)S(1)} %mix.9), channel_id=1, source_target_pairs={{0,8},{8,0},{16,24},{24,16},{1,9},{9,1},{17,25},{25,17},{2,10},{10... | collective-permute-start | bytes 1572872 | tf_op jit(solution)/shard_map/ppermute | solution.py:308
  58.7 26.1 %collective-permute-start.16 = (f32[1024,128]{1,0:T(8,128)S(1)}, f32[1024,128]{1,0:T(8,128)S(1)}, u32[]{:S(2)}, u32[]{:S(2)}) collective-permute-start(f32[1024,128]{1,0:T(8,128)S(1)} %mix.13), channel_id=1, source_target_pairs={{0,16},{8,24},{16,0},{24,8},{1,17},{9,25},{17,1},{25,9},{2,18},{10... | collective-permute-start | bytes 1572872 | tf_op jit(solution)/shard_map/ppermute | solution.py:308
  63.5 28.0 %collective-permute-start.17 = (f32[1024,128]{1,0:T(8,128)S(1)}, f32[1024,128]{1,0:T(8,128)S(1)}, u32[]{:S(2)}, u32[]{:S(2)}) collective-permute-start(f32[1024,128]{1,0:T(8,128)S(1)} %mix.14), channel_id=1, source_target_pairs={{0,8},{8,0},{16,24},{24,16},{1,9},{9,1},{17,25},{25,17},{2,10},{10... | collective-permute-start | bytes 1572872 | tf_op jit(solution)/shard_map/ppermute | solution.py:308
  73.6 22.5 %collective-permute-start.18 = (f32[1024,128]{1,0:T(8,128)S(1)}, f32[1024,128]{1,0:T(8,128)S(1)}, u32[]{:S(2)}, u32[]{:S(2)}) collective-permute-start(f32[1024,128]{1,0:T(8,128)S(1)} %mix.15), channel_id=1, source_target_pairs={{0,16},{8,24},{16,0},{24,8},{1,17},{9,25},{17,1},{25,9},{2,18},{10... | collective-permute-start | bytes 1572872 | tf_op jit(solution)/shard_map/ppermute | solution.py:308
  75.8 21.4 %collective-permute-start.19 = (f32[1024,128]{1,0:T(8,128)S(1)}, f32[1024,128]{1,0:T(8,128)S(1)}, u32[]{:S(2)}, u32[]{:S(2)}) collective-permute-start(f32[1024,128]{1,0:T(8,128)S(1)} %mix.16), channel_id=1, source_target_pairs={{0,8},{8,0},{16,24},{24,16},{1,9},{9,1},{17,25},{25,17},{2,10},{10... | collective-permute-start | bytes 1572872 | tf_op jit(solution)/shard_map/ppermute | solution.py:308
  76.6 24.0 %collective-permute-start.21 = (f32[512,128]{1,0:T(8,128)S(1)}, f32[512,128]{1,0:T(8,128)S(1)}, u32[]{:S(2)}, u32[]{:S(2)}) collective-permute-start(f32[512,128]{1,0:T(8,128)S(1)} %collective-permute-done.20), channel_id=1, source_target_pairs={{0,16},{8,24},{16,0},{24,8},{1,17},{9,25},{17,1},{25,9},{2,18},{10... | collective-permute-start | bytes 786440 | tf_op jit(solution)/shard_map/ppermute | solution.py:308
  84.9 16.0 %collective-permute-start.23 = (f32[512,128]{1,0:T(8,128)S(1)}, f32[512,128]{1,0:T(8,128)S(1)}, u32[]{:S(2)}, u32[]{:S(2)}) collective-permute-start(f32[512,128]{1,0:T(8,128)S(1)} %collective-permute-done.22), channel_id=1, source_target_pairs={{0,8},{8,0},{16,24},{24,16},{1,9},{9,1},{17,25},{25,17},{2,10},{10... | collective-permute-start | bytes 786440 | tf_op jit(solution)/shard_map/ppermute | solution.py:308

commit v11 on v9

--- a/solution.py
+++ b/solution.py
@@ -317,7 +317,7 @@
     direct = [k for k in everyone[1:] if k in lows or k in highs]
     distant = [k for k in everyone[1:] if k not in direct]
     size, step = x.shape[0], SUB * rows
-    first = max(1, half // step * 7 // 16) * step
+    first = max(1, half // step * 5 // 16) * step
     split = part // step // 2 * step
     halves = [(0, split), (split, part - split)]
 

time: 102 us -> 102 us (level)
  starting transfers between devices: 28.4 us -> 29.9 us
  waiting for transfers between devices: 46.3 us -> 44.8 us
    ppermute x24, waiting for transfers between devices: 46.3 us -> 44.8 us  [swap(): lax.ppermute(block, axis, [(i, i ^ k) for i in range(lax.axis_size(axis))])]
    ppermute x24, starting transfers between devices: 28.4 us -> 29.9 us  [swap(): lax.ppermute(block, axis, [(i, i ^ k) for i in range(lax.axis_size(axis))])]
  transfers between devices with their start and end apart: 24 -> 24, of which waited for: 14 -> 12; matrix products, arithmetic and copies ran while one was open for 0% -> 0% of each run, Pallas kernels for 23% -> 23%
where the time goes in v11:
time: 102 us
  waiting for transfers between devices  44.8 us (44%)
  starting transfers between devices  29.9 us (29%)
  Pallas kernels  25.4 us (25%)
  between operations  1.51 us (1%)
    ppermute x24, waiting for transfers between devices, swap(): lax.ppermute(block, axis, [(i, i ^ k) for i in range(lax.axis_size(axis))])  44.8 us
    ppermute x24, starting transfers between devices, swap(): lax.ppermute(block, axis, [(i, i ^ k) for i in range(lax.axis_size(axis))])  29.9 us
    pallas_call x9, Pallas kernels, mix(): pl.pallas_call(functools.partial(mix_kernel, rows, count, [(*job[:3], [bl...  9.92 us
    pallas_call x8, Pallas kernels, put(): pl.pallas_call(functools.partial(put_kernel, entries, part, len(blocks)),...  6.68 us
    pallas_call x3, Pallas kernels, cut(): pl.pallas_call(functools.partial(cut_kernel, places, part), out_shape=[ou...  5.38 us
    pallas_call x2, Pallas kernels, gram(): pl.pallas_call(functools.partial(gram_kernel, rows, groups, pairs), out_s...  2.52 us
  transfers between devices with their start and end apart: 24, of which 12 were waited for; matrix products, arithmetic and copies ran while one was open for 0% of the time, Pallas kernels for 23%

profile of v11, /device:TPU:0, one launch (start us, length us, event | category | flops | bytes accessed | tf_op | source)
XLA Modules:
  0.0 101.6 jit_solution(4479383687799092518)
XLA Ops:
  0.6 1.4 %cut.3 = (f32[1024,128]{1,0:T(8,128)S(1)}, f32[1024,128]{1,0:T(8,128)S(1)}, f32[1024,128]{1,0:T(8,128)S(1)}) custom-call(f32[4096,128]{1,0:T(8,128)} %bitcast.35), custom_call_target="tpu_custom_call" | custom-call | flops 1 | bytes 1 | tf_op jit(solution)/shard_map/cut/pallas_call | solution.py:285
  2.1 3.0 %collective-permute-start = (f32[1024,128]{1,0:T(8,128)S(1)}, f32[1024,128]{1,0:T(8,128)S(1)}, u32[]{:S(2)}, u32[]{:S(2)}) collective-permute-start(f32[1024,128]{1,0:T(8,128)S(1)} %get-tuple-element.67), channel_id=1, source_target_pairs={{0,8},{8,0},{16,24},{24,16},{1,9},{9,1},{17,25},{25,17},{2,10},{10... | collective-permute-start | bytes 1572872 | tf_op jit(solution)/shard_map/ppermute | solution.py:307
  5.1 1.5 %collective-permute-start.3 = (f32[1024,128]{1,0:T(8,128)S(1)}, f32[1024,128]{1,0:T(8,128)S(1)}, u32[]{:S(2)}, u32[]{:S(2)}) collective-permute-start(f32[1024,128]{1,0:T(8,128)S(1)} %get-tuple-element.79), channel_id=1, source_target_pairs={{0,16},{8,24},{16,0},{24,8},{1,17},{9,25},{17,1},{25,9},{2,18},{10... | collective-permute-start | bytes 1572872 | tf_op jit(solution)/shard_map/ppermute | solution.py:307
  6.6 2.9 %cut.4 = (f32[640,128]{1,0:T(8,128)}, f32[1408,128]{1,0:T(8,128)}, f32[640,128]{1,0:T(8,128)}, f32[1408,128]{1,0:T(8,128)}) custom-call(f32[4096,128]{1,0:T(8,128)} %bitcast.20), custom_call_target="tpu_custom_call" | custom-call | flops 1 | bytes 1 | tf_op jit(solution)/shard_map/cut/pallas_call | solution.py:285
  9.5 8.3 %collective-permute-done.refs_1_.refs_5_ = f32[1024,128]{1,0:T(8,128)S(1)} collective-permute-done((f32[1024,128]{1,0:T(8,128)S(1)}, f32[1024,128]{1,0:T(8,128)S(1)}, u32[]{:S(2)}, u32[]{:S(2)}) %collective-permute-start) | collective-permute-done | bytes 524320 | tf_op jit(solution)/shard_map/ppermute | solution.py:307
  17.8 2.1 %collective-permute-start.1 = (f32[640,128]{1,0:T(8,128)}, f32[640,128]{1,0:T(8,128)S(1)}, u32[]{:S(2)}, u32[]{:S(2)}) collective-permute-start(f32[640,128]{1,0:T(8,128)} %get-tuple-element.73), channel_id=1, source_target_pairs={{0,8},{8,0},{16,24},{24,16},{1,9},{9,1},{17,25},{25,17},{2,10},{10... | collective-permute-start | bytes 983048 | tf_op jit(solution)/shard_map/ppermute | solution.py:307
  19.9 1.5 %collective-permute-start.2 = (f32[640,128]{1,0:T(8,128)}, f32[640,128]{1,0:T(8,128)S(1)}, u32[]{:S(2)}, u32[]{:S(2)}) collective-permute-start(f32[640,128]{1,0:T(8,128)} %get-tuple-element.74), channel_id=1, source_target_pairs={{0,16},{8,24},{16,0},{24,8},{1,17},{9,25},{17,1},{25,9},{2,18},{10... | collective-permute-start | bytes 983048 | tf_op jit(solution)/shard_map/ppermute | solution.py:307
  22.5 7.6 %collective-permute-done.3.refs_2_.refs_6_ = f32[1024,128]{1,0:T(8,128)S(1)} collective-permute-done((f32[1024,128]{1,0:T(8,128)S(1)}, f32[1024,128]{1,0:T(8,128)S(1)}, u32[]{:S(2)}, u32[]{:S(2)}) %collective-permute-start.3) | collective-permute-done | bytes 524320 | tf_op jit(solution)/shard_map/ppermute | solution.py:307
  30.1 1.4 %gram.2.refs_4_ = f32[1,2,128]{2,1,0:T(2,128)S(1)} custom-call(f32[1024,128]{1,0:T(8,128)S(1)} %cut.5.refs_0_.refs_3_.refs_4_, f32[1024,128]{1,0:T(8,128)S(1)} %collective-permute-done.refs_1_.refs_5_, f32[1024,128]{1,0:T(8,128)S(1)} %collective-permute-done.3.refs_2_.refs_6_, f32[1024,128]{1,0:T(8,128)S(1)} %cut.5.refs_0_.refs_3_.refs_4_), custom_call_target="tpu_custom_call" | custom-call | flops 1 | bytes 1 | tf_op jit(solution)/shard_map/gram/pallas_call | solution.py:84
  33.2 2.0 %collective-permute-start.6 = (f32[1,2,128]{2,1,0:T(2,128)S(1)}, f32[1,2,128]{2,1,0:T(2,128)S(1)}, u32[]{:S(2)}, u32[]{:S(2)}) collective-permute-start(f32[1,2,128]{2,1,0:T(2,128)S(1)} %gram.3.refs_0_), channel_id=1, source_target_pairs={{0,16},{8,24},{16,0},{24,8},{1,17},{9,25},{17,1},{25,9},{2,18},{10... | collective-permute-start | bytes 3080 | tf_op jit(solution)/shard_map/ppermute | solution.py:307
  35.1 1.4 %collective-permute-start.5 = (f32[1,2,128]{2,1,0:T(2,128)S(1)}, f32[1,2,128]{2,1,0:T(2,128)S(1)}, u32[]{:S(2)}, u32[]{:S(2)}) collective-permute-start(f32[1,2,128]{2,1,0:T(2,128)S(1)} %gram.3.refs_0_), channel_id=1, source_target_pairs={{0,8},{8,0},{16,24},{24,16},{1,9},{9,1},{17,25},{25,17},{2,10},{10... | collective-permute-start | bytes 3080 | tf_op jit(solution)/shard_map/ppermute | solution.py:307
  37.1 1.6 %collective-permute-done.5.refs_1_ = f32[1,2,128]{2,1,0:T(2,128)S(1)} collective-permute-done((f32[1,2,128]{2,1,0:T(2,128)S(1)}, f32[1,2,128]{2,1,0:T(2,128)S(1)}, u32[]{:S(2)}, u32[]{:S(2)}) %collective-permute-start.5) | collective-permute-done | bytes 1056 | tf_op jit(solution)/shard_map/ppermute | solution.py:307
  38.7 1.5 %collective-permute-start.12 = (f32[1408,128]{1,0:T(8,128)S(1)}, f32[1408,128]{1,0:T(8,128)S(1)}, u32[]{:S(2)}, u32[]{:S(2)}) collective-permute-start(f32[1408,128]{1,0:T(8,128)S(1)} %copy-done.1), channel_id=1, source_target_pairs={{0,8},{8,0},{16,24},{24,16},{1,9},{9,1},{17,25},{25,17},{2,10},{10... | collective-permute-start | bytes 2162696 | tf_op jit(solution)/shard_map/ppermute | solution.py:307
  40.2 2.0 %collective-permute-start.13 = (f32[1408,128]{1,0:T(8,128)S(1)}, f32[1408,128]{1,0:T(8,128)S(1)}, u32[]{:S(2)}, u32[]{:S(2)}) collective-permute-start(f32[1408,128]{1,0:T(8,128)S(1)} %copy-done), channel_id=1, source_target_pairs={{0,16},{8,24},{16,0},{24,8},{1,17},{9,25},{17,1},{25,9},{2,18},{10... | collective-permute-start | bytes 2162696 | tf_op jit(solution)/shard_map/ppermute | solution.py:307
  42.3 1.4 %collective-permute-start.9 = (f32[1,2,128]{2,1,0:T(2,128)S(1)}, f32[1,2,128]{2,1,0:T(2,128)S(1)}, u32[]{:S(2)}, u32[]{:S(2)}) collective-permute-start(f32[1,2,128]{2,1,0:T(2,128)S(1)} %add.2.refs_0_), channel_id=1, source_target_pairs={{0,2},{1,3},{2,0},{3,1},{4,6},{5,7},{6,4},{7,5},{8,10},{9,11},{10,... | collective-permute-start | bytes 3080 | tf_op jit(solution)/shard_map/ppermute | solution.py:307
  45.9 2.4 %collective-permute-start.11 = (f32[1,2,128]{2,1,0:T(2,128)S(1)}, f32[1,2,128]{2,1,0:T(2,128)S(1)}, u32[]{:S(2)}, u32[]{:S(2)}) collective-permute-start(f32[1,2,128]{2,1,0:T(2,128)S(1)} %add.3.refs_0_), channel_id=1, source_target_pairs={{0,4},{1,5},{2,6},{3,7},{4,0},{5,1},{6,2},{7,3},{8,12},{9,13},{10,... | collective-permute-start | bytes 3080 | tf_op jit(solution)/shard_map/ppermute | solution.py:307
  49.0 1.5 %collective-permute-done.11.refs_1_ = f32[1,2,128]{2,1,0:T(2,128)S(1)} collective-permute-done((f32[1,2,128]{2,1,0:T(2,128)S(1)}, f32[1,2,128]{2,1,0:T(2,128)S(1)}, u32[]{:S(2)}, u32[]{:S(2)}) %collective-permute-start.11) | collective-permute-done | bytes 1056 | tf_op jit(solution)/shard_map/ppermute | solution.py:307
  53.9 1.5 %collective-permute-start.22 = (f32[512,128]{1,0:T(8,128)S(1)}, f32[512,128]{1,0:T(8,128)S(1)}, u32[]{:S(2)}, u32[]{:S(2)}) collective-permute-start(f32[512,128]{1,0:T(8,128)S(1)} %mix.11), channel_id=1, source_target_pairs={{0,16},{8,24},{16,0},{24,8},{1,17},{9,25},{17,1},{25,9},{2,18},{10... | collective-permute-start | bytes 786440 | tf_op jit(solution)/shard_map/ppermute | solution.py:307
  55.5 1.9 %collective-permute-start.14 = (f32[1024,128]{1,0:T(8,128)S(1)}, f32[1024,128]{1,0:T(8,128)S(1)}, u32[]{:S(2)}, u32[]{:S(2)}) collective-permute-start(f32[1024,128]{1,0:T(8,128)S(1)} %mix.9), channel_id=1, source_target_pairs={{0,8},{8,0},{16,24},{24,16},{1,9},{9,1},{17,25},{25,17},{2,10},{10... | collective-permute-start | bytes 1572872 | tf_op jit(solution)/shard_map/ppermute | solution.py:307
  57.4 1.3 %mix.13 = f32[1024,128]{1,0:T(8,128)S(1)} custom-call(f32[256,128]{1,0:T(8,128)S(1)} %get-tuple-element.105.drive_ref, f32[256,128]{1,0:T(8,128)S(1)} %get-tuple-element.106.repel_ref, f32[4096,128]{1,0:T(8,128)} %bitcast.21, f32[640,128]{1,0:T(8,128)S(1)} %collective-permute-done.1.refs_1_.refs_9_, f32[4096,128]{1,0:T(8,128)} %bitcast.22, ...), custom_call_target="tpu_custom_call" | custom-call | flops 1 | bytes 1 | tf_op jit(solution)/shard_map/mix/pallas_call | solution.py:210
  58.9 1.3 %mix.14 = f32[1024,128]{1,0:T(8,128)S(1)} custom-call(f32[256,128]{1,0:T(8,128)S(1)} %get-tuple-element.105.drive_ref, f32[256,128]{1,0:T(8,128)S(1)} %get-tuple-element.106.repel_ref, f32[4096,128]{1,0:T(8,128)} %bitcast.23, f32[640,128]{1,0:T(8,128)S(1)} %collective-permute-done.2.refs_1_.refs_13_, f32[4096,128]{1,0:T(8,128)} %bitcast.24, ...), custom_call_target="tpu_custom_call" | custom-call | flops 1 | bytes 1 | tf_op jit(solution)/shard_map/mix/pallas_call | solution.py:210
  60.2 2.4 %collective-permute-done.20 = f32[512,128]{1,0:T(8,128)S(1)} collective-permute-done((f32[512,128]{1,0:T(8,128)S(1)}, f32[512,128]{1,0:T(8,128)S(1)}, u32[]{:S(2)}, u32[]{:S(2)}) %collective-permute-start.20) | collective-permute-done | bytes 262176 | tf_op jit(solution)/shard_map/ppermute | solution.py:307
  63.2 1.3 %mix.15 = f32[1024,128]{1,0:T(8,128)S(1)} custom-call(f32[256,128]{1,0:T(8,128)S(1)} %get-tuple-element.105.drive_ref, f32[256,128]{1,0:T(8,128)S(1)} %get-tuple-element.106.repel_ref, f32[4096,128]{1,0:T(8,128)} %bitcast.25, f32[1408,128]{1,0:T(8,128)S(1)} %collective-permute-done.12.refs_3_.refs_1_.refs_11_.refs_17_), custom_call_target="tpu_custom_call" | custom-call | flops 1 | bytes 1 | tf_op jit(solution)/shard_map/mix/pallas_call | solution.py:210
  64.5 9.3 %collective-permute-done.22 = f32[512,128]{1,0:T(8,128)S(1)} collective-permute-done((f32[512,128]{1,0:T(8,128)S(1)}, f32[512,128]{1,0:T(8,128)S(1)}, u32[]{:S(2)}, u32[]{:S(2)}) %collective-permute-start.22) | collective-permute-done | bytes 262176 | tf_op jit(solution)/shard_map/ppermute | solution.py:307
  73.8 1.3 %collective-permute-start.18 = (f32[1024,128]{1,0:T(8,128)S(1)}, f32[1024,128]{1,0:T(8,128)S(1)}, u32[]{:S(2)}, u32[]{:S(2)}) collective-permute-start(f32[1024,128]{1,0:T(8,128)S(1)} %mix.15), channel_id=1, source_target_pairs={{0,16},{8,24},{16,0},{24,8},{1,17},{9,25},{17,1},{25,9},{2,18},{10... | collective-permute-start | bytes 1572872 | tf_op jit(solution)/shard_map/ppermute | solution.py:307
  75.1 1.3 %mix.16 = f32[1024,128]{1,0:T(8,128)S(1)} custom-call(f32[256,128]{1,0:T(8,128)S(1)} %get-tuple-element.105.drive_ref, f32[256,128]{1,0:T(8,128)S(1)} %get-tuple-element.106.repel_ref, f32[4096,128]{1,0:T(8,128)} %bitcast.26, f32[1408,128]{1,0:T(8,128)S(1)} %collective-permute-done.13.refs_3_.refs_1_.refs_15_.refs_19_), custom_call_target="tpu_custom_call" | custom-call | flops 1 | bytes 1 | tf_op jit(solution)/shard_map/mix/pallas_call | solution.py:210
  77.0 1.8 %collective-permute-start.21 = (f32[512,128]{1,0:T(8,128)S(1)}, f32[512,128]{1,0:T(8,128)S(1)}, u32[]{:S(2)}, u32[]{:S(2)}) collective-permute-start(f32[512,128]{1,0:T(8,128)S(1)} %collective-permute-done.20), channel_id=1, source_target_pairs={{0,16},{8,24},{16,0},{24,8},{1,17},{9,25},{17,1},{25,9},{2,18},{10... | collective-permute-start | bytes 786440 | tf_op jit(solution)/shard_map/ppermute | solution.py:307
  78.8 6.3 %collective-permute-done.16.refs_1_ = f32[1024,128]{1,0:T(8,128)S(1)} collective-permute-done((f32[1024,128]{1,0:T(8,128)S(1)}, f32[1024,128]{1,0:T(8,128)S(1)}, u32[]{:S(2)}, u32[]{:S(2)}) %collective-permute-start.16) | collective-permute-done | bytes 524320 | tf_op jit(solution)/shard_map/ppermute | solution.py:307
  85.1 1.5 %collective-permute-start.23 = (f32[512,128]{1,0:T(8,128)S(1)}, f32[512,128]{1,0:T(8,128)S(1)}, u32[]{:S(2)}, u32[]{:S(2)}) collective-permute-start(f32[512,128]{1,0:T(8,128)S(1)} %collective-permute-done.22), channel_id=1, source_target_pairs={{0,8},{8,0},{16,24},{24,16},{1,9},{9,1},{17,25},{25,17},{2,10},{10... | collective-permute-start | bytes 786440 | tf_op jit(solution)/shard_map/ppermute | solution.py:307
  86.6 2.7 %mix.17.refs_0_ = f32[5120,128]{1,0:T(8,128)S(1)} custom-call(f32[256,128]{1,0:T(8,128)S(1)} %get-tuple-element.105.drive_ref, f32[256,128]{1,0:T(8,128)S(1)} %get-tuple-element.106.repel_ref, f32[1024,128]{1,0:T(8,128)S(1)} %cut.5.refs_0_.refs_3_.refs_4_, f32[1024,128]{1,0:T(8,128)S(1)} %collective-permute-done.refs_1_.refs_5_, ...), custom_call_target="tpu_custom_call" | custom-call | flops 1 | bytes 1 | tf_op jit(solution)/shard_map/mix/pallas_call | solution.py:210
  93.5 2.8 %collective-permute-done.18.refs_1_ = f32[1024,128]{1,0:T(8,128)S(1)} collective-permute-done((f32[1024,128]{1,0:T(8,128)S(1)}, f32[1024,128]{1,0:T(8,128)S(1)}, u32[]{:S(2)}, u32[]{:S(2)}) %collective-permute-start.18) | collective-permute-done | bytes 524320 | tf_op jit(solution)/shard_map/ppermute | solution.py:307
  98.0 2.7 %collective-permute-done.21.refs_0_ = f32[512,128]{1,0:T(8,128)S(1)} collective-permute-done((f32[512,128]{1,0:T(8,128)S(1)}, f32[512,128]{1,0:T(8,128)S(1)}, u32[]{:S(2)}, u32[]{:S(2)}) %collective-permute-start.21) | collective-permute-done | bytes 262176 | tf_op jit(solution)/shard_map/ppermute | solution.py:307
  (45 shorter events, 16.9 us)
Async XLA Ops:
  2.1 15.8 %collective-permute-start = (f32[1024,128]{1,0:T(8,128)S(1)}, f32[1024,128]{1,0:T(8,128)S(1)}, u32[]{:S(2)}, u32[]{:S(2)}) collective-permute-start(f32[1024,128]{1,0:T(8,128)S(1)} %get-tuple-element.67), channel_id=1, source_target_pairs={{0,8},{8,0},{16,24},{24,16},{1,9},{9,1},{17,25},{25,17},{2,10},{10... | collective-permute-start | bytes 1572872 | tf_op jit(solution)/shard_map/ppermute | solution.py:307
  5.1 25.0 %collective-permute-start.3 = (f32[1024,128]{1,0:T(8,128)S(1)}, f32[1024,128]{1,0:T(8,128)S(1)}, u32[]{:S(2)}, u32[]{:S(2)}) collective-permute-start(f32[1024,128]{1,0:T(8,128)S(1)} %get-tuple-element.79), channel_id=1, source_target_pairs={{0,16},{8,24},{16,0},{24,8},{1,17},{9,25},{17,1},{25,9},{2,18},{10... | collective-permute-start | bytes 1572872 | tf_op jit(solution)/shard_map/ppermute | solution.py:307
  6.6 24.9 %collective-permute-start.4 = (f32[1024,128]{1,0:T(8,128)S(1)}, f32[1024,128]{1,0:T(8,128)S(1)}, u32[]{:S(2)}, u32[]{:S(2)}) collective-permute-start(f32[1024,128]{1,0:T(8,128)S(1)} %get-tuple-element.80), channel_id=1, source_target_pairs={{0,24},{8,16},{16,8},{24,0},{1,25},{9,17},{17,9},{25,1},{2,26},{10... | collective-permute-start | bytes 1572872 | tf_op jit(solution)/shard_map/ppermute | solution.py:307
  17.8 20.9 %collective-permute-start.1 = (f32[640,128]{1,0:T(8,128)}, f32[640,128]{1,0:T(8,128)S(1)}, u32[]{:S(2)}, u32[]{:S(2)}) collective-permute-start(f32[640,128]{1,0:T(8,128)} %get-tuple-element.73), channel_id=1, source_target_pairs={{0,8},{8,0},{16,24},{24,16},{1,9},{9,1},{17,25},{25,17},{2,10},{10... | collective-permute-start | bytes 983048 | tf_op jit(solution)/shard_map/ppermute | solution.py:307
  19.9 18.8 %collective-permute-start.2 = (f32[640,128]{1,0:T(8,128)}, f32[640,128]{1,0:T(8,128)S(1)}, u32[]{:S(2)}, u32[]{:S(2)}) collective-permute-start(f32[640,128]{1,0:T(8,128)} %get-tuple-element.74), channel_id=1, source_target_pairs={{0,16},{8,24},{16,0},{24,8},{1,17},{9,25},{17,1},{25,9},{2,18},{10... | collective-permute-start | bytes 983048 | tf_op jit(solution)/shard_map/ppermute | solution.py:307
  22.5 16.2 %copy-start.1 = (f32[1408,128]{1,0:T(8,128)S(1)}, f32[1408,128]{1,0:T(8,128)}, u32[]{:S(2)}) copy-start(f32[1408,128]{1,0:T(8,128)} %get-tuple-element.96) | copy-start | bytes 2162692
  22.5 17.8 %copy-start = (f32[1408,128]{1,0:T(8,128)S(1)}, f32[1408,128]{1,0:T(8,128)}, u32[]{:S(2)}) copy-start(f32[1408,128]{1,0:T(8,128)} %get-tuple-element.100) | copy-start | bytes 2162692
  32.6 4.5 %collective-permute-start.7 = (f32[1,2,128]{2,1,0:T(2,128)S(1)}, f32[1,2,128]{2,1,0:T(2,128)S(1)}, u32[]{:S(2)}, u32[]{:S(2)}) collective-permute-start(f32[1,2,128]{2,1,0:T(2,128)S(1)} %gram.3.refs_0_), channel_id=1, source_target_pairs={{0,24},{8,16},{16,8},{24,0},{1,25},{9,17},{17,9},{25,1},{2,26},{10... | collective-permute-start | bytes 3080 | tf_op jit(solution)/shard_map/ppermute | solution.py:307
  33.2 3.9 %collective-permute-start.6 = (f32[1,2,128]{2,1,0:T(2,128)S(1)}, f32[1,2,128]{2,1,0:T(2,128)S(1)}, u32[]{:S(2)}, u32[]{:S(2)}) collective-permute-start(f32[1,2,128]{2,1,0:T(2,128)S(1)} %gram.3.refs_0_), channel_id=1, source_target_pairs={{0,16},{8,24},{16,0},{24,8},{1,17},{9,25},{17,1},{25,9},{2,18},{10... | collective-permute-start | bytes 3080 | tf_op jit(solution)/shard_map/ppermute | solution.py:307
  35.1 3.6 %collective-permute-start.5 = (f32[1,2,128]{2,1,0:T(2,128)S(1)}, f32[1,2,128]{2,1,0:T(2,128)S(1)}, u32[]{:S(2)}, u32[]{:S(2)}) collective-permute-start(f32[1,2,128]{2,1,0:T(2,128)S(1)} %gram.3.refs_0_), channel_id=1, source_target_pairs={{0,8},{8,0},{16,24},{24,16},{1,9},{9,1},{17,25},{25,17},{2,10},{10... | collective-permute-start | bytes 3080 | tf_op jit(solution)/shard_map/ppermute | solution.py:307
  38.7 16.7 %collective-permute-start.12 = (f32[1408,128]{1,0:T(8,128)S(1)}, f32[1408,128]{1,0:T(8,128)S(1)}, u32[]{:S(2)}, u32[]{:S(2)}) collective-permute-start(f32[1408,128]{1,0:T(8,128)S(1)} %copy-done.1), channel_id=1, source_target_pairs={{0,8},{8,0},{16,24},{24,16},{1,9},{9,1},{17,25},{25,17},{2,10},{10... | collective-permute-start | bytes 2162696 | tf_op jit(solution)/shard_map/ppermute | solution.py:307
  40.2 18.5 %collective-permute-start.13 = (f32[1408,128]{1,0:T(8,128)S(1)}, f32[1408,128]{1,0:T(8,128)S(1)}, u32[]{:S(2)}, u32[]{:S(2)}) collective-permute-start(f32[1408,128]{1,0:T(8,128)S(1)} %copy-done), channel_id=1, source_target_pairs={{0,16},{8,24},{16,0},{24,8},{1,17},{9,25},{17,1},{25,9},{2,18},{10... | collective-permute-start | bytes 2162696 | tf_op jit(solution)/shard_map/ppermute | solution.py:307
  42.3 3.0 %collective-permute-start.10 = (f32[1,2,128]{2,1,0:T(2,128)S(1)}, f32[1,2,128]{2,1,0:T(2,128)S(1)}, u32[]{:S(2)}, u32[]{:S(2)}) collective-permute-start(f32[1,2,128]{2,1,0:T(2,128)S(1)} %add.2.refs_0_), channel_id=1, source_target_pairs={{0,3},{1,2},{2,1},{3,0},{4,7},{5,6},{6,5},{7,4},{8,11},{9,10},{10,... | collective-permute-start | bytes 3080 | tf_op jit(solution)/shard_map/ppermute | solution.py:307
  42.3 3.6 %collective-permute-start.9 = (f32[1,2,128]{2,1,0:T(2,128)S(1)}, f32[1,2,128]{2,1,0:T(2,128)S(1)}, u32[]{:S(2)}, u32[]{:S(2)}) collective-permute-start(f32[1,2,128]{2,1,0:T(2,128)S(1)} %add.2.refs_0_), channel_id=1, source_target_pairs={{0,2},{1,3},{2,0},{3,1},{4,6},{5,7},{6,4},{7,5},{8,10},{9,11},{10,... | collective-permute-start | bytes 3080 | tf_op jit(solution)/shard_map/ppermute | solution.py:307
  43.6 2.2 %collective-permute-start.8 = (f32[1,2,128]{2,1,0:T(2,128)S(1)}, f32[1,2,128]{2,1,0:T(2,128)S(1)}, u32[]{:S(2)}, u32[]{:S(2)}) collective-permute-start(f32[1,2,128]{2,1,0:T(2,128)S(1)} %add.2.refs_0_), channel_id=1, source_target_pairs={{0,1},{1,0},{2,3},{3,2},{4,5},{5,4},{6,7},{7,6},{8,9},{9,8},{10,11... | collective-permute-start | bytes 3080 | tf_op jit(solution)/shard_map/ppermute | solution.py:307
  45.9 4.5 %collective-permute-start.11 = (f32[1,2,128]{2,1,0:T(2,128)S(1)}, f32[1,2,128]{2,1,0:T(2,128)S(1)}, u32[]{:S(2)}, u32[]{:S(2)}) collective-permute-start(f32[1,2,128]{2,1,0:T(2,128)S(1)} %add.3.refs_0_), channel_id=1, source_target_pairs={{0,4},{1,5},{2,6},{3,7},{4,0},{5,1},{6,2},{7,3},{8,12},{9,13},{10,... | collective-permute-start | bytes 3080 | tf_op jit(solution)/shard_map/ppermute | solution.py:307
  52.6 23.9 %collective-permute-start.15 = (f32[1024,128]{1,0:T(8,128)S(1)}, f32[1024,128]{1,0:T(8,128)S(1)}, u32[]{:S(2)}, u32[]{:S(2)}) collective-permute-start(f32[1024,128]{1,0:T(8,128)S(1)} %mix.10), channel_id=1, source_target_pairs={{0,16},{8,24},{16,0},{24,8},{1,17},{9,25},{17,1},{25,9},{2,18},{10... | collective-permute-start | bytes 1572872 | tf_op jit(solution)/shard_map/ppermute | solution.py:307
  53.4 9.3 %collective-permute-start.20 = (f32[512,128]{1,0:T(8,128)S(1)}, f32[512,128]{1,0:T(8,128)S(1)}, u32[]{:S(2)}, u32[]{:S(2)}) collective-permute-start(f32[512,128]{1,0:T(8,128)S(1)} %mix.12), channel_id=1, source_target_pairs={{0,8},{8,0},{16,24},{24,16},{1,9},{9,1},{17,25},{25,17},{2,10},{10... | collective-permute-start | bytes 786440 | tf_op jit(solution)/shard_map/ppermute | solution.py:307
  53.9 19.9 %collective-permute-start.22 = (f32[512,128]{1,0:T(8,128)S(1)}, f32[512,128]{1,0:T(8,128)S(1)}, u32[]{:S(2)}, u32[]{:S(2)}) collective-permute-start(f32[512,128]{1,0:T(8,128)S(1)} %mix.11), channel_id=1, source_target_pairs={{0,16},{8,24},{16,0},{24,8},{1,17},{9,25},{17,1},{25,9},{2,18},{10... | collective-permute-start | bytes 786440 | tf_op jit(solution)/shard_map/ppermute | solution.py:307
  55.5 21.5 %collective-permute-start.14 = (f32[1024,128]{1,0:T(8,128)S(1)}, f32[1024,128]{1,0:T(8,128)S(1)}, u32[]{:S(2)}, u32[]{:S(2)}) collective-permute-start(f32[1024,128]{1,0:T(8,128)S(1)} %mix.9), channel_id=1, source_target_pairs={{0,8},{8,0},{16,24},{24,16},{1,9},{9,1},{17,25},{25,17},{2,10},{10... | collective-permute-start | bytes 1572872 | tf_op jit(solution)/shard_map/ppermute | solution.py:307
  58.7 26.3 %collective-permute-start.16 = (f32[1024,128]{1,0:T(8,128)S(1)}, f32[1024,128]{1,0:T(8,128)S(1)}, u32[]{:S(2)}, u32[]{:S(2)}) collective-permute-start(f32[1024,128]{1,0:T(8,128)S(1)} %mix.13), channel_id=1, source_target_pairs={{0,16},{8,24},{16,0},{24,8},{1,17},{9,25},{17,1},{25,9},{2,18},{10... | collective-permute-start | bytes 1572872 | tf_op jit(solution)/shard_map/ppermute | solution.py:307
  62.7 30.0 %collective-permute-start.17 = (f32[1024,128]{1,0:T(8,128)S(1)}, f32[1024,128]{1,0:T(8,128)S(1)}, u32[]{:S(2)}, u32[]{:S(2)}) collective-permute-start(f32[1024,128]{1,0:T(8,128)S(1)} %mix.14), channel_id=1, source_target_pairs={{0,8},{8,0},{16,24},{24,16},{1,9},{9,1},{17,25},{25,17},{2,10},{10... | collective-permute-start | bytes 1572872 | tf_op jit(solution)/shard_map/ppermute | solution.py:307
  73.8 22.5 %collective-permute-start.18 = (f32[1024,128]{1,0:T(8,128)S(1)}, f32[1024,128]{1,0:T(8,128)S(1)}, u32[]{:S(2)}, u32[]{:S(2)}) collective-permute-start(f32[1024,128]{1,0:T(8,128)S(1)} %mix.15), channel_id=1, source_target_pairs={{0,16},{8,24},{16,0},{24,8},{1,17},{9,25},{17,1},{25,9},{2,18},{10... | collective-permute-start | bytes 1572872 | tf_op jit(solution)/shard_map/ppermute | solution.py:307
  76.5 20.7 %collective-permute-start.19 = (f32[1024,128]{1,0:T(8,128)S(1)}, f32[1024,128]{1,0:T(8,128)S(1)}, u32[]{:S(2)}, u32[]{:S(2)}) collective-permute-start(f32[1024,128]{1,0:T(8,128)S(1)} %mix.16), channel_id=1, source_target_pairs={{0,8},{8,0},{16,24},{24,16},{1,9},{9,1},{17,25},{25,17},{2,10},{10... | collective-permute-start | bytes 1572872 | tf_op jit(solution)/shard_map/ppermute | solution.py:307
  77.0 23.8 %collective-permute-start.21 = (f32[512,128]{1,0:T(8,128)S(1)}, f32[512,128]{1,0:T(8,128)S(1)}, u32[]{:S(2)}, u32[]{:S(2)}) collective-permute-start(f32[512,128]{1,0:T(8,128)S(1)} %collective-permute-done.20), channel_id=1, source_target_pairs={{0,16},{8,24},{16,0},{24,8},{1,17},{9,25},{17,1},{25,9},{2,18},{10... | collective-permute-start | bytes 786440 | tf_op jit(solution)/shard_map/ppermute | solution.py:307
  85.1 15.7 %collective-permute-start.23 = (f32[512,128]{1,0:T(8,128)S(1)}, f32[512,128]{1,0:T(8,128)S(1)}, u32[]{:S(2)}, u32[]{:S(2)}) collective-permute-start(f32[512,128]{1,0:T(8,128)S(1)} %collective-permute-done.22), channel_id=1, source_target_pairs={{0,8},{8,0},{16,24},{24,16},{1,9},{9,1},{17,25},{25,17},{2,10},{10... | collective-permute-start | bytes 786440 | tf_op jit(solution)/shard_map/ppermute | solution.py:307
